TPU v7x, 128 devices: a whole 4x4x4 slice. The times are simulated.
128 devices in a mesh: section: 2 (over core), seq: 16 (over y, z), wsh: 4 (over x).
Axes of the slice: x: 4, y: 4, z: 4, core: 2. Of those that a mesh axis runs over, the one named last changes fastest.
Arguments:
- block_input: bfloat16 [4, 2, 2048, 1536], P('wsh', None, 'seq'), may hold values from -6 to 6
- cotangent: bfloat16 [4, 2, 2048, 1536], P('wsh', None, 'seq'), may hold values from -6 to 6
- seg_groups: int32 [4, 2], P('wsh'), may hold values from 6 to 8, as said below
- norm_gain: bfloat16 [2, 1536], P('section', ('seq', 'wsh')), may hold values from 0.5 to 1.5
- w_gate: bfloat16 [2, 1536, 3072], P('section', ('seq', 'wsh')), may hold values from -0.15625 to 0.15625
- w_inner: bfloat16 [2, 1536, 3072], P('section', ('seq', 'wsh')), may hold values from -0.15625 to 0.15625
- w_bc: bfloat16 [2, 1536, 256], P('section', ('seq', 'wsh')), may hold values from -0.15625 to 0.15625
- w_step: bfloat16 [2, 1536, 48], P('section', ('seq', 'wsh')), may hold values from -0.15625 to 0.15625
- conv_inner: bfloat16 [2, 5, 3072], P('section', None, ('seq', 'wsh')), may hold values from -0.5 to 0.5
- conv_bc: bfloat16 [2, 5, 256], P('section', None, ('seq', 'wsh')), may hold values from -0.5 to 0.5
- head_params: float32 [2, 3, 48], P('section', None, 'seq'), as said below
- inner_gain: bfloat16 [2, 3072], P('section', ('seq', 'wsh')), may hold values from 0.5 to 1.5
- w_out: bfloat16 [2, 3072, 1536], P('section', ('seq', 'wsh')), may hold values from -0.109375 to 0.109375
Outputs:
- block_out: bfloat16 [2, 4, 2, 2048, 1536], P('section', 'wsh', None, 'seq')
- input_grad: bfloat16 [2, 4, 2, 2048, 1536], P('section', 'wsh', None, 'seq')
- grad_norm_gain: float32 [2, 1536], P('section', ('seq', 'wsh'))
- grad_w_gate: float32 [2, 1536, 3072], P('section', ('seq', 'wsh'))
- grad_w_inner: float32 [2, 1536, 3072], P('section', ('seq', 'wsh'))
- grad_w_bc: float32 [2, 1536, 256], P('section', ('seq', 'wsh'))
- grad_w_step: float32 [2, 1536, 48], P('section', ('seq', 'wsh'))
- grad_conv_inner: float32 [2, 5, 3072], P('section', None, ('seq', 'wsh'))
- grad_conv_bc: float32 [2, 5, 256], P('section', None, ('seq', 'wsh'))
- grad_head_params: float32 [2, 3, 48], P('section', None, 'seq')
- grad_inner_gain: float32 [2, 3072], P('section', ('seq', 'wsh'))
- grad_w_out: float32 [2, 3072, 1536], P('section', ('seq', 'wsh'))
Inputs may be any that keep to these rules, and one draw needn't show every extreme that they name: `seg_groups`: each sequence's 2 segment lengths add up to 14 blocks; in each sequence one segment has 8 blocks and the others share the rest as evenly as possible. `head_params`: row 0 is the step bias, row 1 the logarithm of the decay factor, row 2 the skip factor.
All inputs are finite; a program needn't handle non-finite values.
Results may differ from a plain program's by a relative error of at most 0.02.
Values may be sent and summed in bfloat16 or wider, within the bound.
A program may use at most 320 MiB of HBM per device.

v0:
```python
import jax
import jax.numpy as jnp
from jax import lax
from jax.sharding import PartitionSpec as P

INNER = 3072
HEADS = 48
HDIM = 64
STATE = 128
BLOCK_LEN = 256


EPS = 1e-05
HIGH = lax.Precision.HIGHEST


def from_behind(shard, axis, by):
    peers = lax.axis_size(axis)
    pairs = [(i, i + by) for i in range(peers) if 0 <= i + by < peers]
    return lax.ppermute(shard, axis, pairs)


def normed(value, gain):
    return value * lax.rsqrt(jnp.mean(value * value, axis=-1, keepdims=True) + EPS) * gain


def gated_norm(mixer_rows, gate_rows, gain):
    return normed(mixer_rows * jax.nn.silu(gate_rows), gain)


def block_step(carried, pieces):
    inner_act, step_size, log_decay, b_rows, c_rows = pieces
    span = log_decay.shape[0]
    cum_rate = jnp.cumsum(log_decay, axis=0)
    rate_gap = cum_rate[:, None, :] - cum_rate[None, :, :]
    causal = (jnp.arange(span)[:, None] >= jnp.arange(span)[None, :])[:, :, None]
    decay_mat = jnp.where(causal, jnp.exp(jnp.where(causal, rate_gap, 0.0)), 0.0)
    scores = jnp.dot(c_rows, b_rows.T, precision=HIGH)
    mix_weights = scores[:, :, None] * decay_mat * step_size[None, :, :]
    mixed_out = jnp.einsum("tsh,shp->thp", mix_weights, inner_act, precision=HIGH)
    mixed_out = mixed_out + jnp.exp(cum_rate)[:, :, None] * jnp.einsum(
        "tn,hpn->thp", c_rows, carried, precision=HIGH
    )
    last_rate = cum_rate[-1]
    carry_w = jnp.exp(last_rate[None, :] - cum_rate) * step_size
    carried = jnp.exp(last_rate)[:, None, None] * carried + jnp.einsum(
        "sh,shp,sn->hpn", carry_w, inner_act, b_rows, precision=HIGH
    )
    return (carried, mixed_out)


def scan_states(inner_act, step_size, log_decay, b_rows, c_rows, carried):
    length = inner_act.shape[0]
    count = length // BLOCK_LEN
    head_count = inner_act.shape[1]
    pieces = (
        inner_act.reshape(count, BLOCK_LEN, head_count, HDIM),
        step_size.reshape(count, BLOCK_LEN, head_count),
        log_decay.reshape(count, BLOCK_LEN, head_count),
        b_rows.reshape(count, BLOCK_LEN, STATE),
        c_rows.reshape(count, BLOCK_LEN, STATE),
    )
    carried, outs = lax.scan(jax.checkpoint(block_step), carried, pieces)
    return (outs.reshape(length, head_count, HDIM), carried)


def mixer_local(
    inner_rows,
    shared_rows,
    step_rows,
    conv_own,
    conv_shared,
    head_vals,
    carried,
    conv_tail,
    live_start,
    live_seg,
):
    length = inner_rows.shape[0]
    own_width = inner_rows.shape[1]
    head_count = head_vals.shape[1]
    pre_conv = jnp.concatenate([inner_rows, shared_rows], axis=1)
    conv_taps = jnp.concatenate([conv_own, conv_shared], axis=1)
    rolled = jnp.roll(pre_conv, -live_start, axis=0)
    padded_rows = jnp.concatenate([conv_tail, rolled], axis=0)
    summed = (
        conv_taps[4]
        + conv_taps[0] * padded_rows[0:length]
        + conv_taps[1] * padded_rows[1 : length + 1]
    )
    summed = (
        summed
        + conv_taps[2] * padded_rows[2 : length + 2]
        + conv_taps[3] * padded_rows[3 : length + 3]
    )
    activated = jax.nn.silu(jnp.roll(summed, live_start, axis=0))
    inner_act = activated[:, :own_width].reshape(length, head_count, HDIM)
    b_rows = activated[:, own_width : own_width + STATE]
    c_rows = activated[:, own_width + STATE :]
    step_size = jax.nn.softplus(step_rows + head_vals[0]) * live_seg[:, None]
    log_decay = -step_size * jnp.exp(head_vals[1])
    mixed_out, carried_next = scan_states(inner_act, step_size, log_decay, b_rows, c_rows, carried)
    mixed_out = mixed_out + head_vals[2][None, :, None] * inner_act
    return (mixed_out.reshape(length, own_width), carried_next, pre_conv[length - 3 :])


def add_pair(left, right):
    return left + right


def per_device(
    block_input,
    cotangent,
    seg_groups,
    norm_gain,
    w_gate,
    w_inner,
    w_bc,
    w_step,
    conv_inner,
    conv_bc,
    head_params,
    inner_gain,
    w_out,
):
    section = lax.axis_index("section")
    seq_pos = lax.axis_index("seq")
    seq_count = lax.axis_size("seq")
    micro_count = block_input.shape[1]
    tok_count = block_input.shape[2]
    feat_dim = block_input.shape[3]
    seg_len = tok_count * seq_count
    head_vals = head_params[0]
    head_count = head_vals.shape[1]
    own_width = head_count * HDIM
    gathered = (
        lax.all_gather(norm_gain[0], ("seq", "wsh"), axis=0, tiled=True),
        lax.all_gather(w_gate[0], ("seq", "wsh"), axis=0, tiled=True),
        lax.all_gather(w_inner[0], ("seq", "wsh"), axis=0, tiled=True),
        lax.all_gather(w_bc[0], ("seq", "wsh"), axis=0, tiled=True),
        lax.all_gather(w_step[0], ("seq", "wsh"), axis=0, tiled=True),
        lax.all_gather(conv_inner[0], ("seq", "wsh"), axis=1, tiled=True),
        lax.all_gather(conv_bc[0], ("seq", "wsh"), axis=1, tiled=True),
        lax.all_gather(inner_gain[0], ("seq", "wsh"), axis=0, tiled=True),
        lax.all_gather(w_out[0], ("seq", "wsh"), axis=0, tiled=True),
    )
    (
        gain_all,
        gate_all,
        inner_all,
        shared_all,
        step_all,
        conv_all,
        conv_shared_all,
        mid_all,
        out_all,
    ) = gathered
    gain_in = gain_all.astype(jnp.float32)
    gain_mid = mid_all.astype(jnp.float32)
    conv_own = lax.dynamic_slice_in_dim(conv_all, seq_pos * own_width, own_width, 1).astype(
        jnp.float32
    )
    conv_shared = conv_shared_all.astype(jnp.float32)
    inputs = block_input[0]
    cot_rows = cotangent[0]
    seg_lengths = seg_groups[0]
    tok_rows = jnp.arange(tok_count, dtype=jnp.int32) + seq_pos * tok_count
    seg_cells = jnp.arange(seg_len, dtype=jnp.int32)
    received = jnp.zeros((tok_count, feat_dim), jnp.bfloat16)
    carried = jnp.zeros((head_count, HDIM, STATE), jnp.float32)
    conv_tail = jnp.zeros((3, own_width + 2 * STATE), jnp.float32)
    outputs = jnp.zeros((micro_count, tok_count, feat_dim), jnp.bfloat16)
    kept_steps = []
    for step_no in range(micro_count + 1):
        mb_index = step_no - section
        is_valid = (mb_index >= 0) & (mb_index < micro_count)
        which_slot = jnp.clip(mb_index, 0, micro_count - 1)
        own_rows = lax.dynamic_index_in_dim(inputs, which_slot, 0, keepdims=False)
        entering = jnp.where(section == 0, own_rows, received)
        residual = entering.astype(jnp.float32)
        live_start = (
            seg_len
            - lax.dynamic_index_in_dim(seg_lengths, which_slot, 0, keepdims=False) * BLOCK_LEN
        )
        live_tok = (tok_rows >= live_start).astype(jnp.float32)
        live_seg = (seg_cells >= live_start).astype(jnp.float32)
        hidden = normed(residual, gain_in).astype(jnp.bfloat16)
        gate_rows = jnp.dot(hidden, gate_all, preferred_element_type=jnp.float32)
        inner_rows = jnp.dot(hidden, inner_all, preferred_element_type=jnp.float32).astype(
            jnp.bfloat16
        )
        shared_rows = jnp.dot(hidden, shared_all, preferred_element_type=jnp.float32).astype(
            jnp.bfloat16
        )
        step_rows = jnp.dot(hidden, step_all, preferred_element_type=jnp.float32).astype(
            jnp.bfloat16
        )
        inner_heads, step_heads = (
            lax.all_to_all(
                inner_rows.reshape(tok_count, seq_count, own_width),
                "seq",
                split_axis=1,
                concat_axis=0,
                tiled=True,
            ),
            lax.all_to_all(
                step_rows.reshape(tok_count, seq_count, head_count),
                "seq",
                split_axis=1,
                concat_axis=0,
                tiled=True,
            ),
        )
        shared_seg = lax.all_gather(shared_rows, "seq", axis=0, tiled=True)
        inner_seg = inner_heads.reshape(seg_len, own_width).astype(jnp.float32)
        step_seg = step_heads.reshape(seg_len, head_count).astype(jnp.float32)
        shared_f = shared_seg.astype(jnp.float32)
        mixer_out, carried_next, tail_next = mixer_local(
            inner_seg,
            shared_f,
            step_seg,
            conv_own,
            conv_shared,
            head_vals,
            carried,
            conv_tail,
            live_start,
            live_seg,
        )
        heads_out = lax.all_to_all(
            mixer_out.astype(jnp.bfloat16).reshape(seg_len, 1, own_width),
            "seq",
            split_axis=0,
            concat_axis=1,
            tiled=True,
        )
        mixer_rows = heads_out.reshape(tok_count, INNER)
        gated = gated_norm(mixer_rows.astype(jnp.float32), gate_rows, gain_mid).astype(jnp.bfloat16)
        branch = jnp.dot(gated, out_all, preferred_element_type=jnp.float32)
        result = (residual + live_tok[:, None] * branch).astype(jnp.bfloat16)
        received = from_behind(result, "section", 1)
        current = lax.dynamic_index_in_dim(outputs, which_slot, 0, keepdims=False)
        outputs = lax.dynamic_update_index_in_dim(
            outputs, jnp.where(is_valid, result, current), which_slot, 0
        )
        kept_steps.append(
            (
                residual,
                hidden,
                gate_rows,
                inner_seg,
                shared_f,
                step_seg,
                carried,
                conv_tail,
                live_start,
                live_tok,
                live_seg,
                mixer_rows,
                gated,
            )
        )
        carried = jnp.where(is_valid, carried_next, carried)
        conv_tail = jnp.where(is_valid, tail_next, conv_tail)
    grad_totals = tuple((jnp.zeros(weight.shape, jnp.float32) for weight in gathered))
    head_total = jnp.zeros(head_vals.shape, jnp.float32)
    grad_state = jnp.zeros((head_count, HDIM, STATE), jnp.float32)
    grad_tail = jnp.zeros((3, own_width + 2 * STATE), jnp.float32)
    received_grad = jnp.zeros((tok_count, feat_dim), jnp.bfloat16)
    grads_in = jnp.zeros((micro_count, tok_count, feat_dim), jnp.bfloat16)
    for back_no in range(micro_count + 1):
        mb_index = micro_count - back_no - section
        is_valid = (mb_index >= 0) & (mb_index < micro_count)
        which_slot = jnp.clip(mb_index, 0, micro_count - 1)
        (
            residual,
            hidden,
            gate_rows,
            inner_seg,
            shared_f,
            step_seg,
            carried_in,
            tail_in,
            live_start,
            live_tok,
            live_seg,
            mixer_rows,
            gated,
        ) = kept_steps[micro_count - back_no]
        own_cot = lax.dynamic_index_in_dim(cot_rows, which_slot, 0, keepdims=False)
        grad_result = jnp.where(section == 1, own_cot, received_grad).astype(jnp.float32)
        grad_branch = (live_tok[:, None] * grad_result).astype(jnp.bfloat16)
        grad_gated = jnp.dot(grad_branch, out_all.T, preferred_element_type=jnp.float32)
        unused, gated_back = jax.vjp(
            gated_norm, mixer_rows.astype(jnp.float32), gate_rows, gain_mid
        )
        grad_mixer, grad_gate, grad_mid_gain = gated_back(grad_gated)
        grad_heads = lax.all_to_all(
            grad_mixer.astype(jnp.bfloat16).reshape(tok_count, seq_count, own_width),
            "seq",
            split_axis=1,
            concat_axis=0,
            tiled=True,
        )

        def local_mixer(
            inner_arg,
            shared_arg,
            step_arg,
            conv_arg,
            shared_conv_arg,
            head_arg,
            state_arg,
            tail_arg,
        ):
            return mixer_local(
                inner_arg,
                shared_arg,
                step_arg,
                conv_arg,
                shared_conv_arg,
                head_arg,
                state_arg,
                tail_arg,
                live_start,
                live_seg,
            )

        unused, mixer_back = jax.vjp(
            local_mixer,
            inner_seg,
            shared_f,
            step_seg,
            conv_own,
            conv_shared,
            head_vals,
            carried_in,
            tail_in,
        )
        (
            grad_inner,
            grad_shared,
            grad_step,
            grad_conv_own,
            grad_conv_shared,
            grad_head,
            state_back,
            tail_back,
        ) = mixer_back(
            (grad_heads.reshape(seg_len, own_width).astype(jnp.float32), grad_state, grad_tail)
        )
        inner_back, step_back = (
            lax.all_to_all(
                grad_inner.astype(jnp.bfloat16).reshape(seg_len, 1, own_width),
                "seq",
                split_axis=0,
                concat_axis=1,
                tiled=True,
            ),
            lax.all_to_all(
                grad_step.astype(jnp.bfloat16).reshape(seg_len, 1, head_count),
                "seq",
                split_axis=0,
                concat_axis=1,
                tiled=True,
            ),
        )
        shared_back = lax.psum_scatter(
            grad_shared.astype(jnp.bfloat16), "seq", scatter_dimension=0, tiled=True
        )
        inner_back = inner_back.reshape(tok_count, INNER)
        step_back = step_back.reshape(tok_count, HEADS)
        gate_back = grad_gate.astype(jnp.bfloat16)
        grad_hidden = jnp.dot(gate_back, gate_all.T, preferred_element_type=jnp.float32)
        grad_hidden = grad_hidden + jnp.dot(
            inner_back, inner_all.T, preferred_element_type=jnp.float32
        )
        grad_hidden = grad_hidden + jnp.dot(
            shared_back, shared_all.T, preferred_element_type=jnp.float32
        )
        grad_hidden = grad_hidden + jnp.dot(
            step_back, step_all.T, preferred_element_type=jnp.float32
        )
        unused, norm_back = jax.vjp(normed, residual, gain_in)
        grad_residual, grad_gain_in = norm_back(grad_hidden)
        sent_grad = (grad_result + grad_residual).astype(jnp.bfloat16)
        received_grad = from_behind(sent_grad, "section", -1)
        current = lax.dynamic_index_in_dim(grads_in, which_slot, 0, keepdims=False)
        grads_in = lax.dynamic_update_index_in_dim(
            grads_in, jnp.where(is_valid, sent_grad, current), which_slot, 0
        )
        grad_conv_all = lax.dynamic_update_slice_in_dim(
            jnp.zeros((5, INNER), jnp.float32), grad_conv_own, seq_pos * own_width, 1
        )
        head_total = head_total + jnp.where(is_valid, grad_head, 0.0)
        grad_state = jnp.where(is_valid, state_back, grad_state)
        grad_tail = jnp.where(is_valid, tail_back, grad_tail)
        grad_gate_w = jnp.dot(hidden.T, gate_back, preferred_element_type=jnp.float32)
        grad_inner_w = jnp.dot(hidden.T, inner_back, preferred_element_type=jnp.float32)
        grad_shared_w = jnp.dot(hidden.T, shared_back, preferred_element_type=jnp.float32)
        grad_step_w = jnp.dot(hidden.T, step_back, preferred_element_type=jnp.float32)
        grad_out_w = jnp.dot(gated.T, grad_branch, preferred_element_type=jnp.float32)
        step_grads = (
            grad_gain_in,
            grad_gate_w,
            grad_inner_w,
            grad_shared_w,
            grad_step_w,
            grad_conv_all,
            grad_conv_shared,
            grad_mid_gain,
            grad_out_w,
        )
        step_grads = tuple((jnp.where(is_valid, piece, 0.0) for piece in step_grads))
        grad_totals = jax.tree.map(add_pair, grad_totals, step_grads)
    shard_totals = (
        lax.psum_scatter(grad_totals[0], ("seq", "wsh"), scatter_dimension=0, tiled=True),
        lax.psum_scatter(grad_totals[1], ("seq", "wsh"), scatter_dimension=0, tiled=True),
        lax.psum_scatter(grad_totals[2], ("seq", "wsh"), scatter_dimension=0, tiled=True),
        lax.psum_scatter(grad_totals[3], ("seq", "wsh"), scatter_dimension=0, tiled=True),
        lax.psum_scatter(grad_totals[4], ("seq", "wsh"), scatter_dimension=0, tiled=True),
        lax.psum_scatter(grad_totals[5], ("seq", "wsh"), scatter_dimension=1, tiled=True),
        lax.psum_scatter(grad_totals[6], ("seq", "wsh"), scatter_dimension=1, tiled=True),
        lax.psum_scatter(grad_totals[7], ("seq", "wsh"), scatter_dimension=0, tiled=True),
        lax.psum_scatter(grad_totals[8], ("seq", "wsh"), scatter_dimension=0, tiled=True),
    )
    head_sum = lax.psum(head_total, "wsh")
    return (
        outputs[None, None],
        grads_in[None, None],
        shard_totals[0][None],
        shard_totals[1][None],
        shard_totals[2][None],
        shard_totals[3][None],
        shard_totals[4][None],
        shard_totals[5][None],
        shard_totals[6][None],
        head_sum[None],
        shard_totals[7][None],
        shard_totals[8][None],
    )


def solution(mesh):
    in_specs = (
        P("wsh", None, "seq", None),
        P("wsh", None, "seq", None),
        P("wsh", None),
        P("section", ("seq", "wsh")),
        P("section", ("seq", "wsh"), None),
        P("section", ("seq", "wsh"), None),
        P("section", ("seq", "wsh"), None),
        P("section", ("seq", "wsh"), None),
        P("section", None, ("seq", "wsh")),
        P("section", None, ("seq", "wsh")),
        P("section", None, "seq"),
        P("section", ("seq", "wsh")),
        P("section", ("seq", "wsh"), None),
    )
    out_specs = (
        P("section", "wsh", None, "seq", None),
        P("section", "wsh", None, "seq", None),
        P("section", ("seq", "wsh")),
        P("section", ("seq", "wsh"), None),
        P("section", ("seq", "wsh"), None),
        P("section", ("seq", "wsh"), None),
        P("section", ("seq", "wsh"), None),
        P("section", None, ("seq", "wsh")),
        P("section", None, ("seq", "wsh")),
        P("section", None, "seq"),
        P("section", ("seq", "wsh")),
        P("section", ("seq", "wsh"), None),
    )
    return jax.shard_map(
        per_device, mesh=mesh, in_specs=in_specs, out_specs=out_specs, check_vma=False
    )
```

profile of v0, /device:TPU:1, one launch (start us, length us, event | category | flops | bytes accessed | tf_op | source)
XLA Modules:
  0.0 4460.5 jit_solution(3897642099661099760)
XLA Ops:
  12.4 296.4 %all-reduce.60 = (bf16[1536]{0:T(1024)(128)(2,1)S(1)}, bf16[3072]{0:T(1024)(128)(2,1)S(1)}) all-reduce(bf16[1536]{0:T(1024)(128)(2,1)S(1)} %dynamic-update-slice.5, bf16[3072]{0:T(1024)(128)(2,1)S(1)} %dynamic-update-slice.6), channel_id=2, replica_groups=mesh['section'=2,'seq'=16,'wsh'=4] {'seq','wsh'}, use_global_device_ids=true, to_apply=%add.53 | all-reduce | flops 4608 | bytes 18432
  309.9 146.1 %all-gather.5 = bf16[1,1536,256]{2,1,0:T(8,128)(2,1)S(1)} all-gather(bf16[1,24,256]{2,1,0:T(8,128)(2,1)} %param.42), channel_id=7, replica_groups=mesh['section'=2,'seq'=16,'wsh'=4] {'seq','wsh'}, dimensions={1}, use_global_device_ids=true | all-gather | bytes 798720 | tf_op jit(solution)/shard_map/all_gather | solution.py:140
  459.6 146.0 %all-gather.1 = bf16[1,1536,48]{2,1,0:T(8,128)(2,1)S(1)} all-gather(bf16[1,24,48]{2,1,0:T(8,128)(2,1)} %param.43), channel_id=3, replica_groups=mesh['section'=2,'seq'=16,'wsh'=4] {'seq','wsh'}, dimensions={1}, use_global_device_ids=true | all-gather | bytes 149760 | tf_op jit(solution)/shard_map/all_gather | solution.py:141
  613.3 165.7 %all-gather.2 = bf16[1,5,3072]{1,0,2:T(2,128)(2,1)} all-gather(bf16[1,5,48]{1,0,2:T(2,128)(2,1)S(1)} %copy.1100), channel_id=4, replica_groups=mesh['section'=2,'seq'=16,'wsh'=4] {'seq','wsh'}, dimensions={2}, use_global_device_ids=true | all-gather | bytes 31200 | tf_op jit(solution)/shard_map/all_gather | solution.py:142
  790.1 145.4 %all-gather.3 = bf16[1,5,256]{1,0,2:T(2,128)(2,1)S(1)} all-gather(bf16[1,5,4]{1,0,2:T(2,128)(2,1)S(1)} %copy.1102), channel_id=5, replica_groups=mesh['section'=2,'seq'=16,'wsh'=4] {'seq','wsh'}, dimensions={2}, use_global_device_ids=true | all-gather | bytes 2600 | tf_op jit(solution)/shard_map/all_gather | solution.py:143
  960.7 106.3 %while.153 = (s32[]{:T(128)}, f32[3,64,128]{2,1,0:T(8,128)S(1)}, f32[8,256,3,64]{1,0,3,2:T(8,128)}, f32[8,256,3]{1,0,2:T(8,128)S(1)}, f32[8,256,3]{1,0,2:T(8,128...) while((s32[]{:T(128)}, f32[3,64,128]{2,1,0:T(8,128)S(1)}, ...), condition=%wide.region_4.6_spmd.clone, body=%wide.region_1.5_spmd.clone.sunk | while | flops 404047360 | bytes 3328984 | solution.py:63
  1085.7 10.2 all-to-all-done.2
  1120.9 169.5 %collective-permute-done = bf16[128,1536]{1,0:T(8,128)(2,1)S(1)} collective-permute-done((bf16[128,1536]{1,0:T(8,128)(2,1)S(1)}, bf16[128,1536]{1,0:T(8,128)(2,1)S(1)}, u32[]{:S(2)}, u32[]{:S(2)}) %collective-permute-start) | collective-permute-done | bytes 393248 | tf_op jit(solution)/shard_map/ppermute | solution.py:20
  1310.2 12.5 all-to-all-done.4
  1323.2 8.9 all-gather.18.cloned.1.call-done
  1351.9 99.3 %while.147 = (s32[]{:T(128)}, f32[3,64,128]{2,1,0:T(8,128)S(1)}, f32[8,256,3,64]{1,0,3,2:T(8,128)}, f32[8,256,3]{1,0,2:T(8,128)S(1)}, f32[8,256,3]{1,0,2:T(8,128...) while((s32[]{:T(128)}, f32[3,64,128]{2,1,0:T(8,128)S(1)}, ...), condition=%wide.region_10.12_spmd, body=%wide.region_7.11_spmd.sunk | while | flops 403998208 | bytes 3328465 | solution.py:63
  1475.2 10.2 all-to-all-done.5
  1533.2 11.9 all-to-all-done.7
  1575.2 113.5 %while.148 = (s32[]{:T(128)}, f32[3,64,128]{2,1,0:T(8,128)S(1)}, f32[8,256,3,64]{1,0,3,2:T(8,128)}, f32[8,256,3]{1,0,2:T(8,128)}, f32[8,256,3]{1,0,2:T(8,128)}, ...) while((s32[]{:T(128)}, f32[3,64,128]{2,1,0:T(8,128)S(1)}, ...), condition=%wide.region_16.18_spmd, body=%wide.region_13.17_spmd.sunk | while | flops 403998208 | bytes 3327449 | solution.py:63
  1709.1 11.1 all-to-all-done.8
  1752.7 40.0 while.149
  1806.3 206.4 %while.154 = (s32[]{:T(128)}, f32[3,64,128]{2,1,0:T(8,128)S(1)}, f32[8,256,3,64]{1,0,3,2:T(8,128)}, f32[8,256,3]{1,2,0:T(4,128)}, f32[8,256,3]{1,2,0:T(4,128)}, ...) while((s32[]{:T(128)}, f32[3,64,128]{2,1,0:T(8,128)S(1)}, ...), condition=%wide.region_35.39_spmd.clone, body=%wide.region_23.38_spmd.clone.sunk | while | flops 986234368 | bytes 9459651 | solution.py:63
  2033.1 11.3 dynamic_update_slice.203
  2044.5 12.5 multiply_reduce_fusion.22
  2064.6 10.5 pad_add_fusion.1
  2084.2 11.3 dynamic_update_slice.204
  2162.4 19.8 reduce-scatter.15.cloned.1.call-done
  2208.1 34.9 while.150
  2256.5 206.4 %while.151 = (s32[]{:T(128)}, f32[3,64,128]{2,1,0:T(8,128)S(1)}, f32[8,256,3,64]{1,0,3,2:T(8,128)}, f32[8,256,3]{1,2,0:T(4,128)}, f32[8,256,3]{1,2,0:T(4,128)}, ...) while((s32[]{:T(128)}, f32[3,64,128]{2,1,0:T(8,128)S(1)}, ...), condition=%wide.region_55.59_spmd, body=%wide.region_43.58_spmd.sunk | while | flops 986209792 | bytes 9263033 | solution.py:63
  2483.6 11.9 dynamic_update_slice.206
  2495.6 12.4 multiply_reduce_fusion.18
  2508.0 9.1 broadcast_multiply_fusion
  2533.3 12.1 dynamic_update_slice.207
  2605.4 23.9 reduce-scatter.17.cloned.1.call-done
  2658.2 39.8 while.155
  2708.5 201.4 %while.152 = (s32[]{:T(128)}, f32[3,64,128]{2,1,0:T(8,128)S(1)}, f32[8,256,3,64]{1,0,3,2:T(8,128)}, f32[8,256,3]{1,2,0:T(4,128)}, f32[8,256,3]{1,2,0:T(4,128)}, ...) while((s32[]{:T(128)}, f32[3,64,128]{2,1,0:T(8,128)S(1)}, ...), condition=%wide.region_75.79_spmd, body=%wide.region_63.78_spmd.sunk | while | flops 986209792 | bytes 9263033 | solution.py:63
  2929.2 11.9 dynamic_update_slice.209
  2941.1 12.4 multiply_reduce_fusion.15
  2970.5 11.9 dynamic_update_slice.210
  3015.0 46.2 %reduce-scatter.19.cloned.1.call-done = bf16[128,256]{1,0:T(8,128)(2,1)} async-done(((bf16[2048,256]{1,0:T(8,128)(2,1)}), bf16[128,256]{1,0:T(8,128)(2,1)}) %reduce-scatter.19.cloned.1.call-update) | async-done | bytes 65552 | tf_op jit(solution)/shard_map/reduce_scatter | solution.py:368
  3065.8 9.1 fusion.419
  3082.9 21.4 select_add_fusion
  3105.5 8.4 fusion.500
  3121.9 21.1 select_add_fusion.2
  3156.7 9.4 fusion.498
  3188.3 21.2 select_add_fusion.1
  3230.4 9.0 psum.7
  3240.0 46.5 %reduce-scatter.29.cloned.1.call-done = f32[48,5]{1,0:T(8,128)} async-done(((f32[3072,5]{1,0:T(8,128)}), f32[48,5]{1,0:T(8,128)}) %reduce-scatter.29.cloned.1.call-update) | async-done | bytes 976
  3296.2 289.3 %all-reduce.59 = (f32[1536]{0:T(1024)S(1)}, f32[5,256]{1,0:T(8,128)S(1)}, f32[3072]{0:T(1024)S(1)}) all-reduce(f32[1536]{0:T(1024)S(1)} %select_add_fusion.4, f32[5,256]{1,0:T(8,128)S(1)} %fusion.459, f32[3072]{0:T(1024)S(1)} %select_add_fusion.3), channel_id=14, replica_groups=mesh['section'=2,'seq'=16,'wsh'=4] {'seq','wsh'}, use_global_device_ids=true, to_apply=%region_81.85.clone | all-reduce | flops 5888 | bytes 47104
  3589.5 138.9 %reduce-scatter.25.cloned.1.call-done = f32[24,256]{1,0:T(8,128)} async-done(((f32[1536,256]{1,0:T(8,128)}), f32[24,256]{1,0:T(8,128)}) %reduce-scatter.25.cloned.1.call-update) | async-done | bytes 24592 | tf_op jit(solution)/shard_map/reduce_scatter | solution.py:420
  3728.3 242.1 %reduce-scatter.27.cloned.1.call-done = f32[48,1536]{1,0:T(8,128)} async-done(((f32[3072,1536]{1,0:T(8,128)}), f32[48,1536]{1,0:T(8,128)}) %reduce-scatter.27.cloned.1.call-update) | async-done | bytes 294928 | tf_op jit(solution)/shard_map/reduce_scatter | solution.py:425
  3970.4 241.0 %reduce-scatter.21.cloned.1.call-done = f32[24,3072]{1,0:T(8,128)} async-done(((f32[1536,3072]{1,0:T(8,128)}), f32[24,3072]{1,0:T(8,128)}) %reduce-scatter.21.cloned.1.call-update) | async-done | bytes 294928 | tf_op jit(solution)/shard_map/reduce_scatter | solution.py:418
  4211.4 242.3 %reduce-scatter.23.cloned.1.call-done = f32[24,3072]{1,0:T(8,128)} async-done(((f32[1536,3072]{1,0:T(8,128)}), f32[24,3072]{1,0:T(8,128)}) %reduce-scatter.23.cloned.1.call-update) | async-done | bytes 294928 | tf_op jit(solution)/shard_map/reduce_scatter | solution.py:419
  (2823 shorter events, 1780.7 us)
Async XLA Ops:
  7.2 771.8 %copy-start.28 = (bf16[1,2,128,1536]{3,2,1,0:T(8,128)(2,1)S(1)}, bf16[1,2,128,1536]{3,2,1,0:T(8,128)(2,1)}, u32[]{:S(2)}) copy-start(bf16[1,2,128,1536]{3,2,1,0:T(8,128)(2,1)} %param.36) | copy-start | bytes 2359300
  7.2 604.6 %copy-start.204 = (f32[1,3,3]{2,0,1:T(1,128)S(1)}, f32[1,3,3]{2,0,1:T(1,128)}, u32[]{:S(2)}) copy-start(f32[1,3,3]{2,0,1:T(1,128)} %param.46) | copy-start | bytes 112
  7.2 604.6 %copy-start.198 = (s32[1,2]{1,0:T(1,128)S(1)}, s32[1,2]{1,0:T(1,128)}, u32[]{:S(2)}) copy-start(s32[1,2]{1,0:T(1,128)} %param.38) | copy-start | bytes 28
  7.2 605.9 %copy-start.211 = (bf16[1,5,48]{2,1,0:T(8,128)(2,1)S(1)}, bf16[1,5,48]{2,1,0:T(8,128)(2,1)}, u32[]{:S(2)}) copy-start(bf16[1,5,48]{2,1,0:T(8,128)(2,1)} %param.44) | copy-start | bytes 1444
  7.2 771.8 %all-gather.22.cloned.1.call-start = ((), (), s32[]{:S(2)}) async-start(), calls=%async_computation.37 | async-start | bytes 9584640 | tf_op jit(solution)/shard_map/all_gather | solution.py:139
  8.0 931.0 %all-gather.16.cloned.1.call-start = ((), (), s32[]{:S(2)}) async-start(), calls=%async_computation.27 | async-start | bytes 1114112 | tf_op jit(solution)/shard_map/all_gather | solution.py:214
  309.9 796.9 %copy-start.157 = (f32[128]{0:T(128)}, f32[128]{0:T(128)S(1)}, u32[]{:S(2)}) copy-start(f32[128]{0:T(128)S(1)} %fusion.471) | copy-start | bytes 1540
  458.9 647.9 %all-gather.24.cloned.1.call-start = ((), (), s32[]{:S(2)}) async-start(), calls=%async_computation.38 | async-start | bytes 9584640 | tf_op jit(solution)/shard_map/all_gather | solution.py:138
  605.6 686.7 %copy-start.71 = (bf16[1,1536,48]{2,1,0:T(8,128)(2,1)}, bf16[1,1536,48]{2,1,0:T(8,128)(2,1)S(1)}, u32[]{:S(2)}) copy-start(bf16[1,1536,48]{2,1,0:T(8,128)(2,1)S(1)} %all-gather.1) | copy-start | bytes 442372
  607.7 177.7 %all-to-all-start = ((bf16[128,16,3]{0,2,1:T(4,128)(2,1)}), bf16[128,16,3]{0,2,1:T(4,128)(2,1)S(1)}, u32[]{:S(2)}, u32[]{:S(2)}) async-start(bf16[128,16,3]{0,2,1:T(4,128)(2,1)} %reshape.1354), calls=%async_computation | async-start | bytes 32768 | tf_op jit(solution)/shard_map/all_to_all | solution.py:206
  611.2 502.6 %all-gather.26.cloned.1.call-start = ((), (), s32[]{:S(2)}) async-start(), calls=%async_computation.39 | async-start | bytes 9584640 | tf_op jit(solution)/shard_map/all_gather | solution.py:145
  785.4 150.7 %all-to-all-start.1 = ((bf16[128,16,192]{0,2,1:T(8,128)(2,1)}), bf16[128,16,192]{0,2,1:T(8,128)(2,1)S(1)}, u32[]{:S(2)}, u32[]{:S(2)}) async-start(bf16[128,16,192]{0,2,1:T(8,128)(2,1)} %bitcast.110), calls=%async_computation.1 | async-start | bytes 1572864 | tf_op jit(solution)/shard_map/all_to_all | solution.py:199
  935.9 401.8 %copy-start.113 = (f32[1,448]{1,0:T(1,128)}, f32[1,448]{1,0:T(1,128)S(1)}, u32[]{:S(2)}) copy-start(f32[1,448]{1,0:T(1,128)S(1)} %get-tuple-element.2413) | copy-start | bytes 5380
  935.9 622.2 %copy-start.111 = (f32[1,448]{1,0:T(1,128)}, f32[1,448]{1,0:T(1,128)S(1)}, u32[]{:S(2)}) copy-start(f32[1,448]{1,0:T(1,128)S(1)} %get-tuple-element.2412) | copy-start | bytes 5380
  1082.0 13.9 all-to-all-start.2
  1085.6 246.5 %all-gather.18.cloned.1.call-start = ((), (), s32[]{:S(2)}) async-start(), calls=%async_computation.28 | async-start | bytes 1114112 | tf_op jit(solution)/shard_map/all_gather | solution.py:214
  1085.7 1115.0 %copy-start.74 = (f32[3072]{0:T(1024)}, f32[3072]{0:T(1024)S(1)}, u32[]{:S(2)}) copy-start(f32[3072]{0:T(1024)S(1)} %convert_element_type.576) | copy-start | bytes 36868
  1119.6 170.8 %collective-permute-start = (bf16[128,1536]{1,0:T(8,128)(2,1)S(1)}, bf16[128,1536]{1,0:T(8,128)(2,1)S(1)}, u32[]{:S(2)}, u32[]{:S(2)}) collective-permute-start(bf16[128,1536]{1,0:T(8,128)(2,1)S(1)} %get-tuple-element.2432), channel_id=1, source_target_pairs={{0,64},{1,65},{2,66},{3,67},{4,68},{5,69},{6,70},{7,71},{8,72},{9,... | collective-permute-start | bytes 1179656 | tf_op jit(solution)/shard_map/ppermute | solution.py:20
  1293.3 9.9 all-to-all-start.3
  1303.1 19.5 all-to-all-start.4
  1468.4 17.1 all-to-all-start.5
  1473.4 80.4 %all-gather.20.cloned.1.call-start = ((), (), s32[]{:S(2)}) async-start(), calls=%async_computation.29 | async-start | bytes 1114112 | tf_op jit(solution)/shard_map/all_gather | solution.py:214
  1504.1 696.5 %copy-start = (f32[128,3072]{1,0:T(8,128)}, f32[128,3072]{1,0:T(8,128)S(1)}, u32[]{:S(2)}) copy-start(f32[128,3072]{1,0:T(8,128)S(1)} %get-tuple-element.2323) | copy-start | bytes 4718596
  1505.8 5.7 collective-permute-start.1
  1511.8 674.1 %copy-start.23 = (bf16[128,1536]{1,0:T(8,128)(2,1)}, bf16[128,1536]{1,0:T(8,128)(2,1)S(1)}, u32[]{:S(2)}) copy-start(bf16[128,1536]{1,0:T(8,128)(2,1)S(1)} %get-tuple-element.2321) | copy-start | bytes 1179652
  1515.8 9.9 all-to-all-start.6
  1525.8 19.4 all-to-all-start.7
  1702.9 17.3 all-to-all-start.8
  1747.5 45.1 %all-to-all-start.9 = ((bf16[128,16,192]{0,2,1:T(8,128)(2,1)}), bf16[128,16,192]{0,2,1:T(8,128)(2,1)S(1)}, u32[]{:S(2)}, u32[]{:S(2)}) async-start(bf16[128,16,192]{0,2,1:T(8,128)(2,1)} %bitcast.1801), calls=%async_computation.9 | async-start | bytes 1572864 | tf_op jit(solution)/shard_map/all_to_all | solution.py:298
  1751.6 430.6 %reduce-scatter.15.cloned.1.call-start = ((), (), s32[]{:S(2)}) async-start(), calls=%async_computation.30 | async-start | bytes 1114112 | tf_op jit(solution)/shard_map/reduce_scatter | solution.py:368
  2109.1 15.9 all-to-all-start.11
  2125.0 17.5 all-to-all-start.10
  2187.0 5.7 collective-permute-start.2
  2203.1 40.9 all-to-all-start.12
  2207.8 421.5 %reduce-scatter.17.cloned.1.call-start = ((), (), s32[]{:S(2)}) async-start(), calls=%async_computation.31 | async-start | bytes 1114112 | tf_op jit(solution)/shard_map/reduce_scatter | solution.py:368
  2557.6 13.1 all-to-all-start.14
  2570.6 19.6 all-to-all-start.13
  2634.3 5.7 collective-permute-start.3
  2652.1 45.9 %all-to-all-start.15 = ((bf16[128,16,192]{0,2,1:T(8,128)(2,1)}), bf16[128,16,192]{0,2,1:T(8,128)(2,1)S(1)}, u32[]{:S(2)}, u32[]{:S(2)}) async-start(bf16[128,16,192]{0,2,1:T(8,128)(2,1)} %bitcast.220), calls=%async_computation.17 | async-start | bytes 1572864 | tf_op jit(solution)/shard_map/all_to_all | solution.py:298
  2656.7 404.5 %reduce-scatter.19.cloned.1.call-start = ((), (), s32[]{:S(2)}) async-start(), calls=%async_computation.32 | async-start | bytes 1114112 | tf_op jit(solution)/shard_map/reduce_scatter | solution.py:368
  2997.9 13.2 all-to-all-start.17
  3004.7 281.9 %reduce-scatter.29.cloned.1.call-start = ((), (), s32[]{:S(2)}) async-start(), calls=%async_computation.40 | async-start | bytes 1597440
  3007.4 582.1 %reduce-scatter.31.cloned.1.call-start = ((), (), s32[]{:S(2)}) async-start(), calls=%async_computation.41 | async-start | bytes 798720
  3014.9 713.4 %reduce-scatter.25.cloned.1.call-start = ((), (), s32[]{:S(2)}) async-start(), calls=%async_computation.35 | async-start | bytes 1597440 | tf_op jit(solution)/shard_map/reduce_scatter | solution.py:420
  3065.7 904.7 %reduce-scatter.27.cloned.1.call-start = ((), (), s32[]{:S(2)}) async-start(), calls=%async_computation.36 | async-start | bytes 19169280 | tf_op jit(solution)/shard_map/reduce_scatter | solution.py:425
  3104.3 1107.1 %reduce-scatter.21.cloned.1.call-start = ((), (), s32[]{:S(2)}) async-start(), calls=%async_computation.33 | async-start | bytes 19169280 | tf_op jit(solution)/shard_map/reduce_scatter | solution.py:418
  3152.2 22.0 all-to-all-start.16
  3156.6 1297.1 %reduce-scatter.23.cloned.1.call-start = ((), (), s32[]{:S(2)}) async-start(), calls=%async_computation.34 | async-start | bytes 19169280 | tf_op jit(solution)/shard_map/reduce_scatter | solution.py:419
  (218 other events, 5039.4 us)
Sparse Core Ops, SparseCore 0:
  10.8 85.2 all-gather.21
  459.0 119.6 all-gather.15
  581.5 84.1 all-gather.23
  668.3 144.0 all-gather.25
  1291.7 40.3 all-gather.17
  1513.4 40.3 all-gather.19
  2102.7 79.4 reduce-scatter.14
  2551.2 78.0 reduce-scatter.16
  2988.4 72.7 reduce-scatter.18
  3066.0 220.5 reduce-scatter.28
  3292.1 215.3 reduce-scatter.30
  3512.8 215.5 reduce-scatter.24
  3734.4 236.0 reduce-scatter.26
  3975.6 235.7 reduce-scatter.20
  4217.3 236.3 reduce-scatter.22
where the time goes:
time: 4480 us; the launch traced here: 4460 us
  waiting for transfers between devices  1260 us (28%)
  blocking collectives  1200 us (27%)
  local copies, waits for them, and re-layouts  849 us (19%)
  matrix products  590 us (13%)
  other arithmetic  432 us (10%)
  starting transfers between devices  104 us (2%)
    unnamed x2, blocking collectives  586 us
    dynamic_update_slice x136, local copies, waits for them, and re-layouts, scan_states(): carried, outs = lax.scan(jax.checkpoint(block_step), carried, pieces)  294 us
    reduce_scatter x1, waiting for transfers between devices, per_device(): lax.psum_scatter(grad_totals[2], ('seq', 'wsh'), scatter_dimension=0, til...  242 us
    reduce_scatter x1, waiting for transfers between devices, per_device(): lax.psum_scatter(grad_totals[8], ('seq', 'wsh'), scatter_dimension=0, til...  242 us
    reduce_scatter x1, waiting for transfers between devices, per_device(): lax.psum_scatter(grad_totals[1], ('seq', 'wsh'), scatter_dimension=0, til...  241 us
    ppermute x4, waiting for transfers between devices, from_behind(): return lax.ppermute(shard, axis, pairs)  177 us
    another operation x219, other arithmetic  175 us
    all_gather x1, blocking collectives, per_device(): lax.all_gather(conv_inner[0], ('seq', 'wsh'), axis=1, tiled=True)  166 us
  transfers between devices with their start and end apart: 37, of which 23 were waited for; matrix products, arithmetic and copies ran while one was open for 13% of the time, Pallas kernels for 0%

commit v1 on v0

v1 whole, which is shorter than its diff:
```python
import functools

import jax
import jax.numpy as jnp
from jax import lax
from jax.experimental import pallas as pl
from jax.experimental.pallas import tpu as pltpu
from jax.sharding import PartitionSpec as P

D = 1536
INNER = 3072
HEADS = 48
STATE = 128
BLOCK_LEN = 256
BLOCKS = 8
TOK = 128
CONV = INNER + 2 * STATE
STEP0 = CONV
SMALL0 = STEP0 + 128
WIN = SMALL0 + 128
HALF = (WIN + INNER) // 2
OWNERS = 16
OWN = 192
EPS = 1e-05
F32 = jnp.float32
BF16 = jnp.bfloat16
MESH = pl.DeviceIdType.MESH
VMEM_LIMIT = 58 * 1024 * 1024
LANES = (0, 1, 2, 8, 9, 10)
ROWS_ALL = ("seq", "wsh")


def dot32(left, right, dims=((1,), (0,))):
    return lax.dot_general(left, right, (dims, ((), ())), preferred_element_type=F32)


def split_left(exact, value, terms):
    total = None
    for _ in range(terms):
        part = value.astype(BF16)
        value = value - part.astype(F32)
        term = dot32(exact, part)
        total = term if total is None else total + term
    return total


def split_right(value, exact, terms, dims=((1,), (0,))):
    total = None
    for _ in range(terms):
        part = value.astype(BF16)
        value = value - part.astype(F32)
        term = dot32(part, exact, dims)
        total = term if total is None else total + term
    return total


def vmem():
    return pl.BlockSpec(memory_space=pltpu.VMEM)


def smem():
    return pl.BlockSpec(memory_space=pltpu.SMEM)


def layer_block(layer, rows, cols):
    return pl.BlockSpec((None, rows, cols), lambda i: (layer, 0, 0))


def whole(*dims):
    return pl.BlockSpec(dims, lambda i: (0,) * len(dims))


def pair_cols(tile, q):
    lane = lax.broadcasted_iota(jnp.int32, (TOK, 128), 1)
    a = jnp.broadcast_to(tile[:, LANES[2 * q] : LANES[2 * q] + 1], (TOK, 128))
    b = jnp.broadcast_to(tile[:, LANES[2 * q + 1] : LANES[2 * q + 1] + 1], (TOK, 128))
    return a, b, jnp.where(lane < 64, a, b)


def pair_row(row, q):
    lane = lax.broadcasted_iota(jnp.int32, (1, 128), 1)
    a = jnp.broadcast_to(row[:, LANES[2 * q] : LANES[2 * q] + 1], (1, 128))
    b = jnp.broadcast_to(row[:, LANES[2 * q + 1] : LANES[2 * q + 1] + 1], (1, 128))
    return jnp.where(lane < 64, a, b)


def to_front(tile, i):
    return pltpu.roll(tile, lax.rem(128 - 16 * i, 128), 1)


def conv_of(cat, taps):
    total = taps[4:5] + taps[3:4] * cat[8 : 8 + TOK]
    for k in range(3):
        total = total + taps[k : k + 1] * cat[5 + k : 5 + k + TOK]
    return total


def tri_of(lower):
    row = lax.broadcasted_iota(jnp.int32, (TOK, TOK), 0)
    col = lax.broadcasted_iota(jnp.int32, (TOK, TOK), 1)
    return row >= col if lower else row <= col


def head_lanes():
    lane = lax.broadcasted_iota(jnp.int32, (TOK, 128), 1)
    return (lane % 8) < 3


def states_body(live_ref, pre_ref, halo_ref, taps_ref, heads_ref, act_ref, dact_ref, dt_ref, cum_ref, ds_ref, dec_ref):
    live = live_ref[0]
    heads = heads_ref[...]
    step = pre_ref[:, STEP0 : STEP0 + 128].astype(F32) + heads[0:1]
    dt = jnp.maximum(step, 0.0) + jnp.log1p(jnp.exp(-jnp.abs(step)))
    dt = jnp.where(head_lanes(), dt, 0.0) * live
    rate = -dt * jnp.exp(heads[1:2])
    cum = split_left(tri_of(True).astype(F32).astype(BF16), rate, 3)
    dt_ref[...] = dt
    cum_ref[...] = cum
    last = jnp.broadcast_to(cum[TOK - 1 : TOK], (TOK, 128))
    dec_ref[...] = jnp.exp(last).T
    weight = dt * jnp.exp(last - cum)

    def conv_tile(cols):
        blk = pre_ref[:, cols].astype(F32)
        cat = jnp.concatenate([halo_ref[:, cols].astype(F32), blk], axis=0)
        summed = conv_of(cat, taps_ref[:, cols])
        sig = 1.0 / (1.0 + jnp.exp(-summed))
        act = summed * sig
        act_ref[:, cols] = act
        dact_ref[:, cols] = sig * (1.0 + summed * (1.0 - sig))
        return act

    b = conv_tile(pl.ds(INNER, 128)).astype(BF16)
    conv_tile(pl.ds(INNER + 128, 128))

    def group(i, carry):
        wt = to_front(weight, i)
        for q in range(3):
            base = pl.multiple_of(i * 384 + q * 128, 128)
            x = conv_tile(pl.ds(base, 128))
            scaled = (x * pair_cols(wt, q)[2]).astype(BF16)
            ds_ref[pl.ds(base, 128), :] = dot32(scaled, b, ((0,), (0,))).astype(BF16)
        return carry

    lax.fori_loop(0, 8, group, 0)


def local_states(live, pre, halo, taps, heads):
    return pl.pallas_call(
        states_body,
        out_shape=(
            jax.ShapeDtypeStruct((TOK, CONV), F32),
            jax.ShapeDtypeStruct((TOK, CONV), F32),
            jax.ShapeDtypeStruct((TOK, 128), F32),
            jax.ShapeDtypeStruct((TOK, 128), F32),
            jax.ShapeDtypeStruct((INNER, STATE), BF16),
            jax.ShapeDtypeStruct((TOK, 128), F32),
        ),
        in_specs=[smem()] + [vmem()] * 4,
        out_specs=(vmem(),) * 6,
        compiler_params=pltpu.CompilerParams(vmem_limit_bytes=VMEM_LIMIT),
        name="local_states",
    )(live, pre, halo, taps, heads)


def scan_body(
    backward, ds_ref, dec_ref, out_ref,
    got, got_dec, kept, fade, ready, final, other,
    send_a, recv_a, send_d, recv_d, send_b, recv_b, send_f, recv_f, own_a, own_d, own_b,
):
    me = lax.axis_index("seq")
    section = lax.axis_index("section")
    barrier = pltpu.get_barrier_semaphore()
    for d in range(1, OWNERS):
        pl.semaphore_signal(
            barrier, inc=1, device_id={"seq": lax.rem(me + d, OWNERS)}, device_id_type=MESH
        )
    pl.semaphore_signal(barrier, inc=1, device_id={"section": 1 - section}, device_id_type=MESH)
    pl.semaphore_wait(barrier, OWNERS)

    def out_copies(d):
        peer = lax.rem(me + d, OWNERS)
        return (
            pltpu.make_async_remote_copy(
                src_ref=ds_ref.at[peer], dst_ref=got.at[me], send_sem=send_a.at[d], recv_sem=recv_a.at[d],
                device_id={"seq": peer}, device_id_type=MESH,
            ),
            pltpu.make_async_remote_copy(
                src_ref=dec_ref.at[peer], dst_ref=got_dec.at[me], send_sem=send_d.at[d], recv_sem=recv_d.at[d],
                device_id={"seq": peer}, device_id_type=MESH,
            ),
        )

    firsts = [out_copies(d) for d in range(1, OWNERS)]
    for one, two in firsts:
        one.start()
        two.start()
    mine = pltpu.make_async_copy(ds_ref.at[me], got.at[me], own_a)
    mine.start()
    mine_dec = pltpu.make_async_copy(dec_ref.at[me], got_dec.at[me], own_d)
    mine_dec.start()
    mine.wait()
    mine_dec.wait()
    for one, two in firsts:
        one.wait()
        two.wait()

    def rows_of(dec):
        return jnp.concatenate([jnp.broadcast_to(dec[h : h + 1], (64, 128)) for h in range(3)], axis=0)

    final[...] = jnp.zeros((OWN, STATE), F32)
    fade[0] = jnp.ones((8, 128), F32)

    def step(n, carry):
        c = OWNERS - 1 - n if backward else n
        state = final[...]
        kept[c] = state
        dec = got_dec[c]
        final[...] = rows_of(dec) * state + got[c].astype(F32)
        fade[n + 1] = fade[n] * dec
        return carry

    lax.fori_loop(0, OWNERS, step, 0)
    swap = pltpu.make_async_remote_copy(
        src_ref=final, dst_ref=other, send_sem=send_f, recv_sem=recv_f,
        device_id={"section": 1 - section}, device_id_type=MESH,
    )
    swap.start()
    swap.wait()
    takes = 0 if backward else 1
    begin = jnp.where(section == takes, other[...], 0.0)

    def finish(n, carry):
        c = OWNERS - 1 - n if backward else n
        ready[c] = (kept[c] + rows_of(fade[n]) * begin).astype(BF16)
        return carry

    lax.fori_loop(0, OWNERS, finish, 0)

    def back_copy(d):
        peer = lax.rem(me + d, OWNERS)
        return pltpu.make_async_remote_copy(
            src_ref=ready.at[peer], dst_ref=out_ref.at[me], send_sem=send_b.at[d], recv_sem=recv_b.at[d],
            device_id={"seq": peer}, device_id_type=MESH,
        )

    seconds = [back_copy(d) for d in range(1, OWNERS)]
    for one in seconds:
        one.start()
    mine = pltpu.make_async_copy(ready.at[me], out_ref.at[me], own_b)
    mine.start()
    mine.wait()
    for one in seconds:
        one.wait()


def scan_states(ds, dec, backward):
    any_spec = pl.BlockSpec(memory_space=pl.ANY)
    sems = pltpu.SemaphoreType.DMA((OWNERS,))
    one = pltpu.SemaphoreType.DMA
    out = pl.pallas_call(
        functools.partial(scan_body, backward),
        out_shape=jax.ShapeDtypeStruct((OWNERS, OWN, STATE), BF16),
        in_specs=[any_spec, any_spec],
        out_specs=any_spec,
        scratch_shapes=[
            pltpu.VMEM((OWNERS, OWN, STATE), BF16),
            pltpu.VMEM((OWNERS, 8, 128), F32),
            pltpu.VMEM((OWNERS, OWN, STATE), F32),
            pltpu.VMEM((OWNERS + 1, 8, 128), F32),
            pltpu.VMEM((OWNERS, OWN, STATE), BF16),
            pltpu.VMEM((OWN, STATE), F32),
            pltpu.VMEM((OWN, STATE), F32),
            sems, sems, sems, sems, sems, sems, one, one, one, one, one,
        ],
        compiler_params=pltpu.CompilerParams(
            collective_id=2 if backward else 1, has_side_effects=True, vmem_limit_bytes=VMEM_LIMIT
        ),
        name="scan_backward" if backward else "scan_forward",
    )(ds.reshape(OWNERS, OWN, STATE), dec.reshape(OWNERS, 8, 128))
    return out.reshape(INNER, STATE)


def mix_body(
    live_ref, act_ref, dt_ref, cum_ref, state_ref, gate_ref, heads_ref, gain_ref, wout_ref, x_ref,
    raw_ref, y_ref, gated_ref, inv_ref, out_ref,
    z_s, cumt_s, square_s,
):
    live = live_ref[0]
    heads = heads_ref[...]
    b = act_ref[:, INNER : INNER + 128].astype(BF16)
    c = act_ref[:, INNER + 128 : CONV].astype(BF16)
    dt = dt_ref[...]
    cum = cum_ref[...]
    cumt_s[...] = cum.T
    causal = tri_of(True)
    scores = dot32(c, b, ((1,), (1,)))
    lane = lax.broadcasted_iota(jnp.int32, (TOK, 128), 1)
    square_s[...] = jnp.zeros((TOK, 128), F32)

    def group(i, carry):
        cum_i = to_front(cum, i)
        dt_i = to_front(dt, i)
        skip_i = pltpu.roll(heads, lax.rem(128 - 16 * i, 128), 1)[2:3]
        rows = cumt_s[pl.ds(pl.multiple_of(16 * i, 16), 16), :]
        for q in range(3):
            base = pl.multiple_of(i * 384 + q * 128, 128)
            cols = pl.ds(base, 128)
            x = act_ref[:, cols]
            cum_a, cum_b, cum_x = pair_cols(cum_i, q)
            u = x * pair_cols(dt_i, q)[2]
            mixes = []
            for cum_h, off in ((cum_a, LANES[2 * q]), (cum_b, LANES[2 * q + 1])):
                gap = cum_h - rows[off : off + 1]
                mixes.append((scores * jnp.exp(jnp.where(causal, gap, -1e30))).astype(BF16))
            terms = jnp.concatenate(
                [jnp.where(lane < 64, u, 0.0).astype(BF16), jnp.where(lane < 64, 0.0, u).astype(BF16)], axis=0
            )
            raw = dot32(jnp.concatenate(mixes, axis=1), terms)
            raw = raw + jnp.exp(cum_x) * dot32(c, state_ref[cols, :], ((1,), (1,)))
            raw_ref[:, cols] = raw
            y = (raw + pair_row(skip_i, q) * x).astype(BF16)
            y_ref[:, cols] = y
            gate = gate_ref[:, cols]
            z = y.astype(F32) * (gate / (1.0 + jnp.exp(-gate)))
            z_s[:, cols] = z
            square_s[...] += z * z
        return carry

    lax.fori_loop(0, 8, group, 0)
    total = jnp.sum(square_s[...], axis=1, keepdims=True)
    inv = jnp.broadcast_to(lax.rsqrt(total / INNER + EPS), (TOK, 128))
    inv_ref[...] = inv

    def scale(i, carry):
        cols = pl.ds(pl.multiple_of(i * 128, 128), 128)
        gated_ref[:, cols] = (z_s[:, cols] * inv * gain_ref[0:1, cols]).astype(BF16)
        return carry

    lax.fori_loop(0, 24, scale, 0)

    def project(n, carry):
        cols = pl.ds(pl.multiple_of(n * 256, 256), 256)
        branch = dot32(gated_ref[...], wout_ref[:, cols])
        out_ref[:, cols] = (x_ref[:, cols].astype(F32) + live * branch).astype(BF16)
        return carry

    lax.fori_loop(0, D // 256, project, 0)


def mix_forward(layer, live, act, dt, cum, states, gate, heads, gain, w_out, x):
    return pl.pallas_call(
        mix_body,
        grid=(1,),
        out_shape=(
            jax.ShapeDtypeStruct((TOK, INNER), F32),
            jax.ShapeDtypeStruct((TOK, INNER), BF16),
            jax.ShapeDtypeStruct((TOK, INNER), BF16),
            jax.ShapeDtypeStruct((TOK, 128), F32),
            jax.ShapeDtypeStruct((TOK, D), BF16),
        ),
        in_specs=[
            smem(), whole(TOK, CONV), whole(TOK, 128), whole(TOK, 128), whole(INNER, STATE), whole(TOK, INNER),
            whole(8, 128), whole(8, INNER), layer_block(layer, INNER, D), whole(TOK, D),
        ],
        out_specs=(
            whole(TOK, INNER), whole(TOK, INNER), whole(TOK, INNER), whole(TOK, 128), whole(TOK, D),
        ),
        scratch_shapes=[
            pltpu.VMEM((TOK, INNER), F32),
            pltpu.VMEM((TOK, 128), F32),
            pltpu.VMEM((TOK, 128), F32),
        ],
        compiler_params=pltpu.CompilerParams(vmem_limit_bytes=VMEM_LIMIT),
        name="mix_forward",
    )(live, act, dt, cum, states, gate, heads, gain, w_out, x)


def gate_back_body(
    live_ref, g_ref, wout_ref, gate_ref, y_ref, gain_ref, inv_ref, act_ref, cum_ref,
    gb_ref, dy_ref, dgate_ref, ggain_ref, ds_ref,
    gg_s, dots_s,
):
    live = live_ref[0]
    gb = (g_ref[...].astype(F32) * live).astype(BF16)
    gb_ref[...] = gb
    inv = inv_ref[...]
    c = act_ref[:, INNER + 128 : CONV].astype(BF16)
    cum = cum_ref[...]
    dots_s[...] = jnp.zeros((TOK, 128), F32)

    def first(i, carry):
        rows = pl.ds(pl.multiple_of(i * 384, 384), 384)
        gg = dot32(gb, wout_ref[rows, :], ((1,), (1,)))
        gg_s[:, rows] = gg
        for q in range(3):
            cols = pl.ds(pl.multiple_of(i * 384 + q * 128, 128), 128)
            gate = gate_ref[:, cols]
            z = y_ref[:, cols].astype(F32) * (gate / (1.0 + jnp.exp(-gate)))
            dots_s[...] += gg[:, 128 * q : 128 * q + 128] * gain_ref[0:1, cols] * z
        return carry

    lax.fori_loop(0, 8, first, 0)
    total = jnp.broadcast_to(jnp.sum(dots_s[...], axis=1, keepdims=True), (TOK, 128))
    shift = total * inv * inv * inv / INNER

    def second(i, carry):
        cum_i = to_front(cum, i)
        for q in range(3):
            cols = pl.ds(pl.multiple_of(i * 384 + q * 128, 128), 128)
            gate = gate_ref[:, cols]
            y = y_ref[:, cols].astype(F32)
            gg = gg_s[:, cols]
            sig = 1.0 / (1.0 + jnp.exp(-gate))
            act = gate * sig
            z = y * act
            dz = gg * gain_ref[0:1, cols] * inv - z * shift
            dy = (dz * act).astype(BF16)
            dy_ref[:, cols] = dy
            dgate_ref[:, cols] = (dz * y * (sig * (1.0 + gate * (1.0 - sig)))).astype(BF16)
            ggain_ref[:, cols] = jnp.broadcast_to(
                jnp.sum(gg * z * inv, axis=0, keepdims=True), (8, 128)
            )
            far = (dy.astype(F32) * jnp.exp(pair_cols(cum_i, q)[2])).astype(BF16)
            ds_ref[cols, :] = dot32(far, c, ((0,), (0,))).astype(BF16)
        return carry

    lax.fori_loop(0, 8, second, 0)


def gate_backward(layer, live, g, w_out, gate, y, gain, inv, act, cum):
    return pl.pallas_call(
        gate_back_body,
        grid=(1,),
        out_shape=(
            jax.ShapeDtypeStruct((TOK, D), BF16),
            jax.ShapeDtypeStruct((TOK, INNER), BF16),
            jax.ShapeDtypeStruct((TOK, INNER), BF16),
            jax.ShapeDtypeStruct((8, INNER), F32),
            jax.ShapeDtypeStruct((INNER, STATE), BF16),
        ),
        in_specs=[
            smem(), whole(TOK, D), layer_block(layer, INNER, D), whole(TOK, INNER), whole(TOK, INNER),
            whole(8, INNER), whole(TOK, 128), whole(TOK, CONV), whole(TOK, 128),
        ],
        out_specs=(
            whole(TOK, D), whole(TOK, INNER), whole(TOK, INNER), whole(8, INNER), whole(INNER, STATE),
        ),
        scratch_shapes=[pltpu.VMEM((TOK, INNER), F32), pltpu.VMEM((TOK, 128), F32)],
        compiler_params=pltpu.CompilerParams(vmem_limit_bytes=VMEM_LIMIT),
        name="gate_backward",
    )(live, g, w_out, gate, y, gain, inv, act, cum)


def mix_back_body(
    live_ref, pre_ref, halo_ref, taps_ref, heads_ref, act_ref, dact_ref, dt_ref, cum_ref, raw_ref, state_ref, dstate_ref, dy_ref,
    gsum_ref, dstep_ref, gtaps_ref, ghead_ref,
    cumt_s, edge_s, dscore_s, gb_s, gc_s, xdu_s, dyy_s, row_s,
):
    live = live_ref[0]
    heads = heads_ref[...]
    b = act_ref[:, INNER : INNER + 128].astype(BF16)
    c = act_ref[:, INNER + 128 : CONV].astype(BF16)
    dt = dt_ref[...]
    cum = cum_ref[...]
    cumt_s[...] = cum.T
    causal = tri_of(True)
    scores = dot32(c, b, ((1,), (1,)))
    lane = lax.broadcasted_iota(jnp.int32, (TOK, 128), 1)
    pick_row = lax.broadcasted_iota(jnp.int32, (128, 128), 0)
    pick_col = lax.broadcasted_iota(jnp.int32, (128, 128), 1)
    picks = []
    for q in range(3):
        target = jnp.where(pick_row < 64, LANES[2 * q], LANES[2 * q + 1])
        picks.append((pick_col == target).astype(F32).astype(BF16))
    for ref in (dscore_s, gb_s, gc_s, xdu_s, dyy_s, row_s, gtaps_ref):
        ref[...] = jnp.zeros_like(ref)

    def conv_back(cols, gact):
        gsum = gact * dact_ref[:, cols]
        gsum_ref[:, cols] = gsum
        blk = pre_ref[:, cols].astype(F32)
        cat = jnp.concatenate([halo_ref[:, cols].astype(F32), blk], axis=0)
        sums = [jnp.sum(gsum * cat[5 + k : 5 + k + TOK], axis=0, keepdims=True) for k in range(4)]
        sums.append(jnp.sum(gsum, axis=0, keepdims=True))
        gtaps_ref[:, cols] = jnp.concatenate(sums + [jnp.zeros((3, 128), F32)], axis=0)

    def group(i, carry):
        back = lax.rem(128 - 16 * i, 128)
        cum_i = to_front(cum, i)
        dt_i = to_front(dt, i)
        skip_i = pltpu.roll(heads, back, 1)[2:3]
        rows = cumt_s[pl.ds(pl.multiple_of(16 * i, 16), 16), :]
        x_du = jnp.zeros((TOK, 128), F32)
        dy_y = jnp.zeros((TOK, 128), F32)
        thin = jnp.zeros((16, 128), F32)
        edges = {}
        for q in range(3):
            cols = pl.ds(pl.multiple_of(i * 384 + q * 128, 128), 128)
            x = act_ref[:, cols]
            cum_a, cum_b, cum_x = pair_cols(cum_i, q)
            dt_x = pair_cols(dt_i, q)[2]
            last_x = cum_x[TOK - 1 : TOK]
            fade = jnp.exp(last_x - cum_x)
            u = x * dt_x
            u16 = u.astype(BF16)
            dy16 = dy_ref[:, cols]
            dy = dy16.astype(F32)
            nil = jnp.zeros_like(dy16)
            dys = jnp.concatenate([jnp.where(lane < 64, dy16, nil), jnp.where(lane < 64, nil, dy16)], axis=0)
            both = dot32(dys, u16, ((1,), (1,)))
            mixes = []
            for n, (cum_h, off) in enumerate(((cum_a, LANES[2 * q]), (cum_b, LANES[2 * q + 1]))):
                gap = cum_h - rows[off : off + 1]
                decay = jnp.exp(jnp.where(causal, gap, -1e30))
                mixes.append((scores * decay).astype(BF16))
                dscore_s[...] += both[n * TOK : n * TOK + TOK] * decay
            du = dot32(jnp.concatenate(mixes, axis=0), dys, ((0,), (0,)))
            state16 = state_ref[cols, :]
            dstate16 = dstate_ref[cols, :]
            du_far = fade * dot32(b, dstate16, ((1,), (1,)))
            du = du + du_far
            gc_s[...] += dot32((dy * jnp.exp(cum_x)).astype(BF16), state16)
            gb_s[...] += dot32((u * fade).astype(BF16), dstate16)
            overlap = state16.astype(F32) * dstate16.astype(F32)
            edges[LANES[2 * q]] = jnp.sum(overlap[:64], axis=0, keepdims=True)
            edges[LANES[2 * q + 1]] = jnp.sum(overlap[64:], axis=0, keepdims=True)
            x_du = x_du + split_right(x * du, picks[q], 2)
            dy_y = dy_y + split_right(dy * raw_ref[:, cols], picks[q], 2)
            thin = thin + split_right(
                jnp.concatenate(
                    [
                        jnp.broadcast_to(jnp.sum(u * du_far, axis=0, keepdims=True), (8, 128)),
                        jnp.broadcast_to(jnp.sum(dy * x, axis=0, keepdims=True), (8, 128)),
                    ],
                    axis=0,
                ),
                picks[q],
                3,
            )
            conv_back(cols, du * dt_x + pair_row(skip_i, q) * dy)
        nothing = jnp.zeros((1, 128), F32)
        edge_s[pl.ds(pl.multiple_of(16 * i, 16), 16), :] = jnp.concatenate(
            [edges.get(k, nothing) for k in range(16)], axis=0
        )
        xdu_s[...] += pltpu.roll(x_du, 16 * i, 1)
        dyy_s[...] += pltpu.roll(dy_y, 16 * i, 1)
        row_s[...] += pltpu.roll(thin, 16 * i, 1)
        return carry

    lax.fori_loop(0, 8, group, 0)
    dscore16 = dscore_s[...].astype(BF16)
    conv_back(pl.ds(INNER, 128), gb_s[...] + dot32(dscore16, c, ((0,), (0,))))
    conv_back(pl.ds(INNER + 128, 128), gc_s[...] + dot32(dscore16, b))
    ones = jnp.ones((128, 128), BF16)
    edge = split_right(edge_s[...], ones, 3).T[0:1] * jnp.exp(cum[TOK - 1 : TOK]) + row_s[0:1]
    x_du = xdu_s[...]
    drate = split_left(tri_of(False).astype(F32).astype(BF16), dyy_s[...] - dt * x_du, 3) + edge
    speed = jnp.exp(heads[1:2])
    ddt = x_du - drate * speed
    step = pre_ref[:, STEP0 : STEP0 + 128].astype(F32) + heads[0:1]
    dstep = jnp.where(head_lanes(), ddt / (1.0 + jnp.exp(-step)), 0.0) * live
    dstep_ref[...] = dstep
    ghead_ref[...] = jnp.concatenate(
        [
            jnp.sum(dstep, axis=0, keepdims=True),
            jnp.sum(-drate * dt * speed, axis=0, keepdims=True),
            row_s[8:9],
            jnp.zeros((5, 128), F32),
        ],
        axis=0,
    )


def mix_backward(live, pre, halo, taps, heads, act, dact, dt, cum, raw, states, dstates, dy):
    tile = pltpu.VMEM((TOK, 128), F32)
    return pl.pallas_call(
        mix_back_body,
        out_shape=(
            jax.ShapeDtypeStruct((TOK, CONV), F32),
            jax.ShapeDtypeStruct((TOK, 128), F32),
            jax.ShapeDtypeStruct((8, CONV), F32),
            jax.ShapeDtypeStruct((8, 128), F32),
        ),
        in_specs=[smem()] + [vmem()] * 12,
        out_specs=(vmem(),) * 4,
        scratch_shapes=[tile, tile, tile, tile, tile, tile, tile, pltpu.VMEM((16, 128), F32)],
        compiler_params=pltpu.CompilerParams(vmem_limit_bytes=VMEM_LIMIT),
        name="mix_backward",
    )(live, pre, halo, taps, heads, act, dact, dt, cum, raw, states, dstates, dy)


def input_back_body(
    gsum_ref, next_ref, dstep_ref, taps_ref, dgate_ref, win_ref, wgate_ref, x_ref, g_ref, gain_ref,
    gpre_ref, out_ref, ggain_ref,
    hid_s,
):
    def conv_tile(i, carry):
        cols = pl.ds(pl.multiple_of(i * 128, 128), 128)
        cat = jnp.concatenate([gsum_ref[:, cols], next_ref[:, cols]], axis=0)
        taps = taps_ref[:, cols]
        total = taps[3:4] * cat[:TOK]
        for k in range(3):
            total = total + taps[k : k + 1] * cat[3 - k : 3 - k + TOK]
        gpre_ref[:, cols] = total.astype(BF16)
        return carry

    lax.fori_loop(0, CONV // 128, conv_tile, 0)
    gpre_ref[:, STEP0 : STEP0 + 128] = dstep_ref[...].astype(BF16)
    gpre_ref[:, SMALL0:WIN] = jnp.zeros((TOK, 128), BF16)

    def project(n, carry):
        rows = pl.ds(pl.multiple_of(n * 256, 256), 256)
        hid_s[:, rows] = dot32(gpre_ref[...], win_ref[rows, :], ((1,), (1,))) + dot32(
            dgate_ref[...], wgate_ref[rows, :], ((1,), (1,))
        )
        return carry

    lax.fori_loop(0, D // 256, project, 0)
    x = x_ref[...].astype(F32)
    grad = hid_s[...]
    inv = lax.rsqrt(jnp.sum(x * x, axis=1, keepdims=True) / D + EPS)
    scaled = grad * gain_ref[0:1, :]
    dots = jnp.sum(scaled * x, axis=1, keepdims=True)
    dx = scaled * inv - x * (dots * inv * inv * inv / D)
    out_ref[...] = (g_ref[...].astype(F32) + dx).astype(BF16)
    ggain_ref[...] = jnp.broadcast_to(jnp.sum(grad * x * inv, axis=0, keepdims=True), (8, D))


def input_backward(layer, gsum, after, dstep, taps, dgate, w_in, w_gate, x, g, gain):
    return pl.pallas_call(
        input_back_body,
        grid=(1,),
        out_shape=(
            jax.ShapeDtypeStruct((TOK, WIN), BF16),
            jax.ShapeDtypeStruct((TOK, D), BF16),
            jax.ShapeDtypeStruct((8, D), F32),
        ),
        in_specs=[
            whole(TOK, CONV), whole(8, CONV), whole(TOK, 128), whole(8, CONV), whole(TOK, INNER),
            layer_block(layer, D, WIN), layer_block(layer, D, INNER), whole(TOK, D), whole(TOK, D), whole(8, D),
        ],
        out_specs=(whole(TOK, WIN), whole(TOK, D), whole(8, D)),
        scratch_shapes=[pltpu.VMEM((TOK, D), F32)],
        compiler_params=pltpu.CompilerParams(vmem_limit_bytes=VMEM_LIMIT),
        name="input_backward",
    )(gsum, after, dstep, taps, dgate, w_in, w_gate, x, g, gain)


def exact_parts(value):
    parts = []
    for _ in range(3):
        part = lax.reduce_precision(value, 8, 7)
        parts.append(part.astype(BF16))
        value = value - part
    return jnp.stack(parts)


def rows8(vector):
    return jnp.broadcast_to(vector[None, :], (8, vector.shape[0]))


def step_lanes(step):
    lead = step.shape[0]
    return jnp.pad(step.reshape(lead, OWNERS, 3), ((0, 0), (0, 0), (0, 5))).reshape(lead, 128)


def pack_small(norm_gain, inner_gain, conv_inner, conv_bc, heads):
    flat = jnp.concatenate(
        [norm_gain, inner_gain, conv_inner.reshape(-1), conv_bc.reshape(-1), exact_parts(heads).reshape(-1)]
    )
    return jnp.pad(flat, (0, 24 * 128 - flat.shape[0])).reshape(24, 128)


def unpack_small(cells):
    rows = cells.reshape(64, 24 * 128)
    norm_gain = rows[:, :24].reshape(D).astype(F32)
    inner_gain = rows[:, 24:72].reshape(INNER).astype(F32)
    conv_inner = rows[:, 72:312].reshape(64, 5, 48).transpose(1, 0, 2).reshape(5, INNER)
    conv_bc = rows[:, 312:332].reshape(64, 5, 4).transpose(1, 0, 2).reshape(5, 2 * STATE)
    taps = jnp.concatenate([conv_inner, conv_bc], axis=1).astype(F32)
    taps = jnp.pad(taps, ((0, 3), (0, 0)))
    heads = rows[::4, 332:359].reshape(OWNERS, 3, 3, 3).astype(F32).sum(axis=1)
    heads = jnp.pad(heads.transpose(1, 0, 2), ((0, 5), (0, 0), (0, 5))).reshape(8, 128)
    return rows8(norm_gain), rows8(inner_gain), taps, heads


def small_grads(norm_gain, inner_gain, taps, heads, seq_pos):
    conv_inner = taps[:5, :INNER].reshape(5, 64, 48).transpose(1, 0, 2).reshape(64, 240)
    conv_bc = taps[:5, INNER:].reshape(5, 64, 4).transpose(1, 0, 2).reshape(64, 20)
    head = heads[:3].reshape(3, OWNERS, 8)[:, :, :3].transpose(1, 0, 2).reshape(OWNERS, 9)
    head = jnp.repeat(head, 4, axis=0)
    flat = jnp.concatenate(
        [norm_gain.reshape(64, 24), inner_gain.reshape(64, 48), conv_inner, conv_bc, head], axis=1
    )
    return jnp.pad(flat, ((0, 0), (0, 24 * 128 - flat.shape[1]))).reshape(D, 128)


def swap_cores(value):
    return lax.ppermute(value, "section", [(0, 1), (1, 0)])


def per_device(
    block_input, cotangent, seg_groups, norm_gain, w_gate, w_inner, w_bc, w_step, conv_inner, conv_bc, head_params,
    inner_gain, w_out,
):
    section = lax.axis_index("section")
    seq_pos = lax.axis_index("seq")
    shard = jnp.concatenate(
        [
            w_inner[0],
            w_bc[0],
            step_lanes(w_step[0]),
            pack_small(norm_gain[0], inner_gain[0], conv_inner[0], conv_bc[0], head_params[0]),
        ],
        axis=1,
    )
    w_in = lax.all_gather(lax.all_gather(shard, ROWS_ALL, axis=0, tiled=True), "section", axis=0)
    w_gates = lax.all_gather(lax.all_gather(w_gate[0], ROWS_ALL, axis=0, tiled=True), "section", axis=0)
    w_outs = lax.all_gather(lax.all_gather(w_out[0], ROWS_ALL, axis=0, tiled=True), "section", axis=0)
    firsts = (BLOCKS - seg_groups[0]) * (BLOCK_LEN // TOK)
    first = jnp.where(section == 0, firsts[0], firsts[1])
    live = (seq_pos >= first).astype(F32).reshape(1)
    ring = [(s * 16 + i, s * 16 + i + 1) for s in range(2) for i in range(15)] + [(15, 16)]
    jump = [(15, 20)]
    unring = [(b, a) for a, b in ring]
    unjump = [(b, a) for a, b in jump]
    axes = ("section", "seq")

    x = lax.dynamic_index_in_dim(block_input[0], section, 0, keepdims=False)
    kept = []
    outs = []
    for layer in range(2):
        gain, mid_gain, taps, heads = unpack_small(w_in[layer, :, SMALL0:])
        x32 = x.astype(F32)
        hidden = (x32 * lax.rsqrt(jnp.mean(x32 * x32, axis=-1, keepdims=True) + EPS) * gain[0]).astype(BF16)
        pre = jnp.dot(hidden, w_in[layer], preferred_element_type=F32).astype(BF16)
        tail = pre[TOK - 8 :]
        near = lax.ppermute(tail, axes, ring)
        far = lax.ppermute(tail, axes, jump)
        halo = jnp.where(
            seq_pos == first,
            jnp.where(section == 0, jnp.zeros_like(near), jnp.where(first == 0, near, far)),
            near,
        )
        gate = jnp.dot(hidden, w_gates[layer], preferred_element_type=F32)
        act, dact, dt, cum, ds, dec = local_states(live, pre, halo, taps, heads)
        states = scan_states(ds, dec, False)
        raw, y, gated, inv, out = mix_forward(
            layer, live, act, dt, cum, states, gate, heads, mid_gain, w_outs, x
        )
        kept.append((x, hidden, pre, halo, gate, act, dact, dt, cum, dec, states, raw, y, gated, inv, gain, mid_gain, taps, heads))
        outs.append(out)
        x = out

    g = lax.dynamic_index_in_dim(cotangent[0], section, 0, keepdims=False)
    grads_in = [None, None]
    pieces = [None, None]
    for layer in (1, 0):
        (x, hidden, pre, halo, gate, act, dact, dt, cum, dec, states, raw, y, gated, inv, gain, mid_gain, taps, heads) = kept[layer]
        gb, dy, dgate, gmid, ds = gate_backward(layer, live, g, w_outs, gate, y, mid_gain, inv, act, cum)
        dstates = scan_states(ds, dec, True)
        gsum, dstep, gtaps, ghead = mix_backward(
            live, pre, halo, taps, heads, act, dact, dt, cum, raw, states, dstates, dy
        )
        head_rows = gsum[:8]
        near = lax.ppermute(head_rows, axes, unring)
        far = lax.ppermute(head_rows, axes, unjump)
        crossing = (section == 0) & (seq_pos == 15) & (firsts[1] != 0)
        after = jnp.where(crossing, far, near) * live
        gpre, g, ggain = input_backward(
            layer, gsum, after, dstep, taps, dgate, w_in, w_gates, x, g, gain
        )
        grads_in[layer] = g
        small = lax.psum(small_grads(ggain[0], gmid[0], gtaps, ghead, seq_pos), "section")
        both_hidden = lax.all_gather(hidden, "section", axis=0, tiled=True)
        both_gb = lax.all_gather(gb, "section", axis=0, tiled=True)
        both_gated = lax.all_gather(gated, "section", axis=0, tiled=True)
        both_g = lax.all_gather(jnp.concatenate([gpre, dgate], axis=1), "section", axis=0, tiled=True)
        own_g = lax.dynamic_slice_in_dim(both_g, section * HALF, HALF, 1)
        own_gb = lax.dynamic_slice_in_dim(both_gb, section * (D // 2), D // 2, 1)
        grad_in = dot32(both_hidden, own_g, ((0,), (0,))).astype(BF16)
        keep = jnp.where(section == 1, small.astype(BF16), grad_in[:, 128:256])
        grad_in = lax.dynamic_update_slice_in_dim(grad_in, keep, 128, 1)
        grad_out = dot32(both_gated, own_gb, ((0,), (0,))).astype(BF16)
        pieces[layer] = (
            lax.psum_scatter(
                lax.psum_scatter(grad_in, "seq", scatter_dimension=0, tiled=True), "wsh", scatter_dimension=0, tiled=True
            ),
            lax.psum_scatter(
                lax.psum_scatter(grad_out, "seq", scatter_dimension=0, tiled=True), "wsh", scatter_dimension=0, tiled=True
            ),
        )

    def settle(first_value, second_value):
        own = jnp.where(section == 0, first_value, second_value)
        got = swap_cores(jnp.where(section == 0, second_value, first_value))
        return jnp.where(section == 0, own, got), jnp.where(section == 0, got, own)

    out_a, out_b = settle(outs[0], outs[1])
    in_a, in_b = settle(grads_in[0], grads_in[1])
    left, right = settle(pieces[0][0], pieces[1][0])
    out_left, out_right = settle(pieces[0][1], pieces[1][1])
    grad = jnp.concatenate([left, right], axis=1).astype(F32)
    grad_out = jnp.concatenate([out_left, out_right], axis=1).astype(F32)
    cells = grad[:, SMALL0:WIN].reshape(-1)
    heads_own = cells[332:341].reshape(3, 3)
    heads_sum = lax.psum(jnp.where(lax.axis_index("wsh") == 0, heads_own, 0.0), "wsh")
    return (
        jnp.stack([out_a, out_b])[None, None],
        jnp.stack([in_a, in_b])[None, None],
        cells[:24][None],
        grad[:, WIN:][None],
        grad[:, :INNER][None],
        grad[:, INNER:CONV][None],
        grad[:, STEP0:SMALL0].reshape(24, OWNERS, 8)[:, :, :3].reshape(24, HEADS)[None],
        cells[72:312].reshape(5, 48)[None],
        cells[312:332].reshape(5, 4)[None],
        heads_sum[None],
        cells[24:72][None],
        grad_out[None],
    )


def solution(mesh):
    weight = P("section", ROWS_ALL, None)
    vector = P("section", ROWS_ALL)
    taps = P("section", None, ROWS_ALL)
    tokens = P("wsh", None, "seq", None)
    heads = P("section", None, "seq")
    result = P("section", "wsh", None, "seq", None)
    return jax.shard_map(
        per_device,
        mesh=mesh,
        in_specs=(
            tokens, tokens, P("wsh", None), vector, weight, weight, weight, weight, taps, taps, heads, vector, weight,
        ),
        out_specs=(
            result, result, vector, weight, weight, weight, weight, taps, taps, heads, vector, weight,
        ),
        check_vma=False,
    )
```

time: 4480 us -> 1160 us (0.26)
  blocking collectives: 1200 us -> 24.1 us
  local copies, waits for them, and re-layouts: 849 us -> 29.8 us
  waiting for transfers between devices: 1260 us -> 716 us
  matrix products: 590 us -> 48.3 us
  other arithmetic: 432 us -> 26.1 us
  Pallas kernels: 0 us -> 271 us
  starting transfers between devices: 104 us -> 26.3 us
    all_gather x4, blocking collectives: 603 us -> 9.99 us  [the longest x2 5.12 us: per_device(): both_gb = lax.all_gather(gb, 'section', axis=0, tiled=True)]
    unnamed x2 -> x0, blocking collectives: 586 us -> none
    reduce_scatter x7 -> x8, waiting for transfers between devices: 954 us -> 393 us  [the longest x2 182 us: per_device(): lax.psum_scatter(grad_in, 'seq', scatter_dimension=0, tiled=True)]
    dot_general x405 -> x8, matrix products: 590 us -> 48.3 us  [the longest x4 24.2 us: dot32(): lax.dot_general(left, right, (dims, ((), ())), preferred_element_type=F32)]
    dynamic_update_slice x142 -> x0, local copies, waits for them, and re-layouts: 365 us -> none  [the longest x136 294 us: scan_states(): carried, outs = lax.scan(jax.checkpoint(block_step), carried, pieces)]
    all_gather x6 -> x10, waiting for transfers between devices: 15.3 us -> 317 us  [the longest x1 88.1 us: per_device(): lax.all_gather(shard, ROWS_ALL, axis=0, tiled=True)]
    pallas_call x0 -> x14, Pallas kernels: none -> 271 us  [the longest x4 133 us: scan_states(): pl.pallas_call(functools.partial(scan_body, backward), out_shape=jax.Shap...]
    another operation x227 -> x3, other arithmetic: 175 us -> 0.15 us  [the longest x1 0.07 us: per_device(): jnp.stack([in_a, in_b])[None, None]]
  transfers between devices with their start and end apart: 37 -> 30, of which waited for: 23 -> 17; matrix products, arithmetic and copies ran while one was open for 13% -> 7% of each run, Pallas kernels for 0% -> 22%
where the time goes in v1:
time: 1160 us
  waiting for transfers between devices  716 us (62%)
  Pallas kernels  271 us (23%)
  matrix products  48.3 us (4%)
  local copies, waits for them, and re-layouts  29.8 us (3%)
  starting transfers between devices  26.3 us (2%)
  other arithmetic  26.1 us (2%)
  blocking collectives  24.1 us (2%)
  between operations  17 us (1%)
    reduce_scatter x2, waiting for transfers between devices, per_device(): lax.psum_scatter(grad_in, 'seq', scatter_dimension=0, tiled=True)  182 us
    pallas_call x4, Pallas kernels, scan_states(): pl.pallas_call(functools.partial(scan_body, backward), out_shape=jax.Shap...  133 us
    reduce_scatter x2, waiting for transfers between devices, per_device(): lax.psum_scatter(grad_out, 'seq', scatter_dimension=0, tiled=True)  126 us
    all_gather x1, waiting for transfers between devices, per_device(): lax.all_gather(shard, ROWS_ALL, axis=0, tiled=True)  88.1 us
    all_gather x1, waiting for transfers between devices, per_device(): lax.all_gather(w_out[0], ROWS_ALL, axis=0, tiled=True)  83.9 us
    all_gather x1, waiting for transfers between devices, per_device(): lax.all_gather(w_gate[0], ROWS_ALL, axis=0, tiled=True)  83.9 us
    reduce_scatter x2, waiting for transfers between devices, per_device(): lax.psum_scatter(lax.psum_scatter(grad_out, 'seq', scatter_dimension=0, t...  42.5 us
    reduce_scatter x2, waiting for transfers between devices, per_device(): lax.psum_scatter(lax.psum_scatter(grad_in, 'seq', scatter_dimension=0, ti...  42.4 us
  transfers between devices with their start and end apart: 30, of which 17 were waited for; matrix products, arithmetic and copies ran while one was open for 7% of the time, Pallas kernels for 22%

profile of v1, /device:TPU:1, one launch (start us, length us, event | category | flops | bytes accessed | tf_op | source)
XLA Modules:
  0.0 1158.8 jit_solution(10090460996938798820)
XLA Ops:
  15.3 88.1 %all-gather.16.cloned.1.call-done = bf16[1536,3584]{1,0:T(8,128)(2,1)} async-done(((bf16[24,3584]{1,0:T(8,128)(2,1)}), bf16[1536,3584]{1,0:T(8,128)(2,1)}) %all-gather.16.cloned.1.call-update) | async-done | bytes 11010064 | tf_op jit(solution)/shard_map/all_gather | solution.py:718
  103.4 83.9 %all-gather.28.cloned.1.call-done = bf16[1,1536,3072]{2,1,0:T(8,128)(2,1)} async-done(((bf16[1,24,3072]{2,1,0:T(8,128)(2,1)}), bf16[1,1536,3072]{2,1,0:T(8,128)(2,1)}) %all-gather.28.cloned.1.call-update) | async-done | bytes 9437200 | tf_op jit(solution)/shard_map/all_gather | solution.py:719
  187.4 83.9 %all-gather.32.cloned.1.call-done = bf16[1,3072,1536]{2,1,0:T(8,128)(2,1)} async-done(((bf16[1,48,1536]{2,1,0:T(8,128)(2,1)}), bf16[1,3072,1536]{2,1,0:T(8,128)(2,1)}) %all-gather.32.cloned.1.call-update) | async-done | bytes 9437200 | tf_op jit(solution)/shard_map/all_gather | solution.py:720
  275.5 37.0 %all-gather.26.cloned.1.call-done = bf16[3072,3584]{1,0:T(8,128)(2,1)} async-done(((bf16[1536,3584]{1,0:T(8,128)(2,1)}), bf16[3072,3584]{1,0:T(8,128)(2,1)}) %all-gather.26.cloned.1.call-update) | async-done | bytes 22020112 | tf_op jit(solution)/shard_map/all_gather | solution.py:718
  313.9 5.8 fusion.6.pre_ref
  319.8 3.3 collective-permute-start
  327.3 24.6 %all-gather.30.cloned.1.call-done.wgate_ref = bf16[2,1536,3072]{2,1,0:T(8,128)(2,1)} async-done(((bf16[1,1536,3072]{2,1,0:T(8,128)(2,1)}), bf16[2,1536,3072]{2,1,0:T(8,128)(2,1)}) %all-gather.30.cloned.1.call-update) | async-done | bytes 18874384 | tf_op jit(solution)/shard_map/all_gather | solution.py:719
  351.9 6.3 fusion.5.gate_ref
  361.2 8.3 local_states.2
  369.4 34.1 %scan_forward.2 = bf16[16,192,128]{2,1,0:T(8,128)(2,1)} custom-call(bf16[16,192,128]{2,1,0:T(8,128)(2,1)} %bitcast.125, f32[16,8,128]{2,1,0:T(8,128)} %bitcast.133), custom_call_target="tpu_custom_call" | custom-call | tf_op jit(solution)/shard_map/scan_forward/pallas_call | solution.py:261
  404.2 13.8 %mix_forward.2 = (f32[128,3072]{1,0:T(8,128)}, bf16[128,3072]{1,0:T(8,128)(2,1)}, bf16[128,3072]{1,0:T(8,128)(2,1)}, f32[128,128]{1,0:T(8,128)}, bf16[128,1536]{1,0:T(8,128)(2,1)}) custom-call(f32[1]{0:T(128)} %bitcast.2.live_ref, f32[128,3328]{1,0:T(8,128)} %get-tuple-element.58.act_ref, f32[128,128]{1,0:T(8,128)} %get-tuple-element.59.dt_ref, ...), custom_call_target="tpu_custom_call" | custom-call | tf_op jit(solution)/shard_map/mix_forward/pallas_call | solution.py:352
  420.4 5.7 fusion.9.pre_ref
  426.1 3.5 collective-permute-start.2
  430.6 6.3 fusion.4.gate_ref
  437.5 7.2 local_states.3
  444.7 31.3 %scan_forward.3 = bf16[16,192,128]{2,1,0:T(8,128)(2,1)} custom-call(bf16[16,192,128]{2,1,0:T(8,128)(2,1)} %bitcast.126, f32[16,8,128]{2,1,0:T(8,128)} %bitcast.135), custom_call_target="tpu_custom_call" | custom-call | tf_op jit(solution)/shard_map/scan_forward/pallas_call | solution.py:261
  476.7 13.8 %mix_forward.3 = (f32[128,3072]{1,0:T(8,128)}, bf16[128,3072]{1,0:T(8,128)(2,1)}, bf16[128,3072]{1,0:T(8,128)(2,1)}, f32[128,128]{1,0:T(8,128)}, bf16[128,1536]{1,0:T(8,128)(2,1)}) custom-call(f32[1]{0:T(128)} %bitcast.2.live_ref, f32[128,3328]{1,0:T(8,128)} %get-tuple-element.64.act_ref, f32[128,128]{1,0:T(8,128)} %get-tuple-element.65.dt_ref, ...), custom_call_target="tpu_custom_call" | custom-call | tf_op jit(solution)/shard_map/mix_forward/pallas_call | solution.py:352
  490.5 14.7 %gate_backward.2 = (bf16[128,1536]{1,0:T(8,128)(2,1)}, bf16[128,3072]{1,0:T(8,128)(2,1)}, bf16[128,3072]{1,0:T(8,128)(2,1)}, f32[8,3072]{1,0:T(8,128)}, bf16[3072,128]{1,0:T(8,128)(2,1)}) custom-call(f32[1]{0:T(128)} %bitcast.2.live_ref, bf16[128,1536]{1,0:T(8,128)(2,1)} %dynamic-slice_bitcast_fusion.g_ref, ...), custom_call_target="tpu_custom_call" | custom-call | tf_op jit(solution)/shard_map/gate_backward/pallas_call | solution.py:432
  505.1 33.3 %scan_backward.2 = bf16[16,192,128]{2,1,0:T(8,128)(2,1)} custom-call(bf16[16,192,128]{2,1,0:T(8,128)(2,1)} %bitcast.124, f32[16,8,128]{2,1,0:T(8,128)} %bitcast.136), custom_call_target="tpu_custom_call" | custom-call | tf_op jit(solution)/shard_map/scan_backward/pallas_call | solution.py:261
  538.5 15.3 %mix_backward.2 = (f32[128,3328]{1,0:T(8,128)}, f32[128,128]{1,0:T(8,128)}, f32[8,3328]{1,0:T(8,128)}, f32[8,128]{1,0:T(8,128)}) custom-call(f32[1]{0:T(128)} %bitcast.2.live_ref, bf16[128,3584]{1,0:T(8,128)(2,1)} %copy-done.6, bf16[8,3584]{1,0:T(8,128)(2,1)} %select_select_fusion.halo_ref, f32[8,3328]{1,0:T(8,128)} %fusion.34.taps_ref, ...), custom_call_target="tpu_custom_call" | custom-call | tf_op jit(solution)/shard_map/mix_backward/pallas_call | solution.py:577
  555.4 3.4 collective-permute-start.6
  562.3 18.2 %input_backward.2 = (bf16[128,3584]{1,0:T(8,128)(2,1)}, bf16[128,1536]{1,0:T(8,128)(2,1)}, f32[8,1536]{1,0:T(8,128)}) custom-call(f32[128,3328]{1,0:T(8,128)} %get-tuple-element.78.gsum_ref, f32[8,3328]{1,0:T(8,128)} %select_multiply_fusion.1.next_ref, f32[128,128]{1,0:T(8,128)} %get-tuple-element.79.dstep_ref, f32[8,3328]{1,0:T(8,128)} %fusion.34.taps_ref, ...), custom_call_target="tpu_custom_call" | custom-call | tf_op jit(solution)/shard_map/input_backward/pallas_call | solution.py:631
  580.5 2.5 pad_maximum_fusion.1
  583.0 14.7 %gate_backward.3 = (bf16[128,1536]{1,0:T(8,128)(2,1)}, bf16[128,3072]{1,0:T(8,128)(2,1)}, bf16[128,3072]{1,0:T(8,128)(2,1)}, f32[8,3072]{1,0:T(8,128)}, bf16[3072,128]{1,0:T(8,128)(2,1)}) custom-call(f32[1]{0:T(128)} %bitcast.2.live_ref, bf16[128,1536]{1,0:T(8,128)(2,1)} %get-tuple-element.81.g_ref, ...), custom_call_target="tpu_custom_call" | custom-call | tf_op jit(solution)/shard_map/gate_backward/pallas_call | solution.py:432
  597.7 33.8 %scan_backward.3 = bf16[16,192,128]{2,1,0:T(8,128)(2,1)} custom-call(bf16[16,192,128]{2,1,0:T(8,128)(2,1)} %bitcast.123, f32[16,8,128]{2,1,0:T(8,128)} %bitcast.134), custom_call_target="tpu_custom_call" | custom-call | tf_op jit(solution)/shard_map/scan_backward/pallas_call | solution.py:261
  631.5 15.3 %mix_backward.3 = (f32[128,3328]{1,0:T(8,128)}, f32[128,128]{1,0:T(8,128)}, f32[8,3328]{1,0:T(8,128)}, f32[8,128]{1,0:T(8,128)}) custom-call(f32[1]{0:T(128)} %bitcast.2.live_ref, bf16[128,3584]{1,0:T(8,128)(2,1)} %copy-done.5, bf16[8,3584]{1,0:T(8,128)(2,1)} %select_select_fusion.1.halo_ref, f32[8,3328]{1,0:T(8,128)} %fusion.32.taps_ref, ...), custom_call_target="tpu_custom_call" | custom-call | tf_op jit(solution)/shard_map/mix_backward/pallas_call | solution.py:577
  648.4 5.4 collective-permute-start.8
  656.6 17.4 %input_backward.3 = (bf16[128,3584]{1,0:T(8,128)(2,1)}, bf16[128,1536]{1,0:T(8,128)(2,1)}, f32[8,1536]{1,0:T(8,128)}) custom-call(f32[128,3328]{1,0:T(8,128)} %get-tuple-element.86.gsum_ref, f32[8,3328]{1,0:T(8,128)} %select_multiply_fusion.next_ref, f32[128,128]{1,0:T(8,128)} %get-tuple-element.87.dstep_ref, f32[8,3328]{1,0:T(8,128)} %fusion.32.taps_ref, ...), custom_call_target="tpu_custom_call" | custom-call | tf_op jit(solution)/shard_map/input_backward/pallas_call | solution.py:631
  674.0 2.5 pad_maximum_fusion
  676.6 2.8 all_gather.65
  679.4 5.0 convolution_convert_fusion.3
  687.7 5.3 convolution_convert_fusion.2
  693.1 2.5 all_gather.62
  702.6 7.9 all-reduce.10
  710.5 7.0 convolution_convert_fusion
  720.6 2.4 all_gather.60
  723.0 6.9 convolution_convert_fusion.1
  731.9 45.0 %reduce-scatter.17.cloned.1.call-done = bf16[192,768]{1,0:T(8,128)(2,1)} async-done(((bf16[3072,768]{1,0:T(8,128)(2,1)}), bf16[192,768]{1,0:T(8,128)(2,1)}) %reduce-scatter.17.cloned.1.call-update) | async-done | bytes 294928 | tf_op jit(solution)/shard_map/reduce_scatter | solution.py:791
  776.9 80.9 %reduce-scatter.21.cloned.1.call-done = bf16[192,768]{1,0:T(8,128)(2,1)} async-done(((bf16[3072,768]{1,0:T(8,128)(2,1)}), bf16[192,768]{1,0:T(8,128)(2,1)}) %reduce-scatter.21.cloned.1.call-update) | async-done | bytes 294928 | tf_op jit(solution)/shard_map/reduce_scatter | solution.py:791
  857.9 92.6 %reduce-scatter.13.cloned.1.call-done = bf16[96,3328]{1,0:T(8,128)(2,1)} async-done(((bf16[1536,3328]{1,0:T(8,128)(2,1)}), bf16[96,3328]{1,0:T(8,128)(2,1)}) %reduce-scatter.13.cloned.1.call-update) | async-done | bytes 638992 | tf_op jit(solution)/shard_map/reduce_scatter | solution.py:788
  953.7 89.2 %reduce-scatter.9.cloned.1.call-done = bf16[96,3328]{1,0:T(8,128)(2,1)} async-done(((bf16[1536,3328]{1,0:T(8,128)(2,1)}), bf16[96,3328]{1,0:T(8,128)(2,1)}) %reduce-scatter.9.cloned.1.call-update) | async-done | bytes 638992 | tf_op jit(solution)/shard_map/reduce_scatter | solution.py:788
  1043.9 19.8 %reduce-scatter.19.cloned.1.call-done = bf16[48,768]{1,0:T(8,128)(2,1)} async-done(((bf16[192,768]{1,0:T(8,128)(2,1)}), bf16[48,768]{1,0:T(8,128)(2,1)}) %reduce-scatter.19.cloned.1.call-update) | async-done | bytes 73744 | tf_op jit(solution)/shard_map/reduce_scatter | solution.py:790
  1063.7 22.7 %reduce-scatter.23.cloned.1.call-done = bf16[48,768]{1,0:T(8,128)(2,1)} async-done(((bf16[192,768]{1,0:T(8,128)(2,1)}), bf16[48,768]{1,0:T(8,128)(2,1)}) %reduce-scatter.23.cloned.1.call-update) | async-done | bytes 73744 | tf_op jit(solution)/shard_map/reduce_scatter | solution.py:790
  1087.4 3.0 collective-permute-start.11
  1092.2 18.6 %reduce-scatter.15.cloned.1.call-done = bf16[24,3328]{1,0:T(8,128)(2,1)} async-done(((bf16[96,3328]{1,0:T(8,128)(2,1)}), bf16[24,3328]{1,0:T(8,128)(2,1)}) %reduce-scatter.15.cloned.1.call-update) | async-done | bytes 159760 | tf_op jit(solution)/shard_map/reduce_scatter | solution.py:787
  1110.8 23.9 %reduce-scatter.11.cloned.1.call-done = bf16[24,3328]{1,0:T(8,128)(2,1)} async-done(((bf16[96,3328]{1,0:T(8,128)(2,1)}), bf16[24,3328]{1,0:T(8,128)(2,1)}) %reduce-scatter.11.cloned.1.call-update) | async-done | bytes 159760 | tf_op jit(solution)/shard_map/reduce_scatter | solution.py:787
  1135.6 2.4 collective-permute-start.10
  1145.1 6.3 psum.23
  (259 shorter events, 64.6 us)
Async XLA Ops:
  7.2 267.5 %copy-start = (bf16[1,2,128,1536]{3,2,1,0:T(8,128)(2,1)S(1)}, bf16[1,2,128,1536]{3,2,1,0:T(8,128)(2,1)}, u32[]{:S(2)}) copy-start(bf16[1,2,128,1536]{3,2,1,0:T(8,128)(2,1)} %param.14) | copy-start | bytes 2359300
  7.2 96.2 %all-gather.16.cloned.1.call-start = ((), (), s32[]{:S(2)}) async-start(), calls=%async_computation.8 | async-start | bytes 11182080 | tf_op jit(solution)/shard_map/all_gather | solution.py:718
  13.7 173.6 %all-gather.28.cloned.1.call-start = ((), (), s32[]{:S(2)}) async-start(), calls=%async_computation.22 | async-start | bytes 9584640 | tf_op jit(solution)/shard_map/all_gather | solution.py:719
  14.5 256.8 %all-gather.32.cloned.1.call-start = ((), (), s32[]{:S(2)}) async-start(), calls=%async_computation.24 | async-start | bytes 9584640 | tf_op jit(solution)/shard_map/all_gather | solution.py:720
  15.2 297.2 %all-gather.26.cloned.1.call-start = ((), (), s32[]{:S(2)}) async-start(), calls=%async_computation.21 | async-start | bytes 33030144 | tf_op jit(solution)/shard_map/all_gather | solution.py:718
  103.4 248.5 %all-gather.30.cloned.1.call-start = ((), (), s32[]{:S(2)}) async-start(), calls=%async_computation.23 | async-start | bytes 28311552 | tf_op jit(solution)/shard_map/all_gather | solution.py:719
  187.4 216.2 %all-gather.34.cloned.1.call-start = ((), (), s32[]{:S(2)}) async-start(), calls=%async_computation.25 | async-start | bytes 28311552 | tf_op jit(solution)/shard_map/all_gather | solution.py:720
  271.3 2.6 copy-start.13
  271.3 408.0 %all-gather.22.cloned.1.call-start = ((), (), s32[]{:S(2)}) async-start(), calls=%async_computation.15 | async-start | bytes 2359296 | tf_op jit(solution)/shard_map/all_gather | solution.py:778
  319.7 38.4 %copy-start.5 = (bf16[128,3584]{1,0:T(8,128)(2,1)}, bf16[128,3584]{1,0:T(8,128)(2,1)S(1)}, u32[]{:S(2)}) copy-start(bf16[128,3584]{1,0:T(8,128)(2,1)S(1)} %fusion.6.pre_ref) | copy-start | bytes 2752516
  319.8 40.8 %collective-permute-start = (bf16[8,3584]{1,0:T(8,128)(2,1)S(1)}, bf16[8,3584]{1,0:T(8,128)(2,1)S(1)}, u32[]{:S(2)}, u32[]{:S(2)}) collective-permute-start(bf16[8,3584]{1,0:T(8,128)(2,1)S(1)} %slice.199), channel_id=1, source_target_pairs={{0,4},{4,8},{8,12},{12,16},{16,20},{20,24},{24,28},{28,32},{32,36}... | collective-permute-start | bytes 172040 | tf_op jit(solution)/shard_map/ppermute | solution.py:739
  323.1 37.5 %collective-permute-start.1 = (bf16[8,3584]{1,0:T(8,128)(2,1)S(1)}, bf16[8,3584]{1,0:T(8,128)(2,1)S(1)}, u32[]{:S(2)}, u32[]{:S(2)}) collective-permute-start(bf16[8,3584]{1,0:T(8,128)(2,1)S(1)} %slice.199), channel_id=1, source_target_pairs={{60,80},{61,81},{62,82},{63,83}} | collective-permute-start | bytes 172040 | tf_op jit(solution)/shard_map/ppermute | solution.py:740
  426.1 10.8 copy-start.6
  426.1 10.8 collective-permute-start.2
  429.7 7.2 collective-permute-start.3
  430.4 257.4 %all-gather.24.cloned.1.call-start = ((), (), s32[]{:S(2)}) async-start(), calls=%async_computation.18 | async-start | bytes 2359296 | tf_op jit(solution)/shard_map/all_gather | solution.py:778
  554.7 4.8 collective-permute-start.5
  555.4 5.6 collective-permute-start.6
  559.5 151.0 %all-gather.20.cloned.1.call-start = ((), (), s32[]{:S(2)}) async-start(), calls=%async_computation.12 | async-start | bytes 5111808 | tf_op jit(solution)/shard_map/all_gather | solution.py:779
  562.3 18.2 %copy-start.7 = (bf16[128,3072]{1,0:T(8,128)(2,1)S(1)}, bf16[128,3072]{1,0:T(8,128)(2,1)}, u32[]{:S(2)}) copy-start(bf16[128,3072]{1,0:T(8,128)(2,1)} %get-tuple-element.80.dgate_ref) | copy-start | bytes 2359300
  583.0 140.0 %all-gather.18.cloned.1.call-start = ((), (), s32[]{:S(2)}) async-start(), calls=%async_computation.9 | async-start | bytes 5111808 | tf_op jit(solution)/shard_map/all_gather | solution.py:779
  647.7 6.0 collective-permute-start.7
  648.4 6.9 collective-permute-start.8
  656.6 17.4 %copy-start.8 = (bf16[128,3072]{1,0:T(8,128)(2,1)S(1)}, bf16[128,3072]{1,0:T(8,128)(2,1)}, u32[]{:S(2)}) copy-start(bf16[128,3072]{1,0:T(8,128)(2,1)} %get-tuple-element.88.dgate_ref) | copy-start | bytes 2359300
  673.9 2.6 copy-start.12
  676.5 100.3 %reduce-scatter.17.cloned.1.call-start = ((), (), s32[]{:S(2)}) async-start(), calls=%async_computation.16 | async-start | bytes 5013504 | tf_op jit(solution)/shard_map/reduce_scatter | solution.py:791
  684.4 1.0 copy-start.11
  684.4 173.5 %reduce-scatter.21.cloned.1.call-start = ((), (), s32[]{:S(2)}) async-start(), calls=%async_computation.19 | async-start | bytes 5013504 | tf_op jit(solution)/shard_map/reduce_scatter | solution.py:791
  693.0 2.6 copy-start.14
  693.0 4.2 copy-start.16
  693.0 4.6 copy-start.15
  693.1 257.5 %reduce-scatter.13.cloned.1.call-start = ((), (), s32[]{:S(2)}) async-start(), calls=%async_computation.13 | async-start | bytes 10862592 | tf_op jit(solution)/shard_map/reduce_scatter | solution.py:788
  693.1 7.6 copy-start.17
  719.5 1.0 copy-start.3
  719.5 323.4 %reduce-scatter.9.cloned.1.call-start = ((), (), s32[]{:S(2)}) async-start(), calls=%async_computation.10 | async-start | bytes 10862592 | tf_op jit(solution)/shard_map/reduce_scatter | solution.py:788
  731.8 218.8 %copy-start.2 = (bf16[128,1536]{1,0:T(8,128)(2,1)S(1)}, bf16[128,1536]{1,0:T(8,128)(2,1)}, u32[]{:S(2)}) copy-start(bf16[128,1536]{1,0:T(8,128)(2,1)} %get-tuple-element.63.x_ref) | copy-start | bytes 1179652
  731.8 218.8 %copy-start.9 = (bf16[128,1536]{1,0:T(8,128)(2,1)S(1)}, bf16[128,1536]{1,0:T(8,128)(2,1)}, u32[]{:S(2)}) copy-start(bf16[128,1536]{1,0:T(8,128)(2,1)} %get-tuple-element.69) | copy-start | bytes 1179652
  731.8 220.5 %copy-start.4 = (bf16[128,1536]{1,0:T(8,128)(2,1)S(1)}, bf16[128,1536]{1,0:T(8,128)(2,1)}, u32[]{:S(2)}) copy-start(bf16[128,1536]{1,0:T(8,128)(2,1)} %get-tuple-element.81.g_ref) | copy-start | bytes 1179652
  731.8 220.5 %copy-start.10 = (bf16[128,1536]{1,0:T(8,128)(2,1)S(1)}, bf16[128,1536]{1,0:T(8,128)(2,1)}, u32[]{:S(2)}) copy-start(bf16[128,1536]{1,0:T(8,128)(2,1)} %get-tuple-element.89) | copy-start | bytes 1179652
  731.8 331.9 %reduce-scatter.19.cloned.1.call-start = ((), (), s32[]{:S(2)}) async-start(), calls=%async_computation.17 | async-start | bytes 368640 | tf_op jit(solution)/shard_map/reduce_scatter | solution.py:790
  776.9 309.5 %reduce-scatter.23.cloned.1.call-start = ((), (), s32[]{:S(2)}) async-start(), calls=%async_computation.20 | async-start | bytes 368640 | tf_op jit(solution)/shard_map/reduce_scatter | solution.py:790
  857.9 252.9 %reduce-scatter.15.cloned.1.call-start = ((), (), s32[]{:S(2)}) async-start(), calls=%async_computation.14 | async-start | bytes 798720 | tf_op jit(solution)/shard_map/reduce_scatter | solution.py:787
  950.6 184.1 %reduce-scatter.11.cloned.1.call-start = ((), (), s32[]{:S(2)}) async-start(), calls=%async_computation.11 | async-start | bytes 798720 | tf_op jit(solution)/shard_map/reduce_scatter | solution.py:787
  950.7 3.0 collective-permute-start.4
  952.4 91.5 %collective-permute-start.9 = (bf16[128,1536]{1,0:T(8,128)(2,1)S(1)}, bf16[128,1536]{1,0:T(8,128)(2,1)S(1)}, u32[]{:S(2)}, u32[]{:S(2)}) collective-permute-start(bf16[128,1536]{1,0:T(8,128)(2,1)S(1)} %broadcast_select_fusion), channel_id=1, source_target_pairs={{0,64},{64,0},{1,65},{65,1},{2,66},{66,2},{3,67},{67,3},{4,68},{68... | collective-permute-start | bytes 1179656 | tf_op jit(solution)/shard_map/ppermute | solution.py:700
  1086.4 65.5 %copy-start.1 = (bf16[1,2,128,1536]{3,2,1,0:T(8,128)(2,1)S(1)}, bf16[1,2,128,1536]{3,2,1,0:T(8,128)(2,1)}, u32[]{:S(2)}) copy-start(bf16[1,2,128,1536]{3,2,1,0:T(8,128)(2,1)} %param.14) | copy-start | bytes 2359300
  1087.4 3.9 collective-permute-start.11
  1135.6 3.4 collective-permute-start.10
  (1 other events, 0.7 us)
Sparse Core Ops, SparseCore 0:
  13.9 89.4 all-gather.15
  106.1 81.1 all-gather.27
  190.1 81.1 all-gather.31
  272.8 39.5 all-gather.25
  314.0 37.8 all-gather.29
  353.4 38.0 all-gather.33
  430.5 12.7 all-gather.21
  559.6 12.0 all-gather.23
  583.1 18.3 all-gather.19
  676.6 18.2 all-gather.17
  698.3 78.5 reduce-scatter.16
  780.1 77.7 reduce-scatter.20
  861.4 89.0 reduce-scatter.12
  954.3 88.5 reduce-scatter.8
  1045.1 18.5 reduce-scatter.18
  1066.0 20.3 reduce-scatter.22
  1088.6 22.0 reduce-scatter.14
  1113.0 21.5 reduce-scatter.10

commit v2 on v1

v2 whole, which is shorter than its diff:
```python
import functools

import jax
import jax.numpy as jnp
from jax import lax
from jax.experimental import pallas as pl
from jax.experimental.pallas import tpu as pltpu
from jax.sharding import PartitionSpec as P

D = 1536
INNER = 3072
HEADS = 48
STATE = 128
BLOCK_LEN = 256
BLOCKS = 8
TOK = 128
CONV = INNER + 2 * STATE
HALF = CONV
GATE0 = 256
CUT = HALF // 2
WALF = D // 2
OWNERS = 16
OWN = 192
EPS = 1e-05
F32 = jnp.float32
BF16 = jnp.bfloat16
MESH = pl.DeviceIdType.MESH
VMEM_LIMIT = 58 * 1024 * 1024
LANES = (0, 1, 2, 8, 9, 10)
ROWS_ALL = ("seq", "wsh")


def dot32(left, right, dims=((1,), (0,))):
    return lax.dot_general(left, right, (dims, ((), ())), preferred_element_type=F32)


def split_left(exact, value, terms):
    total = None
    for _ in range(terms):
        part = value.astype(BF16)
        value = value - part.astype(F32)
        term = dot32(exact, part)
        total = term if total is None else total + term
    return total


def split_right(value, exact, terms, dims=((1,), (0,))):
    total = None
    for _ in range(terms):
        part = value.astype(BF16)
        value = value - part.astype(F32)
        term = dot32(part, exact, dims)
        total = term if total is None else total + term
    return total


def vmem():
    return pl.BlockSpec(memory_space=pltpu.VMEM)


def smem():
    return pl.BlockSpec(memory_space=pltpu.SMEM)


def whole(*dims):
    return pl.BlockSpec(dims, lambda i: (0,) * len(dims))


def pair_cols(tile, q):
    lane = lax.broadcasted_iota(jnp.int32, (TOK, 128), 1)
    a = jnp.broadcast_to(tile[:, LANES[2 * q] : LANES[2 * q] + 1], (TOK, 128))
    b = jnp.broadcast_to(tile[:, LANES[2 * q + 1] : LANES[2 * q + 1] + 1], (TOK, 128))
    return a, b, jnp.where(lane < 64, a, b)


def pair_row(row, q):
    lane = lax.broadcasted_iota(jnp.int32, (1, 128), 1)
    a = jnp.broadcast_to(row[:, LANES[2 * q] : LANES[2 * q] + 1], (1, 128))
    b = jnp.broadcast_to(row[:, LANES[2 * q + 1] : LANES[2 * q + 1] + 1], (1, 128))
    return jnp.where(lane < 64, a, b)


def to_front(tile, i):
    return pltpu.roll(tile, lax.rem(128 - 16 * i, 128), 1)


def conv_of(cat, taps):
    total = taps[4:5] + taps[3:4] * cat[8 : 8 + TOK]
    for k in range(3):
        total = total + taps[k : k + 1] * cat[5 + k : 5 + k + TOK]
    return total


def tri_of(lower):
    row = lax.broadcasted_iota(jnp.int32, (TOK, TOK), 0)
    col = lax.broadcasted_iota(jnp.int32, (TOK, TOK), 1)
    return row >= col if lower else row <= col


def head_lanes():
    lane = lax.broadcasted_iota(jnp.int32, (TOK, 128), 1)
    return (lane % 8) < 3


def input_back_body(
    gsum_ref, next_ref, dstep_ref, taps_ref, dgate_ref, w_ref, x_ref, g_ref, gain_ref,
    gpre_ref, gside_ref, out_ref, ggain_ref,
    hid_s,
):
    def conv_tile(i, carry):
        cols = pl.ds(pl.multiple_of(i * 128, 128), 128)
        cat = jnp.concatenate([gsum_ref[:, cols], next_ref[:, cols]], axis=0)
        taps = taps_ref[:, cols]
        total = taps[3:4] * cat[:TOK]
        for k in range(3):
            total = total + taps[k : k + 1] * cat[3 - k : 3 - k + TOK]
        gpre_ref[:, cols] = total.astype(BF16)
        return carry

    lax.fori_loop(0, CONV // 128, conv_tile, 0)
    gside_ref[:, :128] = dstep_ref[...].astype(BF16)
    gside_ref[:, 128:GATE0] = jnp.zeros((TOK, 128), BF16)
    gside_ref[:, GATE0:] = dgate_ref[...]

    def project(n, carry):
        rows = pl.ds(pl.multiple_of(n * 256, 256), 256)
        hid_s[:, rows] = dot32(gpre_ref[...], w_ref[0, rows, :], ((1,), (1,))) + dot32(
            gside_ref[...], w_ref[1, rows, :], ((1,), (1,))
        )
        return carry

    lax.fori_loop(0, D // 256, project, 0)
    x = x_ref[...].astype(F32)
    grad = hid_s[...]
    inv = lax.rsqrt(jnp.sum(x * x, axis=1, keepdims=True) / D + EPS)
    scaled = grad * gain_ref[0:1, :]
    dots = jnp.sum(scaled * x, axis=1, keepdims=True)
    dx = scaled * inv - x * (dots * inv * inv * inv / D)
    out_ref[...] = (g_ref[...].astype(F32) + dx).astype(BF16)
    ggain_ref[...] = jnp.broadcast_to(jnp.sum(grad * x * inv, axis=0, keepdims=True), (8, D))


def input_backward(gsum, after, dstep, taps, dgate, w_in, x, g, gain):
    return pl.pallas_call(
        input_back_body,
        grid=(1,),
        out_shape=(
            jax.ShapeDtypeStruct((TOK, HALF), BF16),
            jax.ShapeDtypeStruct((TOK, HALF), BF16),
            jax.ShapeDtypeStruct((TOK, D), BF16),
            jax.ShapeDtypeStruct((8, D), F32),
        ),
        in_specs=[
            whole(TOK, CONV), whole(8, CONV), whole(TOK, 128), whole(8, CONV), whole(TOK, INNER),
            whole(2, D, HALF), whole(TOK, D), whole(TOK, D), whole(8, D),
        ],
        out_specs=(whole(TOK, HALF), whole(TOK, HALF), whole(TOK, D), whole(8, D)),
        scratch_shapes=[pltpu.VMEM((TOK, D), F32)],
        compiler_params=pltpu.CompilerParams(vmem_limit_bytes=VMEM_LIMIT),
        name="input_backward",
    )(gsum, after, dstep, taps, dgate, w_in, x, g, gain)


def exact_parts(value):
    parts = []
    for _ in range(3):
        part = lax.reduce_precision(value, 8, 7)
        parts.append(part.astype(BF16))
        value = value - part
    return jnp.stack(parts)


def rows8(vector):
    return jnp.broadcast_to(vector[None, :], (8, vector.shape[0]))


def step_lanes(step):
    lead = step.shape[0]
    return jnp.pad(step.reshape(lead, OWNERS, 3), ((0, 0), (0, 0), (0, 5))).reshape(lead, 128)


def pack_small(norm_gain, inner_gain, conv_inner, conv_bc, heads):
    flat = jnp.concatenate(
        [norm_gain, inner_gain, conv_inner.reshape(-1), conv_bc.reshape(-1), exact_parts(heads).reshape(-1)]
    )
    return jnp.pad(flat, (0, 24 * 128 - flat.shape[0])).reshape(24, 128)


def unpack_small(cells):
    rows = cells.reshape(64, 24 * 128)
    norm_gain = rows[:, :24].reshape(D).astype(F32)
    inner_gain = rows[:, 24:72].reshape(INNER).astype(F32)
    conv_inner = rows[:, 72:312].reshape(64, 5, 48).transpose(1, 0, 2).reshape(5, INNER)
    conv_bc = rows[:, 312:332].reshape(64, 5, 4).transpose(1, 0, 2).reshape(5, 2 * STATE)
    taps = jnp.concatenate([conv_inner, conv_bc], axis=1).astype(F32)
    taps = jnp.pad(taps, ((0, 3), (0, 0)))
    heads = rows[::4, 332:359].reshape(OWNERS, 3, 3, 3).astype(F32).sum(axis=1)
    heads = jnp.pad(heads.transpose(1, 0, 2), ((0, 5), (0, 0), (0, 5))).reshape(8, 128)
    return rows8(norm_gain), rows8(inner_gain), taps, heads


def small_grads(norm_gain, inner_gain, taps, heads, seq_pos):
    conv_inner = taps[:5, :INNER].reshape(5, 64, 48).transpose(1, 0, 2).reshape(64, 240)
    conv_bc = taps[:5, INNER:].reshape(5, 64, 4).transpose(1, 0, 2).reshape(64, 20)
    head = heads[:3].reshape(3, OWNERS, 8)[:, :, :3].transpose(1, 0, 2).reshape(OWNERS, 9)
    head = jnp.repeat(head, 4, axis=0)
    flat = jnp.concatenate(
        [norm_gain.reshape(64, 24), inner_gain.reshape(64, 48), conv_inner, conv_bc, head], axis=1
    )
    return jnp.pad(flat, ((0, 0), (0, 24 * 128 - flat.shape[1]))).reshape(D, 128)


def swap_cores(value):
    return lax.ppermute(value, "section", [(0, 1), (1, 0)])


def places():
    section = lax.axis_index("section")
    seq = lax.axis_index("seq")
    return section, seq // 4, lax.rem(seq, 4), lax.axis_index("wsh")


def x_peer(k):
    return {"wsh": lax.rem(lax.axis_index("wsh") + k, 4)}


def z_peer(k):
    _, y, z, _ = places()
    return {"seq": y * 4 + lax.rem(z + k, 4)}


def y_peer(k):
    _, y, z, _ = places()
    return {"seq": lax.rem(y + k, 4) * 4 + z}


def greet(with_sibling):
    barrier = pltpu.get_barrier_semaphore()
    for k in range(1, 4):
        for peer in (x_peer(k), y_peer(k), z_peer(k)):
            pl.semaphore_signal(barrier, inc=1, device_id=peer, device_id_type=MESH)
    if with_sibling:
        section = lax.axis_index("section")
        pl.semaphore_signal(barrier, inc=1, device_id={"section": 1 - section}, device_id_type=MESH)
    pl.semaphore_wait(barrier, 10 if with_sibling else 9)


def remote(src, dst, sems, index, peer):
    copy = pltpu.make_async_remote_copy(
        src_ref=src, dst_ref=dst, send_sem=sems[0].at[index], recv_sem=sems[1].at[index],
        device_id=peer, device_id_type=MESH,
    )
    copy.start()
    return copy


def gather_body(p_ref, o_ref, p1_ref, o1_ref, w_ref, wo_ref, pa, pb, po, stage, rows_s, stage1, rows1, send_s, recv_s, own_s):
    c, y, z, x = places()
    sems = (send_s, recv_s)
    greet(True)
    started = []

    def go(src, dst, index, peer):
        copy = remote(src, dst, sems, index, peer)
        started.append(copy)
        return copy

    first = [go(p_ref, stage.at[x], k - 1, x_peer(k)) for k in range(1, 4)]
    out_z = [go(o_ref, wo_ref.at[c, y, z, x], 2 + k, z_peer(k)) for k in range(1, 4)]
    own_o = pltpu.make_async_copy(o_ref, wo_ref.at[c, y, z, x], own_s.at[0])
    own_o.start()
    first1 = [go(p1_ref, stage1.at[x], 99 + k, x_peer(k)) for k in range(1, 4)]
    out1_z = [go(o1_ref, po.at[y, z], 102 + k, z_peer(k)) for k in range(1, 4)]
    own_o1 = pltpu.make_async_copy(o1_ref, po.at[y, z], own_s.at[2])
    own_o1.start()
    stage[x] = p_ref[...]
    stage1[x] = p1_ref[...]
    for copy in first:
        copy.wait_recv()
    rows_s[...] = jnp.concatenate([stage[n].astype(F32)[:24] for n in range(4)], axis=0).astype(BF16)
    left = pl.ds(0, CUT)
    right = pl.ds(CUT, CUT)
    a_z = [go(rows_s.at[:, left], w_ref.at[c, y, z, :, left], 5 + k, z_peer(k)) for k in range(1, 4)]
    b_y = [go(rows_s.at[:, right], w_ref.at[c, y, z, :, right], 8 + k, y_peer(k)) for k in range(1, 4)]
    own_w = pltpu.make_async_copy(rows_s, w_ref.at[c, y, z], own_s.at[1])
    own_w.start()
    own_o.wait()
    own_w.wait()
    sibling = {"section": 1 - c}
    arrivals = []
    passed = []
    peers = (y_peer, z_peer, x_peer)

    def band(kind, n, moved):
        if kind == 0:
            return w_ref.at[c, lax.rem(y + 4 - moved, 4), lax.rem(z + 4 - n, 4), :, left]
        if kind == 1:
            return w_ref.at[c, lax.rem(y + 4 - n, 4), lax.rem(z + 4 - moved, 4), :, right]
        return wo_ref.at[c, lax.rem(y + 4 - n, 4), :, lax.rem(x + 4 - moved, 4)]

    def spread_out(j):
        for k in range(1, 4):
            for kind in range(3):
                part = band(kind, j, 0)
                arrivals.append((kind, j, k, go(part, part, 12 + 12 * kind + 3 * j + k - 1, peers[kind](k))))
        for kind in range(3):
            part = band(kind, j, 0)
            passed.append(go(part, part, 48 + 16 * kind + j, sibling))

    for copy in out_z:
        copy.wait_recv()
    out_y = [go(band(2, 0, 0), band(2, 0, 0), 96 + k, y_peer(k)) for k in range(1, 4)]
    spread_out(0)
    for j in range(1, 4):
        a_z[j - 1].wait_recv()
        b_y[j - 1].wait_recv()
        out_y[j - 1].wait_recv()
        spread_out(j)
    for copy in first1:
        copy.wait_recv()
    rows1[...] = jnp.concatenate([stage1[n].astype(F32)[:24] for n in range(4)], axis=0).astype(BF16)
    extra = [go(rows1.at[:, left], pa.at[z], 105 + k, z_peer(k)) for k in range(1, 4)]
    extra += [go(rows1.at[:, right], pb.at[y], 108 + k, y_peer(k)) for k in range(1, 4)]
    own_rows = [
        pltpu.make_async_copy(rows1.at[:, left], pa.at[z], own_s.at[3]),
        pltpu.make_async_copy(rows1.at[:, right], pb.at[y], own_s.at[4]),
    ]
    for copy in own_rows:
        copy.start()
    own_o1.wait()
    for copy in out1_z:
        copy.wait_recv()
    extra += [go(po.at[y], po.at[y], 111 + k, y_peer(k)) for k in range(1, 4)]
    for n, (kind, j, k, copy) in enumerate(arrivals):
        copy.wait_recv()
        part = band(kind, j, k)
        passed.append(go(part, part, 48 + 16 * kind + 4 + n // 3, sibling))
    for copy in passed + extra:
        copy.wait_recv()
    for copy in own_rows:
        copy.wait()
    for copy in started:
        copy.wait_send()


def gather_weights(p, o, p1, o1):
    w, wo, pa, pb, po = pl.pallas_call(
        gather_body,
        out_shape=(
            jax.ShapeDtypeStruct((2, 4, 4, 96, HALF), BF16),
            jax.ShapeDtypeStruct((2, 4, 4, 4, 48, WALF), BF16),
            jax.ShapeDtypeStruct((4, 96, CUT), BF16),
            jax.ShapeDtypeStruct((4, 96, CUT), BF16),
            jax.ShapeDtypeStruct((4, 4, 48, WALF), BF16),
        ),
        in_specs=[vmem()] * 4,
        out_specs=(any_spec(),) * 5,
        scratch_shapes=[
            pltpu.VMEM((4, 32, HALF), BF16),
            pltpu.VMEM((96, HALF), BF16),
            pltpu.VMEM((4, 32, HALF), BF16),
            pltpu.VMEM((96, HALF), BF16),
            pltpu.SemaphoreType.DMA((115,)),
            pltpu.SemaphoreType.DMA((115,)),
            pltpu.SemaphoreType.DMA((5,)),
        ],
        compiler_params=pltpu.CompilerParams(
            collective_id=3, has_side_effects=True, vmem_limit_bytes=VMEM_LIMIT
        ),
        name="gather_weights",
    )(p, o, p1, o1)
    return w, wo, (pa, pb, po)


def fetch(src, dst, sem):
    copy = pltpu.make_async_copy(src, dst, sem)
    copy.start()
    return copy


def greet_seq(with_x):
    me = lax.axis_index("seq")
    section = lax.axis_index("section")
    barrier = pltpu.get_barrier_semaphore()
    for d in range(1, OWNERS):
        pl.semaphore_signal(
            barrier, inc=1, device_id={"seq": lax.rem(me + d, OWNERS)}, device_id_type=MESH
        )
    pl.semaphore_signal(barrier, inc=1, device_id={"section": 1 - section}, device_id_type=MESH)
    if with_x:
        for k in range(1, 4):
            pl.semaphore_signal(barrier, inc=1, device_id=x_peer(k), device_id_type=MESH)
    pl.semaphore_wait(barrier, OWNERS + (3 if with_x else 0))


class Exchange:
    def __init__(self, backward, refs):
        (self.ds, self.got, self.back, self.kept, self.fade, self.final, self.other, self.begin, self.ready,
         self.send_a, self.recv_a, self.send_b, self.recv_b, self.swap_s, self.own_s) = refs
        self.backward = backward
        self.me = lax.axis_index("seq")
        self.section = lax.axis_index("section")

    def first_copy(self, peer, d):
        return pltpu.make_async_remote_copy(
            src_ref=self.ds.at[peer], dst_ref=self.got.at[self.me],
            send_sem=self.send_a.at[d], recv_sem=self.recv_a.at[d],
            device_id={"seq": peer}, device_id_type=MESH,
        )

    def send(self, peer):
        d = lax.rem(peer + OWNERS - self.me, OWNERS)

        @pl.when(d != 0)
        def _():
            self.first_copy(peer, d).start()

        @pl.when(d == 0)
        def _():
            self.got[self.me] = self.ds[self.me]

    def back_copy(self, d):
        peer = lax.rem(self.me + d, OWNERS)
        return pltpu.make_async_remote_copy(
            src_ref=self.ready.at[peer], dst_ref=self.back.at[self.me],
            send_sem=self.send_b.at[d], recv_sem=self.recv_b.at[d],
            device_id={"seq": peer}, device_id_type=MESH,
        )

    def scan(self, decays):
        def rows_of(dec):
            return jnp.concatenate([jnp.broadcast_to(dec[h : h + 1], (64, 128)) for h in range(3)], axis=0)

        for d in range(1, OWNERS):
            self.first_copy(lax.rem(self.me + d, OWNERS), d).wait_recv()
        final, fade, kept = self.final, self.fade, self.kept
        final[...] = jnp.zeros((OWN, STATE), F32)
        fade[0] = jnp.ones((8, 128), F32)

        def step(n, carry):
            c = OWNERS - 1 - n if self.backward else n
            state = final[...]
            kept[c] = state
            dec = decays[c]
            final[...] = rows_of(dec) * state + self.got[c].astype(F32)
            fade[n + 1] = fade[n] * dec
            return carry

        lax.fori_loop(0, OWNERS, step, 0)
        swap = pltpu.make_async_remote_copy(
            src_ref=final, dst_ref=self.other, send_sem=self.swap_s.at[0], recv_sem=self.swap_s.at[1],
            device_id={"section": 1 - self.section}, device_id_type=MESH,
        )
        swap.start()
        takes = 0 if self.backward else 1
        self.begin[...] = jnp.zeros((OWN, STATE), F32)

        @pl.when(self.section == takes)
        def _():
            swap.wait_recv()
            self.begin[...] = self.other[...]

        begin = self.begin[...]
        for d in range(OWNERS):
            c = lax.rem(self.me + d, OWNERS)
            n = OWNERS - 1 - c if self.backward else c
            value = (kept[c] + rows_of(fade[n]) * begin).astype(BF16)
            if d == 0:
                self.back[c] = value
            else:
                self.ready[c] = value
                self.back_copy(d).start()

        @pl.when(self.section != takes)
        def _():
            swap.wait_recv()

        swap.wait_send()

    def finish(self):
        for d in range(1, OWNERS):
            self.back_copy(d).wait_recv()

    def drain(self):
        for d in range(1, OWNERS):
            self.first_copy(lax.rem(self.me + d, OWNERS), d).wait_send()
            self.back_copy(d).wait_send()


def exchange_scratch():
    block = pltpu.VMEM((OWNERS, OWN, STATE), BF16)
    part = pltpu.VMEM((OWN, STATE), F32)
    sems = pltpu.SemaphoreType.DMA((OWNERS,))
    return [
        block, block, block, pltpu.VMEM((OWNERS, OWN, STATE), F32), pltpu.VMEM((OWNERS + 1, 8, 128), F32),
        part, part, part, block, sems, sems, sems, sems,
        pltpu.SemaphoreType.DMA((2,)), pltpu.SemaphoreType.DMA((2,)),
    ]


def head_rows_at(ref, i, q):
    parts = []
    for h in (2 * q, 2 * q + 1):
        parts.append(ref[2 * i + h // 3, pl.ds(64 * (h % 3), 64), :])
    return jnp.concatenate(parts, axis=0)


def store_heads(ref, i, q, value):
    for n, h in enumerate((2 * q, 2 * q + 1)):
        ref[2 * i + h // 3, pl.ds(64 * (h % 3), 64), :] = value[64 * n : 64 * n + 64]


def own_group(n):
    return lax.rem(lax.axis_index("seq") // 2 + n, 8)


class Spread:
    def __init__(self, pa, pb, po, w_ref, wo_ref, send_s, recv_s, own_s):
        self.parts = (pa, pb, po)
        self.w, self.wo = w_ref, wo_ref
        self.sems = (send_s, recv_s)
        self.own_s = own_s
        self.place = places()
        self.started = []
        self.passed = []
        self.arrivals = []
        self.left = pl.ds(0, CUT)
        self.right = pl.ds(CUT, CUT)

    def go(self, src, dst, index, peer):
        copy = remote(src, dst, self.sems, index, peer)
        self.started.append(copy)
        return copy

    def spot(self, kind, n, moved):
        c, y, z, x = self.place
        if kind == 0:
            return self.w.at[c, lax.rem(y + 4 - moved, 4), n, :, self.left]
        if kind == 1:
            return self.w.at[c, n, lax.rem(z + 4 - moved, 4), :, self.right]
        return self.wo.at[c, n, :, lax.rem(x + 4 - moved, 4)]

    def start(self):
        sibling = {"section": 1 - self.place[0]}
        peers = (y_peer, z_peer, x_peer)
        self.own = []
        for n in range(4):
            for k in range(1, 4):
                for kind in range(3):
                    src = self.parts[kind].at[n]
                    copy = self.go(src, self.spot(kind, n, 0), 12 * kind + 3 * n + k - 1, peers[kind](k))
                    self.arrivals.append((kind, n, k, copy))
            for kind in range(3):
                src = self.parts[kind].at[n]
                dst = self.spot(kind, n, 0)
                self.passed.append(self.go(src, dst, 36 + 4 * kind + n, sibling))
                self.own.append(fetch(src, dst, self.own_s.at[4 * kind + n]))

    def forward(self, begin, end):
        sibling = {"section": 1 - self.place[0]}
        for at in range(begin, end):
            kind, n, k, copy = self.arrivals[at]
            copy.wait_recv()
            dst = self.spot(kind, n, k)
            self.passed.append(self.go(dst, dst, 48 + at, sibling))

    def end(self):
        for copy in self.own:
            copy.wait()
        for copy in self.passed:
            copy.wait_recv()
        for copy in self.started:
            copy.wait_send()


def forward_body(rider, *refs):
    (live_ref, pre_ref, side_ref, halo_ref, taps_ref, heads_ref, gain_ref, x_ref, wo_ref) = refs[:9]
    at = 9
    if rider:
        bands = refs[at : at + 3]
        at += 3
    (act_ref, dact_ref, dt_ref, cum_ref, dec_ref, state_ref, raw_ref, y_ref, gated_ref, inv_ref, out_ref) = refs[at : at + 11]
    at += 11
    if rider:
        next_w, next_wo = refs[at : at + 2]
        at += 2
    wo_s, z_s, cumt_s, square_s, dec_s, dec_send, dec_recv, load_s = refs[at : at + 8]
    at += 8
    ex = Exchange(False, refs[at : at + 15])
    at += 15
    load = fetch(wo_ref, wo_s, load_s.at[0])
    greet_seq(rider)
    if rider:
        spread = Spread(*bands, next_w, next_wo, *refs[at : at + 3])
        spread.start()
    me = lax.axis_index("seq")
    live = live_ref[0]
    heads = heads_ref[...]
    step = side_ref[:, :128].astype(BF16).astype(F32) + heads[0:1]
    dt = jnp.maximum(step, 0.0) + jnp.log1p(jnp.exp(-jnp.abs(step)))
    dt = jnp.where(head_lanes(), dt, 0.0) * live
    rate = -dt * jnp.exp(heads[1:2])
    cum = split_left(tri_of(True).astype(F32).astype(BF16), rate, 3)
    dt_ref[...] = dt
    cum_ref[...] = cum
    last = jnp.broadcast_to(cum[TOK - 1 : TOK], (TOK, 128))
    dec_s[...] = jnp.exp(last).T.reshape(OWNERS, 8, 128)
    dec_ref[me] = dec_s[me]

    def dec_copy(d):
        peer = lax.rem(me + d, OWNERS)
        return pltpu.make_async_remote_copy(
            src_ref=dec_s.at[peer], dst_ref=dec_ref.at[me], send_sem=dec_send.at[d], recv_sem=dec_recv.at[d],
            device_id={"seq": peer}, device_id_type=MESH,
        )

    for d in range(1, OWNERS):
        dec_copy(d).start()
    weight = dt * jnp.exp(last - cum)

    def conv_tile(cols):
        blk = pre_ref[:, cols].astype(F32)
        cat = jnp.concatenate([halo_ref[:, cols].astype(F32), blk], axis=0)
        summed = conv_of(cat, taps_ref[:, cols])
        sig = 1.0 / (1.0 + jnp.exp(-summed))
        act = summed * sig
        act_ref[:, cols] = act
        dact_ref[:, cols] = sig * (1.0 + summed * (1.0 - sig))
        return act

    b = conv_tile(pl.ds(INNER, 128)).astype(BF16)
    c = conv_tile(pl.ds(INNER + 128, 128)).astype(BF16)

    def states(n, carry):
        i = own_group(n)
        wt = to_front(weight, i)
        for q in range(3):
            x = conv_tile(pl.ds(pl.multiple_of(i * 384 + q * 128, 128), 128))
            scaled = (x * pair_cols(wt, q)[2]).astype(BF16)
            store_heads(ex.ds, i, q, dot32(scaled, b, ((0,), (0,))).astype(BF16))
        ex.send(2 * i)
        ex.send(2 * i + 1)
        return carry

    lax.fori_loop(0, 8, states, 0)
    for d in range(1, OWNERS):
        dec_copy(d).wait_recv()
    ex.scan(dec_ref)
    if rider:
        spread.forward(0, 9)
    cumt_s[...] = cum.T
    causal = tri_of(True)
    scores = dot32(c, b, ((1,), (1,)))
    lane = lax.broadcasted_iota(jnp.int32, (TOK, 128), 1)
    square_s[...] = jnp.zeros((TOK, 128), F32)

    def inside(i, carry):
        cum_i = to_front(cum, i)
        dt_i = to_front(dt, i)
        rows = cumt_s[pl.ds(pl.multiple_of(16 * i, 16), 16), :]
        for q in range(3):
            cols = pl.ds(pl.multiple_of(i * 384 + q * 128, 128), 128)
            cum_a, cum_b, _ = pair_cols(cum_i, q)
            u = act_ref[:, cols] * pair_cols(dt_i, q)[2]
            mixes = []
            for cum_h, off in ((cum_a, LANES[2 * q]), (cum_b, LANES[2 * q + 1])):
                gap = cum_h - rows[off : off + 1]
                mixes.append((scores * jnp.exp(jnp.where(causal, gap, -1e30))).astype(BF16))
            terms = jnp.concatenate(
                [jnp.where(lane < 64, u, 0.0).astype(BF16), jnp.where(lane < 64, 0.0, u).astype(BF16)], axis=0
            )
            raw_ref[:, cols] = dot32(jnp.concatenate(mixes, axis=1), terms)
        return carry

    lax.fori_loop(0, 8, inside, 0)
    ex.finish()
    save = fetch(ex.back, state_ref, load_s.at[1])

    def across(i, carry):
        cum_i = to_front(cum, i)
        skip_i = pltpu.roll(heads, lax.rem(128 - 16 * i, 128), 1)[2:3]
        for q in range(3):
            cols = pl.ds(pl.multiple_of(i * 384 + q * 128, 128), 128)
            x = act_ref[:, cols]
            state = head_rows_at(ex.back, i, q)
            raw = raw_ref[:, cols] + jnp.exp(pair_cols(cum_i, q)[2]) * dot32(c, state, ((1,), (1,)))
            raw_ref[:, cols] = raw
            y = (raw + pair_row(skip_i, q) * x).astype(BF16)
            y_ref[:, cols] = y
            gate = side_ref[:, pl.ds(pl.multiple_of(GATE0 + i * 384 + q * 128, 128), 128)]
            z = y.astype(F32) * (gate / (1.0 + jnp.exp(-gate)))
            z_s[:, cols] = z
            square_s[...] += z * z
        return carry

    lax.fori_loop(0, 8, across, 0)
    if rider:
        spread.forward(9, 18)
    total = jnp.sum(square_s[...], axis=1, keepdims=True)
    inv = jnp.broadcast_to(lax.rsqrt(total / INNER + EPS), (TOK, 128))
    inv_ref[...] = inv

    def scale(i, carry):
        cols = pl.ds(pl.multiple_of(i * 128, 128), 128)
        gated_ref[:, cols] = (z_s[:, cols] * inv * gain_ref[0:1, cols]).astype(BF16)
        return carry

    lax.fori_loop(0, 24, scale, 0)
    load.wait()
    for half in range(2):

        def project(n, carry):
            cols = pl.ds(pl.multiple_of(n * 256, 256), 256)
            full = pl.ds(pl.multiple_of(half * WALF + n * 256, 256), 256)
            branch = dot32(gated_ref[...], wo_s[half, :, cols])
            out_ref[:, full] = (x_ref[:, full].astype(F32) + live * branch).astype(BF16)
            return carry

        lax.fori_loop(0, WALF // 256, project, 0)
    save.wait()
    if rider:
        spread.forward(18, 36)
        spread.end()
    for d in range(1, OWNERS):
        dec_copy(d).wait_send()
    ex.drain()


def any_spec():
    return pl.BlockSpec(memory_space=pl.ANY)


def block_forward(live, pre, side, halo, taps, heads, gain, x, w_o, bands):
    rider = bands is not None
    tile = pltpu.VMEM((TOK, 128), F32)
    out_shape = [
        jax.ShapeDtypeStruct((TOK, CONV), F32),
        jax.ShapeDtypeStruct((TOK, CONV), F32),
        jax.ShapeDtypeStruct((TOK, 128), F32),
        jax.ShapeDtypeStruct((TOK, 128), F32),
        jax.ShapeDtypeStruct((OWNERS, 8, 128), F32),
        jax.ShapeDtypeStruct((OWNERS, OWN, STATE), BF16),
        jax.ShapeDtypeStruct((TOK, INNER), F32),
        jax.ShapeDtypeStruct((TOK, INNER), BF16),
        jax.ShapeDtypeStruct((TOK, INNER), BF16),
        jax.ShapeDtypeStruct((TOK, 128), F32),
        jax.ShapeDtypeStruct((TOK, D), BF16),
    ]
    out_specs = [vmem()] * 5 + [any_spec()] + [vmem()] * 5
    scratch = [
        pltpu.VMEM((2, INNER, WALF), BF16), pltpu.VMEM((TOK, INNER), F32), tile, tile,
        pltpu.VMEM((OWNERS, 8, 128), F32), pltpu.SemaphoreType.DMA((OWNERS,)), pltpu.SemaphoreType.DMA((OWNERS,)),
        pltpu.SemaphoreType.DMA((2,)),
    ] + exchange_scratch()
    args = [live, pre, side, halo, taps, heads, gain, x, w_o]
    in_specs = [smem()] + [vmem()] * 7 + [any_spec()]
    if rider:
        args += list(bands)
        in_specs += [vmem()] * 3
        out_shape += [
            jax.ShapeDtypeStruct((2, 4, 4, 96, HALF), BF16),
            jax.ShapeDtypeStruct((2, 4, 4, 4, 48, WALF), BF16),
        ]
        out_specs += [any_spec()] * 2
        scratch += [
            pltpu.SemaphoreType.DMA((84,)), pltpu.SemaphoreType.DMA((84,)), pltpu.SemaphoreType.DMA((12,)),
        ]
    return pl.pallas_call(
        functools.partial(forward_body, rider),
        out_shape=tuple(out_shape),
        in_specs=in_specs,
        out_specs=tuple(out_specs),
        scratch_shapes=scratch,
        compiler_params=pltpu.CompilerParams(
            collective_id=1 if rider else 2, has_side_effects=True, vmem_limit_bytes=VMEM_LIMIT
        ),
        name="block_forward",
    )(*args)


class Fold:
    def __init__(self, gi, go, sa, sb, so, ra, rb, ro, send_s, recv_s, own_s):
        self.gi, self.go_ref = gi, go
        self.target = (sa, sb, so)
        self.buf = (ra, rb, ro)
        self.sems = (send_s, recv_s)
        self.own_s = own_s
        self.place = places()
        self.copies = []

    def start(self):
        _, y, z, x = self.place
        left = pl.ds(0, CUT)
        right = pl.ds(CUT, CUT)
        ra, rb, ro = self.buf
        for k in range(1, 4):
            self.copies += [
                remote(self.gi.at[lax.rem(y + k, 4), :, :, left], ra.at[k], self.sems, k - 1, y_peer(k)),
                remote(self.gi.at[:, lax.rem(z + k, 4), :, right], rb.at[k], self.sems, 2 + k, z_peer(k)),
                remote(self.go_ref.at[:, :, lax.rem(x + k, 4)], ro.at[k], self.sems, 5 + k, x_peer(k)),
            ]
        self.own = [
            fetch(self.gi.at[y, :, :, left], ra.at[0], self.own_s.at[0]),
            fetch(self.gi.at[:, z, :, right], rb.at[0], self.own_s.at[1]),
            fetch(self.go_ref.at[:, :, x], ro.at[0], self.own_s.at[2]),
        ]

    def end(self):
        for copy in self.own:
            copy.wait()
        for copy in self.copies:
            copy.wait_recv()
        for buf, target in zip(self.buf, self.target):
            add_blocks(buf, target)
        for copy in self.copies:
            copy.wait_send()


def add_blocks(parts, target):
    rows, cols = parts.shape[-2:]
    lead = parts.shape[1:-2]
    blocks = functools.reduce(lambda a, b: a * b, lead, 1)
    per = rows // 16

    def body(n, carry):
        b = n // per
        at = pl.ds(pl.multiple_of(lax.rem(n, per) * 16, 16), 16)
        spot = (b,) if len(lead) == 1 else (b // lead[1], lax.rem(b, lead[1]))
        total = parts[(0,) + spot + (at, slice(None))].astype(F32)
        for k in range(1, 4):
            total = total + parts[(k,) + spot + (at, slice(None))].astype(F32)
        target[spot + (at, slice(None))] = total.astype(target.dtype)
        return carry

    lax.fori_loop(0, blocks * per, body, 0)


def backward_body(rider, *refs):
    (live_ref, g_ref, side_ref, y_ref, gain_ref, inv_ref, act_ref, dact_ref, dt_ref, cum_ref, raw_ref, pre_ref,
     halo_ref, heads_ref, dec_ref, wo_ref, state_ref) = refs[:17]
    at = 17
    if rider:
        grads = refs[at : at + 2]
        at += 2
    (gb_ref, dgate_ref, gmid_ref, gsum_ref, dstep_ref, gtaps_ref, ghead_ref) = refs[at : at + 7]
    at += 7
    if rider:
        folded = refs[at : at + 3]
        at += 3
    (wo_s, gg_s, dots_s, dy_s, cumt_s, edge_s, dscore_s, gb_s, gc_s, xdu_s, dyy_s, row_s, state_s, load_s) = refs[at : at + 14]
    at += 14
    ex = Exchange(True, refs[at : at + 15])
    at += 15
    load = fetch(wo_ref, wo_s, load_s.at[0])
    load_state = fetch(state_ref, state_s, load_s.at[1])
    greet_seq(rider)
    if rider:
        fold = Fold(*grads, *folded, *refs[at : at + 6])
        fold.start()
    live = live_ref[0]
    heads = heads_ref[...]
    gb = (g_ref[...].astype(F32) * live).astype(BF16)
    gb_ref[...] = gb
    inv = inv_ref[...]
    b = act_ref[:, INNER : INNER + 128].astype(BF16)
    c = act_ref[:, INNER + 128 : CONV].astype(BF16)
    dt = dt_ref[...]
    cum = cum_ref[...]
    dots_s[...] = jnp.zeros((TOK, 128), F32)
    load.wait()

    def first(i, carry):
        rows = pl.ds(pl.multiple_of(i * 384, 384), 384)
        gg = dot32(gb[:, :WALF], wo_s[0, rows, :], ((1,), (1,)))
        gg = gg + dot32(gb[:, WALF:], wo_s[1, rows, :], ((1,), (1,)))
        gg_s[:, rows] = gg
        for q in range(3):
            cols = pl.ds(pl.multiple_of(i * 384 + q * 128, 128), 128)
            gate = side_ref[:, pl.ds(pl.multiple_of(GATE0 + i * 384 + q * 128, 128), 128)]
            z = y_ref[:, cols].astype(F32) * (gate / (1.0 + jnp.exp(-gate)))
            dots_s[...] += gg[:, 128 * q : 128 * q + 128] * gain_ref[0:1, cols] * z
        return carry

    lax.fori_loop(0, 8, first, 0)
    total = jnp.broadcast_to(jnp.sum(dots_s[...], axis=1, keepdims=True), (TOK, 128))
    shift = total * inv * inv * inv / INNER

    def second(n, carry):
        i = own_group(n)
        cum_i = to_front(cum, i)
        for q in range(3):
            cols = pl.ds(pl.multiple_of(i * 384 + q * 128, 128), 128)
            gate = side_ref[:, pl.ds(pl.multiple_of(GATE0 + i * 384 + q * 128, 128), 128)]
            y = y_ref[:, cols].astype(F32)
            gg = gg_s[:, cols]
            sig = 1.0 / (1.0 + jnp.exp(-gate))
            act = gate * sig
            z = y * act
            dz = gg * gain_ref[0:1, cols] * inv - z * shift
            dy = (dz * act).astype(BF16)
            dy_s[:, cols] = dy
            dgate_ref[:, cols] = (dz * y * (sig * (1.0 + gate * (1.0 - sig)))).astype(BF16)
            gmid_ref[:, cols] = jnp.broadcast_to(
                jnp.sum(gg * z * inv, axis=0, keepdims=True), (8, 128)
            )
            far = (dy.astype(F32) * jnp.exp(pair_cols(cum_i, q)[2])).astype(BF16)
            store_heads(ex.ds, i, q, dot32(far, c, ((0,), (0,))).astype(BF16))
        ex.send(2 * i)
        ex.send(2 * i + 1)
        return carry

    lax.fori_loop(0, 8, second, 0)
    ex.scan(dec_ref)
    load_state.wait()
    cumt_s[...] = cum.T
    causal = tri_of(True)
    scores = dot32(c, b, ((1,), (1,)))
    lane = lax.broadcasted_iota(jnp.int32, (TOK, 128), 1)
    pick_row = lax.broadcasted_iota(jnp.int32, (128, 128), 0)
    pick_col = lax.broadcasted_iota(jnp.int32, (128, 128), 1)
    picks = []
    for q in range(3):
        target = jnp.where(pick_row < 64, LANES[2 * q], LANES[2 * q + 1])
        picks.append((pick_col == target).astype(F32).astype(BF16))
    for ref in (dscore_s, gb_s, gc_s, xdu_s, dyy_s, row_s, gtaps_ref):
        ref[...] = jnp.zeros_like(ref)

    def inside(i, carry):
        cum_i = to_front(cum, i)
        dt_i = to_front(dt, i)
        rows = cumt_s[pl.ds(pl.multiple_of(16 * i, 16), 16), :]
        for q in range(3):
            cols = pl.ds(pl.multiple_of(i * 384 + q * 128, 128), 128)
            cum_a, cum_b, cum_x = pair_cols(cum_i, q)
            u16 = (act_ref[:, cols] * pair_cols(dt_i, q)[2]).astype(BF16)
            dy16 = dy_s[:, cols]
            nil = jnp.zeros_like(dy16)
            dys = jnp.concatenate([jnp.where(lane < 64, dy16, nil), jnp.where(lane < 64, nil, dy16)], axis=0)
            both = dot32(dys, u16, ((1,), (1,)))
            mixes = []
            for n, (cum_h, off) in enumerate(((cum_a, LANES[2 * q]), (cum_b, LANES[2 * q + 1]))):
                gap = cum_h - rows[off : off + 1]
                decay = jnp.exp(jnp.where(causal, gap, -1e30))
                mixes.append((scores * decay).astype(BF16))
                dscore_s[...] += both[n * TOK : n * TOK + TOK] * decay
            gg_s[:, cols] = dot32(jnp.concatenate(mixes, axis=0), dys, ((0,), (0,)))
            far = (dy16.astype(F32) * jnp.exp(cum_x)).astype(BF16)
            gc_s[...] += dot32(far, head_rows_at(state_s, i, q))
        return carry

    lax.fori_loop(0, 8, inside, 0)

    def conv_back(cols, gact):
        gsum = gact * dact_ref[:, cols]
        gsum_ref[:, cols] = gsum
        blk = pre_ref[:, cols].astype(F32)
        cat = jnp.concatenate([halo_ref[:, cols].astype(F32), blk], axis=0)
        sums = [jnp.sum(gsum * cat[5 + k : 5 + k + TOK], axis=0, keepdims=True) for k in range(4)]
        sums.append(jnp.sum(gsum, axis=0, keepdims=True))
        gtaps_ref[:, cols] = jnp.concatenate(sums + [jnp.zeros((3, 128), F32)], axis=0)

    ex.finish()

    def across(i, carry):
        cum_i = to_front(cum, i)
        dt_i = to_front(dt, i)
        skip_i = pltpu.roll(heads, lax.rem(128 - 16 * i, 128), 1)[2:3]
        x_du = jnp.zeros((TOK, 128), F32)
        dy_y = jnp.zeros((TOK, 128), F32)
        thin = jnp.zeros((16, 128), F32)
        edges = {}
        for q in range(3):
            cols = pl.ds(pl.multiple_of(i * 384 + q * 128, 128), 128)
            x = act_ref[:, cols]
            cum_x = pair_cols(cum_i, q)[2]
            dt_x = pair_cols(dt_i, q)[2]
            fade = jnp.exp(cum_x[TOK - 1 : TOK] - cum_x)
            u = x * dt_x
            dy = dy_s[:, cols].astype(F32)
            state16 = head_rows_at(state_s, i, q)
            dstate16 = head_rows_at(ex.back, i, q)
            du_far = fade * dot32(b, dstate16, ((1,), (1,)))
            du = gg_s[:, cols] + du_far
            gb_s[...] += dot32((u * fade).astype(BF16), dstate16)
            overlap = state16.astype(F32) * dstate16.astype(F32)
            edges[LANES[2 * q]] = jnp.sum(overlap[:64], axis=0, keepdims=True)
            edges[LANES[2 * q + 1]] = jnp.sum(overlap[64:], axis=0, keepdims=True)
            x_du = x_du + split_right(x * du, picks[q], 2)
            dy_y = dy_y + split_right(dy * raw_ref[:, cols], picks[q], 2)
            thin = thin + split_right(
                jnp.concatenate(
                    [
                        jnp.broadcast_to(jnp.sum(u * du_far, axis=0, keepdims=True), (8, 128)),
                        jnp.broadcast_to(jnp.sum(dy * x, axis=0, keepdims=True), (8, 128)),
                    ],
                    axis=0,
                ),
                picks[q],
                3,
            )
            conv_back(cols, du * dt_x + pair_row(skip_i, q) * dy)
        nothing = jnp.zeros((1, 128), F32)
        edge_s[pl.ds(pl.multiple_of(16 * i, 16), 16), :] = jnp.concatenate(
            [edges.get(k, nothing) for k in range(16)], axis=0
        )
        xdu_s[...] += pltpu.roll(x_du, 16 * i, 1)
        dyy_s[...] += pltpu.roll(dy_y, 16 * i, 1)
        row_s[...] += pltpu.roll(thin, 16 * i, 1)
        return carry

    lax.fori_loop(0, 8, across, 0)
    dscore16 = dscore_s[...].astype(BF16)
    conv_back(pl.ds(INNER, 128), gb_s[...] + dot32(dscore16, c, ((0,), (0,))))
    conv_back(pl.ds(INNER + 128, 128), gc_s[...] + dot32(dscore16, b))
    ones = jnp.ones((128, 128), BF16)
    edge = split_right(edge_s[...], ones, 3).T[0:1] * jnp.exp(cum[TOK - 1 : TOK]) + row_s[0:1]
    x_du = xdu_s[...]
    drate = split_left(tri_of(False).astype(F32).astype(BF16), dyy_s[...] - dt * x_du, 3) + edge
    speed = jnp.exp(heads[1:2])
    ddt = x_du - drate * speed
    step = side_ref[:, :128].astype(BF16).astype(F32) + heads[0:1]
    dstep = jnp.where(head_lanes(), ddt / (1.0 + jnp.exp(-step)), 0.0) * live
    dstep_ref[...] = dstep
    ghead_ref[...] = jnp.concatenate(
        [
            jnp.sum(dstep, axis=0, keepdims=True),
            jnp.sum(-drate * dt * speed, axis=0, keepdims=True),
            row_s[8:9],
            jnp.zeros((5, 128), F32),
        ],
        axis=0,
    )
    if rider:
        fold.end()
    ex.drain()


def fold_shapes():
    return [(4, 96, CUT), (4, 96, CUT), (4, 4, 48, WALF)]


def block_backward(live, g, side, y, gain, inv, act, dact, dt, cum, raw, pre, halo, heads, dec, w_o, states, grads):
    rider = grads is not None
    tile = pltpu.VMEM((TOK, 128), F32)
    out_shape = [
        jax.ShapeDtypeStruct((TOK, D), BF16),
        jax.ShapeDtypeStruct((TOK, INNER), BF16),
        jax.ShapeDtypeStruct((8, INNER), F32),
        jax.ShapeDtypeStruct((TOK, CONV), F32),
        jax.ShapeDtypeStruct((TOK, 128), F32),
        jax.ShapeDtypeStruct((8, CONV), F32),
        jax.ShapeDtypeStruct((8, 128), F32),
    ]
    scratch = [
        pltpu.VMEM((2, INNER, WALF), BF16), pltpu.VMEM((TOK, INNER), F32), tile, pltpu.VMEM((TOK, INNER), BF16),
        tile, tile, tile, tile, tile, tile, tile, pltpu.VMEM((16, 128), F32),
        pltpu.VMEM((OWNERS, OWN, STATE), BF16), pltpu.SemaphoreType.DMA((2,)),
    ] + exchange_scratch()
    args = [live, g, side, y, gain, inv, act, dact, dt, cum, raw, pre, halo, heads, dec, w_o, states]
    in_specs = [smem()] + [vmem()] * 14 + [any_spec()] * 2
    if rider:
        args += list(grads)
        in_specs += [any_spec()] * 2
        out_shape += [jax.ShapeDtypeStruct(shape, BF16) for shape in fold_shapes()]
        scratch += [pltpu.VMEM((4,) + shape, BF16) for shape in fold_shapes()]
        scratch += [pltpu.SemaphoreType.DMA((9,)), pltpu.SemaphoreType.DMA((9,)), pltpu.SemaphoreType.DMA((3,))]
    return pl.pallas_call(
        functools.partial(backward_body, rider),
        out_shape=tuple(out_shape),
        in_specs=in_specs,
        out_specs=(vmem(),) * len(out_shape),
        scratch_shapes=scratch,
        compiler_params=pltpu.CompilerParams(
            collective_id=5 if rider else 6, has_side_effects=True, vmem_limit_bytes=VMEM_LIMIT
        ),
        name="block_backward",
    )(*args)


class Finish:
    def __init__(self, sums, scratch, sems):
        self.sums = sums
        (self.r2a, self.r2b, self.r2o, self.c3, self.r3, self.o2, self.r3o) = scratch
        self.sems = sems
        self.place = places()
        self.started = []

    def go(self, src, dst, index, peer):
        copy = remote(src, dst, self.sems, index, peer)
        self.started.append(copy)
        return copy

    def second(self):
        _, y, z, x = self.place
        sa, sb, so = self.sums
        self.a = [self.go(sa.at[lax.rem(z + k, 4)], self.r2a.at[k], k - 1, z_peer(k)) for k in range(1, 4)]
        self.b = [self.go(sb.at[lax.rem(y + k, 4)], self.r2b.at[k], 2 + k, y_peer(k)) for k in range(1, 4)]
        self.o = [self.go(so.at[lax.rem(y + k, 4)], self.r2o.at[k], 5 + k, y_peer(k)) for k in range(1, 4)]
        self.r2a[0] = sa[z]
        self.r2b[0] = sb[y]
        self.r2o[0] = so[y]

    def third(self):
        _, y, z, x = self.place
        for copy in self.a + self.b:
            copy.wait_recv()
        for n in range(4):
            at = pl.ds(24 * n, 24)
            for parts, cols in ((self.r2a, pl.ds(0, CUT)), (self.r2b, pl.ds(CUT, CUT))):
                total = parts[0, at, :].astype(F32)
                for k in range(1, 4):
                    total = total + parts[k, at, :].astype(F32)
                self.c3[n, :, cols] = total
        self.x = [self.go(self.c3.at[lax.rem(x + k, 4)], self.r3.at[x], 8 + k, x_peer(k)) for k in range(1, 4)]
        for copy in self.o:
            copy.wait_recv()
        add_blocks(self.r2o, self.o2)
        self.z = [self.go(self.o2.at[lax.rem(z + k, 4)], self.r3o.at[k], 11 + k, z_peer(k)) for k in range(1, 4)]
        self.r3[x] = self.c3[x]
        self.r3o[0] = self.o2[z]

    def last(self, in_ref, out_ref):
        for copy in self.x + self.z:
            copy.wait_recv()
        in_ref[...] = self.r3[0] + self.r3[1] + self.r3[2] + self.r3[3]
        total = self.r3o[0].astype(F32)
        for k in range(1, 4):
            total = total + self.r3o[k].astype(F32)
        out_ref[...] = total
        for copy in self.started:
            copy.wait_send()


def reduce_body(gi_ref, go_ref, sa1, sb1, so1, in0_ref, out0_ref, in1_ref, out1_ref, *scratch):
    sums0 = scratch[:3]
    fold = Fold(gi_ref, go_ref, *sums0, *scratch[3:9])
    near = Finish(sums0, scratch[9:16], scratch[16:18])
    far = Finish((sa1, sb1, so1), scratch[18:25], scratch[25:27])
    greet(False)
    fold.start()
    far.second()
    far.third()
    fold.end()
    near.second()
    far.last(in1_ref, out1_ref)
    near.third()
    near.last(in0_ref, out0_ref)


def reduce_grads(grad_in, grad_out, sums):
    sems = pltpu.SemaphoreType.DMA
    finish = [
        pltpu.VMEM((4, 96, CUT), BF16),
        pltpu.VMEM((4, 96, CUT), BF16),
        pltpu.VMEM((4, 4, 48, WALF), BF16),
        pltpu.VMEM((4, 24, HALF), F32),
        pltpu.VMEM((4, 24, HALF), F32),
        pltpu.VMEM((4, 48, WALF), BF16),
        pltpu.VMEM((4, 48, WALF), BF16),
        sems((15,)),
        sems((15,)),
    ]
    return pl.pallas_call(
        reduce_body,
        out_shape=(
            jax.ShapeDtypeStruct((24, HALF), F32),
            jax.ShapeDtypeStruct((48, WALF), F32),
        )
        * 2,
        in_specs=[any_spec()] * 2 + [vmem()] * 3,
        out_specs=(vmem(),) * 4,
        scratch_shapes=[pltpu.VMEM(shape, BF16) for shape in fold_shapes()]
        + [pltpu.VMEM((4,) + shape, BF16) for shape in fold_shapes()]
        + [sems((9,)), sems((9,)), sems((3,))]
        + finish
        + finish,
        compiler_params=pltpu.CompilerParams(
            collective_id=4, has_side_effects=True, vmem_limit_bytes=VMEM_LIMIT
        ),
        name="reduce_grads",
    )(grad_in, grad_out, *sums)


def settle(section, first_value, second_value):
    own = jnp.where(section == 0, first_value, second_value)
    got = swap_cores(jnp.where(section == 0, second_value, first_value))
    return jnp.where(section == 0, own, got), jnp.where(section == 0, got, own)


def per_device(
    block_input, cotangent, seg_groups, norm_gain, w_gate, w_inner, w_bc, w_step, conv_inner, conv_bc, head_params,
    inner_gain, w_out,
):
    section = lax.axis_index("section")
    seq_pos = lax.axis_index("seq")
    main = jnp.concatenate([w_inner[0], w_bc[0]], axis=1)
    side = jnp.concatenate(
        [
            step_lanes(w_step[0]),
            pack_small(norm_gain[0], inner_gain[0], conv_inner[0], conv_bc[0], head_params[0]),
            w_gate[0],
        ],
        axis=1,
    )
    given_in = jnp.where(section == 0, side, main)
    given_out = jnp.where(section == 0, w_out[0][:, WALF:], w_out[0][:, :WALF])
    taken_in = swap_cores(given_in)
    taken_out = swap_cores(given_out)
    kept_in = jnp.where(section == 0, main, side)
    kept_out = jnp.where(section == 0, w_out[0][:, :WALF], w_out[0][:, WALF:])
    half_in = (jnp.where(section == 0, kept_in, taken_in), jnp.where(section == 0, taken_in, kept_in))
    half_out = (jnp.where(section == 0, kept_out, taken_out), jnp.where(section == 0, taken_out, kept_out))
    near_w, near_o, bands = gather_weights(
        jnp.pad(half_in[0], ((0, 8), (0, 0))), half_out[0], jnp.pad(half_in[1], ((0, 8), (0, 0))), half_out[1]
    )
    weights = [(near_w.reshape(2, D, HALF), near_o.reshape(2, INNER, WALF)), None]
    firsts = (BLOCKS - seg_groups[0]) * (BLOCK_LEN // TOK)
    first = jnp.where(section == 0, firsts[0], firsts[1])
    live = (seq_pos >= first).astype(F32).reshape(1)
    ring = [(s * 16 + i, s * 16 + i + 1) for s in range(2) for i in range(15)] + [(15, 16)]
    jump = [(15, 20)]
    unring = [(b, a) for a, b in ring]
    unjump = [(b, a) for a, b in jump]
    axes = ("section", "seq")

    x = lax.dynamic_index_in_dim(block_input[0], section, 0, keepdims=False)
    kept = []
    outs = []
    for layer in range(2):
        w_in, w_o = weights[layer]
        gain, mid_gain, taps, heads = unpack_small(w_in[1, :, 128:GATE0])
        x32 = x.astype(F32)
        hidden = (x32 * lax.rsqrt(jnp.mean(x32 * x32, axis=-1, keepdims=True) + EPS) * gain[0]).astype(BF16)
        pre = jnp.dot(hidden, w_in[0], preferred_element_type=F32).astype(BF16)
        tail = pre[TOK - 8 :]
        near = lax.ppermute(tail, axes, ring)
        far = lax.ppermute(tail, axes, jump)
        halo = jnp.where(
            seq_pos == first,
            jnp.where(section == 0, jnp.zeros_like(near), jnp.where(first == 0, near, far)),
            near,
        )
        wide = jnp.dot(hidden, w_in[1], preferred_element_type=F32)
        act, dact, dt, cum, dec, states, raw, y, gated, inv, out, *later = block_forward(
            live, pre, wide, halo, taps, heads, mid_gain, x, w_o, bands if layer == 0 else None
        )
        if layer == 0:
            weights[1] = (later[0].reshape(2, D, HALF), later[1].reshape(2, INNER, WALF))
        kept.append((x, hidden, pre, halo, wide, act, dact, dt, cum, dec, states, raw, y, gated, inv, gain, mid_gain, taps, heads))
        outs.append(out)
        x = out

    g = lax.dynamic_index_in_dim(cotangent[0], section, 0, keepdims=False)
    grads_in = [None, None]
    grads = None
    for layer in (1, 0):
        w_in, w_o = weights[layer]
        (x, hidden, pre, halo, wide, act, dact, dt, cum, dec, states, raw, y, gated, inv, gain, mid_gain, taps, heads) = kept[layer]
        gb, dgate, gmid, gsum, dstep, gtaps, ghead, *folded = block_backward(
            live, g, wide, y, mid_gain, inv, act, dact, dt, cum, raw, pre, halo, heads, dec, w_o, states, grads
        )
        head_rows = gsum[:8]
        near = lax.ppermute(head_rows, axes, unring)
        far = lax.ppermute(head_rows, axes, unjump)
        crossing = (section == 0) & (seq_pos == 15) & (firsts[1] != 0)
        after = jnp.where(crossing, far, near) * live
        gpre, gside, g, ggain = input_backward(gsum, after, dstep, taps, dgate, w_in, x, g, gain)
        grads_in[layer] = g
        small = small_grads(ggain[0], gmid[0], gtaps, ghead, seq_pos)
        small = small + swap_cores(small)
        other_gated = swap_cores(gated)
        other_hidden = swap_cores(hidden)
        other_gb = swap_cores(jnp.where(section == 0, gb[:, WALF:], gb[:, :WALF]))
        own_gb = jnp.where(section == 0, gb[:, :WALF], gb[:, WALF:])
        other_g = swap_cores(jnp.where(section == 0, gside, gpre))
        own_g = jnp.where(section == 0, gpre, gside)
        pair = lambda own, other: jnp.concatenate([own, other], axis=0)
        grad_in = dot32(pair(hidden, other_hidden), pair(own_g, other_g), ((0,), (0,))).astype(BF16)
        keep = jnp.where(section == 1, small.astype(BF16), grad_in[:, 128:256])
        grad_in = lax.dynamic_update_slice_in_dim(grad_in, keep, 128, 1)
        grad_out = dot32(pair(gated, other_gated), pair(own_gb, other_gb), ((0,), (0,))).astype(BF16)
        grads = (grad_in.reshape(4, 4, 96, HALF), grad_out.reshape(4, 4, 4, 48, WALF))

    in0, wo0, in1, wo1 = reduce_grads(*grads, folded)
    out_a, out_b = settle(section, outs[0], outs[1])
    in_a, in_b = settle(section, grads_in[0], grads_in[1])
    main, side = settle(section, in0, in1)
    out_left, out_right = settle(section, wo0, wo1)
    grad_out = jnp.concatenate([out_left, out_right], axis=1)
    cells = side[:, 128:GATE0].reshape(-1)
    return (
        jnp.stack([out_a, out_b])[None, None],
        jnp.stack([in_a, in_b])[None, None],
        cells[:24][None],
        side[:, GATE0:][None],
        main[:, :INNER][None],
        main[:, INNER:][None],
        side[:, :128].reshape(24, OWNERS, 8)[:, :, :3].reshape(24, HEADS)[None],
        cells[72:312].reshape(5, 48)[None],
        cells[312:332].reshape(5, 4)[None],
        cells[332:341].reshape(3, 3)[None],
        cells[24:72][None],
        grad_out[None],
    )


def solution(mesh):
    weight = P("section", ROWS_ALL, None)
    vector = P("section", ROWS_ALL)
    taps = P("section", None, ROWS_ALL)
    tokens = P("wsh", None, "seq", None)
    heads = P("section", None, "seq")
    result = P("section", "wsh", None, "seq", None)
    return jax.shard_map(
        per_device,
        mesh=mesh,
        in_specs=(
            tokens, tokens, P("wsh", None), vector, weight, weight, weight, weight, taps, taps, heads, vector, weight,
        ),
        out_specs=(
            result, result, vector, weight, weight, weight, weight, taps, taps, heads, vector, weight,
        ),
        check_vma=False,
    )
```

time: 1160 us -> 786 us (0.68)
  waiting for transfers between devices: 716 us -> 0.06 us
  Pallas kernels: 271 us -> 589 us
  local copies, waits for them, and re-layouts: 29.8 us -> 69.9 us
  blocking collectives: 24.1 us -> 0 us
  between operations: 17 us -> 3.9 us
  other arithmetic: 26.1 us -> 38.5 us
    reduce_scatter x8 -> x0, waiting for transfers between devices: 393 us -> none  [the longest x2 182 us: per_device(): lax.psum_scatter(grad_in, 'seq', scatter_dimension=0, tiled=True)]
    pallas_call x12 -> x6, Pallas kernels: 236 us -> 555 us  [the longest x2 153 us: block_forward(): pl.pallas_call(functools.partial(forward_body, rider), out_shape=tuple(ou...]
    all_gather x10 -> x0, waiting for transfers between devices: 317 us -> none  [the longest x1 88.1 us: per_device(): lax.all_gather(shard, ROWS_ALL, axis=0, tiled=True)]
    slice x7 -> x12, local copies, waits for them, and re-layouts: 4.79 us -> 35.4 us  [the longest x2 29.6 us: per_device(): wide = jnp.dot(hidden, w_in[1], preferred_element_type=F32)]
    psum x2 -> x0, blocking collectives: 14.1 us -> none  [the longest x1 7.88 us: per_device(): lax.psum(small_grads(ggain[0], gmid[0], gtaps, ghead, seq_pos), 'section')]
    select_n x1 -> x8, other arithmetic: 0.07 us -> 13.2 us  [the longest x2 4.96 us: per_device(): own_g = jnp.where(section == 0, gpre, gside)]
  transfers between devices with their start and end apart: 30 -> 24, of which waited for: 17 -> 0; matrix products, arithmetic and copies ran while one was open for 7% -> 14% of each run, Pallas kernels for 22% -> 43%
where the time goes in v2:
time: 786 us; the launch traced here: 777 us
  Pallas kernels  589 us (75%)
  local copies, waits for them, and re-layouts  69.9 us (9%)
  matrix products  41.7 us (5%)
  other arithmetic  38.5 us (5%)
  starting transfers between devices  34.3 us (4%)
    pallas_call x2, Pallas kernels, block_forward(): pl.pallas_call(functools.partial(forward_body, rider), out_shape=tuple(ou...  153 us
    pallas_call x2, Pallas kernels, block_backward(): pl.pallas_call(functools.partial(backward_body, rider), out_shape=tuple(o...  147 us
    pallas_call x1, Pallas kernels, gather_weights(): pl.pallas_call(gather_body, out_shape=(jax.ShapeDtypeStruct((2, 4, 4, 96,...  129 us
    pallas_call x1, Pallas kernels, reduce_grads(): pl.pallas_call(reduce_body, out_shape=(jax.ShapeDtypeStruct((24, HALF), F...  125 us
    pallas_call x2, Pallas kernels, input_backward(): pl.pallas_call(input_back_body, grid=(1,), out_shape=(jax.ShapeDtypeStruc...  34.4 us
    slice x2, local copies, waits for them, and re-layouts, per_device(): wide = jnp.dot(hidden, w_in[1], preferred_element_type=F32)  29.6 us
    dot_general x4, matrix products, dot32(): lax.dot_general(left, right, (dims, ((), ())), preferred_element_type=F32)  25 us
  transfers between devices with their start and end apart: 24, of which 0 were waited for; matrix products, arithmetic and copies ran while one was open for 14% of the time, Pallas kernels for 43%

profile of v2, /device:TPU:1, one launch (start us, length us, event | category | flops | bytes accessed | tf_op | source)
XLA Modules:
  0.0 777.3 jit_solution(6387547313182231116)
XLA Ops:
  3.2 1.4 concatenate.49
  5.5 1.1 broadcast_select_fusion.18
  6.6 1.5 collective-permute-start
  8.1 0.9 broadcast_select_fusion.26
  9.8 1.8 fusion.12
  14.9 1.6 broadcast_select_fusion.24
  16.5 1.1 broadcast_select_fusion.16
  19.0 129.0 %gather_weights.1 = (bf16[2,4,4,96,3328]{4,3,2,1,0:T(8,128)(2,1)}, bf16[2,4,4,4,48,768]{5,4,3,2,1,0:T(8,128)(2,1)}, bf16[4,96,1664]{2,1,0:T(8,128)(2,1)}, bf16[4...) custom-call(bf16[32,3328]{1,0:T(8,128)(2,1)} %pad.42.p_ref, bf16[48,768]{1,0:T(8,128)(2,1)} %get-tuple-element.203.o_ref, ...), custom_call_target="tpu_custom_call" | custom-call | tf_op jit(solution)/shard_map/gather_weights/pallas_call | solution.py:347
  148.0 14.8 %fusion.55 = (bf16[1,4,4,96,3328]{4,3,2,1,0:T(8,128)(2,1)}, bf16[1,4,4,96,3328]{4,3,2,1,0:T(8,128)(2,1)}) fusion(bf16[2,4,4,96,3328]{4,3,2,1,0:T(8,128)(2,1)} %get-tuple-element.70), kind=kLoop, calls=%fused_computation.136 | loop fusion | bytes 40894464 | tf_op jit(solution)/shard_map/slice | solution.py:1243
  162.8 1.2 slice.230
  164.9 5.6 convolution_convert_fusion.5.refs_1_.refs_11_
  170.6 2.5 collective-permute-start.2
  175.5 2.8 fusion.39.refs_2_
  180.0 3.2 collective-permute-start.17
  187.8 109.1 %block_forward.2 = (f32[128,3328]{1,0:T(8,128)}, f32[128,3328]{1,0:T(8,128)}, f32[128,128]{1,0:T(8,128)}, f32[128,128]{1,0:T(8,128)}, f32[16,8,128]{2,1,0:T(8,12...) custom-call(f32[1]{0:T(128)} %bitcast.2.refs_0_, ...), custom_call_target="tpu_custom_call" | custom-call | tf_op jit(solution)/shard_map/block_forward/pallas_call | solution.py:768
  296.9 14.8 %fusion.54 = (bf16[1,4,4,96,3328]{4,3,2,1,0:T(8,128)(2,1)}, bf16[1,4,4,96,3328]{4,3,2,1,0:T(8,128)(2,1)}) fusion(bf16[2,4,4,96,3328]{4,3,2,1,0:T(8,128)(2,1)} %get-tuple-element.76), kind=kLoop, calls=%fused_computation.135 | loop fusion | bytes 40894464 | tf_op jit(solution)/shard_map/slice | solution.py:1243
  311.7 1.0 slice.236
  313.7 5.6 convolution_convert_fusion.4.refs_1_.refs_11_
  319.3 3.6 collective-permute-start.4
  326.0 2.7 fusion.58.refs_2_
  334.2 44.3 %block_forward.3 = (f32[128,3328]{1,0:T(8,128)}, f32[128,3328]{1,0:T(8,128)}, f32[128,128]{1,0:T(8,128)}, f32[128,128]{1,0:T(8,128)}, f32[16,8,128]{2,1,0:T(8,12...) custom-call(f32[1]{0:T(128)} %bitcast.2.refs_0_, ...), custom_call_target="tpu_custom_call" | custom-call | tf_op jit(solution)/shard_map/block_forward/pallas_call | solution.py:768
  378.4 47.6 %block_backward.2 = (bf16[128,1536]{1,0:T(8,128)(2,1)}, bf16[128,3072]{1,0:T(8,128)(2,1)}, f32[8,3072]{1,0:T(8,128)}, f32[128,3328]{1,0:T(8,128)}, f32[128,128]{...) custom-call(f32[1]{0:T(128)} %bitcast.2.refs_0_, bf16[128,1536]{1,0:T(8,128)(2,1)} %dynamic-slice_bitcast_fusion.refs_1_.g_ref, ...), custom_call_target="tpu_custom_call" | custom-call | tf_op jit(solution)/shard_map/block_backward/pallas_call | solution.py:1067
  427.6 7.2 collective-permute-start.8
  438.0 1.8 broadcast_select_fusion.11
  443.6 17.2 %input_backward.2 = (bf16[128,3328]{1,0:T(8,128)(2,1)}, bf16[128,3328]{1,0:T(8,128)(2,1)}, bf16[128,1536]{1,0:T(8,128)(2,1)}, f32[8,1536]{1,0:T(8,128)}) custom-call(f32[128,3328]{1,0:T(8,128)} %get-tuple-element.88.gsum_ref, f32[8,3328]{1,0:T(8,128)} %select_multiply_fusion.1.next_ref, f32[128,128]{1,0:T(8,128)} %get-tuple-element.89.dstep_ref, ...), custom_call_target="tpu_custom_call" | custom-call | tf_op jit(solution)/shard_map/input_backward/pallas_call | solution.py:144
  460.8 2.5 broadcast_select_fusion.3
  465.2 1.2 select_bitcast_fusion.3
  466.4 0.9 maximum_bitcast_fusion
  467.9 5.0 convolution_convert_fusion.3
  472.9 6.7 convolution_convert_fusion.1
  479.6 1.9 fusion.26
  481.5 99.2 %block_backward.3 = (bf16[128,1536]{1,0:T(8,128)(2,1)}, bf16[128,3072]{1,0:T(8,128)(2,1)}, f32[8,3072]{1,0:T(8,128)}, f32[128,3328]{1,0:T(8,128)}, f32[128,128]{...) custom-call(f32[1]{0:T(128)} %bitcast.2.refs_0_, ...), custom_call_target="tpu_custom_call" | custom-call | tf_op jit(solution)/shard_map/block_backward/pallas_call | solution.py:1067
  582.3 7.1 collective-permute-start.15
  591.8 1.7 broadcast_select_fusion.9
  596.7 17.2 %input_backward.3 = (bf16[128,3328]{1,0:T(8,128)(2,1)}, bf16[128,3328]{1,0:T(8,128)(2,1)}, bf16[128,1536]{1,0:T(8,128)(2,1)}, f32[8,1536]{1,0:T(8,128)}) custom-call(f32[128,3328]{1,0:T(8,128)} %get-tuple-element.109.gsum_ref, f32[8,3328]{1,0:T(8,128)} %select_multiply_fusion.next_ref, f32[128,128]{1,0:T(8,128)} %get-tuple-element.110.dstep_ref, ...), custom_call_target="tpu_custom_call" | custom-call | tf_op jit(solution)/shard_map/input_backward/pallas_call | solution.py:144
  614.0 1.8 broadcast_select_fusion.4
  615.8 2.4 broadcast_select_fusion.1
  620.6 5.1 convolution_convert_fusion.2
  625.7 1.1 select_bitcast_fusion.1
  626.8 0.9 maximum_bitcast_fusion.1
  627.7 8.2 %convolution_convert_fusion = bf16[1536,3328]{1,0:T(8,128)(2,1)} fusion(bf16[128,3328]{1,0:T(8,128)(2,1)} %collective-permute-done.18, bf16[128,3328]{1,0:T(8,128)(2,1)S(1)} %get-tuple-element.182, bf16[128,1536]{1,0:T(8,128)(2,1)} %collective-permute-done.17, bf16[128,1536]{1,0:T(8,128)(2,1)} %fusion.14), kind=kOutput, calls=%fused_computation | convolution fusion | flops 2627338240 | bytes 12713984 | tf_op jit(solution)/shard_map/dot_general | solution.py:34
  635.9 2.0 fusion.28
  637.9 125.3 %reduce_grads.1 = (f32[24,3328]{1,0:T(8,128)}, f32[48,768]{1,0:T(8,128)}, f32[24,3328]{1,0:T(8,128)}, f32[48,768]{1,0:T(8,128)}) custom-call(bf16[4,4,96,3328]{3,2,1,0:T(8,128)(2,1)} %bitcast.48.gi_ref, bf16[4,4,4,48,768]{4,3,2,1,0:T(8,128)(2,1)} %bitcast.126, bf16[4,96,1664]{2,1,0:T(8,128)(2,1)} %get-tuple-element.121.sa1, ...), custom_call_target="tpu_custom_call" | custom-call | tf_op jit(solution)/shard_map/reduce_grads/pallas_call | solution.py:1163
  763.3 0.9 broadcast_select_fusion.22
  764.2 3.1 collective-permute-start.23
  767.3 1.0 broadcast_select_fusion.15
  768.4 1.0 broadcast_select_fusion.21
  770.1 1.0 broadcast_select_fusion.12
  (231 shorter events, 52.7 us)
Async XLA Ops:
  0.6 10.9 %copy-start = (bf16[1,2,128,1536]{3,2,1,0:T(8,128)(2,1)S(1)}, bf16[1,2,128,1536]{3,2,1,0:T(8,128)(2,1)}, u32[]{:S(2)}) copy-start(bf16[1,2,128,1536]{3,2,1,0:T(8,128)(2,1)} %param.14) | copy-start | bytes 2359300
  6.6 9.9 %collective-permute-start = (bf16[24,3328]{1,0:T(8,128)(2,1)S(1)}, bf16[24,3328]{1,0:T(8,128)(2,1)S(1)}, u32[]{:S(2)}, u32[]{:S(2)}) collective-permute-start(bf16[24,3328]{1,0:T(8,128)(2,1)S(1)} %broadcast_select_fusion.18), channel_id=1, source_target_pairs={{0,64},{64,0},{1,65},{65,1},{2,66},{66,2},{3,67},{67,3},{4,68},{68... | collective-permute-start | bytes 479240 | tf_op jit(solution)/shard_map/ppermute | solution.py:214
  9.0 5.9 collective-permute-start.1
  148.0 16.9 %copy-start.9 = (bf16[1,2,128,1536]{3,2,1,0:T(8,128)(2,1)S(1)}, bf16[1,2,128,1536]{3,2,1,0:T(8,128)(2,1)}, u32[]{:S(2)}) copy-start(bf16[1,2,128,1536]{3,2,1,0:T(8,128)(2,1)} %param.13) | copy-start | bytes 2359300
  162.8 12.6 %slice-start.3 = ((s8[10223616]{0:T(1024)(128)(4,1)}), s8[1835008]{0:T(1024)(128)(4,1)S(1)}, s32[]{:S(2)}) async-start(s8[10223616]{0:T(1024)(128)(4,1)} %bitcast.116), calls=%async_computation.3 | async-start | bytes 3670016
  164.2 0.7 copy-start.14
  164.9 10.5 %slice-start.4 = ((s8[10223616]{0:T(1024)(128)(4,1)}), s8[4194304]{0:T(1024)(128)(4,1)S(1)}, s32[]{:S(2)}) async-start(s8[10223616]{0:T(1024)(128)(4,1)} %bitcast.116), calls=%async_computation.4 | async-start | bytes 8388608
  164.9 10.5 %slice-start.5 = ((s8[10223616]{0:T(1024)(128)(4,1)}), s8[4194304]{0:T(1024)(128)(4,1)S(1)}, s32[]{:S(2)}) async-start(s8[10223616]{0:T(1024)(128)(4,1)} %bitcast.116), calls=%async_computation.5 | async-start | bytes 8388608
  164.9 10.5 %copy-start.10 = (bf16[1,2,128,1536]{3,2,1,0:T(8,128)(2,1)S(1)}, bf16[1,2,128,1536]{3,2,1,0:T(8,128)(2,1)}, u32[]{:S(2)}) copy-start(bf16[1,2,128,1536]{3,2,1,0:T(8,128)(2,1)} %param.13) | copy-start | bytes 2359300
  170.6 7.7 copy-start.6
  170.6 15.9 %collective-permute-start.2 = (bf16[8,3328]{1,0:T(8,128)(2,1)S(1)}, bf16[8,3328]{1,0:T(8,128)(2,1)S(1)}, u32[]{:S(2)}, u32[]{:S(2)}) collective-permute-start(bf16[8,3328]{1,0:T(8,128)(2,1)S(1)} %slice.232), channel_id=1, source_target_pairs={{0,4},{4,8},{8,12},{12,16},{16,20},{20,24},{24,28},{28,32},{32,36}... | collective-permute-start | bytes 159752 | tf_op jit(solution)/shard_map/ppermute | solution.py:1236
  173.1 13.4 %collective-permute-start.3 = (bf16[8,3328]{1,0:T(8,128)(2,1)S(1)}, bf16[8,3328]{1,0:T(8,128)(2,1)S(1)}, u32[]{:S(2)}, u32[]{:S(2)}) collective-permute-start(bf16[8,3328]{1,0:T(8,128)(2,1)S(1)} %slice.232), channel_id=1, source_target_pairs={{60,80},{61,81},{62,82},{63,83}} | collective-permute-start | bytes 159752 | tf_op jit(solution)/shard_map/ppermute | solution.py:1237
  175.5 3.6 copy-start.8
  180.0 447.7 %collective-permute-start.17 = (bf16[128,1536]{1,0:T(8,128)(2,1)}, bf16[128,1536]{1,0:T(8,128)(2,1)}, u32[]{:S(2)}, u32[]{:S(2)}) collective-permute-start(bf16[128,1536]{1,0:T(8,128)(2,1)} %fusion.14), channel_id=1, source_target_pairs={{0,64},{64,0},{1,65},{65,1},{2,66},{66,2},{3,67},{67,3},{4,68},{68... | collective-permute-start | bytes 1179656 | tf_op jit(solution)/shard_map/ppermute | solution.py:214
  296.9 16.2 %copy-start.2 = (bf16[128,1536]{1,0:T(8,128)(2,1)S(1)}, bf16[128,1536]{1,0:T(8,128)(2,1)}, u32[]{:S(2)}) copy-start(bf16[128,1536]{1,0:T(8,128)(2,1)} %get-tuple-element.75.refs_7_.x_ref) | copy-start | bytes 1179652
  312.7 13.3 %slice-start = ((s8[10223616]{0:T(1024)(128)(4,1)}), s8[1835008]{0:T(1024)(128)(4,1)S(1)}, s32[]{:S(2)}) async-start(s8[10223616]{0:T(1024)(128)(4,1)} %bitcast.113), calls=%async_computation | async-start | bytes 3670016
  312.9 0.7 copy-start.13
  313.7 12.4 %slice-start.1 = ((s8[10223616]{0:T(1024)(128)(4,1)}), s8[4194304]{0:T(1024)(128)(4,1)S(1)}, s32[]{:S(2)}) async-start(s8[10223616]{0:T(1024)(128)(4,1)} %bitcast.113), calls=%async_computation.1 | async-start | bytes 8388608
  313.7 12.4 %slice-start.2 = ((s8[10223616]{0:T(1024)(128)(4,1)}), s8[4194304]{0:T(1024)(128)(4,1)S(1)}, s32[]{:S(2)}) async-start(s8[10223616]{0:T(1024)(128)(4,1)} %bitcast.113), calls=%async_computation.2 | async-start | bytes 8388608
  319.2 9.5 %copy-start.5 = (bf16[128,3328]{1,0:T(8,128)(2,1)}, bf16[128,3328]{1,0:T(8,128)(2,1)S(1)}, u32[]{:S(2)}) copy-start(bf16[128,3328]{1,0:T(8,128)(2,1)S(1)} %convolution_convert_fusion.4.refs_1_.refs_11_) | copy-start | bytes 2555908
  319.3 13.6 %collective-permute-start.4 = (bf16[8,3328]{1,0:T(8,128)(2,1)S(1)}, bf16[8,3328]{1,0:T(8,128)(2,1)S(1)}, u32[]{:S(2)}, u32[]{:S(2)}) collective-permute-start(bf16[8,3328]{1,0:T(8,128)(2,1)S(1)} %slice.238), channel_id=1, source_target_pairs={{0,4},{4,8},{8,12},{12,16},{16,20},{20,24},{24,28},{28,32},{32,36}... | collective-permute-start | bytes 159752 | tf_op jit(solution)/shard_map/ppermute | solution.py:1236
  322.9 10.0 %collective-permute-start.5 = (bf16[8,3328]{1,0:T(8,128)(2,1)S(1)}, bf16[8,3328]{1,0:T(8,128)(2,1)S(1)}, u32[]{:S(2)}, u32[]{:S(2)}) collective-permute-start(bf16[8,3328]{1,0:T(8,128)(2,1)S(1)} %slice.238), channel_id=1, source_target_pairs={{60,80},{61,81},{62,82},{63,83}} | collective-permute-start | bytes 159752 | tf_op jit(solution)/shard_map/ppermute | solution.py:1237
  325.2 147.7 %collective-permute-start.9 = (bf16[128,1536]{1,0:T(8,128)(2,1)S(1)}, bf16[128,1536]{1,0:T(8,128)(2,1)}, u32[]{:S(2)}, u32[]{:S(2)}) collective-permute-start(bf16[128,1536]{1,0:T(8,128)(2,1)S(1)} %fusion.17), channel_id=1, source_target_pairs={{0,64},{64,0},{1,65},{65,1},{2,66},{66,2},{3,67},{67,3},{4,68},{68... | collective-permute-start | bytes 1179656 | tf_op jit(solution)/shard_map/ppermute | solution.py:214
  378.4 58.0 %copy-start.3 = (bf16[128,1536]{1,0:T(8,128)(2,1)S(1)}, bf16[128,1536]{1,0:T(8,128)(2,1)}, u32[]{:S(2)}) copy-start(bf16[128,1536]{1,0:T(8,128)(2,1)} %get-tuple-element.75.refs_7_.x_ref) | copy-start | bytes 1179652
  378.4 57.9 %copy-start.11 = (bf16[128,1536]{1,0:T(8,128)(2,1)S(1)}, bf16[128,1536]{1,0:T(8,128)(2,1)}, u32[]{:S(2)}) copy-start(bf16[128,1536]{1,0:T(8,128)(2,1)} %get-tuple-element.78) | copy-start | bytes 1179652
  426.9 14.7 %collective-permute-start.7 = (f32[8,3328]{1,0:T(8,128)S(1)}, f32[8,3328]{1,0:T(8,128)S(1)}, u32[]{:S(2)}, u32[]{:S(2)}) collective-permute-start(f32[8,3328]{1,0:T(8,128)S(1)} %slice.197), channel_id=1, source_target_pairs={{80,60},{81,61},{82,62},{83,63}} | collective-permute-start | bytes 319496 | tf_op jit(solution)/shard_map/ppermute | solution.py:1264
  427.6 14.6 %collective-permute-start.8 = (f32[8,3328]{1,0:T(8,128)S(1)}, f32[8,3328]{1,0:T(8,128)S(1)}, u32[]{:S(2)}, u32[]{:S(2)}) collective-permute-start(f32[8,3328]{1,0:T(8,128)S(1)} %slice.197), channel_id=1, source_target_pairs={{4,0},{8,4},{12,8},{16,12},{20,16},{24,20},{28,24},{32,28},{36,32}... | collective-permute-start | bytes 319496 | tf_op jit(solution)/shard_map/ppermute | solution.py:1263
  437.2 27.5 %collective-permute-start.6 = (bf16[128,1536]{1,0:T(8,128)(2,1)}, bf16[128,1536]{1,0:T(8,128)(2,1)}, u32[]{:S(2)}, u32[]{:S(2)}) collective-permute-start(bf16[128,1536]{1,0:T(8,128)(2,1)} %broadcast_select_fusion.6), channel_id=1, source_target_pairs={{0,64},{64,0},{1,65},{65,1},{2,66},{66,2},{3,67},{67,3},{4,68},{68... | collective-permute-start | bytes 1179656 | tf_op jit(solution)/shard_map/ppermute | solution.py:214
  441.6 25.7 %collective-permute-start.12 = (bf16[128,3072]{1,0:T(8,128)(2,1)}, bf16[128,3072]{1,0:T(8,128)(2,1)}, u32[]{:S(2)}, u32[]{:S(2)}) collective-permute-start(bf16[128,3072]{1,0:T(8,128)(2,1)} %get-tuple-element.107), channel_id=1, source_target_pairs={{0,64},{64,0},{1,65},{65,1},{2,66},{66,2},{3,67},{67,3},{4,68},{68... | collective-permute-start | bytes 2359304 | tf_op jit(solution)/shard_map/ppermute | solution.py:214
  442.2 25.2 %collective-permute-start.13 = (bf16[128,768]{1,0:T(8,128)(2,1)}, bf16[128,768]{1,0:T(8,128)(2,1)}, u32[]{:S(2)}, u32[]{:S(2)}) collective-permute-start(bf16[128,768]{1,0:T(8,128)(2,1)} %get-tuple-element.199), channel_id=1, source_target_pairs={{0,64},{64,0},{1,65},{65,1},{2,66},{66,2},{3,67},{67,3},{4,68},{68... | collective-permute-start | bytes 589832 | tf_op jit(solution)/shard_map/ppermute | solution.py:214
  460.7 4.5 copy-start.4
  464.7 8.2 %collective-permute-start.10 = (bf16[128,3328]{1,0:T(8,128)(2,1)}, bf16[128,3328]{1,0:T(8,128)(2,1)S(1)}, u32[]{:S(2)}, u32[]{:S(2)}) collective-permute-start(bf16[128,3328]{1,0:T(8,128)(2,1)} %get-tuple-element.185), channel_id=1, source_target_pairs={{0,64},{64,0},{1,65},{65,1},{2,66},{66,2},{3,67},{67,3},{4,68},{68... | collective-permute-start | bytes 2555912 | tf_op jit(solution)/shard_map/ppermute | solution.py:214
  467.4 152.8 %collective-permute-start.20 = (bf16[128,3072]{1,0:T(8,128)(2,1)}, bf16[128,3072]{1,0:T(8,128)(2,1)}, u32[]{:S(2)}, u32[]{:S(2)}) collective-permute-start(bf16[128,3072]{1,0:T(8,128)(2,1)} %get-tuple-element.119), channel_id=1, source_target_pairs={{0,64},{64,0},{1,65},{65,1},{2,66},{66,2},{3,67},{67,3},{4,68},{68... | collective-permute-start | bytes 2359304 | tf_op jit(solution)/shard_map/ppermute | solution.py:214
  467.4 12.2 %collective-permute-start.11 = (f32[1536,128]{1,0:T(8,128)S(1)}, f32[1536,128]{1,0:T(8,128)S(1)}, u32[]{:S(2)}, u32[]{:S(2)}) collective-permute-start(f32[1536,128]{1,0:T(8,128)S(1)} %reshape.276), channel_id=1, source_target_pairs={{0,64},{64,0},{1,65},{65,1},{2,66},{66,2},{3,67},{67,3},{4,68},{68... | collective-permute-start | bytes 2359304 | tf_op jit(solution)/shard_map/ppermute | solution.py:214
  581.7 13.8 %collective-permute-start.14 = (f32[8,3328]{1,0:T(8,128)S(1)}, f32[8,3328]{1,0:T(8,128)S(1)}, u32[]{:S(2)}, u32[]{:S(2)}) collective-permute-start(f32[8,3328]{1,0:T(8,128)S(1)} %slice.207), channel_id=1, source_target_pairs={{80,60},{81,61},{82,62},{83,63}} | collective-permute-start | bytes 319496 | tf_op jit(solution)/shard_map/ppermute | solution.py:1264
  582.3 13.1 %collective-permute-start.15 = (f32[8,3328]{1,0:T(8,128)S(1)}, f32[8,3328]{1,0:T(8,128)S(1)}, u32[]{:S(2)}, u32[]{:S(2)}) collective-permute-start(f32[8,3328]{1,0:T(8,128)S(1)} %slice.207), channel_id=1, source_target_pairs={{4,0},{8,4},{12,8},{16,12},{20,16},{24,20},{28,24},{32,28},{36,32}... | collective-permute-start | bytes 319496 | tf_op jit(solution)/shard_map/ppermute | solution.py:1263
  595.4 25.2 %collective-permute-start.21 = (bf16[128,768]{1,0:T(8,128)(2,1)}, bf16[128,768]{1,0:T(8,128)(2,1)}, u32[]{:S(2)}, u32[]{:S(2)}) collective-permute-start(bf16[128,768]{1,0:T(8,128)(2,1)} %get-tuple-element.197), channel_id=1, source_target_pairs={{0,64},{64,0},{1,65},{65,1},{2,66},{66,2},{3,67},{67,3},{4,68},{68... | collective-permute-start | bytes 589832 | tf_op jit(solution)/shard_map/ppermute | solution.py:214
  596.7 17.2 %copy-start.7 = (bf16[128,1536]{1,0:T(8,128)(2,1)S(1)}, bf16[128,1536]{1,0:T(8,128)(2,1)}, u32[]{:S(2)}) copy-start(bf16[128,1536]{1,0:T(8,128)(2,1)} %get-tuple-element.91.refs_1_.g_ref) | copy-start | bytes 1179652
  615.8 9.9 %collective-permute-start.16 = (bf16[128,1536]{1,0:T(8,128)(2,1)}, bf16[128,1536]{1,0:T(8,128)(2,1)}, u32[]{:S(2)}, u32[]{:S(2)}) collective-permute-start(bf16[128,1536]{1,0:T(8,128)(2,1)} %broadcast_select_fusion.4), channel_id=1, source_target_pairs={{0,64},{64,0},{1,65},{65,1},{2,66},{66,2},{3,67},{67,3},{4,68},{68... | collective-permute-start | bytes 1179656 | tf_op jit(solution)/shard_map/ppermute | solution.py:214
  618.2 9.5 %collective-permute-start.18 = (bf16[128,3328]{1,0:T(8,128)(2,1)}, bf16[128,3328]{1,0:T(8,128)(2,1)}, u32[]{:S(2)}, u32[]{:S(2)}) collective-permute-start(bf16[128,3328]{1,0:T(8,128)(2,1)} %get-tuple-element.183), channel_id=1, source_target_pairs={{0,64},{64,0},{1,65},{65,1},{2,66},{66,2},{3,67},{67,3},{4,68},{68... | collective-permute-start | bytes 2555912 | tf_op jit(solution)/shard_map/ppermute | solution.py:214
  620.2 15.8 %collective-permute-start.19 = (f32[1536,128]{1,0:T(8,128)S(1)}, f32[1536,128]{1,0:T(8,128)S(1)}, u32[]{:S(2)}, u32[]{:S(2)}) collective-permute-start(f32[1536,128]{1,0:T(8,128)S(1)} %reshape.286), channel_id=1, source_target_pairs={{0,64},{64,0},{1,65},{65,1},{2,66},{66,2},{3,67},{67,3},{4,68},{68... | collective-permute-start | bytes 2359304 | tf_op jit(solution)/shard_map/ppermute | solution.py:214
  620.6 5.1 copy-start.12
  637.9 138.9 %copy-start.1 = (bf16[1,2,128,1536]{3,2,1,0:T(8,128)(2,1)S(1)}, bf16[1,2,128,1536]{3,2,1,0:T(8,128)(2,1)}, u32[]{:S(2)}) copy-start(bf16[1,2,128,1536]{3,2,1,0:T(8,128)(2,1)} %param.14) | copy-start | bytes 2359300
  764.2 4.2 collective-permute-start.23
  768.3 1.8 collective-permute-start.22

commit v3 on v1

v3 whole, which is shorter than its diff:
```python
import functools
import types

import jax
import jax.numpy as jnp
from jax import lax
from jax.experimental import pallas as pl
from jax.experimental.pallas import tpu as pltpu
from jax.sharding import PartitionSpec as P

D = 1536
INNER = 3072
HEADS = 48
STATE = 128
BLOCK_LEN = 256
BLOCKS = 8
TOK = 128
CONV = INNER + 2 * STATE
HALF = CONV
GATE0 = 256
CUT = HALF // 2
WALF = D // 2
OWNERS = 16
OWN = 192
EPS = 1e-05
F32 = jnp.float32
BF16 = jnp.bfloat16
MESH = pl.DeviceIdType.MESH
VMEM_LIMIT = 60 * 1024 * 1024
LANES = (0, 1, 2, 8, 9, 10)
ROWS_ALL = ("seq", "wsh")
ROW_MID, ROW_NORM = 5, 6
ROW_BIAS, ROW_DECAY, ROW_SKIP = 5, 6, 7


def dot32(left, right, dims=((1,), (0,))):
    return lax.dot_general(left, right, (dims, ((), ())), preferred_element_type=F32)


def split_left(exact, value, terms):
    total = None
    for _ in range(terms):
        part = value.astype(BF16)
        value = value - part.astype(F32)
        term = dot32(exact, part)
        total = term if total is None else total + term
    return total


def split_right(value, exact, terms, dims=((1,), (0,))):
    total = None
    for _ in range(terms):
        part = value.astype(BF16)
        value = value - part.astype(F32)
        term = dot32(part, exact, dims)
        total = term if total is None else total + term
    return total


def pair_cols(tile, q):
    lane = lax.broadcasted_iota(jnp.int32, (TOK, 128), 1)
    a = jnp.broadcast_to(tile[:, LANES[2 * q] : LANES[2 * q] + 1], (TOK, 128))
    b = jnp.broadcast_to(tile[:, LANES[2 * q + 1] : LANES[2 * q + 1] + 1], (TOK, 128))
    return a, b, jnp.where(lane < 64, a, b)


def pair_row(row, q):
    lane = lax.broadcasted_iota(jnp.int32, (1, 128), 1)
    a = jnp.broadcast_to(row[:, LANES[2 * q] : LANES[2 * q] + 1], (1, 128))
    b = jnp.broadcast_to(row[:, LANES[2 * q + 1] : LANES[2 * q + 1] + 1], (1, 128))
    return jnp.where(lane < 64, a, b)


def to_front(tile, i):
    return pltpu.roll(tile, lax.rem(128 - 16 * i, 128), 1)


def conv_of(cat, taps):
    total = taps[4:5] + taps[3:4] * cat[8 : 8 + TOK]
    for k in range(3):
        total = total + taps[k : k + 1] * cat[5 + k : 5 + k + TOK]
    return total


def tri_of(lower):
    row = lax.broadcasted_iota(jnp.int32, (TOK, TOK), 0)
    col = lax.broadcasted_iota(jnp.int32, (TOK, TOK), 1)
    return row >= col if lower else row <= col


def head_lanes():
    lane = lax.broadcasted_iota(jnp.int32, (TOK, 128), 1)
    return (lane % 8) < 3


def group_cols(i, q):
    return pl.ds(pl.multiple_of(i * 384 + q * 128, 128), 128)


def gate_cols(i, q):
    return pl.ds(pl.multiple_of(GATE0 + i * 384 + q * 128, 128), 128)


def in_hbm(*shape, dtype=BF16):
    return jax.ShapeDtypeStruct(shape, dtype), pl.BlockSpec(memory_space=pl.ANY)


def in_vmem(*shape, dtype=F32):
    return jax.ShapeDtypeStruct(shape, dtype), pl.BlockSpec(memory_space=pltpu.VMEM)


def call(body, name, ident, inputs, outputs, scratch):
    spaces = {"h": pl.ANY, "v": pltpu.VMEM, "s": pltpu.SMEM}
    names = [key for key in inputs] + [key for key in outputs] + [key for key in scratch]

    def kernel(*refs):
        body(types.SimpleNamespace(**dict(zip(names, refs))))

    out = pl.pallas_call(
        kernel,
        out_shape=tuple(shape for shape, _ in outputs.values()),
        in_specs=[pl.BlockSpec(memory_space=spaces[kind]) for kind, _ in inputs.values()],
        out_specs=tuple(spec for _, spec in outputs.values()),
        scratch_shapes=list(scratch.values()),
        compiler_params=pltpu.CompilerParams(
            collective_id=ident, has_side_effects=True, vmem_limit_bytes=VMEM_LIMIT
        ),
        name=name,
    )(*[value for _, value in inputs.values()])
    return types.SimpleNamespace(**dict(zip(outputs, out)))


def dma_sems(count):
    return pltpu.SemaphoreType.DMA((count,))


def places():
    section = lax.axis_index("section")
    seq = lax.axis_index("seq")
    return section, seq // 4, lax.rem(seq, 4), lax.axis_index("wsh")


def x_peer(k):
    return {"wsh": lax.rem(lax.axis_index("wsh") + k, 4)}


def z_peer(k):
    _, y, z, _ = places()
    return {"seq": y * 4 + lax.rem(z + k, 4)}


def y_peer(k):
    _, y, z, _ = places()
    return {"seq": lax.rem(y + k, 4) * 4 + z}


def sibling():
    return {"section": 1 - lax.axis_index("section")}


def say_hello(peer):
    pl.semaphore_signal(pltpu.get_barrier_semaphore(), inc=1, device_id=peer, device_id_type=MESH)


def greet_axes():
    for k in range(1, 4):
        for peer in (x_peer(k), y_peer(k), z_peer(k)):
            say_hello(peer)
    say_hello(sibling())
    pl.semaphore_wait(pltpu.get_barrier_semaphore(), 10)


def fetch(src, dst, sem):
    copy = pltpu.make_async_copy(src, dst, sem)
    copy.start()
    return copy


class Net:
    def __init__(self, send, recv):
        self.send, self.recv = send, recv
        self.count = 0
        self.started = []

    def go(self, src, dst, peer):
        copy = pltpu.make_async_remote_copy(
            src_ref=src, dst_ref=dst, send_sem=self.send.at[self.count], recv_sem=self.recv.at[self.count],
            device_id=peer, device_id_type=MESH,
        )
        copy.start()
        self.count += 1
        self.started.append(copy)
        return copy

    def drain(self):
        for copy in self.started:
            copy.wait_send()


class Gather:
    def __init__(self, net, p, o, w, wo, stage, rows, own):
        self.net, self.p, self.o, self.w, self.wo = net, p, o, w, wo
        self.stage, self.rows, self.own = stage, rows, own
        self.place = places()
        self.left, self.right = pl.ds(0, CUT), pl.ds(CUT, CUT)
        self.near, self.far, self.passed = {}, {}, []
        self.peers = (y_peer, z_peer, x_peer)

    def band(self, kind, j, moved):
        c, y, z, x = self.place
        if kind == 0:
            return self.w.at[c, lax.rem(y + 4 - moved, 4), lax.rem(z + 4 - j, 4), :, self.left]
        if kind == 1:
            return self.w.at[c, lax.rem(y + 4 - j, 4), lax.rem(z + 4 - moved, 4), :, self.right]
        return self.wo.at[c, lax.rem(y + 4 - j, 4), :, lax.rem(x + 4 - moved, 4)]

    def pass_on(self, part):
        self.passed.append(self.net.go(part, part, sibling()))

    def begin(self):
        c, y, z, x = self.place
        go = self.net.go
        self.first, self.oz = [], []
        for k in range(1, 4):
            self.first.append(go(self.p, self.stage.at[x], x_peer(k)))
            self.oz.append(go(self.o, self.wo.at[c, y, z, x], z_peer(k)))
        self.own_o = fetch(self.o, self.wo.at[c, y, z, x], self.own.at[0])
        self.stage[x] = self.p[...]

    def rows_in(self):
        c, y, z, x = self.place
        go = self.net.go
        for copy in self.first:
            copy.wait_recv()
        self.rows[...] = jnp.concatenate(
            [self.stage[n].astype(F32)[:24] for n in range(4)], axis=0
        ).astype(BF16)
        self.az, self.by, self.oy = [], [], []
        for k in range(1, 4):
            self.az.append(go(self.rows.at[:, self.left], self.w.at[c, y, z, :, self.left], z_peer(k)))
            self.by.append(go(self.rows.at[:, self.right], self.w.at[c, y, z, :, self.right], y_peer(k)))
        own_w = fetch(self.rows, self.w.at[c, y, z], self.own.at[1])
        self.own_o.wait()
        for copy in self.oz:
            copy.wait_recv()
        lane = self.wo.at[c, y, :, x]
        for k in range(1, 4):
            self.oy.append(go(lane, lane, y_peer(k)))
        own_w.wait()
        self.spread(0)

    def spread(self, j):
        if j:
            for copies in (self.az, self.by, self.oy):
                copies[j - 1].wait_recv()
        for k in (1, 3):
            for kind in range(3):
                part = self.band(kind, j, 0)
                self.near[kind, j, k] = self.net.go(part, part, self.peers[kind](k))
        for kind in range(3):
            self.pass_on(self.band(kind, j, 0))

    def relay(self, j):
        for k in (1, 3):
            for kind in range(3):
                self.near[kind, j, k].wait_recv()
                part = self.band(kind, j, k)
                if (k == 1) == (j < 2):
                    self.far[kind, j] = self.net.go(part, part, self.peers[kind](k))
                self.pass_on(part)

    def last(self, j):
        for kind in range(3):
            self.far[kind, j].wait_recv()
            self.pass_on(self.band(kind, j, 2))

    def end(self):
        for copy in self.passed:
            copy.wait_recv()


def gather_scratch():
    return {
        "stage": pltpu.VMEM((4, 32, HALF), BF16),
        "rows": pltpu.VMEM((96, HALF), BF16),
        "own": dma_sems(2),
        "net_send": dma_sems(150),
        "net_recv": dma_sems(150),
    }


def lane_at(shape):
    return lax.broadcasted_iota(jnp.int32, shape, 1)


def place_chunks(cells, width, total):
    tiles = [jnp.zeros((8, 128), F32) for _ in range(total // 128)]
    lane = lane_at((8, 128))
    for d in range(64):
        t, off = (width * d) // 128, (width * d) % 128
        moved = pltpu.roll(cells(d), off, 1) if off else cells(d)
        stop = off + width
        tiles[t] = jnp.where((lane >= off) & (lane < min(stop, 128)), moved, tiles[t])
        if stop > 128:
            tiles[t + 1] = jnp.where(lane < stop - 128, moved, tiles[t + 1])
    return tiles


def take_chunk(ref, base, width, d):
    start = base + width * d
    t, off = start // 128, start % 128
    tile = ref[:, 128 * t : 128 * t + 128]
    tile = pltpu.roll(tile, 128 - off, 1) if off else tile
    if off + width > 128:
        after = pltpu.roll(ref[:, 128 * t + 128 : 128 * t + 256], 128 - off, 1)
        tile = jnp.where(lane_at((8, 128)) < 128 - off, tile, after)
    return tile


def start_body(r):
    c, y, z, x = places()
    greet_axes()
    net = Net(r.net_send, r.net_recv)
    pad = jnp.zeros((8, 1), F32)

    def tall(value):
        return jnp.concatenate(
            [value.astype(F32), jnp.broadcast_to(pad, (8, value.shape[1]))], axis=0
        ).astype(BF16)

    r.mine[0, :, :INNER] = tall(r.inner[...])
    r.mine[0, :, INNER:] = tall(r.bc[...])
    r.mine[1, :, :128] = tall(r.step[...])
    r.mine[1, :, 128:GATE0] = jnp.zeros((32, 128), BF16)
    r.mine[1, :, GATE0:] = tall(r.gate[...])
    given = pl.ds(pl.multiple_of((1 - c) * WALF, 128), WALF)
    swaps = [
        net.go(r.mine.at[1 - c], r.half.at[c], sibling()),
        net.go(r.out.at[:, given], r.halo.at[c], sibling()),
    ]
    small = [net.go(r.blob, r.cells.at[c, y, z, x], x_peer(k)) for k in range(1, 4)]
    r.half[c] = r.mine[c]
    r.halo[c] = jnp.where(c == 0, r.out[:, :WALF], r.out[:, WALF:])
    r.cells[c, y, z, x] = r.blob[...]
    for copy in swaps:
        copy.wait_recv()
    ga = Gather(net, r.half.at[0], r.halo.at[0], r.w, r.wo, r.stage, r.rows, r.own)
    ga.begin()
    for copy in small:
        copy.wait_recv()
    small = [net.go(r.cells.at[c, y, z], r.cells.at[c, y, z], z_peer(k)) for k in range(1, 4)]
    ga.rows_in()
    for copy in small:
        copy.wait_recv()
    small = [net.go(r.cells.at[c, y], r.cells.at[c, y], y_peer(k)) for k in range(1, 4)]
    for j in range(1, 4):
        ga.spread(j)
    for copy in small:
        copy.wait_recv()
    pair = net.go(r.cells.at[c], r.cells.at[c], sibling())
    ga.relay(0)
    r.p1[...] = r.half[1]
    r.o1[...] = r.halo[1]
    ga.relay(1)
    pair.wait_recv()
    for layer in range(2):
        def first_tile(d):
            return r.cells[layer, d // 16, (d // 4) % 4, d % 4, 0:8]

        def second_tile(d):
            return r.cells[layer, d // 16, (d // 4) % 4, d % 4, 8:16]

        for t, tile in enumerate(place_chunks(first_tile, 48, INNER)):
            r.taps[layer, :, 128 * t : 128 * t + 128] = tile
        for t, tile in enumerate(place_chunks(second_tile, 4, 2 * STATE)):
            r.taps[layer, :, INNER + 128 * t : INNER + 128 * t + 128] = tile
        for t, tile in enumerate(place_chunks(first_tile, 24, D)):
            r.gain[layer, :, 128 * t : 128 * t + 128] = tile
        lane = lane_at((8, 128))
        heads = jnp.zeros((8, 128), F32)
        for j in range(OWNERS):
            moved = pltpu.roll(second_tile(4 * j), 8 * j, 1) if j else second_tile(0)
            heads = jnp.where((lane >= 8 * j) & (lane < 8 * j + 3), moved, heads)
        r.heads[layer] = heads
    ga.relay(2)
    ga.relay(3)
    for j in range(4):
        ga.last(j)
    ga.end()
    net.drain()


def start_up(inner, bc, step, gate, out, blob):
    return call(
        start_body, "gather_weights", 1,
        {
            "inner": ("v", inner), "bc": ("v", bc), "step": ("v", step), "gate": ("v", gate), "out": ("v", out),
            "blob": ("v", blob),
        },
        {
            "w": in_hbm(2, 4, 4, 96, HALF),
            "wo": in_hbm(2, 4, 4, 4, 48, WALF),
            "p1": in_vmem(32, HALF, dtype=BF16),
            "o1": in_vmem(48, WALF, dtype=BF16),
            "taps": in_vmem(2, 8, CONV),
            "gain": in_vmem(2, 8, D),
            "heads": in_vmem(2, 8, 128),
        },
        {
            "mine": pltpu.VMEM((2, 32, HALF), BF16),
            "half": pltpu.VMEM((2, 32, HALF), BF16),
            "halo": pltpu.VMEM((2, 48, WALF), BF16),
            "cells": pltpu.VMEM((2, 4, 4, 4, 16, 128), F32),
            **gather_scratch(),
        },
    )


class Exchange:
    def __init__(self, backward, r):
        self.backward, self.r = backward, r
        self.me = lax.axis_index("seq")
        self.section = lax.axis_index("section")

    def first_copy(self, peer, d):
        r = self.r
        return pltpu.make_async_remote_copy(
            src_ref=r.ds.at[peer], dst_ref=r.got.at[self.me], send_sem=r.send_a.at[d], recv_sem=r.recv_a.at[d],
            device_id={"seq": peer}, device_id_type=MESH,
        )

    def send(self, peer):
        d = lax.rem(peer + OWNERS - self.me, OWNERS)

        @pl.when(d != 0)
        def _():
            self.first_copy(peer, d).start()

        @pl.when(d == 0)
        def _():
            self.r.got[self.me] = self.r.ds[self.me]

    def back_copy(self, d):
        r = self.r
        peer = lax.rem(self.me + d, OWNERS)
        return pltpu.make_async_remote_copy(
            src_ref=r.ready.at[peer], dst_ref=r.back.at[self.me], send_sem=r.send_b.at[d], recv_sem=r.recv_b.at[d],
            device_id={"seq": peer}, device_id_type=MESH,
        )

    def scan(self, decays):
        r = self.r

        def rows_of(dec):
            return jnp.concatenate([jnp.broadcast_to(dec[h : h + 1], (64, 128)) for h in range(3)], axis=0)

        for d in range(1, OWNERS):
            self.first_copy(lax.rem(self.me + d, OWNERS), d).wait_recv()
        r.final[...] = jnp.zeros((OWN, STATE), F32)
        r.fade[0] = jnp.ones((8, 128), F32)

        def step(n, carry):
            c = OWNERS - 1 - n if self.backward else n
            state = r.final[...]
            r.kept[c] = state
            dec = decays[c]
            r.final[...] = rows_of(dec) * state + r.got[c].astype(F32)
            r.fade[n + 1] = r.fade[n] * dec
            return carry

        lax.fori_loop(0, OWNERS, step, 0)
        swap = pltpu.make_async_remote_copy(
            src_ref=r.final, dst_ref=r.other, send_sem=r.swap_s.at[0], recv_sem=r.swap_s.at[1],
            device_id=sibling(), device_id_type=MESH,
        )
        swap.start()
        takes = 0 if self.backward else 1
        r.begin[...] = jnp.zeros((OWN, STATE), F32)

        @pl.when(self.section == takes)
        def _():
            swap.wait_recv()
            r.begin[...] = r.other[...]

        begin = r.begin[...]
        for d in range(OWNERS):
            c = lax.rem(self.me + d, OWNERS)
            n = OWNERS - 1 - c if self.backward else c
            value = (r.kept[c] + rows_of(r.fade[n]) * begin).astype(BF16)
            if d == 0:
                r.back[c] = value
            else:
                r.ready[c] = value
                self.back_copy(d).start()

        @pl.when(self.section != takes)
        def _():
            swap.wait_recv()

        swap.wait_send()

    def finish(self):
        for d in range(1, OWNERS):
            self.back_copy(d).wait_recv()

    def drain(self):
        for d in range(1, OWNERS):
            self.first_copy(lax.rem(self.me + d, OWNERS), d).wait_send()
            self.back_copy(d).wait_send()


def exchange_scratch():
    block = pltpu.VMEM((OWNERS, OWN, STATE), BF16)
    part = pltpu.VMEM((OWN, STATE), F32)
    return {
        "ds": block, "got": block, "back": block, "ready": block,
        "kept": pltpu.VMEM((OWNERS, OWN, STATE), F32), "fade": pltpu.VMEM((OWNERS + 1, 8, 128), F32),
        "final": part, "other": part, "begin": part,
        "send_a": dma_sems(OWNERS), "recv_a": dma_sems(OWNERS), "send_b": dma_sems(OWNERS), "recv_b": dma_sems(OWNERS),
        "swap_s": dma_sems(2),
    }


def head_rows_at(ref, i, q):
    parts = []
    for h in (2 * q, 2 * q + 1):
        parts.append(ref[2 * i + h // 3, pl.ds(64 * (h % 3), 64), :])
    return jnp.concatenate(parts, axis=0)


def store_heads(ref, i, q, value):
    for n, h in enumerate((2 * q, 2 * q + 1)):
        ref[2 * i + h // 3, pl.ds(64 * (h % 3), 64), :] = value[64 * n : 64 * n + 64]


def own_group(n):
    return lax.rem(lax.axis_index("seq") // 2 + n, 8)


def greet_layer(rider, forward):
    me = lax.axis_index("seq")
    section = lax.axis_index("section")
    wsh = lax.axis_index("wsh")
    barrier = pltpu.get_barrier_semaphore()
    for d in range(1, OWNERS):
        say_hello({"seq": lax.rem(me + d, OWNERS)})
    say_hello(sibling())
    if rider:
        for k in range(1, 4):
            say_hello(x_peer(k))
    count = OWNERS + (3 if rider else 0)
    late = {"section": 0, "seq": 15, "wsh": wsh}
    if forward:

        @pl.when((section == 1) & ((me == 0) | (me == 4)))
        def _():
            pl.semaphore_signal(barrier, inc=1, device_id=late, device_id_type=MESH)

        more = jnp.where((section == 0) & (me == 15), 2, 0)
    else:

        @pl.when((section == 0) & (me == 15))
        def _():
            for seq in (0, 4):
                pl.semaphore_signal(
                    barrier, inc=1, device_id={"section": 1, "seq": seq, "wsh": wsh}, device_id_type=MESH
                )

        more = jnp.where((section == 1) & ((me == 0) | (me == 4)), 1, 0)
    pl.semaphore_wait(barrier, count + more)


def halo_copy(src, dst, sems, n, section, seq):
    return pltpu.make_async_remote_copy(
        src_ref=src, dst_ref=dst, send_sem=sems.at[n], recv_sem=sems.at[2 + n],
        device_id={"section": section, "seq": seq, "wsh": lax.axis_index("wsh")}, device_id_type=MESH,
    )


class Halo:
    def __init__(self, src, near, far, sems, forward):
        me = lax.axis_index("seq")
        section = lax.axis_index("section")
        edge = 15 if forward else 0
        if forward:
            crossing = (section == 0) & (me == 15)
            jumping = crossing
            self.has_near = (me > 0) | (section == 1)
            self.has_far = (section == 1) & (me == 4)
            target = (1, jnp.where(me == 15, 0, me + 1))
            near_section = jnp.where(crossing, 1, section)
            far_seq, far_section = 4, 1
        else:
            crossing = (section == 1) & (me == 0)
            jumping = (section == 1) & (me == 4)
            self.has_near = (me < 15) | (section == 0)
            self.has_far = (section == 0) & (me == 15)
            target = (0, jnp.where(me == 0, 15, me - 1))
            near_section = jnp.where(crossing, 0, section)
            far_seq, far_section = 15, 0
        self.sends_near = (me != edge) | crossing
        self.sends_far = jumping
        self.near, self.far = near, far
        self.near_copy = halo_copy(src, near, sems, 0, near_section, target[1])
        self.far_copy = halo_copy(src, far, sems, 1, far_section, far_seq)

    def start(self):
        @pl.when(self.sends_near)
        def _():
            self.near_copy.start()

        @pl.when(self.sends_far)
        def _():
            self.far_copy.start()

        @pl.when(jnp.logical_not(self.has_near))
        def _():
            self.near[...] = jnp.zeros_like(self.near)

        @pl.when(jnp.logical_not(self.has_far))
        def _():
            self.far[...] = jnp.zeros_like(self.far)

    def wait(self):
        @pl.when(self.has_near)
        def _():
            self.near_copy.wait_recv()

        @pl.when(self.has_far)
        def _():
            self.far_copy.wait_recv()

    def drain(self):
        @pl.when(self.sends_near)
        def _():
            self.near_copy.wait_send()

        @pl.when(self.sends_far)
        def _():
            self.far_copy.wait_send()


def forward_body(layer, rider, r):
    section = lax.axis_index("section")
    me = lax.axis_index("seq")
    loads = [fetch(r.w.at[n], r.w_s.at[n], r.load.at[n]) for n in range(2)]
    load_o = fetch(r.wo, r.wo_s, r.load.at[2])
    greet_layer(rider, True)
    net = Net(r.pair_send, r.pair_recv)
    if rider:
        ga = Gather(Net(r.net_send, r.net_recv), r.p1, r.o1, r.next_w, r.next_wo, r.stage, r.rows, r.own)
        ga.begin()
    ex = Exchange(False, r)
    live = r.flags[0]
    heads = r.heads[layer]
    x32 = r.x[...].astype(F32)
    hidden_inv = lax.rsqrt(jnp.sum(x32 * x32, axis=1, keepdims=True) / D + EPS)
    r.hidden[...] = (x32 * hidden_inv * r.gain[layer, ROW_NORM : ROW_NORM + 1, :]).astype(BF16)
    loads[0].wait()

    def project_main(n, carry):
        cols = pl.ds(pl.multiple_of(n * 256, 256), 256)
        r.pre[:, cols] = dot32(r.hidden[...], r.w_s[0, :, cols]).astype(BF16)
        return carry

    lax.fori_loop(0, HALF // 256, project_main, 0)
    r.tail[...] = r.pre[TOK - 16 :, :]
    halo = Halo(r.tail, r.halo_near, r.halo_far, r.halo_s, True)
    halo.start()
    if rider:
        ga.rows_in()
    loads[1].wait()

    def project_side(n, carry):
        cols = pl.ds(pl.multiple_of(n * 256, 256), 256)
        r.side[:, cols] = dot32(r.hidden[...], r.w_s[1, :, cols])
        return carry

    lax.fori_loop(0, HALF // 256, project_side, 0)
    pairs = [net.go(r.hidden, r.both_hidden.at[section], sibling())]
    owns = [fetch(r.hidden, r.both_hidden.at[section], r.load.at[3])]
    step = r.side[:, :128].astype(BF16).astype(F32) + heads[ROW_BIAS : ROW_BIAS + 1]
    dt = jnp.maximum(step, 0.0) + jnp.log1p(jnp.exp(-jnp.abs(step)))
    dt = jnp.where(head_lanes(), dt, 0.0) * live
    rate = -dt * jnp.exp(heads[ROW_DECAY : ROW_DECAY + 1])
    cum = split_left(tri_of(True).astype(F32).astype(BF16), rate, 3)
    r.dt[...] = dt
    r.cum[...] = cum
    last = jnp.broadcast_to(cum[TOK - 1 : TOK], (TOK, 128))
    r.dec_s[...] = jnp.exp(last).T.reshape(OWNERS, 8, 128)
    r.dec[me] = r.dec_s[me]

    def dec_copy(d):
        peer = lax.rem(me + d, OWNERS)
        return pltpu.make_async_remote_copy(
            src_ref=r.dec_s.at[peer], dst_ref=r.dec.at[me], send_sem=r.dec_send.at[d], recv_sem=r.dec_recv.at[d],
            device_id={"seq": peer}, device_id_type=MESH,
        )

    for d in range(1, OWNERS):
        dec_copy(d).start()
    weight = dt * jnp.exp(last - cum)
    halo.wait()
    r.halo[...] = jnp.where(
        r.flags[1] > 0.0, r.halo_near[...], jnp.where(r.flags[2] > 0.0, r.halo_far[...], jnp.zeros_like(r.halo_far))
    )

    def conv_tile(cols):
        blk = r.pre[:, cols].astype(F32)
        cat = jnp.concatenate([r.halo[:, cols].astype(F32)[8:], blk], axis=0)
        summed = conv_of(cat, r.taps[layer, :, cols])
        sig = 1.0 / (1.0 + jnp.exp(-summed))
        act = summed * sig
        r.act[:, cols] = act
        r.dact[:, cols] = sig * (1.0 + summed * (1.0 - sig))
        return act

    b = conv_tile(pl.ds(INNER, 128)).astype(BF16)
    c = conv_tile(pl.ds(INNER + 128, 128)).astype(BF16)

    def states(n, carry):
        i = own_group(n)
        wt = to_front(weight, i)
        for q in range(3):
            x = conv_tile(group_cols(i, q))
            scaled = (x * pair_cols(wt, q)[2]).astype(BF16)
            store_heads(r.ds, i, q, dot32(scaled, b, ((0,), (0,))).astype(BF16))
        ex.send(2 * i)
        ex.send(2 * i + 1)
        return carry

    lax.fori_loop(0, 8, states, 0)
    if rider:
        ga.spread(1)
    for d in range(1, OWNERS):
        dec_copy(d).wait_recv()
    ex.scan(r.dec)
    if rider:
        ga.spread(2)
        ga.spread(3)
    r.cumt[...] = cum.T
    causal = tri_of(True)
    scores = dot32(c, b, ((1,), (1,)))
    lane = lax.broadcasted_iota(jnp.int32, (TOK, 128), 1)
    r.square[...] = jnp.zeros((TOK, 128), F32)

    def inside(i, carry):
        cum_i = to_front(cum, i)
        dt_i = to_front(dt, i)
        rows = r.cumt[pl.ds(pl.multiple_of(16 * i, 16), 16), :]
        for q in range(3):
            cols = group_cols(i, q)
            cum_a, cum_b, _ = pair_cols(cum_i, q)
            u = r.act[:, cols] * pair_cols(dt_i, q)[2]
            mixes = []
            for cum_h, off in ((cum_a, LANES[2 * q]), (cum_b, LANES[2 * q + 1])):
                gap = cum_h - rows[off : off + 1]
                mixes.append((scores * jnp.exp(jnp.where(causal, gap, -1e30))).astype(BF16))
            terms = jnp.concatenate(
                [jnp.where(lane < 64, u, 0.0).astype(BF16), jnp.where(lane < 64, 0.0, u).astype(BF16)], axis=0
            )
            r.raw[:, cols] = dot32(jnp.concatenate(mixes, axis=1), terms)
        return carry

    lax.fori_loop(0, 8, inside, 0)
    if rider:
        ga.relay(0)
    ex.finish()
    save = fetch(r.back, r.states, r.load.at[4])

    def across(i, carry):
        cum_i = to_front(cum, i)
        skip_i = pltpu.roll(heads, lax.rem(128 - 16 * i, 128), 1)[ROW_SKIP : ROW_SKIP + 1]
        for q in range(3):
            cols = group_cols(i, q)
            state = head_rows_at(r.back, i, q)
            raw = r.raw[:, cols] + jnp.exp(pair_cols(cum_i, q)[2]) * dot32(c, state, ((1,), (1,)))
            r.raw[:, cols] = raw
            y = (raw + pair_row(skip_i, q) * r.act[:, cols]).astype(BF16)
            r.y[:, cols] = y
            gate = r.side[:, gate_cols(i, q)]
            z = y.astype(F32) * (gate / (1.0 + jnp.exp(-gate)))
            r.z[:, cols] = z
            r.square[...] += z * z
        return carry

    lax.fori_loop(0, 8, across, 0)
    if rider:
        ga.relay(1)
    total = jnp.sum(r.square[...], axis=1, keepdims=True)
    inv = jnp.broadcast_to(lax.rsqrt(total / INNER + EPS), (TOK, 128))
    r.inv[...] = inv

    def scale(i, carry):
        cols = pl.ds(pl.multiple_of(i * 128, 128), 128)
        mid = r.taps[layer, ROW_MID : ROW_MID + 1, cols]
        r.gated[:, cols] = (r.z[:, cols] * inv * mid).astype(BF16)
        return carry

    lax.fori_loop(0, 24, scale, 0)
    pairs.append(net.go(r.gated, r.both_gated.at[section], sibling()))
    owns.append(fetch(r.gated, r.both_gated.at[section], r.load.at[5]))
    load_o.wait()
    for half in range(2):

        def project(n, carry):
            cols = pl.ds(pl.multiple_of(n * 256, 256), 256)
            full = pl.ds(pl.multiple_of(half * WALF + n * 256, 256), 256)
            branch = dot32(r.gated[...], r.wo_s[half, :, cols])
            r.result[:, full] = (r.x[:, full].astype(F32) + live * branch).astype(BF16)
            return carry

        lax.fori_loop(0, WALF // 256, project, 0)
    if rider:
        ga.relay(2)
        ga.relay(3)
        for j in range(4):
            ga.last(j)
        ga.end()
        ga.net.drain()
    save.wait()
    for copy in owns:
        copy.wait()
    for copy in pairs:
        copy.wait_recv()
    net.drain()
    halo.drain()
    for d in range(1, OWNERS):
        dec_copy(d).wait_send()
    ex.drain()


def block_forward(layer, flags, x, w, wo, small, shards):
    rider = shards is not None
    inputs = {
        "flags": ("s", flags), "x": ("v", x), "w": ("h", w), "wo": ("h", wo), "taps": ("v", small.taps),
        "gain": ("v", small.gain), "heads": ("v", small.heads),
    }
    outputs = {
        "act": in_vmem(TOK, CONV), "dact": in_vmem(TOK, CONV), "side": in_vmem(TOK, HALF), "raw": in_vmem(TOK, INNER),
        "dt": in_vmem(TOK, 128), "cum": in_vmem(TOK, 128), "inv": in_vmem(TOK, 128),
        "dec": in_vmem(OWNERS, 8, 128), "pre": in_vmem(TOK, CONV, dtype=BF16), "halo": in_vmem(16, CONV, dtype=BF16),
        "y": in_vmem(TOK, INNER, dtype=BF16), "result": in_vmem(TOK, D, dtype=BF16),
        "states": in_hbm(OWNERS, OWN, STATE), "both_hidden": in_hbm(2, TOK, D), "both_gated": in_hbm(2, TOK, INNER),
    }
    tile = pltpu.VMEM((TOK, 128), F32)
    edge = pltpu.VMEM((16, CONV), BF16)
    scratch = {
        "w_s": pltpu.VMEM((2, D, HALF), BF16), "wo_s": pltpu.VMEM((2, INNER, WALF), BF16),
        "hidden": pltpu.VMEM((TOK, D), BF16), "gated": pltpu.VMEM((TOK, INNER), BF16),
        "z": pltpu.VMEM((TOK, INNER), F32), "cumt": tile, "square": tile,
        "tail": edge, "halo_near": edge, "halo_far": edge, "halo_s": dma_sems(4),
        "dec_s": pltpu.VMEM((OWNERS, 8, 128), F32), "dec_send": dma_sems(OWNERS), "dec_recv": dma_sems(OWNERS),
        "load": dma_sems(6), "pair_send": dma_sems(2), "pair_recv": dma_sems(2),
        **exchange_scratch(),
    }
    if rider:
        inputs.update({"p1": ("v", shards[0]), "o1": ("v", shards[1])})
        outputs.update({"next_w": in_hbm(2, 4, 4, 96, HALF), "next_wo": in_hbm(2, 4, 4, 4, 48, WALF)})
        scratch.update(gather_scratch())
    return call(
        functools.partial(forward_body, layer, rider), "block_forward", 2 + layer, inputs, outputs, scratch
    )


def add_rows(target, first, second, *more):
    rows, lead = target.shape[-2], target.shape[:-2]
    per = rows // 16
    blocks = functools.reduce(lambda a, b: a * b, lead, 1)

    def body(n, carry):
        b = n // per
        spot = (b,) if len(lead) == 1 else (b // lead[1], lax.rem(b, lead[1]))
        at = spot + (pl.ds(pl.multiple_of(lax.rem(n, per) * 16, 16), 16), slice(None))
        total = first[at].astype(F32) + second[at].astype(F32)
        for ref in more:
            total = total + ref[at].astype(F32)
        target[at] = total.astype(target.dtype)
        return carry

    lax.fori_loop(0, blocks * per, body, 0)


def fold_shapes():
    return [(4, 96, CUT), (4, 96, CUT), (4, 4, 48, WALF)]


class Fold:
    def __init__(self, net, gi, go, r):
        self.net, self.gi, self.go_ref = net, gi, go
        self.h, self.m, self.s = (r.ha, r.hb, r.ho), (r.ma, r.mb, r.mo), (r.sa, r.sb, r.so)
        self.own = r.fold_own
        self.place = places()
        self.peers = (y_peer, z_peer, x_peer)

    def part(self, kind, t, half):
        _, y, z, x = self.place
        at = pl.ds(2 * half, 2) if half is not None else slice(None)
        if kind == 0:
            return self.gi.at[lax.rem(y + t, 4), at, :, pl.ds(0, CUT)]
        if kind == 1:
            return self.gi.at[at, lax.rem(z + t, 4), :, pl.ds(CUT, CUT)]
        return self.go_ref.at[at, :, lax.rem(x + t, 4)]

    def begin(self):
        go = self.net.go
        self.hops, self.direct, self.loads = {}, {}, []
        for half, k in ((0, 1), (1, 3)):
            for kind in range(3):
                self.hops[kind, half] = go(
                    self.part(kind, 2, half), self.h[kind].at[pl.ds(2 * half, 2)], self.peers[kind](k)
                )
        for half, k in ((1, 1), (0, 3)):
            for kind in range(3):
                side = 0 if k == 1 else 1
                self.direct[kind, side] = go(
                    self.part(kind, k, half), self.s[kind].at[side, pl.ds(2 * half, 2)], self.peers[kind](k)
                )
        for kind in range(3):
            self.loads.append(
                [
                    fetch(self.part(kind, 1, 0), self.m[kind].at[pl.ds(0, 2)], self.own.at[3 * kind]),
                    fetch(self.part(kind, 3, 1), self.m[kind].at[pl.ds(2, 2)], self.own.at[3 * kind + 1]),
                ]
            )

    def combine(self, kind):
        for copy in self.loads[kind]:
            copy.wait()
        for half in range(2):
            self.hops[kind, half].wait_recv()
        add_rows(self.m[kind], self.m[kind], self.h[kind])
        peer = self.peers[kind]
        for half, k in ((0, 1), (1, 3)):
            at = pl.ds(2 * half, 2)
            self.hops[kind, half] = self.net.go(self.m[kind].at[at], self.s[kind].at[half, at], peer(k))
        self.loads[kind] = [fetch(self.part(kind, 0, None), self.h[kind], self.own.at[3 * kind + 2])]

    def settle(self, kind):
        for copy in self.loads[kind]:
            copy.wait()
        for side in range(2):
            self.direct[kind, side].wait_recv()
            self.hops[kind, side].wait_recv()
        add_rows(self.h[kind], self.h[kind], self.s[kind].at[0], self.s[kind].at[1])


class Finish:
    def __init__(self, net, r):
        self.net, self.r = net, r
        self.place = places()

    def second(self, kind):
        _, y, z, _ = self.place
        r, go = self.r, self.net.go
        if kind == 0:
            self.a = [go(r.ha.at[lax.rem(z + k, 4)], r.r2a.at[k], z_peer(k)) for k in range(1, 4)]
            r.r2a[0] = r.ha[z]
        elif kind == 1:
            self.b = [go(r.hb.at[lax.rem(y + k, 4)], r.r2b.at[k], y_peer(k)) for k in range(1, 4)]
            r.r2b[0] = r.hb[y]
        else:
            self.o = [go(r.ho.at[lax.rem(y + k, 4)], r.r2o.at[k], y_peer(k)) for k in range(1, 4)]
            r.r2o[0] = r.ho[y]

    def third(self):
        _, y, z, x = self.place
        r, go = self.r, self.net.go
        for copy in self.a + self.b:
            copy.wait_recv()
        for n in range(4):
            at = pl.ds(24 * n, 24)
            for parts, cols in ((r.r2a, pl.ds(0, CUT)), (r.r2b, pl.ds(CUT, CUT))):
                total = parts[0, at, :].astype(F32)
                for k in range(1, 4):
                    total = total + parts[k, at, :].astype(F32)
                r.c3[n, :, cols] = total
        self.x = [go(r.c3.at[lax.rem(x + k, 4)], r.r3.at[x], x_peer(k)) for k in range(1, 4)]
        for copy in self.o:
            copy.wait_recv()
        add_rows(r.o2, r.r2o.at[0], r.r2o.at[1], r.r2o.at[2], r.r2o.at[3])
        self.z = [go(r.o2.at[lax.rem(z + k, 4)], r.r3o.at[k], z_peer(k)) for k in range(1, 4)]
        r.r3[x] = r.c3[x]
        r.r3o[0] = r.o2[z]

    def last(self, in_ref, out_ref):
        r = self.r
        for copy in self.x + self.z:
            copy.wait_recv()
        in_ref[...] = r.r3[0] + r.r3[1] + r.r3[2] + r.r3[3]
        total = r.r3o[0].astype(F32)
        for k in range(1, 4):
            total = total + r.r3o[k].astype(F32)
        out_ref[...] = total


def fold_scratch():
    a, b, o = fold_shapes()
    return {
        "ha": pltpu.VMEM(a, BF16), "hb": pltpu.VMEM(b, BF16), "ho": pltpu.VMEM(o, BF16),
        "ma": pltpu.VMEM(a, BF16), "mb": pltpu.VMEM(b, BF16), "mo": pltpu.VMEM(o, BF16),
        "sa": pltpu.VMEM((2,) + a, BF16), "sb": pltpu.VMEM((2,) + b, BF16), "so": pltpu.VMEM((2,) + o, BF16),
        "fold_own": dma_sems(9),
        "r2a": pltpu.VMEM(a, BF16), "r2b": pltpu.VMEM(b, BF16), "r2o": pltpu.VMEM(o, BF16),
        "c3": pltpu.VMEM((4, 24, HALF), F32), "r3": pltpu.VMEM((4, 24, HALF), F32),
        "o2": pltpu.VMEM((4, 48, WALF), BF16), "r3o": pltpu.VMEM((4, 48, WALF), BF16),
        "net_send": dma_sems(48), "net_recv": dma_sems(48),
    }


SLOTS = 3


def backward_body(layer, rider, r):
    section = lax.axis_index("section")
    load_state = fetch(r.states, r.state_s, r.load.at[0])

    def wo_tile(i):
        rows = pl.ds(pl.multiple_of(i * 384, 384), 384)
        slot = lax.rem(i, SLOTS)
        return pltpu.make_async_copy(r.wo.at[:, rows], r.wo_s.at[slot], r.wo_load.at[slot])

    def w_tile(n):
        slot = lax.rem(n, SLOTS)
        rows = pl.ds(pl.multiple_of((n // 2) * 256, 256), 256)
        return pltpu.make_async_copy(r.w.at[lax.rem(n, 2), rows], r.w_s.at[slot], r.w_load.at[slot])

    for n in range(SLOTS):
        wo_tile(n).start()
        w_tile(n).start()
    greet_layer(rider, False)
    net = Net(r.pair_send, r.pair_recv)
    if rider:
        fold = Fold(Net(r.net_send, r.net_recv), r.gi, r.go, r)
        fold.begin()
        rest = Finish(fold.net, r)
    ex = Exchange(True, r)
    live = r.flags[0]
    heads = r.heads[layer]
    r.gb[...] = (r.g[...].astype(F32) * live).astype(BF16)
    inv = r.inv[...]
    b = r.act[:, INNER : INNER + 128].astype(BF16)
    c = r.act[:, INNER + 128 : CONV].astype(BF16)
    dt = r.dt[...]
    cum = r.cum[...]
    r.dots[...] = jnp.zeros((TOK, 128), F32)
    own_half = pl.ds(pl.multiple_of(section * WALF, 128), WALF)
    other_half = pl.ds(pl.multiple_of((1 - section) * WALF, 128), WALF)
    pairs = [net.go(r.gb.at[:, other_half], r.both_gb.at[section], sibling())]
    owns = [fetch(r.gb.at[:, own_half], r.both_gb.at[section], r.load.at[1])]

    def first(i, carry):
        slot = lax.rem(i, SLOTS)
        wo_tile(i).wait()
        gg = dot32(r.gb[:, :WALF], r.wo_s[slot, 0], ((1,), (1,)))
        gg = gg + dot32(r.gb[:, WALF:], r.wo_s[slot, 1], ((1,), (1,)))

        @pl.when(i + SLOTS < 8)
        def _():
            wo_tile(i + SLOTS).start()

        r.gg[:, pl.ds(pl.multiple_of(i * 384, 384), 384)] = gg
        for q in range(3):
            cols = group_cols(i, q)
            gate = r.side[:, gate_cols(i, q)]
            z = r.y[:, cols].astype(F32) * (gate / (1.0 + jnp.exp(-gate)))
            mid = r.taps[layer, ROW_MID : ROW_MID + 1, cols]
            r.dots[...] += gg[:, 128 * q : 128 * q + 128] * mid * z
        return carry

    lax.fori_loop(0, 8, first, 0)
    total = jnp.broadcast_to(jnp.sum(r.dots[...], axis=1, keepdims=True), (TOK, 128))
    shift = total * inv * inv * inv / INNER
    r.gtaps[...] = jnp.zeros_like(r.gtaps)

    def second(n, carry):
        i = own_group(n)
        cum_i = to_front(cum, i)
        for q in range(3):
            cols = group_cols(i, q)
            gate = r.side[:, gate_cols(i, q)]
            y = r.y[:, cols].astype(F32)
            gg = r.gg[:, cols]
            sig = 1.0 / (1.0 + jnp.exp(-gate))
            act = gate * sig
            z = y * act
            dz = gg * r.taps[layer, ROW_MID : ROW_MID + 1, cols] * inv - z * shift
            dy = (dz * act).astype(BF16)
            r.dy[:, cols] = dy
            r.gside[:, gate_cols(i, q)] = (dz * y * (sig * (1.0 + gate * (1.0 - sig)))).astype(BF16)
            r.gtaps[ROW_MID : ROW_MID + 1, cols] = jnp.sum(gg * z * inv, axis=0, keepdims=True)
            far = (dy.astype(F32) * jnp.exp(pair_cols(cum_i, q)[2])).astype(BF16)
            store_heads(r.ds, i, q, dot32(far, c, ((0,), (0,))).astype(BF16))
        ex.send(2 * i)
        ex.send(2 * i + 1)
        return carry

    lax.fori_loop(0, 8, second, 0)
    if rider:
        for kind in (2, 0, 1):
            fold.combine(kind)
    ex.scan(r.dec)
    load_state.wait()
    r.cumt[...] = cum.T
    causal = tri_of(True)
    scores = dot32(c, b, ((1,), (1,)))
    lane = lax.broadcasted_iota(jnp.int32, (TOK, 128), 1)
    pick_row = lax.broadcasted_iota(jnp.int32, (128, 128), 0)
    pick_col = lax.broadcasted_iota(jnp.int32, (128, 128), 1)
    picks = []
    for q in range(3):
        target = jnp.where(pick_row < 64, LANES[2 * q], LANES[2 * q + 1])
        picks.append((pick_col == target).astype(F32).astype(BF16))
    for ref in (r.dscore, r.grad_b, r.grad_c, r.xdu, r.dyy, r.thin):
        ref[...] = jnp.zeros_like(ref)

    def inside(i, carry):
        cum_i = to_front(cum, i)
        dt_i = to_front(dt, i)
        rows = r.cumt[pl.ds(pl.multiple_of(16 * i, 16), 16), :]
        for q in range(3):
            cols = group_cols(i, q)
            cum_a, cum_b, cum_x = pair_cols(cum_i, q)
            u16 = (r.act[:, cols] * pair_cols(dt_i, q)[2]).astype(BF16)
            dy16 = r.dy[:, cols]
            nil = jnp.zeros_like(dy16)
            dys = jnp.concatenate([jnp.where(lane < 64, dy16, nil), jnp.where(lane < 64, nil, dy16)], axis=0)
            both = dot32(dys, u16, ((1,), (1,)))
            mixes = []
            for n, (cum_h, off) in enumerate(((cum_a, LANES[2 * q]), (cum_b, LANES[2 * q + 1]))):
                gap = cum_h - rows[off : off + 1]
                decay = jnp.exp(jnp.where(causal, gap, -1e30))
                mixes.append((scores * decay).astype(BF16))
                r.dscore[...] += both[n * TOK : n * TOK + TOK] * decay
            r.gg[:, cols] = dot32(jnp.concatenate(mixes, axis=0), dys, ((0,), (0,)))
            far = (dy16.astype(F32) * jnp.exp(cum_x)).astype(BF16)
            r.grad_c[...] += dot32(far, head_rows_at(r.state_s, i, q))
        return carry

    lax.fori_loop(0, 8, inside, 0)
    if rider:
        for kind in (2, 0, 1):
            fold.settle(kind)
            rest.second(kind)

    def conv_back(cols, gact):
        gsum = gact * r.dact[:, cols]
        r.gsum[:, cols] = gsum
        blk = r.pre[:, cols].astype(F32)
        cat = jnp.concatenate([r.halo[:, cols].astype(F32)[8:], blk], axis=0)
        sums = [jnp.sum(gsum * cat[5 + k : 5 + k + TOK], axis=0, keepdims=True) for k in range(4)]
        sums.append(jnp.sum(gsum, axis=0, keepdims=True))
        r.gtaps[0:5, cols] = jnp.concatenate(sums, axis=0)

    ex.finish()

    def across(i, carry):
        cum_i = to_front(cum, i)
        dt_i = to_front(dt, i)
        skip_i = pltpu.roll(heads, lax.rem(128 - 16 * i, 128), 1)[ROW_SKIP : ROW_SKIP + 1]
        x_du = jnp.zeros((TOK, 128), F32)
        dy_y = jnp.zeros((TOK, 128), F32)
        thin = jnp.zeros((16, 128), F32)
        edges = {}
        for q in range(3):
            cols = group_cols(i, q)
            x = r.act[:, cols]
            cum_x = pair_cols(cum_i, q)[2]
            dt_x = pair_cols(dt_i, q)[2]
            fade = jnp.exp(cum_x[TOK - 1 : TOK] - cum_x)
            u = x * dt_x
            dy = r.dy[:, cols].astype(F32)
            state16 = head_rows_at(r.state_s, i, q)
            dstate16 = head_rows_at(r.back, i, q)
            du_far = fade * dot32(b, dstate16, ((1,), (1,)))
            du = r.gg[:, cols] + du_far
            r.grad_b[...] += dot32((u * fade).astype(BF16), dstate16)
            overlap = state16.astype(F32) * dstate16.astype(F32)
            edges[LANES[2 * q]] = jnp.sum(overlap[:64], axis=0, keepdims=True)
            edges[LANES[2 * q + 1]] = jnp.sum(overlap[64:], axis=0, keepdims=True)
            x_du = x_du + split_right(x * du, picks[q], 2)
            dy_y = dy_y + split_right(dy * r.raw[:, cols], picks[q], 2)
            thin = thin + split_right(
                jnp.concatenate(
                    [
                        jnp.broadcast_to(jnp.sum(u * du_far, axis=0, keepdims=True), (8, 128)),
                        jnp.broadcast_to(jnp.sum(dy * x, axis=0, keepdims=True), (8, 128)),
                    ],
                    axis=0,
                ),
                picks[q],
                3,
            )
            conv_back(cols, du * dt_x + pair_row(skip_i, q) * dy)
        nothing = jnp.zeros((1, 128), F32)
        r.edge[pl.ds(pl.multiple_of(16 * i, 16), 16), :] = jnp.concatenate(
            [edges.get(k, nothing) for k in range(16)], axis=0
        )
        r.xdu[...] += pltpu.roll(x_du, 16 * i, 1)
        r.dyy[...] += pltpu.roll(dy_y, 16 * i, 1)
        r.thin[...] += pltpu.roll(thin, 16 * i, 1)
        return carry

    lax.fori_loop(0, 8, across, 0)
    dscore16 = r.dscore[...].astype(BF16)
    conv_back(pl.ds(INNER, 128), r.grad_b[...] + dot32(dscore16, c, ((0,), (0,))))
    conv_back(pl.ds(INNER + 128, 128), r.grad_c[...] + dot32(dscore16, b))
    r.tail[...] = r.gsum[:8, :]
    halo = Halo(r.tail, r.halo_near, r.halo_far, r.halo_s, False)
    halo.start()
    ones = jnp.ones((128, 128), BF16)
    edge = split_right(r.edge[...], ones, 3).T[0:1] * jnp.exp(cum[TOK - 1 : TOK]) + r.thin[0:1]
    x_du = r.xdu[...]
    drate = split_left(tri_of(False).astype(F32).astype(BF16), r.dyy[...] - dt * x_du, 3) + edge
    speed = jnp.exp(heads[ROW_DECAY : ROW_DECAY + 1])
    ddt = x_du - drate * speed
    step = r.side[:, :128].astype(BF16).astype(F32) + heads[ROW_BIAS : ROW_BIAS + 1]
    dstep = jnp.where(head_lanes(), ddt / (1.0 + jnp.exp(-step)), 0.0) * live
    r.gside[:, :128] = dstep.astype(BF16)
    r.gside[:, 128:GATE0] = jnp.zeros((TOK, 128), BF16)
    r.ghead[...] = jnp.concatenate(
        [
            jnp.zeros((5, 128), F32),
            jnp.sum(dstep, axis=0, keepdims=True),
            jnp.sum(-drate * dt * speed, axis=0, keepdims=True),
            r.thin[8:9],
        ],
        axis=0,
    )
    halo.wait()
    after = jnp.where(r.flags[3] > 0.0, r.halo_far[...], r.halo_near[...])
    r.halo_near[...] = jnp.where(live > 0.0, after, jnp.zeros_like(after))

    def conv_tile(i, carry):
        cols = pl.ds(pl.multiple_of(i * 128, 128), 128)
        cat = jnp.concatenate([r.gsum[:, cols], r.halo_near[:, cols]], axis=0)
        taps = r.taps[layer, :, cols]
        total = taps[3:4] * cat[:TOK]
        for k in range(3):
            total = total + taps[k : k + 1] * cat[3 - k : 3 - k + TOK]
        r.gpre[:, cols] = total.astype(BF16)
        return carry

    lax.fori_loop(0, CONV // 128, conv_tile, 0)

    @pl.when(section == 0)
    def _():
        net_copy(net, r.gside, r.both_g.at[0], 1).start()
        pltpu.make_async_copy(r.gpre, r.both_g.at[0], r.load.at[2]).start()

    @pl.when(section == 1)
    def _():
        net_copy(net, r.gpre, r.both_g.at[1], 1).start()
        pltpu.make_async_copy(r.gside, r.both_g.at[1], r.load.at[2]).start()

    def project(n, carry):
        rows = pl.ds(pl.multiple_of(n * 256, 256), 256)
        w_tile(2 * n).wait()
        value = dot32(r.gpre[...], r.w_s[lax.rem(2 * n, SLOTS)], ((1,), (1,)))

        @pl.when(2 * n + SLOTS < 12)
        def _():
            w_tile(2 * n + SLOTS).start()

        w_tile(2 * n + 1).wait()
        value = value + dot32(r.gside[...], r.w_s[lax.rem(2 * n + 1, SLOTS)], ((1,), (1,)))

        @pl.when(2 * n + 1 + SLOTS < 12)
        def _():
            w_tile(2 * n + 1 + SLOTS).start()

        r.hid[:, rows] = value
        return carry

    lax.fori_loop(0, D // 256, project, 0)
    x = r.x[...].astype(F32)
    grad = r.hid[...]
    inv_x = lax.rsqrt(jnp.sum(x * x, axis=1, keepdims=True) / D + EPS)
    scaled = grad * r.gain[layer, ROW_NORM : ROW_NORM + 1, :]
    dots = jnp.sum(scaled * x, axis=1, keepdims=True)
    dx = scaled * inv_x - x * (dots * inv_x * inv_x * inv_x / D)
    r.result[...] = (r.g[...].astype(F32) + dx).astype(BF16)
    r.ggain[...] = jnp.broadcast_to(jnp.sum(grad * x * inv_x, axis=0, keepdims=True), (8, D))
    if rider:
        rest.third()
        rest.last(r.fin_in, r.fin_out)
        fold.net.drain()
    for copy in owns:
        copy.wait()
    pltpu.make_async_copy(r.gpre, r.both_g.at[section], r.load.at[2]).wait()
    for copy in pairs:
        copy.wait_recv()
    swap = net_copy(net, r.gpre, r.both_g.at[section], 1)
    swap.wait_recv()
    swap.wait_send()
    net.drain()
    halo.drain()
    ex.drain()


def net_copy(net, src, dst, n):
    return pltpu.make_async_remote_copy(
        src_ref=src, dst_ref=dst, send_sem=net.send.at[n], recv_sem=net.recv.at[n],
        device_id=sibling(), device_id_type=MESH,
    )


def block_backward(layer, flags, g, x, w, wo, small, kept, grads):
    rider = grads is not None
    inputs = {
        "flags": ("s", flags), "g": ("v", g), "x": ("v", x), "w": ("h", w), "wo": ("h", wo), "taps": ("v", small.taps),
        "gain": ("v", small.gain), "heads": ("v", small.heads), "states": ("h", kept.states),
    }
    for key in ("act", "dact", "side", "raw", "dt", "cum", "inv", "dec", "pre", "halo", "y"):
        inputs[key] = ("v", getattr(kept, key))
    outputs = {
        "result": in_vmem(TOK, D, dtype=BF16), "both_gb": in_hbm(2, TOK, WALF), "both_g": in_hbm(2, TOK, HALF),
        "gtaps": in_vmem(8, CONV), "ggain": in_vmem(8, D), "ghead": in_vmem(8, 128),
    }
    tile = pltpu.VMEM((TOK, 128), F32)
    edge = pltpu.VMEM((8, CONV), F32)
    scratch = {
        "wo_s": pltpu.VMEM((SLOTS, 2, 384, WALF), BF16), "w_s": pltpu.VMEM((SLOTS, 256, HALF), BF16),
        "wo_load": dma_sems(SLOTS), "w_load": dma_sems(SLOTS), "load": dma_sems(3),
        "state_s": pltpu.VMEM((OWNERS, OWN, STATE), BF16),
        "gb": pltpu.VMEM((TOK, D), BF16), "gg": pltpu.VMEM((TOK, INNER), F32), "dy": pltpu.VMEM((TOK, INNER), BF16),
        "gsum": pltpu.VMEM((TOK, CONV), F32), "gpre": pltpu.VMEM((TOK, HALF), BF16), "gside": pltpu.VMEM((TOK, HALF), BF16),
        "hid": pltpu.VMEM((TOK, D), F32),
        "dots": tile, "cumt": tile, "edge": tile, "dscore": tile, "grad_b": tile, "grad_c": tile, "xdu": tile, "dyy": tile,
        "thin": pltpu.VMEM((16, 128), F32),
        "tail": edge, "halo_near": edge, "halo_far": edge, "halo_s": dma_sems(4),
        "pair_send": dma_sems(2), "pair_recv": dma_sems(2),
        **exchange_scratch(),
    }
    if rider:
        inputs.update({"gi": ("h", grads[0]), "go": ("h", grads[1])})
        outputs.update({"fin_in": in_vmem(24, HALF), "fin_out": in_vmem(48, WALF)})
        scratch.update(fold_scratch())
    return call(
        functools.partial(backward_body, layer, rider), "block_backward", 4 + layer, inputs, outputs, scratch
    )


def reduce_body(r):
    c, y, z, x = places()
    greet_axes()
    net = Net(r.net_send, r.net_recv)
    fold = Fold(net, r.gi, r.go, r)
    rest = Finish(net, r)
    fold.begin()
    row = lax.broadcasted_iota(jnp.int32, (8, 128), 0)
    lane = lane_at((8, 128))
    for layer in range(2):
        taps, gain, heads = r.gtaps.at[layer], r.ggain.at[layer], r.ghead.at[layer]
        for d in range(64):
            cell = (layer, d // 16, (d // 4) % 4, d % 4)
            first = jnp.where(lane < 48, take_chunk(taps, 0, 48, d), 0.0)
            norm = jnp.where(lane < 24, take_chunk(gain, 0, 24, d), 0.0)
            r.cells[cell + (slice(0, 8),)] = jnp.where(row == ROW_NORM, norm, first)
            second = jnp.where(lane < 4, take_chunk(taps, INNER, 4, d), 0.0)
            head = jnp.where(lane < 3, take_chunk(heads, 0, 8, d // 4), 0.0)
            r.cells[cell + (slice(8, 16),)] = jnp.where(row >= 5, head, second)
    pair = net.go(r.cells.at[1 - c], r.other, sibling())
    other_in = net.go(r.far_in, r.got_in, sibling())
    other_out = net.go(r.far_out, r.got_out, sibling())
    pair.wait_recv()
    r.sum0[...] = r.cells[c] + r.other[...]
    hops = [net.go(r.sum0.at[lax.rem(y + k, 4)], r.in_y.at[k], y_peer(k)) for k in range(1, 4)]
    for kind in (2, 0, 1):
        fold.combine(kind)
    for copy in hops:
        copy.wait_recv()
    r.sum1[...] = r.sum0[y] + r.in_y[1] + r.in_y[2] + r.in_y[3]
    hops = [net.go(r.sum1.at[lax.rem(z + k, 4)], r.in_z.at[k], z_peer(k)) for k in range(1, 4)]
    for kind in (2, 0, 1):
        fold.settle(kind)
        rest.second(kind)
    for copy in hops:
        copy.wait_recv()
    r.sum2[...] = r.sum1[z] + r.in_z[1] + r.in_z[2] + r.in_z[3]
    r.in_x[x] = r.sum2[x]
    hops = [net.go(r.sum2.at[lax.rem(x + k, 4)], r.in_x.at[x], x_peer(k)) for k in range(1, 4)]
    rest.third()
    for copy in hops:
        copy.wait_recv()
    r.blob[...] = r.in_x[0] + r.in_x[1] + r.in_x[2] + r.in_x[3]
    rest.last(r.near_in, r.near_out)
    near_in = net.go(r.near_in, r.got_near_in, sibling())
    near_out = net.go(r.near_out, r.got_near_out, sibling())
    for copy in (other_in, other_out, near_in, near_out):
        copy.wait_recv()

    @pl.when(c == 0)
    def _():
        r.inner[...] = r.near_in[:, :INNER]
        r.bc[...] = r.near_in[:, INNER:]
        r.step[...] = r.got_near_in[:, :128]
        r.gate[...] = r.got_near_in[:, GATE0:]
        r.out[:, :WALF] = r.near_out[...]
        r.out[:, WALF:] = r.got_near_out[...]

    @pl.when(c == 1)
    def _():
        r.inner[...] = r.got_in[:, :INNER]
        r.bc[...] = r.got_in[:, INNER:]
        r.step[...] = r.far_in[:, :128]
        r.gate[...] = r.far_in[:, GATE0:]
        r.out[:, :WALF] = r.got_out[...]
        r.out[:, WALF:] = r.far_out[...]

    net.drain()


def reduce_all(grads, far, gtaps, ggain, ghead):
    cell = (4, 4, 16, 128)
    return call(
        reduce_body, "reduce_grads", 6,
        {
            "gi": ("h", grads[0]), "go": ("h", grads[1]), "far_in": ("v", far[0]), "far_out": ("v", far[1]),
            "gtaps": ("v", gtaps), "ggain": ("v", ggain), "ghead": ("v", ghead),
        },
        {
            "inner": in_vmem(24, INNER), "bc": in_vmem(24, 2 * STATE), "step": in_vmem(24, 128),
            "gate": in_vmem(24, INNER), "out": in_vmem(48, D), "blob": in_vmem(16, 128),
        },
        {
            "near_in": pltpu.VMEM((24, HALF), F32), "near_out": pltpu.VMEM((48, WALF), F32),
            "got_near_in": pltpu.VMEM((24, HALF), F32), "got_near_out": pltpu.VMEM((48, WALF), F32),
            "got_in": pltpu.VMEM((24, HALF), F32), "got_out": pltpu.VMEM((48, WALF), F32),
            "cells": pltpu.VMEM((2, 4) + cell, F32), "other": pltpu.VMEM((4,) + cell, F32),
            "sum0": pltpu.VMEM((4,) + cell, F32), "in_y": pltpu.VMEM((4,) + cell, F32),
            "sum1": pltpu.VMEM(cell, F32), "in_z": pltpu.VMEM((4,) + cell[1:], F32),
            "sum2": pltpu.VMEM(cell[1:], F32), "in_x": pltpu.VMEM((4, 16, 128), F32),
            **fold_scratch(),
        },
    )


def step_lanes(step):
    lead = step.shape[0]
    return jnp.pad(step.reshape(lead, OWNERS, 3), ((0, 0), (0, 0), (0, 5))).reshape(lead, 128)


def small_blob(norm_gain, inner_gain, conv_inner, conv_bc, heads):
    def row(value):
        return jnp.pad(value.astype(F32), ((0, 0), (0, 128 - value.shape[1])))

    return jnp.concatenate(
        [
            row(conv_inner), row(inner_gain[None]), row(norm_gain[None]), jnp.zeros((1, 128), F32),
            row(conv_bc), row(heads),
        ],
        axis=0,
    )


def settle(section, first_value, second_value):
    own = jnp.where(section == 0, first_value, second_value)
    got = lax.ppermute(jnp.where(section == 0, second_value, first_value), "section", [(0, 1), (1, 0)])
    return jnp.stack([jnp.where(section == 0, own, got), jnp.where(section == 0, got, own)])


def per_device(
    block_input, cotangent, seg_groups, norm_gain, w_gate, w_inner, w_bc, w_step, conv_inner, conv_bc, head_params,
    inner_gain, w_out,
):
    section = lax.axis_index("section")
    seq_pos = lax.axis_index("seq")
    small = start_up(
        w_inner[0], w_bc[0], step_lanes(w_step[0]), w_gate[0], w_out[0],
        small_blob(norm_gain[0], inner_gain[0], conv_inner[0], conv_bc[0], head_params[0]),
    )
    weights = [(small.w.reshape(2, D, HALF), small.wo.reshape(2, INNER, WALF)), None]
    firsts = (BLOCKS - seg_groups[0]) * (BLOCK_LEN // TOK)
    first = jnp.where(section == 0, firsts[0], firsts[1])
    at_start = seq_pos == first
    flags = jnp.stack(
        [
            seq_pos >= first,
            jnp.logical_not(at_start) | ((section == 1) & (first == 0)),
            at_start & (section == 1) & (first != 0),
            (section == 0) & (seq_pos == 15) & (firsts[1] != 0),
        ]
    ).astype(F32)

    x = lax.dynamic_index_in_dim(block_input[0], section, 0, keepdims=False)
    kept, inputs = [], []
    for layer in range(2):
        w, wo = weights[layer]
        made = block_forward(
            layer, flags, x, w, wo, small, (small.p1, small.o1) if layer == 0 else None
        )
        if layer == 0:
            weights[1] = (made.next_w.reshape(2, D, HALF), made.next_wo.reshape(2, INNER, WALF))
        kept.append(made)
        inputs.append(x)
        x = made.result

    g = lax.dynamic_index_in_dim(cotangent[0], section, 0, keepdims=False)
    grads = None
    backs = [None, None]
    for layer in (1, 0):
        w, wo = weights[layer]
        back = block_backward(layer, flags, g, inputs[layer], w, wo, small, kept[layer], grads)
        backs[layer] = back
        g = back.result
        hidden = kept[layer].both_hidden.reshape(2 * TOK, D)
        gated = kept[layer].both_gated.reshape(2 * TOK, INNER)
        grad_in = dot32(hidden, back.both_g.reshape(2 * TOK, HALF), ((0,), (0,))).astype(BF16)
        grad_out = dot32(gated, back.both_gb.reshape(2 * TOK, WALF), ((0,), (0,))).astype(BF16)
        grads = (grad_in.reshape(4, 4, 96, HALF), grad_out.reshape(4, 4, 4, 48, WALF))

    final = reduce_all(
        grads, (backs[0].fin_in, backs[0].fin_out),
        jnp.stack([backs[0].gtaps, backs[1].gtaps]), jnp.stack([backs[0].ggain, backs[1].ggain]),
        jnp.stack([backs[0].ghead, backs[1].ghead]),
    )
    blob = final.blob
    return (
        settle(section, kept[0].result, kept[1].result)[None, None],
        settle(section, backs[0].result, backs[1].result)[None, None],
        blob[ROW_NORM : ROW_NORM + 1, :24],
        final.gate[None],
        final.inner[None],
        final.bc[None],
        final.step.reshape(24, OWNERS, 8)[:, :, :3].reshape(24, HEADS)[None],
        blob[None, 0:5, :48],
        blob[None, 8:13, :4],
        blob[None, 13:16, :3],
        blob[ROW_MID : ROW_MID + 1, :48],
        final.out[None],
    )


def solution(mesh):
    weight = P("section", ROWS_ALL, None)
    vector = P("section", ROWS_ALL)
    taps = P("section", None, ROWS_ALL)
    tokens = P("wsh", None, "seq", None)
    heads = P("section", None, "seq")
    result = P("section", "wsh", None, "seq", None)
    return jax.shard_map(
        per_device,
        mesh=mesh,
        in_specs=(
            tokens, tokens, P("wsh", None), vector, weight, weight, weight, weight, taps, taps, heads, vector, weight,
        ),
        out_specs=(
            result, result, vector, weight, weight, weight, weight, taps, taps, heads, vector, weight,
        ),
        check_vma=False,
    )
```

time: 1160 us -> 615 us (0.53)
  waiting for transfers between devices: 716 us -> 0.01 us
  Pallas kernels: 271 us -> 558 us
  matrix products: 48.3 us -> 20.4 us
  starting transfers between devices: 26.3 us -> 2.14 us
  blocking collectives: 24.1 us -> 0 us
  other arithmetic: 26.1 us -> 10.3 us
  between operations: 17 us -> 2.86 us
  local copies, waits for them, and re-layouts: 29.8 us -> 16.9 us
    reduce_scatter x8 -> x0, waiting for transfers between devices: 393 us -> none  [the longest x2 182 us: per_device(): lax.psum_scatter(grad_in, 'seq', scatter_dimension=0, tiled=True)]
    all_gather x10 -> x0, waiting for transfers between devices: 317 us -> none  [the longest x1 88.1 us: per_device(): lax.all_gather(shard, ROWS_ALL, axis=0, tiled=True)]
    pallas_call x14 -> x6, Pallas kernels: 271 us -> 558 us  [call(): pl.pallas_call(kernel, out_shape=tuple((shape for shape, _ in outputs.val...]
    dot_general x4 -> x0, matrix products: 24.1 us -> none  [the longest x2 12.6 us: per_device(): gate = jnp.dot(hidden, w_gates[layer], preferred_element_type=F32)]
    ppermute x12 -> x2, starting transfers between devices: 25.4 us -> 2.14 us  [settle(): lax.ppermute(jnp.where(section == 0, second_value, first_value), 'section...]
    psum x2 -> x0, blocking collectives: 14.1 us -> none  [the longest x1 7.88 us: per_device(): lax.psum(small_grads(ggain[0], gmid[0], gtaps, ghead, seq_pos), 'section')]
  transfers between devices with their start and end apart: 30 -> 2, of which waited for: 17 -> 0; matrix products, arithmetic and copies ran while one was open for 7% -> 6% of each run, Pallas kernels for 22% -> 47%
where the time goes in v3:
time: 615 us; the launch traced here: 611 us
  Pallas kernels  558 us (91%)
  matrix products  20.4 us (3%)
  local copies, waits for them, and re-layouts  16.9 us (3%)
  other arithmetic  10.3 us (2%)
    pallas_call x6, Pallas kernels, call(): pl.pallas_call(kernel, out_shape=tuple((shape for shape, _ in outputs.val...  558 us
    dot_general x4, matrix products, dot32(): lax.dot_general(left, right, (dims, ((), ())), preferred_element_type=F32)  20.4 us
  transfers between devices with their start and end apart: 2, of which 0 were waited for; matrix products, arithmetic and copies ran while one was open for 6% of the time, Pallas kernels for 47%

profile of v3, /device:TPU:1, one launch (start us, length us, event | category | flops | bytes accessed | tf_op | source)
XLA Modules:
  0.0 610.9 jit_solution(6433837054215632373)
XLA Ops:
  0.6 0.0 copy-start
  0.7 0.7 subtract_multiply_fusion
  1.4 0.6 fusion
  4.0 0.8 copy.34
  4.7 0.7 copy.51
  5.4 0.8 copy.33
  6.2 0.7 copy.35.refs_2_
  6.9 0.7 pad_convert_fusion.2
  7.6 0.7 pad_convert_fusion
  8.3 0.8 dynamic-slice_bitcast_fusion.1.refs_1_.refs_2_
  9.1 0.6 add_convert_fusion.refs_0_
  9.7 1.2 concatenate.3.refs_5_
  10.9 106.6 %gather_weights.1 = (bf16[2,4,4,96,3328]{4,3,2,1,0:T(8,128)(2,1)}, bf16[2,4,4,4,48,768]{5,4,3,2,1,0:T(8,128)(2,1)}, bf16[32,3328]{1,0:T(8,128)(2,1)}, bf16[48,76...) custom-call(bf16[24,3072]{1,0:T(8,128)(2,1)} %bitcast.92, ...), custom_call_target="tpu_custom_call" | custom-call | tf_op jit(solution)/shard_map/gather_weights/pallas_call | solution.py:119
  117.5 116.1 %block_forward.2 = (f32[128,3328]{1,0:T(8,128)}, f32[128,3328]{1,0:T(8,128)}, f32[128,3328]{1,0:T(8,128)}, f32[128,3072]{1,0:T(8,128)}, f32[128,128]{1,0:T(8,128...) custom-call(f32[4]{0:T(128)} %add_convert_fusion.refs_0_, ...), custom_call_target="tpu_custom_call" | custom-call | tf_op jit(solution)/shard_map/block_forward/pallas_call | solution.py:119
  233.6 51.4 %block_forward.3 = (f32[128,3328]{1,0:T(8,128)}, f32[128,3328]{1,0:T(8,128)}, f32[128,3328]{1,0:T(8,128)}, f32[128,3072]{1,0:T(8,128)}, f32[128,128]{1,0:T(8,128...) custom-call(f32[4]{0:T(128)} %add_convert_fusion.refs_0_, ...), custom_call_target="tpu_custom_call" | custom-call | tf_op jit(solution)/shard_map/block_forward/pallas_call | solution.py:119
  285.0 0.1 broadcast_select_fusion.2
  285.1 1.3 collective-permute-start
  286.4 0.8 dynamic-slice_bitcast_fusion.refs_1_
  287.1 59.3 %block_backward.2 = (bf16[128,1536]{1,0:T(8,128)(2,1)}, bf16[2,128,768]{2,1,0:T(8,128)(2,1)}, bf16[2,128,3328]{2,1,0:T(8,128)(2,1)}, f32[8,3328]{1,0:T(8,128)}, f32[8,1536]{1,0:T(8,128)}, /*index=5*/f32[8,128]{1,0:T(8,128)}) custom-call(f32[4]{0:T(128)} %add_convert_fusion.refs_0_, bf16[128,1536]{1,0:T(8,128)(2,1)} %dynamic-slice_bitcast_fusion.refs_1_, ...), custom_call_target="tpu_custom_call" | custom-call | tf_op jit(solution)/shard_map/block_backward/pallas_call | solution.py:119
  346.5 4.7 bitcast_convert_fusion.3
  351.2 5.5 bitcast_convert_fusion.1
  356.6 120.5 %block_backward.3 = (bf16[128,1536]{1,0:T(8,128)(2,1)}, bf16[2,128,768]{2,1,0:T(8,128)(2,1)}, bf16[2,128,3328]{2,1,0:T(8,128)(2,1)}, f32[8,3328]{1,0:T(8,128)}, ...) custom-call(f32[4]{0:T(128)} %add_convert_fusion.refs_0_, ...), custom_call_target="tpu_custom_call" | custom-call | tf_op jit(solution)/shard_map/block_backward/pallas_call | solution.py:119
  477.1 1.2 broadcast_select_fusion
  478.3 0.9 collective-permute-start.1
  479.1 1.3 pad_maximum_fusion.2.refs_6_
  480.4 1.4 pad_maximum_fusion.1.refs_5_
  481.9 1.6 pad_maximum_fusion.refs_4_
  483.5 4.8 bitcast_convert_fusion.2
  488.3 5.5 bitcast_convert_fusion
  493.8 104.5 %reduce_grads.1 = (f32[24,3072]{1,0:T(8,128)}, f32[24,256]{1,0:T(8,128)}, f32[24,128]{1,0:T(8,128)}, f32[24,3072]{1,0:T(8,128)}, f32[48,1536]{1,0:T(8,128)}, /*index=5*/f32[16,128]{1,0:T(8,128)}) custom-call(bf16[4,4,96,3328]{3,2,1,0:T(8,128)(2,1)} %bitcast.82, bf16[4,4,4,48,768]{4,3,2,1,0:T(8,128)(2,1)} %bitcast.88, f32[24,3328]{1,0:T(8,128)} %get-tuple-element.116.refs_2_, ...), custom_call_target="tpu_custom_call" | custom-call | tf_op jit(solution)/shard_map/reduce_grads/pallas_call | solution.py:119
  598.3 1.2 slice.34
  599.5 1.2 slice.29
  600.7 0.7 slice.32
  601.3 0.7 slice_bitcast_fusion.1
  602.0 0.6 copy.44
  602.6 0.7 copy.41
  603.3 0.7 slice_bitcast_fusion
  603.9 0.6 copy.43
  604.5 0.8 copy.40
  605.3 0.7 copy.42
  606.0 0.1 select_bitcast_fusion.3
  606.1 0.9 maximum_bitcast_fusion
  607.1 0.1 select_bitcast_fusion.1
  607.2 0.9 maximum_bitcast_fusion.1
  608.1 0.7 copy.56
  608.9 0.7 copy.57
  609.6 0.6 copy.58
  610.2 0.7 copy.59
  (49 shorter events, 0.1 us)
Async XLA Ops:
  0.6 7.6 %copy-start = (bf16[1,2,128,1536]{3,2,1,0:T(8,128)(2,1)S(1)}, bf16[1,2,128,1536]{3,2,1,0:T(8,128)(2,1)}, u32[]{:S(2)}) copy-start(bf16[1,2,128,1536]{3,2,1,0:T(8,128)(2,1)} %param.13) | copy-start | bytes 2359300
  233.6 51.4 %copy-start.2 = (bf16[128,1536]{1,0:T(8,128)(2,1)S(1)}, bf16[128,1536]{1,0:T(8,128)(2,1)}, u32[]{:S(2)}) copy-start(bf16[128,1536]{1,0:T(8,128)(2,1)} %get-tuple-element.78.refs_1_.refs_2_) | copy-start | bytes 1179652
  233.6 52.8 %copy-start.16 = (bf16[1,2,128,1536]{3,2,1,0:T(8,128)(2,1)S(1)}, bf16[1,2,128,1536]{3,2,1,0:T(8,128)(2,1)}, u32[]{:S(2)}) copy-start(bf16[1,2,128,1536]{3,2,1,0:T(8,128)(2,1)} %param.14) | copy-start | bytes 2359300
  285.1 320.9 %collective-permute-start = (bf16[128,1536]{1,0:T(8,128)(2,1)S(1)}, bf16[128,1536]{1,0:T(8,128)(2,1)S(1)}, u32[]{:S(2)}, u32[]{:S(2)}) collective-permute-start(bf16[128,1536]{1,0:T(8,128)(2,1)S(1)} %broadcast_select_fusion.2), channel_id=1, source_target_pairs={{0,64},{64,0},{1,65},{65,1},{2,66},{66,2},{3,67},{67,3},{4,68},{68... | collective-permute-start | bytes 1179656 | tf_op jit(solution)/shard_map/ppermute | solution.py:1459
  287.1 59.3 %copy-start.6 = (bf16[2,128,3072]{2,1,0:T(8,128)(2,1)S(1)}, bf16[2,128,3072]{2,1,0:T(8,128)(2,1)}, u32[]{:S(2)}) copy-start(bf16[2,128,3072]{2,1,0:T(8,128)(2,1)} %get-tuple-element.109) | copy-start | bytes 4718596
  346.4 4.7 copy-start.8
  346.4 4.7 copy-start.12
  356.6 120.5 %copy-start.4 = (bf16[128,1536]{1,0:T(8,128)(2,1)S(1)}, bf16[128,1536]{1,0:T(8,128)(2,1)}, u32[]{:S(2)}) copy-start(bf16[128,1536]{1,0:T(8,128)(2,1)} %get-tuple-element.94.refs_1_) | copy-start | bytes 1179652
  356.6 122.5 %copy-start.20 = (f32[8,128]{1,0:T(8,128)S(1)}, f32[8,128]{1,0:T(8,128)}, u32[]{:S(2)}) copy-start(f32[8,128]{1,0:T(8,128)} %get-tuple-element.123) | copy-start | bytes 12292
  356.6 123.8 %copy-start.18 = (f32[8,1536]{1,0:T(8,128)S(1)}, f32[8,1536]{1,0:T(8,128)}, u32[]{:S(2)}) copy-start(f32[8,1536]{1,0:T(8,128)} %get-tuple-element.121) | copy-start | bytes 147460
  356.6 125.2 %copy-start.17 = (f32[8,3328]{1,0:T(8,128)S(1)}, f32[8,3328]{1,0:T(8,128)}, u32[]{:S(2)}) copy-start(f32[8,3328]{1,0:T(8,128)} %get-tuple-element.119) | copy-start | bytes 319492
  477.1 6.4 %copy-start.5 = (bf16[2,128,3072]{2,1,0:T(8,128)(2,1)S(1)}, bf16[2,128,3072]{2,1,0:T(8,128)(2,1)}, u32[]{:S(2)}) copy-start(bf16[2,128,3072]{2,1,0:T(8,128)(2,1)} %get-tuple-element.114) | copy-start | bytes 4718596
  478.3 128.8 %collective-permute-start.1 = (bf16[128,1536]{1,0:T(8,128)(2,1)S(1)}, bf16[128,1536]{1,0:T(8,128)(2,1)S(1)}, u32[]{:S(2)}, u32[]{:S(2)}) collective-permute-start(bf16[128,1536]{1,0:T(8,128)(2,1)S(1)} %broadcast_select_fusion), channel_id=1, source_target_pairs={{0,64},{64,0},{1,65},{65,1},{2,66},{66,2},{3,67},{67,3},{4,68},{68... | collective-permute-start | bytes 1179656 | tf_op jit(solution)/shard_map/ppermute | solution.py:1459
  483.5 4.8 copy-start.7
  483.5 4.8 copy-start.11
  493.7 112.3 %copy-start.3 = (bf16[128,1536]{1,0:T(8,128)(2,1)S(1)}, bf16[128,1536]{1,0:T(8,128)(2,1)}, u32[]{:S(2)}) copy-start(bf16[128,1536]{1,0:T(8,128)(2,1)} %get-tuple-element.78.refs_1_.refs_2_) | copy-start | bytes 1179652
  493.7 112.3 %copy-start.9 = (bf16[128,1536]{1,0:T(8,128)(2,1)S(1)}, bf16[128,1536]{1,0:T(8,128)(2,1)}, u32[]{:S(2)}) copy-start(bf16[128,1536]{1,0:T(8,128)(2,1)} %get-tuple-element.81) | copy-start | bytes 1179652
  606.0 1.1 copy-start.10
  607.1 1.1 copy-start.15
  607.1 1.8 copy-start.14
  607.1 3.8 copy-start.1
  607.2 2.4 copy-start.19
  607.2 3.0 copy-start.13

commit v4 on v3

--- a/solution.py
+++ b/solution.py
@@ -20,13 +20,17 @@
 GATE0 = 256
 CUT = HALF // 2
 WALF = D // 2
+WCUT = WALF // 2
+ECOLS = INNER // 2
+LCOLS = HALF // 2 + 128
+LSPLIT = LCOLS
 OWNERS = 16
 OWN = 192
 EPS = 1e-05
 F32 = jnp.float32
 BF16 = jnp.bfloat16
 MESH = pl.DeviceIdType.MESH
-VMEM_LIMIT = 60 * 1024 * 1024
+VMEM_LIMIT = 61 * 1024 * 1024
 LANES = (0, 1, 2, 8, 9, 10)
 ROWS_ALL = ("seq", "wsh")
 ROW_MID, ROW_NORM = 5, 6
@@ -202,17 +206,21 @@
         self.net, self.p, self.o, self.w, self.wo = net, p, o, w, wo
         self.stage, self.rows, self.own = stage, rows, own
         self.place = places()
-        self.left, self.right = pl.ds(0, CUT), pl.ds(CUT, CUT)
-        self.near, self.far, self.passed = {}, {}, []
-        self.peers = (y_peer, z_peer, x_peer)
-
-    def band(self, kind, j, moved):
+        self.near, self.far, self.inner, self.passed = {}, {}, {}, []
+        self.peers = (y_peer, z_peer, x_peer, x_peer)
+        self.inner_peers = (z_peer, y_peer, y_peer, z_peer)
+
+    def band(self, kind, j, moved, half=None):
         c, y, z, x = self.place
+        rows = slice(None) if half is None else pl.ds(48 * half, 48)
+        many = slice(None) if half is None else pl.ds(2 * half, 2)
         if kind == 0:
-            return self.w.at[c, lax.rem(y + 4 - moved, 4), lax.rem(z + 4 - j, 4), :, self.left]
+            return self.w.at[c, lax.rem(y + 4 - moved, 4), lax.rem(z + 4 - j, 4), rows, pl.ds(0, CUT)]
         if kind == 1:
-            return self.w.at[c, lax.rem(y + 4 - j, 4), lax.rem(z + 4 - moved, 4), :, self.right]
-        return self.wo.at[c, lax.rem(y + 4 - j, 4), :, lax.rem(x + 4 - moved, 4)]
+            return self.w.at[c, lax.rem(y + 4 - j, 4), lax.rem(z + 4 - moved, 4), rows, pl.ds(CUT, CUT)]
+        if kind == 2:
+            return self.wo.at[c, lax.rem(y + 4 - j, 4), many, lax.rem(x + 4 - moved, 4), :, pl.ds(0, WCUT)]
+        return self.wo.at[c, many, lax.rem(z + 4 - j, 4), lax.rem(x + 4 - moved, 4), :, pl.ds(WCUT, WCUT)]
 
     def pass_on(self, part):
         self.passed.append(self.net.go(part, part, sibling()))
@@ -220,11 +228,13 @@
     def begin(self):
         c, y, z, x = self.place
         go = self.net.go
-        self.first, self.oz = [], []
+        self.first, self.spots = [], []
+        spot = self.wo.at[c, y, z, x]
         for k in range(1, 4):
             self.first.append(go(self.p, self.stage.at[x], x_peer(k)))
-            self.oz.append(go(self.o, self.wo.at[c, y, z, x], z_peer(k)))
-        self.own_o = fetch(self.o, self.wo.at[c, y, z, x], self.own.at[0])
+            for cols, peer in ((pl.ds(0, WCUT), z_peer), (pl.ds(WCUT, WCUT), y_peer)):
+                self.spots.append(go(self.o.at[:, cols], spot.at[:, cols], peer(k)))
+        self.own_o = fetch(self.o, spot, self.own.at[0])
         self.stage[x] = self.p[...]
 
     def rows_in(self):
@@ -235,34 +245,42 @@
         self.rows[...] = jnp.concatenate(
             [self.stage[n].astype(F32)[:24] for n in range(4)], axis=0
         ).astype(BF16)
-        self.az, self.by, self.oy = [], [], []
-        for k in range(1, 4):
-            self.az.append(go(self.rows.at[:, self.left], self.w.at[c, y, z, :, self.left], z_peer(k)))
-            self.by.append(go(self.rows.at[:, self.right], self.w.at[c, y, z, :, self.right], y_peer(k)))
+        for k in (1, 3):
+            for kind, cols in ((0, pl.ds(0, CUT)), (1, pl.ds(CUT, CUT))):
+                self.inner[kind, k] = go(
+                    self.rows.at[:, cols], self.band(kind, 0, 0), self.inner_peers[kind](k)
+                )
         own_w = fetch(self.rows, self.w.at[c, y, z], self.own.at[1])
         self.own_o.wait()
-        for copy in self.oz:
+        for copy in self.spots:
             copy.wait_recv()
-        lane = self.wo.at[c, y, :, x]
-        for k in range(1, 4):
-            self.oy.append(go(lane, lane, y_peer(k)))
+        for k in (1, 3):
+            for kind in (2, 3):
+                part = self.band(kind, 0, 0)
+                self.inner[kind, k] = go(part, part, self.inner_peers[kind](k))
         own_w.wait()
         self.spread(0)
 
     def spread(self, j):
-        if j:
-            for copies in (self.az, self.by, self.oy):
-                copies[j - 1].wait_recv()
+        if j in (1, 3):
+            for kind in range(4):
+                self.inner[kind, j].wait_recv()
+                part = self.band(kind, j, 0, 0 if j == 1 else 1)
+                self.inner[kind, 2, j] = self.net.go(part, part, self.inner_peers[kind](j))
+        if j == 2:
+            for kind in range(4):
+                self.inner[kind, 2, 1].wait_recv()
+                self.inner[kind, 2, 3].wait_recv()
         for k in (1, 3):
-            for kind in range(3):
+            for kind in range(4):
                 part = self.band(kind, j, 0)
                 self.near[kind, j, k] = self.net.go(part, part, self.peers[kind](k))
-        for kind in range(3):
+        for kind in range(4):
             self.pass_on(self.band(kind, j, 0))
 
     def relay(self, j):
         for k in (1, 3):
-            for kind in range(3):
+            for kind in range(4):
                 self.near[kind, j, k].wait_recv()
                 part = self.band(kind, j, k)
                 if (k == 1) == (j < 2):
@@ -270,7 +288,7 @@
                 self.pass_on(part)
 
     def last(self, j):
-        for kind in range(3):
+        for kind in range(4):
             self.far[kind, j].wait_recv()
             self.pass_on(self.band(kind, j, 2))
 
@@ -284,8 +302,6 @@
         "stage": pltpu.VMEM((4, 32, HALF), BF16),
         "rows": pltpu.VMEM((96, HALF), BF16),
         "own": dma_sems(2),
-        "net_send": dma_sems(150),
-        "net_recv": dma_sems(150),
     }
 
 
@@ -317,10 +333,8 @@
     return tile
 
 
-def start_body(r):
+def start_body(r, net, after):
     c, y, z, x = places()
-    greet_axes()
-    net = Net(r.net_send, r.net_recv)
     pad = jnp.zeros((8, 1), F32)
 
     def tall(value):
@@ -336,31 +350,30 @@
     given = pl.ds(pl.multiple_of((1 - c) * WALF, 128), WALF)
     swaps = [
         net.go(r.mine.at[1 - c], r.half.at[c], sibling()),
-        net.go(r.out.at[:, given], r.halo.at[c], sibling()),
+        net.go(r.out.at[:, given], r.half_o.at[c], sibling()),
     ]
     small = [net.go(r.blob, r.cells.at[c, y, z, x], x_peer(k)) for k in range(1, 4)]
     r.half[c] = r.mine[c]
-    r.halo[c] = jnp.where(c == 0, r.out[:, :WALF], r.out[:, WALF:])
+    r.half_o[c] = jnp.where(c == 0, r.out[:, :WALF], r.out[:, WALF:])
     r.cells[c, y, z, x] = r.blob[...]
     for copy in swaps:
         copy.wait_recv()
-    ga = Gather(net, r.half.at[0], r.halo.at[0], r.w, r.wo, r.stage, r.rows, r.own)
+    ga = Gather(net, r.half.at[0], r.half_o.at[0], r.w0, r.wo0, r.stage0, r.rows0, r.own0)
     ga.begin()
     for copy in small:
         copy.wait_recv()
     small = [net.go(r.cells.at[c, y, z], r.cells.at[c, y, z], z_peer(k)) for k in range(1, 4)]
     ga.rows_in()
+    after.begin()
     for copy in small:
         copy.wait_recv()
     small = [net.go(r.cells.at[c, y], r.cells.at[c, y], y_peer(k)) for k in range(1, 4)]
-    for j in range(1, 4):
+    for j in (1, 3, 2):
         ga.spread(j)
     for copy in small:
         copy.wait_recv()
     pair = net.go(r.cells.at[c], r.cells.at[c], sibling())
     ga.relay(0)
-    r.p1[...] = r.half[1]
-    r.o1[...] = r.halo[1]
     ga.relay(1)
     pair.wait_recv()
     for layer in range(2):
@@ -382,38 +395,23 @@
             moved = pltpu.roll(second_tile(4 * j), 8 * j, 1) if j else second_tile(0)
             heads = jnp.where((lane >= 8 * j) & (lane < 8 * j + 3), moved, heads)
         r.heads[layer] = heads
+    after.rows_in()
+    ga.relay(3)
     ga.relay(2)
-    ga.relay(3)
-    for j in range(4):
+    after.spread(1)
+    after.spread(3)
+    for j in (0, 1, 3, 2):
         ga.last(j)
+    after.spread(2)
     ga.end()
-    net.drain()
-
-
-def start_up(inner, bc, step, gate, out, blob):
-    return call(
-        start_body, "gather_weights", 1,
-        {
-            "inner": ("v", inner), "bc": ("v", bc), "step": ("v", step), "gate": ("v", gate), "out": ("v", out),
-            "blob": ("v", blob),
-        },
-        {
-            "w": in_hbm(2, 4, 4, 96, HALF),
-            "wo": in_hbm(2, 4, 4, 4, 48, WALF),
-            "p1": in_vmem(32, HALF, dtype=BF16),
-            "o1": in_vmem(48, WALF, dtype=BF16),
-            "taps": in_vmem(2, 8, CONV),
-            "gain": in_vmem(2, 8, D),
-            "heads": in_vmem(2, 8, 128),
-        },
-        {
-            "mine": pltpu.VMEM((2, 32, HALF), BF16),
-            "half": pltpu.VMEM((2, 32, HALF), BF16),
-            "halo": pltpu.VMEM((2, 48, WALF), BF16),
-            "cells": pltpu.VMEM((2, 4, 4, 4, 16, 128), F32),
-            **gather_scratch(),
-        },
-    )
+
+
+TURNS = (1, 4, 3, 12, 5, 15, 7, 13, 2, 8, 6, 9, 14, 11, 10)
+
+
+def seq_peer(d):
+    _, y, z, _ = places()
+    return lax.rem(y + d // 4, 4) * 4 + lax.rem(z + d % 4, 4)
 
 
 class Exchange:
@@ -430,7 +428,8 @@
         )
 
     def send(self, peer):
-        d = lax.rem(peer + OWNERS - self.me, OWNERS)
+        _, y, z, _ = places()
+        d = lax.rem(peer // 4 + 4 - y, 4) * 4 + lax.rem(lax.rem(peer, 4) + 4 - z, 4)
 
         @pl.when(d != 0)
         def _():
@@ -442,7 +441,7 @@
 
     def back_copy(self, d):
         r = self.r
-        peer = lax.rem(self.me + d, OWNERS)
+        peer = seq_peer(d)
         return pltpu.make_async_remote_copy(
             src_ref=r.ready.at[peer], dst_ref=r.back.at[self.me], send_sem=r.send_b.at[d], recv_sem=r.recv_b.at[d],
             device_id={"seq": peer}, device_id_type=MESH,
@@ -454,8 +453,8 @@
         def rows_of(dec):
             return jnp.concatenate([jnp.broadcast_to(dec[h : h + 1], (64, 128)) for h in range(3)], axis=0)
 
-        for d in range(1, OWNERS):
-            self.first_copy(lax.rem(self.me + d, OWNERS), d).wait_recv()
+        for d in TURNS:
+            self.first_copy(seq_peer(d), d).wait_recv()
         r.final[...] = jnp.zeros((OWN, STATE), F32)
         r.fade[0] = jnp.ones((8, 128), F32)
 
@@ -483,8 +482,8 @@
             r.begin[...] = r.other[...]
 
         begin = r.begin[...]
-        for d in range(OWNERS):
-            c = lax.rem(self.me + d, OWNERS)
+        for d in TURNS + (0,):
+            c = seq_peer(d)
             n = OWNERS - 1 - c if self.backward else c
             value = (r.kept[c] + rows_of(r.fade[n]) * begin).astype(BF16)
             if d == 0:
@@ -500,12 +499,12 @@
         swap.wait_send()
 
     def finish(self):
-        for d in range(1, OWNERS):
+        for d in TURNS:
             self.back_copy(d).wait_recv()
 
     def drain(self):
         for d in range(1, OWNERS):
-            self.first_copy(lax.rem(self.me + d, OWNERS), d).wait_send()
+            self.first_copy(seq_peer(d), d).wait_send()
             self.back_copy(d).wait_send()
 
 
@@ -643,13 +642,19 @@
 def forward_body(layer, rider, r):
     section = lax.axis_index("section")
     me = lax.axis_index("seq")
-    loads = [fetch(r.w.at[n], r.w_s.at[n], r.load.at[n]) for n in range(2)]
-    load_o = fetch(r.wo, r.wo_s, r.load.at[2])
-    greet_layer(rider, True)
     net = Net(r.pair_send, r.pair_recv)
     if rider:
-        ga = Gather(Net(r.net_send, r.net_recv), r.p1, r.o1, r.next_w, r.next_wo, r.stage, r.rows, r.own)
-        ga.begin()
+        greet_layer(rider, True)
+        bulk = Net(r.net_send, r.net_recv)
+        ga = Gather(bulk, r.half.at[1], r.half_o.at[1], r.next_w, r.next_wo, r.stage, r.rows, r.own)
+        start_body(r, bulk, ga)
+        w, wo = r.w0.reshape(2, D, HALF), r.wo0.reshape(2, INNER, WALF)
+    else:
+        w, wo = r.w, r.wo
+    loads = [fetch(w.at[n], r.w_s.at[n], r.load.at[n]) for n in range(2)]
+    load_o = fetch(wo, r.wo_s, r.load.at[2])
+    if not rider:
+        greet_layer(rider, True)
     ex = Exchange(False, r)
     live = r.flags[0]
     heads = r.heads[layer]
@@ -667,8 +672,6 @@
     r.tail[...] = r.pre[TOK - 16 :, :]
     halo = Halo(r.tail, r.halo_near, r.halo_far, r.halo_s, True)
     halo.start()
-    if rider:
-        ga.rows_in()
     loads[1].wait()
 
     def project_side(n, carry):
@@ -677,6 +680,8 @@
         return carry
 
     lax.fori_loop(0, HALF // 256, project_side, 0)
+    if rider:
+        ga.relay(0)
     pairs = [net.go(r.hidden, r.both_hidden.at[section], sibling())]
     owns = [fetch(r.hidden, r.both_hidden.at[section], r.load.at[3])]
     step = r.side[:, :128].astype(BF16).astype(F32) + heads[ROW_BIAS : ROW_BIAS + 1]
@@ -731,13 +736,12 @@
 
     lax.fori_loop(0, 8, states, 0)
     if rider:
-        ga.spread(1)
+        ga.relay(1)
     for d in range(1, OWNERS):
         dec_copy(d).wait_recv()
     ex.scan(r.dec)
     if rider:
-        ga.spread(2)
-        ga.spread(3)
+        ga.relay(3)
     r.cumt[...] = cum.T
     causal = tri_of(True)
     scores = dot32(c, b, ((1,), (1,)))
@@ -764,7 +768,7 @@
 
     lax.fori_loop(0, 8, inside, 0)
     if rider:
-        ga.relay(0)
+        ga.relay(2)
     ex.finish()
     save = fetch(r.back, r.states, r.load.at[4])
 
@@ -786,7 +790,8 @@
 
     lax.fori_loop(0, 8, across, 0)
     if rider:
-        ga.relay(1)
+        ga.last(0)
+        ga.last(1)
     total = jnp.sum(r.square[...], axis=1, keepdims=True)
     inv = jnp.broadcast_to(lax.rsqrt(total / INNER + EPS), (TOK, 128))
     r.inv[...] = inv
@@ -812,12 +817,10 @@
 
         lax.fori_loop(0, WALF // 256, project, 0)
     if rider:
-        ga.relay(2)
-        ga.relay(3)
-        for j in range(4):
+        for j in (3, 2):
             ga.last(j)
         ga.end()
-        ga.net.drain()
+        bulk.drain()
     save.wait()
     for copy in owns:
         copy.wait()
@@ -830,12 +833,18 @@
     ex.drain()
 
 
-def block_forward(layer, flags, x, w, wo, small, shards):
-    rider = shards is not None
-    inputs = {
-        "flags": ("s", flags), "x": ("v", x), "w": ("h", w), "wo": ("h", wo), "taps": ("v", small.taps),
-        "gain": ("v", small.gain), "heads": ("v", small.heads),
-    }
+def block_forward(layer, flags, x, given):
+    rider = layer == 0
+    inputs = {"flags": ("s", flags), "x": ("v", x)}
+    if rider:
+        for key in ("inner", "bc", "step", "gate", "out", "blob"):
+            inputs[key] = ("v", given[key])
+    else:
+        w, wo, small = given
+        inputs.update({
+            "w": ("h", w), "wo": ("h", wo), "taps": ("v", small.taps), "gain": ("v", small.gain),
+            "heads": ("v", small.heads),
+        })
     outputs = {
         "act": in_vmem(TOK, CONV), "dact": in_vmem(TOK, CONV), "side": in_vmem(TOK, HALF), "raw": in_vmem(TOK, INNER),
         "dt": in_vmem(TOK, 128), "cum": in_vmem(TOK, 128), "inv": in_vmem(TOK, 128),
@@ -855,74 +864,97 @@
         **exchange_scratch(),
     }
     if rider:
-        inputs.update({"p1": ("v", shards[0]), "o1": ("v", shards[1])})
-        outputs.update({"next_w": in_hbm(2, 4, 4, 96, HALF), "next_wo": in_hbm(2, 4, 4, 4, 48, WALF)})
+        outputs.update({
+            "w0": in_hbm(2, 4, 4, 96, HALF), "wo0": in_hbm(2, 4, 4, 4, 48, WALF),
+            "next_w": in_hbm(2, 4, 4, 96, HALF), "next_wo": in_hbm(2, 4, 4, 4, 48, WALF),
+            "taps": in_vmem(2, 8, CONV), "gain": in_vmem(2, 8, D), "heads": in_vmem(2, 8, 128),
+        })
+        scratch.update({
+            "mine": pltpu.VMEM((2, 32, HALF), BF16), "half": pltpu.VMEM((2, 32, HALF), BF16),
+            "half_o": pltpu.VMEM((2, 48, WALF), BF16), "cells": pltpu.VMEM((2, 4, 4, 4, 16, 128), F32),
+            "net_send": dma_sems(400), "net_recv": dma_sems(400),
+        })
+        scratch.update({key + "0": value for key, value in gather_scratch().items()})
         scratch.update(gather_scratch())
     return call(
         functools.partial(forward_body, layer, rider), "block_forward", 2 + layer, inputs, outputs, scratch
     )
 
 
-def add_rows(target, first, second, *more):
-    rows, lead = target.shape[-2], target.shape[:-2]
-    per = rows // 16
+def add_rows(target, *parts):
+    lead = target.shape[:-2]
     blocks = functools.reduce(lambda a, b: a * b, lead, 1)
 
-    def body(n, carry):
-        b = n // per
+    def body(b, carry):
         spot = (b,) if len(lead) == 1 else (b // lead[1], lax.rem(b, lead[1]))
-        at = spot + (pl.ds(pl.multiple_of(lax.rem(n, per) * 16, 16), 16), slice(None))
-        total = first[at].astype(F32) + second[at].astype(F32)
-        for ref in more:
-            total = total + ref[at].astype(F32)
-        target[at] = total.astype(target.dtype)
+        total = parts[0][spot].astype(F32)
+        for ref in parts[1:]:
+            total = total + ref[spot].astype(F32)
+        target[spot] = total.astype(target.dtype)
         return carry
 
-    lax.fori_loop(0, blocks * per, body, 0)
-
-
-def fold_shapes():
-    return [(4, 96, CUT), (4, 96, CUT), (4, 4, 48, WALF)]
+    lax.fori_loop(0, blocks, body, 0)
+
+
+def fold_scratch(tag, cols, with_out):
+    shapes = {"a": (4, 96, cols // 2), "b": (4, 96, cols // 2)}
+    if with_out:
+        shapes["o"] = (4, 4, 48, WALF)
+    scratch = {}
+    for key, shape in shapes.items():
+        scratch[tag + "m" + key] = pltpu.VMEM(shape, BF16)
+        scratch[tag + "s" + key] = pltpu.VMEM((2,) + shape, BF16)
+    scratch[tag + "own"] = dma_sems(9)
+    return scratch
+
+
+def fold_targets(tag, cols, with_out, make):
+    targets = {tag + "ha": make(4, 96, cols // 2), tag + "hb": make(4, 96, cols // 2)}
+    if with_out:
+        targets[tag + "ho"] = make(4, 4, 48, WALF)
+    return targets
 
 
 class Fold:
-    def __init__(self, net, gi, go, r):
-        self.net, self.gi, self.go_ref = net, gi, go
-        self.h, self.m, self.s = (r.ha, r.hb, r.ho), (r.ma, r.mb, r.mo), (r.sa, r.sb, r.so)
-        self.own = r.fold_own
+    def __init__(self, net, r, tag, cols, gi, go):
+        self.net, self.gi, self.go_ref, self.cut = net, gi, go, cols // 2
+        self.kinds = (0, 1, 2) if go is not None else (0, 1)
+        keys = "abo"
+        self.h = [getattr(r, tag + "h" + keys[n]) for n in self.kinds]
+        self.m = [getattr(r, tag + "m" + keys[n]) for n in self.kinds]
+        self.s = [getattr(r, tag + "s" + keys[n]) for n in self.kinds]
+        self.own = getattr(r, tag + "own")
         self.place = places()
         self.peers = (y_peer, z_peer, x_peer)
+        self.hops, self.direct, self.loads = {}, {}, {}
 
     def part(self, kind, t, half):
         _, y, z, x = self.place
         at = pl.ds(2 * half, 2) if half is not None else slice(None)
         if kind == 0:
-            return self.gi.at[lax.rem(y + t, 4), at, :, pl.ds(0, CUT)]
+            return self.gi.at[lax.rem(y + t, 4), at, :, pl.ds(0, self.cut)]
         if kind == 1:
-            return self.gi.at[at, lax.rem(z + t, 4), :, pl.ds(CUT, CUT)]
+            return self.gi.at[at, lax.rem(z + t, 4), :, pl.ds(self.cut, self.cut)]
         return self.go_ref.at[at, :, lax.rem(x + t, 4)]
 
-    def begin(self):
+    def begin(self, kinds):
         go = self.net.go
-        self.hops, self.direct, self.loads = {}, {}, []
         for half, k in ((0, 1), (1, 3)):
-            for kind in range(3):
+            for kind in kinds:
                 self.hops[kind, half] = go(
                     self.part(kind, 2, half), self.h[kind].at[pl.ds(2 * half, 2)], self.peers[kind](k)
                 )
         for half, k in ((1, 1), (0, 3)):
-            for kind in range(3):
+            for kind in kinds:
                 side = 0 if k == 1 else 1
                 self.direct[kind, side] = go(
                     self.part(kind, k, half), self.s[kind].at[side, pl.ds(2 * half, 2)], self.peers[kind](k)
                 )
-        for kind in range(3):
-            self.loads.append(
-                [
-                    fetch(self.part(kind, 1, 0), self.m[kind].at[pl.ds(0, 2)], self.own.at[3 * kind]),
-                    fetch(self.part(kind, 3, 1), self.m[kind].at[pl.ds(2, 2)], self.own.at[3 * kind + 1]),
-                ]
-            )
+        for kind in kinds:
+            self.loads[kind] = [
+                fetch(self.part(kind, 1, 0), self.m[kind].at[pl.ds(0, 2)], self.own.at[3 * kind]),
+                fetch(self.part(kind, 3, 1), self.m[kind].at[pl.ds(2, 2)], self.own.at[3 * kind + 1]),
+            ]
 
     def combine(self, kind):
         for copy in self.loads[kind]:
@@ -946,94 +978,142 @@
 
 
 class Finish:
-    def __init__(self, net, r):
-        self.net, self.r = net, r
+    def __init__(self, net, r, tag, cols, sums):
+        self.net, self.sums, self.cut, self.cols = net, sums, cols // 2, cols
+        for key in ("r2a", "r2b", "c3", "r3") + (("r2o", "o2", "r3o") if len(sums) > 2 else ()):
+            setattr(self, key, getattr(r, tag + key))
         self.place = places()
 
-    def second(self, kind):
+    def second(self):
         _, y, z, _ = self.place
-        r, go = self.r, self.net.go
-        if kind == 0:
-            self.a = [go(r.ha.at[lax.rem(z + k, 4)], r.r2a.at[k], z_peer(k)) for k in range(1, 4)]
-            r.r2a[0] = r.ha[z]
-        elif kind == 1:
-            self.b = [go(r.hb.at[lax.rem(y + k, 4)], r.r2b.at[k], y_peer(k)) for k in range(1, 4)]
-            r.r2b[0] = r.hb[y]
-        else:
-            self.o = [go(r.ho.at[lax.rem(y + k, 4)], r.r2o.at[k], y_peer(k)) for k in range(1, 4)]
-            r.r2o[0] = r.ho[y]
+        go = self.net.go
+        ha, hb = self.sums[:2]
+        self.a, self.b, self.o = [], [], []
+        for k in range(1, 4):
+            self.a.append(go(ha.at[lax.rem(z + k, 4)], self.r2a.at[k], z_peer(k)))
+            self.b.append(go(hb.at[lax.rem(y + k, 4)], self.r2b.at[k], y_peer(k)))
+        self.r2a[0] = ha[z]
+        self.r2b[0] = hb[y]
+        if len(self.sums) > 2:
+            ho = self.sums[2]
+            one, two = pl.ds(0, WCUT), pl.ds(WCUT, WCUT)
+            for k in range(1, 4):
+                self.o.append(go(ho.at[lax.rem(y + k, 4), :, :, one], self.r2o.at[0, k], y_peer(k)))
+                self.o.append(go(ho.at[:, lax.rem(z + k, 4), :, two], self.r2o.at[1, k], z_peer(k)))
+            self.r2o[0, 0] = ho[y, :, :, :WCUT]
+            for n in range(4):
+                self.r2o[1, 0, n] = ho[n, z, :, WCUT:]
 
     def third(self):
         _, y, z, x = self.place
-        r, go = self.r, self.net.go
+        go = self.net.go
         for copy in self.a + self.b:
             copy.wait_recv()
         for n in range(4):
             at = pl.ds(24 * n, 24)
-            for parts, cols in ((r.r2a, pl.ds(0, CUT)), (r.r2b, pl.ds(CUT, CUT))):
+            for parts, cols in ((self.r2a, pl.ds(0, self.cut)), (self.r2b, pl.ds(self.cut, self.cut))):
                 total = parts[0, at, :].astype(F32)
                 for k in range(1, 4):
                     total = total + parts[k, at, :].astype(F32)
-                r.c3[n, :, cols] = total
-        self.x = [go(r.c3.at[lax.rem(x + k, 4)], r.r3.at[x], x_peer(k)) for k in range(1, 4)]
-        for copy in self.o:
+                self.c3[n, :, cols] = total
+        self.x = [go(self.c3.at[lax.rem(x + k, 4)], self.r3.at[x], x_peer(k)) for k in range(1, 4)]
+        self.r3[x] = self.c3[x]
+        if self.o:
+            for copy in self.o:
+                copy.wait_recv()
+            for n in range(2):
+                add_rows(self.o2.at[n], *[self.r2o.at[n, k] for k in range(4)])
+            for k in range(1, 4):
+                self.x.append(go(self.o2.at[0, lax.rem(z + k, 4)], self.r3o.at[0, k], z_peer(k)))
+                self.x.append(go(self.o2.at[1, lax.rem(y + k, 4)], self.r3o.at[1, k], y_peer(k)))
+            self.r3o[0, 0] = self.o2[0, z]
+            self.r3o[1, 0] = self.o2[1, y]
+
+    def last(self, in_ref, out_ref=None):
+        for copy in self.x:
             copy.wait_recv()
-        add_rows(r.o2, r.r2o.at[0], r.r2o.at[1], r.r2o.at[2], r.r2o.at[3])
-        self.z = [go(r.o2.at[lax.rem(z + k, 4)], r.r3o.at[k], z_peer(k)) for k in range(1, 4)]
-        r.r3[x] = r.c3[x]
-        r.r3o[0] = r.o2[z]
-
-    def last(self, in_ref, out_ref):
-        r = self.r
-        for copy in self.x + self.z:
-            copy.wait_recv()
-        in_ref[...] = r.r3[0] + r.r3[1] + r.r3[2] + r.r3[3]
-        total = r.r3o[0].astype(F32)
-        for k in range(1, 4):
-            total = total + r.r3o[k].astype(F32)
-        out_ref[...] = total
-
-
-def fold_scratch():
-    a, b, o = fold_shapes()
-    return {
-        "ha": pltpu.VMEM(a, BF16), "hb": pltpu.VMEM(b, BF16), "ho": pltpu.VMEM(o, BF16),
-        "ma": pltpu.VMEM(a, BF16), "mb": pltpu.VMEM(b, BF16), "mo": pltpu.VMEM(o, BF16),
-        "sa": pltpu.VMEM((2,) + a, BF16), "sb": pltpu.VMEM((2,) + b, BF16), "so": pltpu.VMEM((2,) + o, BF16),
-        "fold_own": dma_sems(9),
-        "r2a": pltpu.VMEM(a, BF16), "r2b": pltpu.VMEM(b, BF16), "r2o": pltpu.VMEM(o, BF16),
-        "c3": pltpu.VMEM((4, 24, HALF), F32), "r3": pltpu.VMEM((4, 24, HALF), F32),
-        "o2": pltpu.VMEM((4, 48, WALF), BF16), "r3o": pltpu.VMEM((4, 48, WALF), BF16),
-        "net_send": dma_sems(48), "net_recv": dma_sems(48),
+        in_ref[...] = self.r3[0] + self.r3[1] + self.r3[2] + self.r3[3]
+        if self.o:
+            for n in range(2):
+                total = self.r3o[n, 0].astype(F32)
+                for k in range(1, 4):
+                    total = total + self.r3o[n, k].astype(F32)
+                out_ref[:, WCUT * n : WCUT * n + WCUT] = total
+
+
+def finish_scratch(tag, cols, with_out):
+    cut = cols // 2
+    scratch = {
+        tag + "r2a": pltpu.VMEM((4, 96, cut), BF16), tag + "r2b": pltpu.VMEM((4, 96, cut), BF16),
+        tag + "c3": pltpu.VMEM((4, 24, cols), F32), tag + "r3": pltpu.VMEM((4, 24, cols), F32),
     }
-
-
-SLOTS = 3
+    if with_out:
+        scratch[tag + "r2o"] = pltpu.VMEM((2, 4, 4, 48, WCUT), BF16)
+        scratch[tag + "o2"] = pltpu.VMEM((2, 4, 48, WCUT), BF16)
+        scratch[tag + "r3o"] = pltpu.VMEM((2, 4, 48, WCUT), BF16)
+    return scratch
+
+
+def net_scratch(count):
+    return {"net_send": dma_sems(count), "net_recv": dma_sems(count)}
+
+
+def early_products(r, which):
+    left, right, stage, target = (
+        (r.gated2, r.gb2, r.stage_o, r.go) if which == 0 else (r.hid2, r.dg2, r.stage_e, r.ge)
+    )
+    tile = stage.shape[1]
+
+    def body(i, carry):
+        slot = lax.rem(i, 2)
+        rows = pl.ds(pl.multiple_of(i * tile, tile), tile)
+        copy = pltpu.make_async_copy(stage.at[slot], target.at[rows], r.stage_s.at[2 * which + slot])
+
+        @pl.when(i >= 2)
+        def _():
+            copy.wait()
+
+        stage[slot] = dot32(left[:, rows], right[...], ((0,), (0,))).astype(BF16)
+        copy.start()
+        return carry
+
+    lax.fori_loop(0, target.shape[0] // tile, body, 0)
+    for slot in range(2):
+        pltpu.make_async_copy(stage.at[slot], target.at[pl.ds(0, tile)], r.stage_s.at[2 * which + slot]).wait()
 
 
 def backward_body(layer, rider, r):
     section = lax.axis_index("section")
+    slots_o, slots_w = r.wo_s.shape[0], r.w_s.shape[0]
     load_state = fetch(r.states, r.state_s, r.load.at[0])
+    load_two = [fetch(r.both_hidden, r.hid2, r.load.at[3]), fetch(r.both_gated, r.gated2, r.load.at[4])]
 
     def wo_tile(i):
         rows = pl.ds(pl.multiple_of(i * 384, 384), 384)
-        slot = lax.rem(i, SLOTS)
+        slot = lax.rem(i, slots_o)
         return pltpu.make_async_copy(r.wo.at[:, rows], r.wo_s.at[slot], r.wo_load.at[slot])
 
     def w_tile(n):
-        slot = lax.rem(n, SLOTS)
+        slot = lax.rem(n, slots_w)
         rows = pl.ds(pl.multiple_of((n // 2) * 256, 256), 256)
         return pltpu.make_async_copy(r.w.at[lax.rem(n, 2), rows], r.w_s.at[slot], r.w_load.at[slot])
 
-    for n in range(SLOTS):
+    for n in range(slots_o):
         wo_tile(n).start()
+    for n in range(slots_w):
         w_tile(n).start()
-    greet_layer(rider, False)
+    greet_layer(True, False)
     net = Net(r.pair_send, r.pair_recv)
+    bulk = Net(r.net_send, r.net_recv)
     if rider:
-        fold = Fold(Net(r.net_send, r.net_recv), r.gi, r.go, r)
-        fold.begin()
-        rest = Finish(fold.net, r)
+        late = Fold(bulk, r, "l", LCOLS, r.gl, None)
+        late.begin((0, 1))
+        early_end = Finish(bulk, r, "e", ECOLS, (r.e1a, r.e1b, r.e1o))
+        early_end.second()
+        late_end = Finish(bulk, r, "l", LCOLS, late.h)
+    early = Fold(
+        bulk, r, "e", ECOLS, r.ge.reshape(4, 4, 96, ECOLS), r.go.reshape(4, 4, 4, 48, WALF)
+    )
     ex = Exchange(True, r)
     live = r.flags[0]
     heads = r.heads[layer]
@@ -1044,20 +1124,24 @@
     dt = r.dt[...]
     cum = r.cum[...]
     r.dots[...] = jnp.zeros((TOK, 128), F32)
-    own_half = pl.ds(pl.multiple_of(section * WALF, 128), WALF)
     other_half = pl.ds(pl.multiple_of((1 - section) * WALF, 128), WALF)
-    pairs = [net.go(r.gb.at[:, other_half], r.both_gb.at[section], sibling())]
-    owns = [fetch(r.gb.at[:, own_half], r.both_gb.at[section], r.load.at[1])]
+    own_rows = pl.ds(pl.multiple_of(section * TOK, 128), TOK)
+    pairs = [net.go(r.gb.at[:, other_half], r.gb2.at[own_rows], sibling())]
+    r.gb2[own_rows, :] = jnp.where(section == 0, r.gb[:, :WALF], r.gb[:, WALF:])
+    load_two[1].wait()
+    pairs[0].wait_recv()
+    early_products(r, 0)
+    early.begin((2,))
 
     def first(i, carry):
-        slot = lax.rem(i, SLOTS)
+        slot = lax.rem(i, slots_o)
         wo_tile(i).wait()
         gg = dot32(r.gb[:, :WALF], r.wo_s[slot, 0], ((1,), (1,)))
         gg = gg + dot32(r.gb[:, WALF:], r.wo_s[slot, 1], ((1,), (1,)))
 
-        @pl.when(i + SLOTS < 8)
-        def _():
-            wo_tile(i + SLOTS).start()
+        @pl.when(i + slots_o < 8)
+        def _():
+            wo_tile(i + slots_o).start()
 
         r.gg[:, pl.ds(pl.multiple_of(i * 384, 384), 384)] = gg
         for q in range(3):
@@ -1096,10 +1180,19 @@
         return carry
 
     lax.fori_loop(0, 8, second, 0)
+    other_cols = pl.ds(pl.multiple_of(GATE0 + (1 - section) * ECOLS, 128), ECOLS)
+    pairs.append(net.go(r.gside.at[:, other_cols], r.dg2.at[own_rows], sibling()))
+    r.dg2[own_rows, :] = jnp.where(
+        section == 0, r.gside[:, GATE0 : GATE0 + ECOLS], r.gside[:, GATE0 + ECOLS :]
+    )
     if rider:
-        for kind in (2, 0, 1):
-            fold.combine(kind)
+        late.combine(0)
+        late.combine(1)
+    load_two[0].wait()
+    pairs[1].wait_recv()
+    early_products(r, 1)
     ex.scan(r.dec)
+    early.begin((0, 1))
     load_state.wait()
     r.cumt[...] = cum.T
     causal = tri_of(True)
@@ -1139,9 +1232,9 @@
 
     lax.fori_loop(0, 8, inside, 0)
     if rider:
-        for kind in (2, 0, 1):
-            fold.settle(kind)
-            rest.second(kind)
+        late.settle(0)
+        late.settle(1)
+        late_end.second()
 
     def conv_back(cols, gact):
         gsum = gact * r.dact[:, cols]
@@ -1202,6 +1295,9 @@
         return carry
 
     lax.fori_loop(0, 8, across, 0)
+    early.combine(2)
+    early.combine(0)
+    early.combine(1)
     dscore16 = r.dscore[...].astype(BF16)
     conv_back(pl.ds(INNER, 128), r.grad_b[...] + dot32(dscore16, c, ((0,), (0,))))
     conv_back(pl.ds(INNER + 128, 128), r.grad_c[...] + dot32(dscore16, b))
@@ -1242,57 +1338,85 @@
         return carry
 
     lax.fori_loop(0, CONV // 128, conv_tile, 0)
+    if rider:
+        early_end.third()
+        late_end.third()
+
+    tail_cols = HALF - LCOLS
+    side_cols = pl.ds(0, GATE0)
+    moves = (
+        net_copy(net, r.gpre.at[:, pl.ds(LCOLS, tail_cols)], r.both_gl.at[0, :, pl.ds(0, tail_cols)], 2),
+        net_copy(net, r.gside.at[:, side_cols], r.both_gl.at[0, :, pl.ds(tail_cols, GATE0)], 3),
+        net_copy(net, r.gpre.at[:, pl.ds(0, LCOLS)], r.both_gl.at[1], 2),
+    )
+    keeps = (
+        pltpu.make_async_copy(r.gpre.at[:, pl.ds(LCOLS, tail_cols)], r.both_gl.at[1, :, pl.ds(0, tail_cols)], r.load.at[1]),
+        pltpu.make_async_copy(r.gside.at[:, side_cols], r.both_gl.at[1, :, pl.ds(tail_cols, GATE0)], r.load.at[2]),
+        pltpu.make_async_copy(r.gpre.at[:, pl.ds(0, LCOLS)], r.both_gl.at[0], r.load.at[1]),
+    )
 
     @pl.when(section == 0)
     def _():
-        net_copy(net, r.gside, r.both_g.at[0], 1).start()
-        pltpu.make_async_copy(r.gpre, r.both_g.at[0], r.load.at[2]).start()
+        moves[0].start()
+        moves[1].start()
+        keeps[2].start()
 
     @pl.when(section == 1)
     def _():
-        net_copy(net, r.gpre, r.both_g.at[1], 1).start()
-        pltpu.make_async_copy(r.gside, r.both_g.at[1], r.load.at[2]).start()
+        moves[2].start()
+        keeps[0].start()
+        keeps[1].start()
 
     def project(n, carry):
         rows = pl.ds(pl.multiple_of(n * 256, 256), 256)
         w_tile(2 * n).wait()
-        value = dot32(r.gpre[...], r.w_s[lax.rem(2 * n, SLOTS)], ((1,), (1,)))
-
-        @pl.when(2 * n + SLOTS < 12)
-        def _():
-            w_tile(2 * n + SLOTS).start()
+        value = dot32(r.gpre[...], r.w_s[lax.rem(2 * n, slots_w)], ((1,), (1,)))
+
+        @pl.when(2 * n + slots_w < 12)
+        def _():
+            w_tile(2 * n + slots_w).start()
 
         w_tile(2 * n + 1).wait()
-        value = value + dot32(r.gside[...], r.w_s[lax.rem(2 * n + 1, SLOTS)], ((1,), (1,)))
-
-        @pl.when(2 * n + 1 + SLOTS < 12)
-        def _():
-            w_tile(2 * n + 1 + SLOTS).start()
-
-        r.hid[:, rows] = value
+        value = value + dot32(r.gside[...], r.w_s[lax.rem(2 * n + 1, slots_w)], ((1,), (1,)))
+
+        @pl.when(2 * n + 1 + slots_w < 12)
+        def _():
+            w_tile(2 * n + 1 + slots_w).start()
+
+        r.gg[:, rows] = value
         return carry
 
     lax.fori_loop(0, D // 256, project, 0)
     x = r.x[...].astype(F32)
-    grad = r.hid[...]
+    grad = r.gg[:, :D]
     inv_x = lax.rsqrt(jnp.sum(x * x, axis=1, keepdims=True) / D + EPS)
     scaled = grad * r.gain[layer, ROW_NORM : ROW_NORM + 1, :]
     dots = jnp.sum(scaled * x, axis=1, keepdims=True)
     dx = scaled * inv_x - x * (dots * inv_x * inv_x * inv_x / D)
     r.result[...] = (r.g[...].astype(F32) + dx).astype(BF16)
     r.ggain[...] = jnp.broadcast_to(jnp.sum(grad * x * inv_x, axis=0, keepdims=True), (8, D))
+    for kind in range(3):
+        early.settle(kind)
     if rider:
-        rest.third()
-        rest.last(r.fin_in, r.fin_out)
-        fold.net.drain()
-    for copy in owns:
-        copy.wait()
-    pltpu.make_async_copy(r.gpre, r.both_g.at[section], r.load.at[2]).wait()
-    for copy in pairs:
-        copy.wait_recv()
-    swap = net_copy(net, r.gpre, r.both_g.at[section], 1)
-    swap.wait_recv()
-    swap.wait_send()
+        early_end.last(r.fin_e, r.fin_o)
+        late_end.last(r.fin_l)
+    bulk.drain()
+
+    @pl.when(section == 0)
+    def _():
+        moves[0].wait_send()
+        moves[1].wait_send()
+        keeps[2].wait()
+        moves[2].wait_recv()
+
+    @pl.when(section == 1)
+    def _():
+        moves[2].wait_send()
+        keeps[0].wait()
+        keeps[1].wait()
+        moves[0].wait_recv()
+        moves[1].wait_recv()
+
     net.drain()
     halo.drain()
     ex.drain()
@@ -1310,32 +1434,42 @@
     inputs = {
         "flags": ("s", flags), "g": ("v", g), "x": ("v", x), "w": ("h", w), "wo": ("h", wo), "taps": ("v", small.taps),
         "gain": ("v", small.gain), "heads": ("v", small.heads), "states": ("h", kept.states),
+        "both_hidden": ("h", kept.both_hidden.reshape(2 * TOK, D)),
+        "both_gated": ("h", kept.both_gated.reshape(2 * TOK, INNER)),
     }
     for key in ("act", "dact", "side", "raw", "dt", "cum", "inv", "dec", "pre", "halo", "y"):
         inputs[key] = ("v", getattr(kept, key))
     outputs = {
-        "result": in_vmem(TOK, D, dtype=BF16), "both_gb": in_hbm(2, TOK, WALF), "both_g": in_hbm(2, TOK, HALF),
+        "result": in_vmem(TOK, D, dtype=BF16), "both_gl": in_hbm(2, TOK, LCOLS),
         "gtaps": in_vmem(8, CONV), "ggain": in_vmem(8, D), "ghead": in_vmem(8, 128),
+        "ge": in_hbm(D, ECOLS), "go": in_hbm(INNER, WALF),
+        **fold_targets("e", ECOLS, True, lambda *shape: in_vmem(*shape, dtype=BF16)),
     }
     tile = pltpu.VMEM((TOK, 128), F32)
     edge = pltpu.VMEM((8, CONV), F32)
+    slots, tile_rows = (2, 128) if rider else (4, 512)
     scratch = {
-        "wo_s": pltpu.VMEM((SLOTS, 2, 384, WALF), BF16), "w_s": pltpu.VMEM((SLOTS, 256, HALF), BF16),
-        "wo_load": dma_sems(SLOTS), "w_load": dma_sems(SLOTS), "load": dma_sems(3),
+        "wo_s": pltpu.VMEM((slots, 2, 384, WALF), BF16), "w_s": pltpu.VMEM((slots, 256, HALF), BF16),
+        "wo_load": dma_sems(slots), "w_load": dma_sems(slots), "load": dma_sems(5),
+        "hid2": pltpu.VMEM((2 * TOK, D), BF16), "gated2": pltpu.VMEM((2 * TOK, INNER), BF16),
+        "gb2": pltpu.VMEM((2 * TOK, WALF), BF16), "dg2": pltpu.VMEM((2 * TOK, ECOLS), BF16),
+        "stage_o": pltpu.VMEM((2, tile_rows, WALF), BF16), "stage_e": pltpu.VMEM((2, tile_rows, ECOLS), BF16), "stage_s": dma_sems(4),
         "state_s": pltpu.VMEM((OWNERS, OWN, STATE), BF16),
         "gb": pltpu.VMEM((TOK, D), BF16), "gg": pltpu.VMEM((TOK, INNER), F32), "dy": pltpu.VMEM((TOK, INNER), BF16),
         "gsum": pltpu.VMEM((TOK, CONV), F32), "gpre": pltpu.VMEM((TOK, HALF), BF16), "gside": pltpu.VMEM((TOK, HALF), BF16),
-        "hid": pltpu.VMEM((TOK, D), F32),
         "dots": tile, "cumt": tile, "edge": tile, "dscore": tile, "grad_b": tile, "grad_c": tile, "xdu": tile, "dyy": tile,
         "thin": pltpu.VMEM((16, 128), F32),
         "tail": edge, "halo_near": edge, "halo_far": edge, "halo_s": dma_sems(4),
-        "pair_send": dma_sems(2), "pair_recv": dma_sems(2),
-        **exchange_scratch(),
+        "pair_send": dma_sems(4), "pair_recv": dma_sems(4),
+        **exchange_scratch(), **fold_scratch("e", ECOLS, True), **net_scratch(64),
     }
     if rider:
-        inputs.update({"gi": ("h", grads[0]), "go": ("h", grads[1])})
-        outputs.update({"fin_in": in_vmem(24, HALF), "fin_out": in_vmem(48, WALF)})
-        scratch.update(fold_scratch())
+        inputs.update({"gl": ("h", grads[0]), "e1a": ("v", grads[1]), "e1b": ("v", grads[2]), "e1o": ("v", grads[3])})
+        outputs.update({"fin_e": in_vmem(24, ECOLS), "fin_l": in_vmem(24, LCOLS), "fin_o": in_vmem(48, WALF)})
+        scratch.update(fold_scratch("l", LCOLS, False))
+        scratch.update(fold_targets("l", LCOLS, False, lambda *shape: pltpu.VMEM(shape, BF16)))
+        scratch.update(finish_scratch("e", ECOLS, True))
+        scratch.update(finish_scratch("l", LCOLS, False))
     return call(
         functools.partial(backward_body, layer, rider), "block_backward", 4 + layer, inputs, outputs, scratch
     )
@@ -1345,9 +1479,11 @@
     c, y, z, x = places()
     greet_axes()
     net = Net(r.net_send, r.net_recv)
-    fold = Fold(net, r.gi, r.go, r)
-    rest = Finish(net, r)
-    fold.begin()
+    late = Fold(net, r, "l", LCOLS, r.gl, None)
+    late.begin((0, 1))
+    early_end = Finish(net, r, "e", ECOLS, (r.e0a, r.e0b, r.e0o))
+    early_end.second()
+    late_end = Finish(net, r, "l", LCOLS, late.h)
     row = lax.broadcasted_iota(jnp.int32, (8, 128), 0)
     lane = lane_at((8, 128))
     for layer in range(2):
@@ -1361,52 +1497,58 @@
             head = jnp.where(lane < 3, take_chunk(heads, 0, 8, d // 4), 0.0)
             r.cells[cell + (slice(8, 16),)] = jnp.where(row >= 5, head, second)
     pair = net.go(r.cells.at[1 - c], r.other, sibling())
-    other_in = net.go(r.far_in, r.got_in, sibling())
-    other_out = net.go(r.far_out, r.got_out, sibling())
+    others = [
+        net.go(r.far_e, r.got_far_e, sibling()),
+        net.go(r.far_l, r.got_far_l, sibling()),
+        net.go(r.far_o, r.got_far_o, sibling()),
+    ]
     pair.wait_recv()
     r.sum0[...] = r.cells[c] + r.other[...]
     hops = [net.go(r.sum0.at[lax.rem(y + k, 4)], r.in_y.at[k], y_peer(k)) for k in range(1, 4)]
-    for kind in (2, 0, 1):
-        fold.combine(kind)
+    late.combine(0)
+    late.combine(1)
+    early_end.third()
     for copy in hops:
         copy.wait_recv()
     r.sum1[...] = r.sum0[y] + r.in_y[1] + r.in_y[2] + r.in_y[3]
     hops = [net.go(r.sum1.at[lax.rem(z + k, 4)], r.in_z.at[k], z_peer(k)) for k in range(1, 4)]
-    for kind in (2, 0, 1):
-        fold.settle(kind)
-        rest.second(kind)
+    late.settle(0)
+    late.settle(1)
+    late_end.second()
     for copy in hops:
         copy.wait_recv()
     r.sum2[...] = r.sum1[z] + r.in_z[1] + r.in_z[2] + r.in_z[3]
     r.in_x[x] = r.sum2[x]
     hops = [net.go(r.sum2.at[lax.rem(x + k, 4)], r.in_x.at[x], x_peer(k)) for k in range(1, 4)]
-    rest.third()
+    early_end.last(r.near_e, r.near_o)
+    others.append(net.go(r.near_e, r.got_near_e, sibling()))
+    others.append(net.go(r.near_o, r.got_near_o, sibling()))
+    late_end.third()
     for copy in hops:
         copy.wait_recv()
     r.blob[...] = r.in_x[0] + r.in_x[1] + r.in_x[2] + r.in_x[3]
-    rest.last(r.near_in, r.near_out)
-    near_in = net.go(r.near_in, r.got_near_in, sibling())
-    near_out = net.go(r.near_out, r.got_near_out, sibling())
-    for copy in (other_in, other_out, near_in, near_out):
+    late_end.last(r.near_l)
+    others.append(net.go(r.near_l, r.got_near_l, sibling()))
+    for copy in others:
         copy.wait_recv()
+
+    def put(first_l, second_l, first_e, second_e, first_o, second_o):
+        r.inner[:, :LCOLS] = first_l[...]
+        r.inner[:, LCOLS:] = second_l[:, : INNER - LCOLS]
+        r.bc[...] = second_l[:, INNER - LCOLS : CONV - LCOLS]
+        r.step[...] = second_l[:, CONV - LCOLS : CONV - LCOLS + 128]
+        r.gate[:, :ECOLS] = first_e[...]
+        r.gate[:, ECOLS:] = second_e[...]
+        r.out[:, :WALF] = first_o[...]
+        r.out[:, WALF:] = second_o[...]
 
     @pl.when(c == 0)
     def _():
-        r.inner[...] = r.near_in[:, :INNER]
-        r.bc[...] = r.near_in[:, INNER:]
-        r.step[...] = r.got_near_in[:, :128]
-        r.gate[...] = r.got_near_in[:, GATE0:]
-        r.out[:, :WALF] = r.near_out[...]
-        r.out[:, WALF:] = r.got_near_out[...]
+        put(r.near_l, r.got_near_l, r.near_e, r.got_near_e, r.near_o, r.got_near_o)
 
     @pl.when(c == 1)
     def _():
-        r.inner[...] = r.got_in[:, :INNER]
-        r.bc[...] = r.got_in[:, INNER:]
-        r.step[...] = r.far_in[:, :128]
-        r.gate[...] = r.far_in[:, GATE0:]
-        r.out[:, :WALF] = r.got_out[...]
-        r.out[:, WALF:] = r.far_out[...]
+        put(r.got_far_l, r.far_l, r.got_far_e, r.far_e, r.got_far_o, r.far_o)
 
     net.drain()
 
@@ -1416,7 +1558,8 @@
     return call(
         reduce_body, "reduce_grads", 6,
         {
-            "gi": ("h", grads[0]), "go": ("h", grads[1]), "far_in": ("v", far[0]), "far_out": ("v", far[1]),
+            "gl": ("h", grads[0]), "e0a": ("v", grads[1]), "e0b": ("v", grads[2]), "e0o": ("v", grads[3]),
+            "far_e": ("v", far[0]), "far_l": ("v", far[1]), "far_o": ("v", far[2]),
             "gtaps": ("v", gtaps), "ggain": ("v", ggain), "ghead": ("v", ghead),
         },
         {
@@ -1424,14 +1567,18 @@
             "gate": in_vmem(24, INNER), "out": in_vmem(48, D), "blob": in_vmem(16, 128),
         },
         {
-            "near_in": pltpu.VMEM((24, HALF), F32), "near_out": pltpu.VMEM((48, WALF), F32),
-            "got_near_in": pltpu.VMEM((24, HALF), F32), "got_near_out": pltpu.VMEM((48, WALF), F32),
-            "got_in": pltpu.VMEM((24, HALF), F32), "got_out": pltpu.VMEM((48, WALF), F32),
+            **{
+                name + part: pltpu.VMEM(shape, F32)
+                for name in ("near_", "got_near_", "got_far_")
+                for part, shape in (("e", (24, ECOLS)), ("l", (24, LCOLS)), ("o", (48, WALF)))
+            },
             "cells": pltpu.VMEM((2, 4) + cell, F32), "other": pltpu.VMEM((4,) + cell, F32),
             "sum0": pltpu.VMEM((4,) + cell, F32), "in_y": pltpu.VMEM((4,) + cell, F32),
             "sum1": pltpu.VMEM(cell, F32), "in_z": pltpu.VMEM((4,) + cell[1:], F32),
             "sum2": pltpu.VMEM(cell[1:], F32), "in_x": pltpu.VMEM((4, 16, 128), F32),
-            **fold_scratch(),
+            **fold_scratch("l", LCOLS, False),
+            **fold_targets("l", LCOLS, False, lambda *shape: pltpu.VMEM(shape, BF16)),
+            **finish_scratch("e", ECOLS, True), **finish_scratch("l", LCOLS, False), **net_scratch(64),
         },
     )
 
@@ -1466,11 +1613,10 @@
 ):
     section = lax.axis_index("section")
     seq_pos = lax.axis_index("seq")
-    small = start_up(
-        w_inner[0], w_bc[0], step_lanes(w_step[0]), w_gate[0], w_out[0],
-        small_blob(norm_gain[0], inner_gain[0], conv_inner[0], conv_bc[0], head_params[0]),
-    )
-    weights = [(small.w.reshape(2, D, HALF), small.wo.reshape(2, INNER, WALF)), None]
+    shards = {
+        "inner": w_inner[0], "bc": w_bc[0], "step": step_lanes(w_step[0]), "gate": w_gate[0], "out": w_out[0],
+        "blob": small_blob(norm_gain[0], inner_gain[0], conv_inner[0], conv_bc[0], head_params[0]),
+    }
     firsts = (BLOCKS - seg_groups[0]) * (BLOCK_LEN // TOK)
     first = jnp.where(section == 0, firsts[0], firsts[1])
     at_start = seq_pos == first
@@ -1484,34 +1630,28 @@
     ).astype(F32)
 
     x = lax.dynamic_index_in_dim(block_input[0], section, 0, keepdims=False)
-    kept, inputs = [], []
-    for layer in range(2):
-        w, wo = weights[layer]
-        made = block_forward(
-            layer, flags, x, w, wo, small, (small.p1, small.o1) if layer == 0 else None
-        )
-        if layer == 0:
-            weights[1] = (made.next_w.reshape(2, D, HALF), made.next_wo.reshape(2, INNER, WALF))
-        kept.append(made)
-        inputs.append(x)
-        x = made.result
+    start = block_forward(0, flags, x, shards)
+    weights = (
+        (start.w0.reshape(2, D, HALF), start.wo0.reshape(2, INNER, WALF)),
+        (start.next_w.reshape(2, D, HALF), start.next_wo.reshape(2, INNER, WALF)),
+    )
+    kept = [start, block_forward(1, flags, start.result, weights[1] + (start,))]
+    inputs = [x, start.result]
 
     g = lax.dynamic_index_in_dim(cotangent[0], section, 0, keepdims=False)
     grads = None
     backs = [None, None]
     for layer in (1, 0):
         w, wo = weights[layer]
-        back = block_backward(layer, flags, g, inputs[layer], w, wo, small, kept[layer], grads)
+        back = block_backward(layer, flags, g, inputs[layer], w, wo, start, kept[layer], grads)
         backs[layer] = back
         g = back.result
         hidden = kept[layer].both_hidden.reshape(2 * TOK, D)
-        gated = kept[layer].both_gated.reshape(2 * TOK, INNER)
-        grad_in = dot32(hidden, back.both_g.reshape(2 * TOK, HALF), ((0,), (0,))).astype(BF16)
-        grad_out = dot32(gated, back.both_gb.reshape(2 * TOK, WALF), ((0,), (0,))).astype(BF16)
-        grads = (grad_in.reshape(4, 4, 96, HALF), grad_out.reshape(4, 4, 4, 48, WALF))
+        grad_late = dot32(hidden, back.both_gl.reshape(2 * TOK, LCOLS), ((0,), (0,))).astype(BF16)
+        grads = (grad_late.reshape(4, 4, 96, LCOLS), back.eha, back.ehb, back.eho)
 
     final = reduce_all(
-        grads, (backs[0].fin_in, backs[0].fin_out),
+        grads, (backs[0].fin_e, backs[0].fin_l, backs[0].fin_o),
         jnp.stack([backs[0].gtaps, backs[1].gtaps]), jnp.stack([backs[0].ggain, backs[1].ggain]),
         jnp.stack([backs[0].ghead, backs[1].ghead]),
     )

time: 615 us -> 546 us (0.89)
  Pallas kernels: 558 us -> 501 us
  matrix products: 20.4 us -> 10.5 us
    pallas_call x6 -> x5, Pallas kernels: 558 us -> 501 us  [call(): pl.pallas_call(kernel, out_shape=tuple((shape for shape, _ in outputs.val...]
    dot_general x4 -> x2, matrix products: 20.4 us -> 10.5 us  [dot32(): lax.dot_general(left, right, (dims, ((), ())), preferred_element_type=F32)]
  transfers between devices with their start and end apart: 2 -> 2, of which waited for: 0 -> 0; matrix products, arithmetic and copies ran while one was open for 6% -> 4% of each run, Pallas kernels for 47% -> 48%
where the time goes in v4:
time: 546 us; the launch traced here: 545 us
  Pallas kernels  501 us (92%)
  local copies, waits for them, and re-layouts  17 us (3%)
  matrix products  10.5 us (2%)
  other arithmetic  10.3 us (2%)
    pallas_call x5, Pallas kernels, call(): pl.pallas_call(kernel, out_shape=tuple((shape for shape, _ in outputs.val...  501 us
  transfers between devices with their start and end apart: 2, of which 0 were waited for; matrix products, arithmetic and copies ran while one was open for 4% of the time, Pallas kernels for 48%

profile of v4, /device:TPU:1, one launch (start us, length us, event | category | flops | bytes accessed | tf_op | source)
XLA Modules:
  0.0 544.7 jit_solution(445830513027646669)
XLA Ops:
  0.6 0.0 copy-start
  0.7 0.7 subtract_multiply_fusion
  1.4 0.6 fusion
  4.0 0.8 copy.32
  4.7 0.7 copy.45
  5.4 0.8 copy.31
  6.2 0.7 copy.33.refs_4_
  6.9 0.7 pad_convert_fusion.2
  7.6 0.7 pad_convert_fusion
  8.3 0.8 dynamic-slice_bitcast_fusion.1.refs_1_.refs_2_
  9.1 0.6 add_convert_fusion.refs_0_
  9.7 1.2 concatenate.3.refs_7_
  10.9 189.6 %block_forward.2 = (f32[128,3328]{1,0:T(8,128)}, f32[128,3328]{1,0:T(8,128)}, f32[128,3328]{1,0:T(8,128)}, f32[128,3072]{1,0:T(8,128)}, f32[128,128]{1,0:T(8,128...) custom-call(f32[4]{0:T(128)} %add_convert_fusion.refs_0_, ...), custom_call_target="tpu_custom_call" | custom-call | tf_op jit(solution)/shard_map/block_forward/pallas_call | solution.py:123
  200.5 0.0 copy-start.12
  200.5 51.1 %block_forward.3 = (f32[128,3328]{1,0:T(8,128)}, f32[128,3328]{1,0:T(8,128)}, f32[128,3328]{1,0:T(8,128)}, f32[128,3072]{1,0:T(8,128)}, f32[128,128]{1,0:T(8,128...) custom-call(f32[4]{0:T(128)} %add_convert_fusion.refs_0_, ...), custom_call_target="tpu_custom_call" | custom-call | tf_op jit(solution)/shard_map/block_forward/pallas_call | solution.py:123
  251.6 0.8 broadcast_select_fusion.2
  252.4 1.3 collective-permute-start
  253.8 0.8 dynamic-slice_bitcast_fusion.refs_1_
  254.6 74.1 %block_backward.2 = (bf16[128,1536]{1,0:T(8,128)(2,1)}, bf16[2,128,1792]{2,1,0:T(8,128)(2,1)}, f32[8,3328]{1,0:T(8,128)}, f32[8,1536]{1,0:T(8,128)}, f32[8,128]{...) custom-call(f32[4]{0:T(128)} %add_convert_fusion.refs_0_, ...), custom_call_target="tpu_custom_call" | custom-call | tf_op jit(solution)/shard_map/block_backward/pallas_call | solution.py:123
  328.7 5.2 bitcast_convert_fusion.1
  334.0 113.4 %block_backward.3 = (bf16[128,1536]{1,0:T(8,128)(2,1)}, bf16[2,128,1792]{2,1,0:T(8,128)(2,1)}, f32[8,3328]{1,0:T(8,128)}, f32[8,1536]{1,0:T(8,128)}, f32[8,128]{...) custom-call(f32[4]{0:T(128)} %add_convert_fusion.refs_0_, ...), custom_call_target="tpu_custom_call" | custom-call | tf_op jit(solution)/shard_map/block_backward/pallas_call | solution.py:123
  447.4 1.8 broadcast_select_fusion
  449.2 1.6 collective-permute-start.1
  450.9 5.3 bitcast_convert_fusion
  456.1 0.6 pad_maximum_fusion.2.refs_9_
  456.7 0.6 pad_maximum_fusion.1.refs_8_
  457.4 0.7 pad_maximum_fusion.refs_7_
  458.1 72.9 %reduce_grads.1 = (f32[24,3072]{1,0:T(8,128)}, f32[24,256]{1,0:T(8,128)}, f32[24,128]{1,0:T(8,128)}, f32[24,3072]{1,0:T(8,128)}, f32[48,1536]{1,0:T(8,128)}, /*index=5*/f32[16,128]{1,0:T(8,128)}) custom-call(bf16[4,4,96,1792]{3,2,1,0:T(8,128)(2,1)} %bitcast.76, bf16[4,96,768]{2,1,0:T(8,128)(2,1)} %get-tuple-element.118.refs_1_, ...), custom_call_target="tpu_custom_call" | custom-call | tf_op jit(solution)/shard_map/reduce_grads/pallas_call | solution.py:123
  531.1 1.3 slice.34
  532.3 1.2 slice.29
  533.5 0.7 slice.32
  534.2 0.7 slice_bitcast_fusion.1
  534.9 0.6 copy.40
  535.5 0.7 copy.37
  536.1 0.7 slice_bitcast_fusion
  536.8 0.6 copy.39
  537.4 0.8 copy.36
  538.2 0.7 copy.38
  538.9 0.0 collective-permute-done
  538.9 0.1 select_bitcast_fusion.3
  539.0 0.9 maximum_bitcast_fusion
  539.9 0.0 collective-permute-done.1
  539.9 1.1 select_bitcast_fusion.1
  541.0 0.9 maximum_bitcast_fusion.1
  542.0 0.7 copy.50
  542.7 0.7 copy.51
  543.4 0.6 copy.52
  544.0 0.7 copy.53
  (44 shorter events, 0.1 us)
Async XLA Ops:
  0.6 7.6 %copy-start = (bf16[1,2,128,1536]{3,2,1,0:T(8,128)(2,1)S(1)}, bf16[1,2,128,1536]{3,2,1,0:T(8,128)(2,1)}, u32[]{:S(2)}) copy-start(bf16[1,2,128,1536]{3,2,1,0:T(8,128)(2,1)} %param.13) | copy-start | bytes 2359300
  200.5 51.1 %copy-start.2 = (bf16[128,1536]{1,0:T(8,128)(2,1)S(1)}, bf16[128,1536]{1,0:T(8,128)(2,1)}, u32[]{:S(2)}) copy-start(bf16[128,1536]{1,0:T(8,128)(2,1)} %get-tuple-element.74.refs_1_.refs_2_) | copy-start | bytes 1179652
  200.5 53.3 %copy-start.12 = (bf16[1,2,128,1536]{3,2,1,0:T(8,128)(2,1)S(1)}, bf16[1,2,128,1536]{3,2,1,0:T(8,128)(2,1)}, u32[]{:S(2)}) copy-start(bf16[1,2,128,1536]{3,2,1,0:T(8,128)(2,1)} %param.14) | copy-start | bytes 2359300
  252.4 286.5 %collective-permute-start = (bf16[128,1536]{1,0:T(8,128)(2,1)}, bf16[128,1536]{1,0:T(8,128)(2,1)S(1)}, u32[]{:S(2)}, u32[]{:S(2)}) collective-permute-start(bf16[128,1536]{1,0:T(8,128)(2,1)} %broadcast_select_fusion.2), channel_id=1, source_target_pairs={{0,64},{64,0},{1,65},{65,1},{2,66},{66,2},{3,67},{67,3},{4,68},{68... | collective-permute-start | bytes 1179656 | tf_op jit(solution)/shard_map/ppermute | solution.py:1606
  254.6 74.1 %copy-start.5 = (bf16[2,128,1536]{2,1,0:T(8,128)(2,1)S(1)}, bf16[2,128,1536]{2,1,0:T(8,128)(2,1)}, u32[]{:S(2)}) copy-start(bf16[2,128,1536]{2,1,0:T(8,128)(2,1)} %get-tuple-element.82) | copy-start | bytes 2359300
  334.0 113.4 %copy-start.6 = (bf16[128,1536]{1,0:T(8,128)(2,1)S(1)}, bf16[128,1536]{1,0:T(8,128)(2,1)}, u32[]{:S(2)}) copy-start(bf16[128,1536]{1,0:T(8,128)(2,1)} %get-tuple-element.95.refs_1_) | copy-start | bytes 1179652
  334.0 116.9 %copy-start.4 = (bf16[2,128,1536]{2,1,0:T(8,128)(2,1)S(1)}, bf16[2,128,1536]{2,1,0:T(8,128)(2,1)}, u32[]{:S(2)}) copy-start(bf16[2,128,1536]{2,1,0:T(8,128)(2,1)} %get-tuple-element.99) | copy-start | bytes 2359300
  449.2 6.9 %copy-start.18 = (f32[8,128]{1,0:T(8,128)S(1)}, f32[8,128]{1,0:T(8,128)}, u32[]{:S(2)}) copy-start(f32[8,128]{1,0:T(8,128)} %get-tuple-element.129) | copy-start | bytes 12292
  449.2 6.9 %copy-start.19 = (f32[8,128]{1,0:T(8,128)S(1)}, f32[8,128]{1,0:T(8,128)}, u32[]{:S(2)}) copy-start(f32[8,128]{1,0:T(8,128)} %get-tuple-element.128) | copy-start | bytes 12292
  449.2 7.5 %copy-start.15 = (f32[8,1536]{1,0:T(8,128)S(1)}, f32[8,1536]{1,0:T(8,128)}, u32[]{:S(2)}) copy-start(f32[8,1536]{1,0:T(8,128)} %get-tuple-element.127) | copy-start | bytes 147460
  449.2 7.5 %copy-start.16 = (f32[8,1536]{1,0:T(8,128)S(1)}, f32[8,1536]{1,0:T(8,128)}, u32[]{:S(2)}) copy-start(f32[8,1536]{1,0:T(8,128)} %get-tuple-element.126) | copy-start | bytes 147460
  449.2 90.7 %collective-permute-start.1 = (bf16[128,1536]{1,0:T(8,128)(2,1)}, bf16[128,1536]{1,0:T(8,128)(2,1)}, u32[]{:S(2)}, u32[]{:S(2)}) collective-permute-start(bf16[128,1536]{1,0:T(8,128)(2,1)} %broadcast_select_fusion), channel_id=1, source_target_pairs={{0,64},{64,0},{1,65},{65,1},{2,66},{66,2},{3,67},{67,3},{4,68},{68... | collective-permute-start | bytes 1179656 | tf_op jit(solution)/shard_map/ppermute | solution.py:1606
  450.8 6.6 %copy-start.13 = (f32[8,3328]{1,0:T(8,128)S(1)}, f32[8,3328]{1,0:T(8,128)}, u32[]{:S(2)}) copy-start(f32[8,3328]{1,0:T(8,128)} %get-tuple-element.125) | copy-start | bytes 319492
  450.8 6.6 %copy-start.14 = (f32[8,3328]{1,0:T(8,128)S(1)}, f32[8,3328]{1,0:T(8,128)}, u32[]{:S(2)}) copy-start(f32[8,3328]{1,0:T(8,128)} %get-tuple-element.124) | copy-start | bytes 319492
  457.4 81.5 %copy-start.3 = (bf16[128,1536]{1,0:T(8,128)(2,1)S(1)}, bf16[128,1536]{1,0:T(8,128)(2,1)}, u32[]{:S(2)}) copy-start(bf16[128,1536]{1,0:T(8,128)(2,1)} %get-tuple-element.74.refs_1_.refs_2_) | copy-start | bytes 1179652
  457.4 81.5 %copy-start.7 = (bf16[128,1536]{1,0:T(8,128)(2,1)S(1)}, bf16[128,1536]{1,0:T(8,128)(2,1)}, u32[]{:S(2)}) copy-start(bf16[128,1536]{1,0:T(8,128)(2,1)} %get-tuple-element.80) | copy-start | bytes 1179652
  458.1 81.8 %copy-start.8 = (bf16[128,1536]{1,0:T(8,128)(2,1)S(1)}, bf16[128,1536]{1,0:T(8,128)(2,1)}, u32[]{:S(2)}) copy-start(bf16[128,1536]{1,0:T(8,128)(2,1)} %get-tuple-element.116) | copy-start | bytes 1179652
  458.1 86.6 %copy-start.1 = (bf16[1,2,128,1536]{3,2,1,0:T(8,128)(2,1)S(1)}, bf16[1,2,128,1536]{3,2,1,0:T(8,128)(2,1)}, u32[]{:S(2)}) copy-start(bf16[1,2,128,1536]{3,2,1,0:T(8,128)(2,1)} %param.13) | copy-start | bytes 2359300
  531.0 11.6 %copy-start.10 = (f32[24,3072]{1,0:T(8,128)S(1)}, f32[24,3072]{1,0:T(8,128)}, u32[]{:S(2)}) copy-start(f32[24,3072]{1,0:T(8,128)} %get-tuple-element.132) | copy-start | bytes 884740
  531.1 12.3 %copy-start.17 = (f32[24,256]{1,0:T(8,128)S(1)}, f32[24,256]{1,0:T(8,128)}, u32[]{:S(2)}) copy-start(f32[24,256]{1,0:T(8,128)} %get-tuple-element.133) | copy-start | bytes 73732
  531.1 12.9 %copy-start.9 = (f32[48,1536]{1,0:T(8,128)S(1)}, f32[48,1536]{1,0:T(8,128)}, u32[]{:S(2)}) copy-start(f32[48,1536]{1,0:T(8,128)} %get-tuple-element.135) | copy-start | bytes 884740
  538.9 3.1 copy-start.11

commit v5 on v4

--- a/solution.py
+++ b/solution.py
@@ -113,18 +113,50 @@
     return jax.ShapeDtypeStruct(shape, dtype), pl.BlockSpec(memory_space=pltpu.VMEM)
 
 
+def saved(*shape, dtype=F32):
+    return jax.ShapeDtypeStruct(shape, dtype), None
+
+
 def call(body, name, ident, inputs, outputs, scratch):
-    spaces = {"h": pl.ANY, "v": pltpu.VMEM, "s": pltpu.SMEM}
-    names = [key for key in inputs] + [key for key in outputs] + [key for key in scratch]
+    spaces = {"h": pl.ANY, "v": pltpu.VMEM, "s": pltpu.SMEM, "p": pl.ANY}
+    early = [key for key, (kind, _) in inputs.items() if kind == "p"]
+    late = [key for key, (_, spec) in outputs.items() if spec is None]
+    scratch = dict(scratch)
+    for key in early:
+        scratch[key] = pltpu.VMEM(inputs[key][1].shape, inputs[key][1].dtype)
+    for key in late:
+        scratch[key] = pltpu.VMEM(outputs[key][0].shape, outputs[key][0].dtype)
+    if early or late:
+        scratch["move_sems"] = dma_sems(len(early) + len(late))
+    names = [key + "_far" if key in early else key for key in inputs]
+    names += [key + "_far" if key in late else key for key in outputs] + list(scratch)
 
     def kernel(*refs):
-        body(types.SimpleNamespace(**dict(zip(names, refs))))
+        r = types.SimpleNamespace(**dict(zip(names, refs)))
+
+        def mover(key):
+            near, far = getattr(r, key), getattr(r, key + "_far")
+            src, dst = (far, near) if key in early else (near, far)
+            return pltpu.make_async_copy(src, dst, r.move_sems.at[(early + late).index(key)])
+
+        def start(*keys):
+            for key in keys:
+                mover(key).start()
+
+        def wait(*keys):
+            for key in keys:
+                mover(key).wait()
+
+        r.move, r.moved = start, wait
+        body(r)
 
     out = pl.pallas_call(
         kernel,
         out_shape=tuple(shape for shape, _ in outputs.values()),
         in_specs=[pl.BlockSpec(memory_space=spaces[kind]) for kind, _ in inputs.values()],
-        out_specs=tuple(spec for _, spec in outputs.values()),
+        out_specs=tuple(
+            pl.BlockSpec(memory_space=pl.ANY) if spec is None else spec for _, spec in outputs.values()
+        ),
         scratch_shapes=list(scratch.values()),
         compiler_params=pltpu.CompilerParams(
             collective_id=ident, has_side_effects=True, vmem_limit_bytes=VMEM_LIMIT
@@ -242,9 +274,10 @@
         go = self.net.go
         for copy in self.first:
             copy.wait_recv()
-        self.rows[...] = jnp.concatenate(
-            [self.stage[n].astype(F32)[:24] for n in range(4)], axis=0
-        ).astype(BF16)
+        for side in range(2):
+            self.rows[:, CUT * side : CUT * side + CUT] = jnp.concatenate(
+                [self.stage[n].astype(F32)[24 * side : 24 * side + 24] for n in range(4)], axis=0
+            ).astype(BF16)
         for k in (1, 3):
             for kind, cols in ((0, pl.ds(0, CUT)), (1, pl.ds(CUT, CUT))):
                 self.inner[kind, k] = go(
@@ -299,7 +332,7 @@
 
 def gather_scratch():
     return {
-        "stage": pltpu.VMEM((4, 32, HALF), BF16),
+        "stage": pltpu.VMEM((4, 48, CUT), BF16),
         "rows": pltpu.VMEM((96, HALF), BF16),
         "own": dma_sems(2),
     }
@@ -335,18 +368,29 @@
 
 def start_body(r, net, after):
     c, y, z, x = places()
-    pad = jnp.zeros((8, 1), F32)
-
-    def tall(value):
-        return jnp.concatenate(
-            [value.astype(F32), jnp.broadcast_to(pad, (8, value.shape[1]))], axis=0
-        ).astype(BF16)
-
-    r.mine[0, :, :INNER] = tall(r.inner[...])
-    r.mine[0, :, INNER:] = tall(r.bc[...])
-    r.mine[1, :, :128] = tall(r.step[...])
-    r.mine[1, :, 128:GATE0] = jnp.zeros((32, 128), BF16)
-    r.mine[1, :, GATE0:] = tall(r.gate[...])
+
+    def stacked(first, second):
+        return jnp.concatenate([first.astype(F32), second.astype(F32)], axis=0).astype(BF16)
+
+    r.wide[...] = jnp.zeros_like(r.wide)
+    r.wide[0:24, 0:48] = r.step[...].astype(F32)
+    lane24 = lane_at((24, 128))
+    spread_step = jnp.zeros((24, 128), F32)
+    for n in range(OWNERS):
+        moved = pltpu.roll(r.wide[0:24, :], 5 * n, 1) if n else r.wide[0:24, :]
+        spread_step = jnp.where((lane24 >= 8 * n) & (lane24 < 8 * n + 3), moved, spread_step)
+    gate_cut = CUT - GATE0
+    r.mine[0, :, : INNER - CUT] = stacked(r.inner[:, : INNER - CUT], r.inner[:, CUT:])
+    r.mine[0, :, INNER - CUT :] = stacked(r.inner[:, INNER - CUT : CUT], r.bc[...])
+    r.mine[1, :, :128] = stacked(spread_step, r.gate[:, gate_cut : gate_cut + 128])
+    r.mine[1, :, 128:GATE0] = stacked(jnp.zeros((24, 128), F32), r.gate[:, gate_cut + 128 : gate_cut + GATE0])
+    r.mine[1, :, GATE0:] = stacked(r.gate[:, :gate_cut], r.gate[:, gate_cut + GATE0 :])
+    r.blob[...] = jnp.zeros_like(r.blob)
+    r.blob[0:5, 0:48] = r.conv_inner[...].astype(F32)
+    r.blob[ROW_MID : ROW_MID + 1, 0:48] = r.mid[...].astype(F32)
+    r.blob[ROW_NORM : ROW_NORM + 1, 0:24] = r.norm[...].astype(F32)
+    r.blob[8:13, 0:4] = r.conv_bc[...].astype(F32)
+    r.blob[13:16, 0:3] = r.head[...]
     given = pl.ds(pl.multiple_of((1 - c) * WALF, 128), WALF)
     swaps = [
         net.go(r.mine.at[1 - c], r.half.at[c], sibling()),
@@ -569,6 +613,24 @@
     pl.semaphore_wait(barrier, count + more)
 
 
+def flags_of(seg):
+    section = lax.axis_index("section")
+    seq = lax.axis_index("seq")
+    starts = [(BLOCKS - seg[0, n]) * (BLOCK_LEN // TOK) for n in range(2)]
+    first = jnp.where(section == 0, starts[0], starts[1])
+    at_start = seq == first
+    second = section == 1
+
+    def number(cond):
+        return jnp.where(cond, 1.0, 0.0)
+
+    live = number(seq >= first)
+    near = number(jnp.logical_not(at_start) | (second & (first == 0)))
+    far = number(at_start & second & (first != 0))
+    cross = number((section == 0) & (seq == 15) & (starts[1] != 0))
+    return live, near, far, cross
+
+
 def halo_copy(src, dst, sems, n, section, seq):
     return pltpu.make_async_remote_copy(
         src_ref=src, dst_ref=dst, send_sem=sems.at[n], recv_sem=sems.at[2 + n],
@@ -656,9 +718,11 @@
     if not rider:
         greet_layer(rider, True)
     ex = Exchange(False, r)
-    live = r.flags[0]
+    flags = flags_of(r.flags)
+    live = flags[0]
     heads = r.heads[layer]
-    x32 = r.x[...].astype(F32)
+    x_ref = r.x.at[section] if rider else r.x
+    x32 = x_ref[...].astype(F32)
     hidden_inv = lax.rsqrt(jnp.sum(x32 * x32, axis=1, keepdims=True) / D + EPS)
     r.hidden[...] = (x32 * hidden_inv * r.gain[layer, ROW_NORM : ROW_NORM + 1, :]).astype(BF16)
     loads[0].wait()
@@ -682,6 +746,7 @@
     lax.fori_loop(0, HALF // 256, project_side, 0)
     if rider:
         ga.relay(0)
+    r.move("pre", "side")
     pairs = [net.go(r.hidden, r.both_hidden.at[section], sibling())]
     owns = [fetch(r.hidden, r.both_hidden.at[section], r.load.at[3])]
     step = r.side[:, :128].astype(BF16).astype(F32) + heads[ROW_BIAS : ROW_BIAS + 1]
@@ -707,7 +772,7 @@
     weight = dt * jnp.exp(last - cum)
     halo.wait()
     r.halo[...] = jnp.where(
-        r.flags[1] > 0.0, r.halo_near[...], jnp.where(r.flags[2] > 0.0, r.halo_far[...], jnp.zeros_like(r.halo_far))
+        flags[1] > 0.0, r.halo_near[...], jnp.where(flags[2] > 0.0, r.halo_far[...], jnp.zeros_like(r.halo_far))
     )
 
     def conv_tile(cols):
@@ -735,6 +800,7 @@
         return carry
 
     lax.fori_loop(0, 8, states, 0)
+    r.move("act", "dact")
     if rider:
         ga.relay(1)
     for d in range(1, OWNERS):
@@ -789,6 +855,7 @@
         return carry
 
     lax.fori_loop(0, 8, across, 0)
+    r.move("raw", "y")
     if rider:
         ga.last(0)
         ga.last(1)
@@ -812,7 +879,7 @@
             cols = pl.ds(pl.multiple_of(n * 256, 256), 256)
             full = pl.ds(pl.multiple_of(half * WALF + n * 256, 256), 256)
             branch = dot32(r.gated[...], r.wo_s[half, :, cols])
-            r.result[:, full] = (r.x[:, full].astype(F32) + live * branch).astype(BF16)
+            r.result[:, full] = (x_ref[:, full].astype(F32) + live * branch).astype(BF16)
             return carry
 
         lax.fori_loop(0, WALF // 256, project, 0)
@@ -821,6 +888,26 @@
             ga.last(j)
         ga.end()
         bulk.drain()
+    if not rider:
+        cross = [
+            pltpu.make_async_remote_copy(
+                src_ref=src, dst_ref=r.finals.at[section], send_sem=r.final_s.at[0], recv_sem=r.final_s.at[1],
+                device_id=sibling(), device_id_type=MESH,
+            )
+            for src in (r.result, r.x)
+        ]
+        stay = [pltpu.make_async_copy(src, r.finals.at[section], r.final_s.at[2]) for src in (r.x, r.result)]
+        for n in range(2):
+
+            @pl.when(section == n)
+            def _():
+                cross[n].start()
+                stay[n].start()
+
+        cross[0].wait_recv()
+        cross[0].wait_send()
+        stay[0].wait()
+    r.moved("pre", "side", "act", "dact", "raw", "y")
     save.wait()
     for copy in owns:
         copy.wait()
@@ -837,8 +924,8 @@
     rider = layer == 0
     inputs = {"flags": ("s", flags), "x": ("v", x)}
     if rider:
-        for key in ("inner", "bc", "step", "gate", "out", "blob"):
-            inputs[key] = ("v", given[key])
+        for key, value in given.items():
+            inputs[key] = ("v", value)
     else:
         w, wo, small = given
         inputs.update({
@@ -846,10 +933,10 @@
             "heads": ("v", small.heads),
         })
     outputs = {
-        "act": in_vmem(TOK, CONV), "dact": in_vmem(TOK, CONV), "side": in_vmem(TOK, HALF), "raw": in_vmem(TOK, INNER),
+        "act": saved(TOK, CONV), "dact": saved(TOK, CONV), "side": saved(TOK, HALF), "raw": saved(TOK, INNER),
         "dt": in_vmem(TOK, 128), "cum": in_vmem(TOK, 128), "inv": in_vmem(TOK, 128),
-        "dec": in_vmem(OWNERS, 8, 128), "pre": in_vmem(TOK, CONV, dtype=BF16), "halo": in_vmem(16, CONV, dtype=BF16),
-        "y": in_vmem(TOK, INNER, dtype=BF16), "result": in_vmem(TOK, D, dtype=BF16),
+        "dec": in_vmem(OWNERS, 8, 128), "pre": saved(TOK, CONV, dtype=BF16), "halo": in_vmem(16, CONV, dtype=BF16),
+        "y": saved(TOK, INNER, dtype=BF16), "result": in_vmem(TOK, D, dtype=BF16),
         "states": in_hbm(OWNERS, OWN, STATE), "both_hidden": in_hbm(2, TOK, D), "both_gated": in_hbm(2, TOK, INNER),
     }
     tile = pltpu.VMEM((TOK, 128), F32)
@@ -863,6 +950,9 @@
         "load": dma_sems(6), "pair_send": dma_sems(2), "pair_recv": dma_sems(2),
         **exchange_scratch(),
     }
+    if not rider:
+        outputs["finals"] = in_hbm(2, TOK, D)
+        scratch["final_s"] = dma_sems(3)
     if rider:
         outputs.update({
             "w0": in_hbm(2, 4, 4, 96, HALF), "wo0": in_hbm(2, 4, 4, 4, 48, WALF),
@@ -870,7 +960,8 @@
             "taps": in_vmem(2, 8, CONV), "gain": in_vmem(2, 8, D), "heads": in_vmem(2, 8, 128),
         })
         scratch.update({
-            "mine": pltpu.VMEM((2, 32, HALF), BF16), "half": pltpu.VMEM((2, 32, HALF), BF16),
+            "mine": pltpu.VMEM((2, 48, CUT), BF16), "half": pltpu.VMEM((2, 48, CUT), BF16),
+            "wide": pltpu.VMEM((24, 128), F32), "blob": pltpu.VMEM((16, 128), F32),
             "half_o": pltpu.VMEM((2, 48, WALF), BF16), "cells": pltpu.VMEM((2, 4, 4, 4, 16, 128), F32),
             "net_send": dma_sems(400), "net_recv": dma_sems(400),
         })
@@ -1100,6 +1191,7 @@
 
     for n in range(slots_o):
         wo_tile(n).start()
+    r.move("side", "y", "act", "raw", "dact", "pre")
     for n in range(slots_w):
         w_tile(n).start()
     greet_layer(True, False)
@@ -1115,12 +1207,12 @@
         bulk, r, "e", ECOLS, r.ge.reshape(4, 4, 96, ECOLS), r.go.reshape(4, 4, 4, 48, WALF)
     )
     ex = Exchange(True, r)
-    live = r.flags[0]
+    flags = flags_of(r.flags)
+    live = flags[0]
     heads = r.heads[layer]
-    r.gb[...] = (r.g[...].astype(F32) * live).astype(BF16)
+    g_ref = r.g if rider else r.g.at[section]
+    r.gb[...] = (g_ref[...].astype(F32) * live).astype(BF16)
     inv = r.inv[...]
-    b = r.act[:, INNER : INNER + 128].astype(BF16)
-    c = r.act[:, INNER + 128 : CONV].astype(BF16)
     dt = r.dt[...]
     cum = r.cum[...]
     r.dots[...] = jnp.zeros((TOK, 128), F32)
@@ -1152,7 +1244,11 @@
             r.dots[...] += gg[:, 128 * q : 128 * q + 128] * mid * z
         return carry
 
+    r.moved("side", "y")
     lax.fori_loop(0, 8, first, 0)
+    r.moved("act")
+    b = r.act[:, INNER : INNER + 128].astype(BF16)
+    c = r.act[:, INNER + 128 : CONV].astype(BF16)
     total = jnp.broadcast_to(jnp.sum(r.dots[...], axis=1, keepdims=True), (TOK, 128))
     shift = total * inv * inv * inv / INNER
     r.gtaps[...] = jnp.zeros_like(r.gtaps)
@@ -1245,6 +1341,7 @@
         sums.append(jnp.sum(gsum, axis=0, keepdims=True))
         r.gtaps[0:5, cols] = jnp.concatenate(sums, axis=0)
 
+    r.moved("raw", "dact", "pre")
     ex.finish()
 
     def across(i, carry):
@@ -1324,7 +1421,7 @@
         axis=0,
     )
     halo.wait()
-    after = jnp.where(r.flags[3] > 0.0, r.halo_far[...], r.halo_near[...])
+    after = jnp.where(flags[3] > 0.0, r.halo_far[...], r.halo_near[...])
     r.halo_near[...] = jnp.where(live > 0.0, after, jnp.zeros_like(after))
 
     def conv_tile(i, carry):
@@ -1387,19 +1484,38 @@
         return carry
 
     lax.fori_loop(0, D // 256, project, 0)
-    x = r.x[...].astype(F32)
+    x = (r.x[section] if rider else r.x[...]).astype(F32)
     grad = r.gg[:, :D]
     inv_x = lax.rsqrt(jnp.sum(x * x, axis=1, keepdims=True) / D + EPS)
     scaled = grad * r.gain[layer, ROW_NORM : ROW_NORM + 1, :]
     dots = jnp.sum(scaled * x, axis=1, keepdims=True)
     dx = scaled * inv_x - x * (dots * inv_x * inv_x * inv_x / D)
-    r.result[...] = (r.g[...].astype(F32) + dx).astype(BF16)
+    r.result[...] = (g_ref[...].astype(F32) + dx).astype(BF16)
     r.ggain[...] = jnp.broadcast_to(jnp.sum(grad * x * inv_x, axis=0, keepdims=True), (8, D))
     for kind in range(3):
         early.settle(kind)
     if rider:
         early_end.last(r.fin_e, r.fin_o)
         late_end.last(r.fin_l)
+    if rider:
+        cross = [
+            pltpu.make_async_remote_copy(
+                src_ref=src, dst_ref=r.finals.at[section], send_sem=r.final_s.at[0], recv_sem=r.final_s.at[1],
+                device_id=sibling(), device_id_type=MESH,
+            )
+            for src in (r.g, r.result)
+        ]
+        stay = [pltpu.make_async_copy(src, r.finals.at[section], r.final_s.at[2]) for src in (r.result, r.g)]
+        for n in range(2):
+
+            @pl.when(section == n)
+            def _():
+                cross[n].start()
+                stay[n].start()
+
+        cross[0].wait_recv()
+        cross[0].wait_send()
+        stay[0].wait()
     bulk.drain()
 
     @pl.when(section == 0)
@@ -1437,8 +1553,10 @@
         "both_hidden": ("h", kept.both_hidden.reshape(2 * TOK, D)),
         "both_gated": ("h", kept.both_gated.reshape(2 * TOK, INNER)),
     }
-    for key in ("act", "dact", "side", "raw", "dt", "cum", "inv", "dec", "pre", "halo", "y"):
+    for key in ("dt", "cum", "inv", "dec", "halo"):
         inputs[key] = ("v", getattr(kept, key))
+    for key in ("side", "y", "act", "raw", "dact", "pre"):
+        inputs[key] = ("p", getattr(kept, key))
     outputs = {
         "result": in_vmem(TOK, D, dtype=BF16), "both_gl": in_hbm(2, TOK, LCOLS),
         "gtaps": in_vmem(8, CONV), "ggain": in_vmem(8, D), "ghead": in_vmem(8, 128),
@@ -1465,6 +1583,8 @@
     }
     if rider:
         inputs.update({"gl": ("h", grads[0]), "e1a": ("v", grads[1]), "e1b": ("v", grads[2]), "e1o": ("v", grads[3])})
+        outputs["finals"] = in_hbm(2, TOK, D)
+        scratch["final_s"] = dma_sems(3)
         outputs.update({"fin_e": in_vmem(24, ECOLS), "fin_l": in_vmem(24, LCOLS), "fin_o": in_vmem(48, WALF)})
         scratch.update(fold_scratch("l", LCOLS, False))
         scratch.update(fold_targets("l", LCOLS, False, lambda *shape: pltpu.VMEM(shape, BF16)))
@@ -1487,7 +1607,7 @@
     row = lax.broadcasted_iota(jnp.int32, (8, 128), 0)
     lane = lane_at((8, 128))
     for layer in range(2):
-        taps, gain, heads = r.gtaps.at[layer], r.ggain.at[layer], r.ghead.at[layer]
+        taps, gain, heads = (getattr(r, key + str(layer)) for key in ("gtaps", "ggain", "ghead"))
         for d in range(64):
             cell = (layer, d // 16, (d // 4) % 4, d % 4)
             first = jnp.where(lane < 48, take_chunk(taps, 0, 48, d), 0.0)
@@ -1526,7 +1646,12 @@
     late_end.third()
     for copy in hops:
         copy.wait_recv()
-    r.blob[...] = r.in_x[0] + r.in_x[1] + r.in_x[2] + r.in_x[3]
+    blob = r.in_x[0] + r.in_x[1] + r.in_x[2] + r.in_x[3]
+    r.conv_inner[...] = blob[0:5, :48]
+    r.mid[...] = blob[ROW_MID : ROW_MID + 1, :48]
+    r.norm[...] = blob[ROW_NORM : ROW_NORM + 1, :24]
+    r.conv_bc[...] = blob[8:13, :4]
+    r.head[...] = blob[13:16, :3]
     late_end.last(r.near_l)
     others.append(net.go(r.near_l, r.got_near_l, sibling()))
     for copy in others:
@@ -1536,7 +1661,13 @@
         r.inner[:, :LCOLS] = first_l[...]
         r.inner[:, LCOLS:] = second_l[:, : INNER - LCOLS]
         r.bc[...] = second_l[:, INNER - LCOLS : CONV - LCOLS]
-        r.step[...] = second_l[:, CONV - LCOLS : CONV - LCOLS + 128]
+        wide = second_l[:, CONV - LCOLS : CONV - LCOLS + 128]
+        lane24 = lane_at((24, 128))
+        steps = jnp.zeros((24, 128), F32)
+        for n in range(OWNERS):
+            moved = pltpu.roll(wide, 128 - 5 * n, 1) if n else wide
+            steps = jnp.where((lane24 >= 3 * n) & (lane24 < 3 * n + 3), moved, steps)
+        r.step[...] = steps[:, :HEADS]
         r.gate[:, :ECOLS] = first_e[...]
         r.gate[:, ECOLS:] = second_e[...]
         r.out[:, :WALF] = first_o[...]
@@ -1553,18 +1684,21 @@
     net.drain()
 
 
-def reduce_all(grads, far, gtaps, ggain, ghead):
+def reduce_all(grads, far, backs):
     cell = (4, 4, 16, 128)
     return call(
         reduce_body, "reduce_grads", 6,
         {
             "gl": ("h", grads[0]), "e0a": ("v", grads[1]), "e0b": ("v", grads[2]), "e0o": ("v", grads[3]),
             "far_e": ("v", far[0]), "far_l": ("v", far[1]), "far_o": ("v", far[2]),
-            "gtaps": ("v", gtaps), "ggain": ("v", ggain), "ghead": ("v", ghead),
+            **{
+                key + str(n): ("v", getattr(backs[n], key)) for n in range(2) for key in ("gtaps", "ggain", "ghead")
+            },
         },
         {
-            "inner": in_vmem(24, INNER), "bc": in_vmem(24, 2 * STATE), "step": in_vmem(24, 128),
-            "gate": in_vmem(24, INNER), "out": in_vmem(48, D), "blob": in_vmem(16, 128),
+            "inner": in_vmem(24, INNER), "bc": in_vmem(24, 2 * STATE), "step": in_vmem(24, HEADS),
+            "gate": in_vmem(24, INNER), "out": in_vmem(48, D), "conv_inner": in_vmem(5, 48), "mid": in_vmem(1, 48),
+            "norm": in_vmem(1, 24), "conv_bc": in_vmem(5, 4), "head": in_vmem(3, 3),
         },
         {
             **{
@@ -1583,53 +1717,33 @@
     )
 
 
-def step_lanes(step):
-    lead = step.shape[0]
-    return jnp.pad(step.reshape(lead, OWNERS, 3), ((0, 0), (0, 0), (0, 5))).reshape(lead, 128)
-
-
-def small_blob(norm_gain, inner_gain, conv_inner, conv_bc, heads):
-    def row(value):
-        return jnp.pad(value.astype(F32), ((0, 0), (0, 128 - value.shape[1])))
-
-    return jnp.concatenate(
-        [
-            row(conv_inner), row(inner_gain[None]), row(norm_gain[None]), jnp.zeros((1, 128), F32),
-            row(conv_bc), row(heads),
-        ],
-        axis=0,
-    )
-
-
-def settle(section, first_value, second_value):
-    own = jnp.where(section == 0, first_value, second_value)
-    got = lax.ppermute(jnp.where(section == 0, second_value, first_value), "section", [(0, 1), (1, 0)])
-    return jnp.stack([jnp.where(section == 0, own, got), jnp.where(section == 0, got, own)])
+def deliver_body(*refs):
+    count = len(refs) // 2
+    for given, made in zip(refs[:count], refs[count:]):
+        made[...] = given[...]
+
+
+def deliver(*arrays):
+    return pl.pallas_call(
+        deliver_body,
+        out_shape=tuple(jax.ShapeDtypeStruct(value.shape, value.dtype) for value in arrays),
+        in_specs=[pl.BlockSpec(memory_space=pltpu.VMEM)] * len(arrays),
+        out_specs=(pl.BlockSpec(memory_space=pltpu.VMEM),) * len(arrays),
+        compiler_params=pltpu.CompilerParams(vmem_limit_bytes=VMEM_LIMIT),
+        name="deliver",
+    )(*arrays)
 
 
 def per_device(
     block_input, cotangent, seg_groups, norm_gain, w_gate, w_inner, w_bc, w_step, conv_inner, conv_bc, head_params,
     inner_gain, w_out,
 ):
-    section = lax.axis_index("section")
-    seq_pos = lax.axis_index("seq")
     shards = {
-        "inner": w_inner[0], "bc": w_bc[0], "step": step_lanes(w_step[0]), "gate": w_gate[0], "out": w_out[0],
-        "blob": small_blob(norm_gain[0], inner_gain[0], conv_inner[0], conv_bc[0], head_params[0]),
+        "inner": w_inner[0], "bc": w_bc[0], "step": w_step[0], "gate": w_gate[0], "out": w_out[0],
+        "norm": norm_gain, "mid": inner_gain, "conv_inner": conv_inner[0], "conv_bc": conv_bc[0], "head": head_params[0],
     }
-    firsts = (BLOCKS - seg_groups[0]) * (BLOCK_LEN // TOK)
-    first = jnp.where(section == 0, firsts[0], firsts[1])
-    at_start = seq_pos == first
-    flags = jnp.stack(
-        [
-            seq_pos >= first,
-            jnp.logical_not(at_start) | ((section == 1) & (first == 0)),
-            at_start & (section == 1) & (first != 0),
-            (section == 0) & (seq_pos == 15) & (firsts[1] != 0),
-        ]
-    ).astype(F32)
-
-    x = lax.dynamic_index_in_dim(block_input[0], section, 0, keepdims=False)
+    flags = seg_groups
+    x = block_input[0]
     start = block_forward(0, flags, x, shards)
     weights = (
         (start.w0.reshape(2, D, HALF), start.wo0.reshape(2, INNER, WALF)),
@@ -1638,7 +1752,7 @@
     kept = [start, block_forward(1, flags, start.result, weights[1] + (start,))]
     inputs = [x, start.result]
 
-    g = lax.dynamic_index_in_dim(cotangent[0], section, 0, keepdims=False)
+    g = cotangent[0]
     grads = None
     backs = [None, None]
     for layer in (1, 0):
@@ -1650,24 +1764,19 @@
         grad_late = dot32(hidden, back.both_gl.reshape(2 * TOK, LCOLS), ((0,), (0,))).astype(BF16)
         grads = (grad_late.reshape(4, 4, 96, LCOLS), back.eha, back.ehb, back.eho)
 
-    final = reduce_all(
-        grads, (backs[0].fin_e, backs[0].fin_l, backs[0].fin_o),
-        jnp.stack([backs[0].gtaps, backs[1].gtaps]), jnp.stack([backs[0].ggain, backs[1].ggain]),
-        jnp.stack([backs[0].ghead, backs[1].ghead]),
-    )
-    blob = final.blob
-    return (
-        settle(section, kept[0].result, kept[1].result)[None, None],
-        settle(section, backs[0].result, backs[1].result)[None, None],
-        blob[ROW_NORM : ROW_NORM + 1, :24],
+    final = reduce_all(grads, (backs[0].fin_e, backs[0].fin_l, backs[0].fin_o), backs)
+    return deliver(
+        kept[1].finals[None, None],
+        backs[0].finals[None, None],
+        final.norm,
         final.gate[None],
         final.inner[None],
         final.bc[None],
-        final.step.reshape(24, OWNERS, 8)[:, :, :3].reshape(24, HEADS)[None],
-        blob[None, 0:5, :48],
-        blob[None, 8:13, :4],
-        blob[None, 13:16, :3],
-        blob[ROW_MID : ROW_MID + 1, :48],
+        final.step[None],
+        final.conv_inner[None],
+        final.conv_bc[None],
+        final.head[None],
+        final.mid,
         final.out[None],
     )
 

time: 546 us -> 519 us (0.951)
  local copies, waits for them, and re-layouts: 17 us -> 6.44 us
  other arithmetic: 10.3 us -> 0 us
  transfers between devices with their start and end apart: 2 -> 0, of which waited for: 0 -> 0; matrix products, arithmetic and copies ran while one was open for 4% -> 0% of each run, Pallas kernels for 48% -> 0%
where the time goes in v5:
time: 519 us
  Pallas kernels  501 us (97%)
  matrix products  10.5 us (2%)
  local copies, waits for them, and re-layouts  6.44 us (1%)
    pallas_call x5, Pallas kernels, call(): pl.pallas_call(kernel, out_shape=tuple((shape for shape, _ in outputs.val...  498 us
    dot_general x2, matrix products, dot32(): lax.dot_general(left, right, (dims, ((), ())), preferred_element_type=F32)  10.5 us

profile of v5, /device:TPU:1, one launch (start us, length us, event | category | flops | bytes accessed | tf_op | source)
XLA Modules:
  0.0 518.5 jit_solution(5148585293514732598)
XLA Ops:
  0.6 1.4 copy.25.refs_10_
  2.0 1.3 copy.38
  3.3 185.1 %block_forward.2 = (f32[128,3328]{1,0:T(8,128)}, f32[128,3328]{1,0:T(8,128)}, f32[128,3328]{1,0:T(8,128)}, f32[128,3072]{1,0:T(8,128)}, f32[128,128]{1,0:T(8,128...) custom-call(s32[1,2]{1,0:T(1,128)} %refs_0_.7, ...), custom_call_target="tpu_custom_call" | custom-call | tf_op jit(solution)/shard_map/block_forward/pallas_call | solution.py:153
  188.3 50.3 %block_forward.3 = (f32[128,3328]{1,0:T(8,128)}, f32[128,3328]{1,0:T(8,128)}, f32[128,3328]{1,0:T(8,128)}, f32[128,3072]{1,0:T(8,128)}, f32[128,128]{1,0:T(8,128...) custom-call(s32[1,2]{1,0:T(1,128)} %refs_0_.7, ...), custom_call_target="tpu_custom_call" | custom-call | tf_op jit(solution)/shard_map/block_forward/pallas_call | solution.py:153
  238.7 0.0 copy-start.1
  238.7 74.1 %block_backward.2 = (bf16[128,1536]{1,0:T(8,128)(2,1)}, bf16[2,128,1792]{2,1,0:T(8,128)(2,1)}, f32[8,3328]{1,0:T(8,128)}, f32[8,1536]{1,0:T(8,128)}, f32[8,128]{...) custom-call(s32[1,2]{1,0:T(1,128)} %refs_0_.7, ...), custom_call_target="tpu_custom_call" | custom-call | tf_op jit(solution)/shard_map/block_backward/pallas_call | solution.py:153
  312.8 0.0 copy-done.1
  312.8 5.2 %bitcast_convert_fusion.1 = bf16[1536,1792]{1,0:T(8,128)(2,1)} fusion(bf16[2,128,1536]{2,1,0:T(8,128)(2,1)S(1)} %copy-done.1, bf16[2,128,1792]{2,1,0:T(8,128)(2,1)} %get-tuple-element.116), kind=kOutput, calls=%fused_computation.1 | convolution fusion | flops 1412038656 | bytes 7208960 | tf_op jit(solution)/shard_map/dot_general | solution.py:41
  318.0 0.0 copy-start
  318.0 114.8 %block_backward.3 = (bf16[128,1536]{1,0:T(8,128)(2,1)}, bf16[2,128,1792]{2,1,0:T(8,128)(2,1)}, f32[8,3328]{1,0:T(8,128)}, f32[8,1536]{1,0:T(8,128)}, f32[8,128]{...) custom-call(s32[1,2]{1,0:T(1,128)} %refs_0_.7, ...), custom_call_target="tpu_custom_call" | custom-call | tf_op jit(solution)/shard_map/block_backward/pallas_call | solution.py:153
  432.8 0.0 copy-done
  432.8 5.2 %bitcast_convert_fusion = bf16[1536,1792]{1,0:T(8,128)(2,1)} fusion(bf16[2,128,1536]{2,1,0:T(8,128)(2,1)S(1)} %copy-done, bf16[2,128,1792]{2,1,0:T(8,128)(2,1)} %get-tuple-element.121), kind=kOutput, calls=%fused_computation | convolution fusion | flops 1412038656 | bytes 7208960 | tf_op jit(solution)/shard_map/dot_general | solution.py:41
  438.0 73.5 %reduce_grads.1 = (f32[24,3072]{1,0:T(8,128)}, f32[24,256]{1,0:T(8,128)}, f32[24,48]{1,0:T(8,128)}, f32[24,3072]{1,0:T(8,128)}, f32[48,1536]{1,0:T(8,128)}, /*in...) custom-call(bf16[4,4,96,1792]{3,2,1,0:T(8,128)(2,1)} %bitcast.45, ...), custom_call_target="tpu_custom_call" | custom-call | tf_op jit(solution)/shard_map/reduce_grads/pallas_call | solution.py:153
  511.5 3.2 deliver.1
  514.7 1.2 copy.32
  516.0 1.3 copy.31
  517.3 1.3 copy.30
Async XLA Ops:
  238.7 74.1 %copy-start.1 = (bf16[2,128,1536]{2,1,0:T(8,128)(2,1)S(1)}, bf16[2,128,1536]{2,1,0:T(8,128)(2,1)}, u32[]{:S(2)}) copy-start(bf16[2,128,1536]{2,1,0:T(8,128)(2,1)} %get-tuple-element.86) | copy-start | bytes 2359300
  318.0 114.8 %copy-start = (bf16[2,128,1536]{2,1,0:T(8,128)(2,1)S(1)}, bf16[2,128,1536]{2,1,0:T(8,128)(2,1)}, u32[]{:S(2)}) copy-start(bf16[2,128,1536]{2,1,0:T(8,128)(2,1)} %get-tuple-element.103) | copy-start | bytes 2359300

commit v6 on v5

--- a/solution.py
+++ b/solution.py
@@ -389,8 +389,10 @@
     r.blob[0:5, 0:48] = r.conv_inner[...].astype(F32)
     r.blob[ROW_MID : ROW_MID + 1, 0:48] = r.mid[...].astype(F32)
     r.blob[ROW_NORM : ROW_NORM + 1, 0:24] = r.norm[...].astype(F32)
-    r.blob[8:13, 0:4] = r.conv_bc[...].astype(F32)
-    r.blob[13:16, 0:3] = r.head[...]
+    r.square_s[...] = jnp.zeros_like(r.square_s)
+    r.square_s[0:4, 0:5] = r.conv_bc[0].astype(F32)
+    r.blob[8:13, 0:4] = r.square_s[...].T[0:5, 0:4]
+    r.blob[13:16, 0:3] = r.head[:, 0, :]
     given = pl.ds(pl.multiple_of((1 - c) * WALF, 128), WALF)
     swaps = [
         net.go(r.mine.at[1 - c], r.half.at[c], sibling()),
@@ -439,15 +441,16 @@
             moved = pltpu.roll(second_tile(4 * j), 8 * j, 1) if j else second_tile(0)
             heads = jnp.where((lane >= 8 * j) & (lane < 8 * j + 3), moved, heads)
         r.heads[layer] = heads
+    ga.relay(3)
     after.rows_in()
-    ga.relay(3)
     ga.relay(2)
+    for j in (0, 1, 3):
+        ga.last(j)
     after.spread(1)
     after.spread(3)
-    for j in (0, 1, 3, 2):
-        ga.last(j)
+    ga.last(2)
+    ga.end()
     after.spread(2)
-    ga.end()
 
 
 TURNS = (1, 4, 3, 12, 5, 15, 7, 13, 2, 8, 6, 9, 14, 11, 10)
@@ -743,10 +746,9 @@
         r.side[:, cols] = dot32(r.hidden[...], r.w_s[1, :, cols])
         return carry
 
-    lax.fori_loop(0, HALF // 256, project_side, 0)
-    if rider:
-        ga.relay(0)
-    r.move("pre", "side")
+    early_tiles = 1 if rider else HALF // 256
+    lax.fori_loop(0, early_tiles, project_side, 0)
+    r.move("pre")
     pairs = [net.go(r.hidden, r.both_hidden.at[section], sibling())]
     owns = [fetch(r.hidden, r.both_hidden.at[section], r.load.at[3])]
     step = r.side[:, :128].astype(BF16).astype(F32) + heads[ROW_BIAS : ROW_BIAS + 1]
@@ -801,6 +803,10 @@
 
     lax.fori_loop(0, 8, states, 0)
     r.move("act", "dact")
+    lax.fori_loop(early_tiles, HALF // 256, project_side, 0)
+    r.move("side")
+    if rider:
+        ga.relay(0)
     if rider:
         ga.relay(1)
     for d in range(1, OWNERS):
@@ -888,25 +894,6 @@
             ga.last(j)
         ga.end()
         bulk.drain()
-    if not rider:
-        cross = [
-            pltpu.make_async_remote_copy(
-                src_ref=src, dst_ref=r.finals.at[section], send_sem=r.final_s.at[0], recv_sem=r.final_s.at[1],
-                device_id=sibling(), device_id_type=MESH,
-            )
-            for src in (r.result, r.x)
-        ]
-        stay = [pltpu.make_async_copy(src, r.finals.at[section], r.final_s.at[2]) for src in (r.x, r.result)]
-        for n in range(2):
-
-            @pl.when(section == n)
-            def _():
-                cross[n].start()
-                stay[n].start()
-
-        cross[0].wait_recv()
-        cross[0].wait_send()
-        stay[0].wait()
     r.moved("pre", "side", "act", "dact", "raw", "y")
     save.wait()
     for copy in owns:
@@ -950,9 +937,6 @@
         "load": dma_sems(6), "pair_send": dma_sems(2), "pair_recv": dma_sems(2),
         **exchange_scratch(),
     }
-    if not rider:
-        outputs["finals"] = in_hbm(2, TOK, D)
-        scratch["final_s"] = dma_sems(3)
     if rider:
         outputs.update({
             "w0": in_hbm(2, 4, 4, 96, HALF), "wo0": in_hbm(2, 4, 4, 4, 48, WALF),
@@ -962,6 +946,7 @@
         scratch.update({
             "mine": pltpu.VMEM((2, 48, CUT), BF16), "half": pltpu.VMEM((2, 48, CUT), BF16),
             "wide": pltpu.VMEM((24, 128), F32), "blob": pltpu.VMEM((16, 128), F32),
+            "square_s": pltpu.VMEM((128, 128), F32),
             "half_o": pltpu.VMEM((2, 48, WALF), BF16), "cells": pltpu.VMEM((2, 4, 4, 4, 16, 128), F32),
             "net_send": dma_sems(400), "net_recv": dma_sems(400),
         })
@@ -1441,15 +1426,16 @@
 
     tail_cols = HALF - LCOLS
     side_cols = pl.ds(0, GATE0)
+    both_gl = r.both_gl if rider else r.gl2
     moves = (
-        net_copy(net, r.gpre.at[:, pl.ds(LCOLS, tail_cols)], r.both_gl.at[0, :, pl.ds(0, tail_cols)], 2),
-        net_copy(net, r.gside.at[:, side_cols], r.both_gl.at[0, :, pl.ds(tail_cols, GATE0)], 3),
-        net_copy(net, r.gpre.at[:, pl.ds(0, LCOLS)], r.both_gl.at[1], 2),
+        net_copy(net, r.gpre.at[:, pl.ds(LCOLS, tail_cols)], both_gl.at[0, :, pl.ds(0, tail_cols)], 2),
+        net_copy(net, r.gside.at[:, side_cols], both_gl.at[0, :, pl.ds(tail_cols, GATE0)], 3),
+        net_copy(net, r.gpre.at[:, pl.ds(0, LCOLS)], both_gl.at[1], 2),
     )
     keeps = (
-        pltpu.make_async_copy(r.gpre.at[:, pl.ds(LCOLS, tail_cols)], r.both_gl.at[1, :, pl.ds(0, tail_cols)], r.load.at[1]),
-        pltpu.make_async_copy(r.gside.at[:, side_cols], r.both_gl.at[1, :, pl.ds(tail_cols, GATE0)], r.load.at[2]),
-        pltpu.make_async_copy(r.gpre.at[:, pl.ds(0, LCOLS)], r.both_gl.at[0], r.load.at[1]),
+        pltpu.make_async_copy(r.gpre.at[:, pl.ds(LCOLS, tail_cols)], both_gl.at[1, :, pl.ds(0, tail_cols)], r.load.at[1]),
+        pltpu.make_async_copy(r.gside.at[:, side_cols], both_gl.at[1, :, pl.ds(tail_cols, GATE0)], r.load.at[2]),
+        pltpu.make_async_copy(r.gpre.at[:, pl.ds(0, LCOLS)], both_gl.at[0], r.load.at[1]),
     )
 
     @pl.when(section == 0)
@@ -1492,31 +1478,9 @@
     dx = scaled * inv_x - x * (dots * inv_x * inv_x * inv_x / D)
     r.result[...] = (g_ref[...].astype(F32) + dx).astype(BF16)
     r.ggain[...] = jnp.broadcast_to(jnp.sum(grad * x * inv_x, axis=0, keepdims=True), (8, D))
-    for kind in range(3):
-        early.settle(kind)
     if rider:
         early_end.last(r.fin_e, r.fin_o)
         late_end.last(r.fin_l)
-    if rider:
-        cross = [
-            pltpu.make_async_remote_copy(
-                src_ref=src, dst_ref=r.finals.at[section], send_sem=r.final_s.at[0], recv_sem=r.final_s.at[1],
-                device_id=sibling(), device_id_type=MESH,
-            )
-            for src in (r.g, r.result)
-        ]
-        stay = [pltpu.make_async_copy(src, r.finals.at[section], r.final_s.at[2]) for src in (r.result, r.g)]
-        for n in range(2):
-
-            @pl.when(section == n)
-            def _():
-                cross[n].start()
-                stay[n].start()
-
-        cross[0].wait_recv()
-        cross[0].wait_send()
-        stay[0].wait()
-    bulk.drain()
 
     @pl.when(section == 0)
     def _():
@@ -1533,6 +1497,22 @@
         moves[0].wait_recv()
         moves[1].wait_recv()
 
+    if not rider:
+        tile = r.stage_l.shape[1]
+        late_grads = jnp.concatenate([r.gl2[0], r.gl2[1]], axis=0)
+        writes = []
+        for n in range(D // tile):
+            rows = pl.ds(n * tile, tile)
+            if n >= 2:
+                writes[n - 2].wait()
+            r.stage_l[n % 2] = dot32(r.hid2[:, rows], late_grads, ((0,), (0,))).astype(BF16)
+            writes.append(fetch(r.stage_l.at[n % 2], r.glate.at[rows], r.late_s.at[n % 2]))
+    for kind in range(3):
+        early.settle(kind)
+    if not rider:
+        for copy in writes[-2:]:
+            copy.wait()
+    bulk.drain()
     net.drain()
     halo.drain()
     ex.drain()
@@ -1558,14 +1538,14 @@
     for key in ("side", "y", "act", "raw", "dact", "pre"):
         inputs[key] = ("p", getattr(kept, key))
     outputs = {
-        "result": in_vmem(TOK, D, dtype=BF16), "both_gl": in_hbm(2, TOK, LCOLS),
+        "result": in_vmem(TOK, D, dtype=BF16),
         "gtaps": in_vmem(8, CONV), "ggain": in_vmem(8, D), "ghead": in_vmem(8, 128),
         "ge": in_hbm(D, ECOLS), "go": in_hbm(INNER, WALF),
         **fold_targets("e", ECOLS, True, lambda *shape: in_vmem(*shape, dtype=BF16)),
     }
     tile = pltpu.VMEM((TOK, 128), F32)
     edge = pltpu.VMEM((8, CONV), F32)
-    slots, tile_rows = (2, 128) if rider else (4, 512)
+    slots, tile_rows = (2, 128) if rider else (3, 512)
     scratch = {
         "wo_s": pltpu.VMEM((slots, 2, 384, WALF), BF16), "w_s": pltpu.VMEM((slots, 256, HALF), BF16),
         "wo_load": dma_sems(slots), "w_load": dma_sems(slots), "load": dma_sems(5),
@@ -1581,10 +1561,14 @@
         "pair_send": dma_sems(4), "pair_recv": dma_sems(4),
         **exchange_scratch(), **fold_scratch("e", ECOLS, True), **net_scratch(64),
     }
+    if not rider:
+        outputs["glate"] = in_hbm(D, LCOLS)
+        scratch.update({
+            "gl2": pltpu.VMEM((2, TOK, LCOLS), BF16), "stage_l": pltpu.VMEM((2, 256, LCOLS), BF16), "late_s": dma_sems(2),
+        })
     if rider:
+        outputs["both_gl"] = in_hbm(2, TOK, LCOLS)
         inputs.update({"gl": ("h", grads[0]), "e1a": ("v", grads[1]), "e1b": ("v", grads[2]), "e1o": ("v", grads[3])})
-        outputs["finals"] = in_hbm(2, TOK, D)
-        scratch["final_s"] = dma_sems(3)
         outputs.update({"fin_e": in_vmem(24, ECOLS), "fin_l": in_vmem(24, LCOLS), "fin_o": in_vmem(48, WALF)})
         scratch.update(fold_scratch("l", LCOLS, False))
         scratch.update(fold_targets("l", LCOLS, False, lambda *shape: pltpu.VMEM(shape, BF16)))
@@ -1604,6 +1588,24 @@
     early_end = Finish(net, r, "e", ECOLS, (r.e0a, r.e0b, r.e0o))
     early_end.second()
     late_end = Finish(net, r, "l", LCOLS, late.h)
+    results = []
+    for n, (first, second, target) in enumerate(((r.y0, r.y1, r.ys), (r.x0, r.x1, r.xs))):
+        cross = [
+            pltpu.make_async_remote_copy(
+                src_ref=src, dst_ref=target.at[c], send_sem=r.final_s.at[3 * n], recv_sem=r.final_s.at[3 * n + 1],
+                device_id=sibling(), device_id_type=MESH,
+            )
+            for src in (second, first)
+        ]
+        stay = [pltpu.make_async_copy(src, target.at[c], r.final_s.at[3 * n + 2]) for src in (first, second)]
+        for core in range(2):
+
+            @pl.when(c == core)
+            def _():
+                cross[core].start()
+                stay[core].start()
+
+        results.append((cross[0], stay[0]))
     row = lax.broadcasted_iota(jnp.int32, (8, 128), 0)
     lane = lane_at((8, 128))
     for layer in range(2):
@@ -1647,15 +1649,23 @@
     for copy in hops:
         copy.wait_recv()
     blob = r.in_x[0] + r.in_x[1] + r.in_x[2] + r.in_x[3]
-    r.conv_inner[...] = blob[0:5, :48]
+    for n in range(5):
+        r.conv_inner[n] = blob[n : n + 1, :48]
     r.mid[...] = blob[ROW_MID : ROW_MID + 1, :48]
     r.norm[...] = blob[ROW_NORM : ROW_NORM + 1, :24]
-    r.conv_bc[...] = blob[8:13, :4]
-    r.head[...] = blob[13:16, :3]
+    r.square_s[...] = jnp.zeros_like(r.square_s)
+    r.square_s[0:16, :] = blob
+    r.conv_bc[0] = r.square_s[...].T[0:4, 8:13]
+    for n in range(3):
+        r.head[n] = blob[13 + n : 14 + n, :3]
     late_end.last(r.near_l)
     others.append(net.go(r.near_l, r.got_near_l, sibling()))
     for copy in others:
         copy.wait_recv()
+    for cross, stay in results:
+        cross.wait_recv()
+        cross.wait_send()
+        stay.wait()
 
     def put(first_l, second_l, first_e, second_e, first_o, second_o):
         r.inner[:, :LCOLS] = first_l[...]
@@ -1684,21 +1694,23 @@
     net.drain()
 
 
-def reduce_all(grads, far, backs):
+def reduce_all(grads, far, backs, outs):
     cell = (4, 4, 16, 128)
     return call(
         reduce_body, "reduce_grads", 6,
         {
             "gl": ("h", grads[0]), "e0a": ("v", grads[1]), "e0b": ("v", grads[2]), "e0o": ("v", grads[3]),
+            "y0": ("v", outs[0]), "y1": ("v", outs[1]), "x0": ("v", backs[0].result), "x1": ("v", backs[1].result),
             "far_e": ("v", far[0]), "far_l": ("v", far[1]), "far_o": ("v", far[2]),
             **{
                 key + str(n): ("v", getattr(backs[n], key)) for n in range(2) for key in ("gtaps", "ggain", "ghead")
             },
         },
         {
+            "ys": in_hbm(2, TOK, D), "xs": in_hbm(2, TOK, D),
             "inner": in_vmem(24, INNER), "bc": in_vmem(24, 2 * STATE), "step": in_vmem(24, HEADS),
-            "gate": in_vmem(24, INNER), "out": in_vmem(48, D), "conv_inner": in_vmem(5, 48), "mid": in_vmem(1, 48),
-            "norm": in_vmem(1, 24), "conv_bc": in_vmem(5, 4), "head": in_vmem(3, 3),
+            "gate": in_vmem(24, INNER), "out": in_vmem(48, D), "conv_inner": in_vmem(5, 1, 48), "mid": in_vmem(1, 48),
+            "norm": in_vmem(1, 24), "conv_bc": in_vmem(1, 4, 5), "head": in_vmem(3, 1, 3),
         },
         {
             **{
@@ -1706,6 +1718,7 @@
                 for name in ("near_", "got_near_", "got_far_")
                 for part, shape in (("e", (24, ECOLS)), ("l", (24, LCOLS)), ("o", (48, WALF)))
             },
+            "final_s": dma_sems(6), "square_s": pltpu.VMEM((128, 128), F32),
             "cells": pltpu.VMEM((2, 4) + cell, F32), "other": pltpu.VMEM((4,) + cell, F32),
             "sum0": pltpu.VMEM((4,) + cell, F32), "in_y": pltpu.VMEM((4,) + cell, F32),
             "sum1": pltpu.VMEM(cell, F32), "in_z": pltpu.VMEM((4,) + cell[1:], F32),
@@ -1740,7 +1753,8 @@
 ):
     shards = {
         "inner": w_inner[0], "bc": w_bc[0], "step": w_step[0], "gate": w_gate[0], "out": w_out[0],
-        "norm": norm_gain, "mid": inner_gain, "conv_inner": conv_inner[0], "conv_bc": conv_bc[0], "head": head_params[0],
+        "norm": norm_gain, "mid": inner_gain, "conv_inner": conv_inner[0], "conv_bc": conv_bc.transpose(0, 2, 1),
+        "head": head_params.transpose(1, 0, 2),
     }
     flags = seg_groups
     x = block_input[0]
@@ -1760,24 +1774,23 @@
         back = block_backward(layer, flags, g, inputs[layer], w, wo, start, kept[layer], grads)
         backs[layer] = back
         g = back.result
-        hidden = kept[layer].both_hidden.reshape(2 * TOK, D)
-        grad_late = dot32(hidden, back.both_gl.reshape(2 * TOK, LCOLS), ((0,), (0,))).astype(BF16)
+        if layer == 1:
+            grad_late = back.glate
+        else:
+            hidden = kept[layer].both_hidden.reshape(2 * TOK, D)
+            grad_late = dot32(hidden, back.both_gl.reshape(2 * TOK, LCOLS), ((0,), (0,))).astype(BF16)
         grads = (grad_late.reshape(4, 4, 96, LCOLS), back.eha, back.ehb, back.eho)
 
-    final = reduce_all(grads, (backs[0].fin_e, backs[0].fin_l, backs[0].fin_o), backs)
-    return deliver(
-        kept[1].finals[None, None],
-        backs[0].finals[None, None],
-        final.norm,
-        final.gate[None],
-        final.inner[None],
-        final.bc[None],
-        final.step[None],
-        final.conv_inner[None],
-        final.conv_bc[None],
-        final.head[None],
-        final.mid,
-        final.out[None],
+    final = reduce_all(
+        grads, (backs[0].fin_e, backs[0].fin_l, backs[0].fin_o), backs, (kept[0].result, kept[1].result)
+    )
+    ys, xs, norm, gate, inner, bc, step, conv_inner_grad, conv_bc_grad, head, mid, out = deliver(
+        final.ys[None, None], final.xs[None, None], final.norm, final.gate[None], final.inner[None], final.bc[None],
+        final.step[None], final.conv_inner, final.conv_bc, final.head, final.mid, final.out[None],
+    )
+    return (
+        ys, xs, norm, gate, inner, bc, step, conv_inner_grad.transpose(1, 0, 2), conv_bc_grad.transpose(0, 2, 1),
+        head.transpose(1, 0, 2), mid, out,
     )
 
 

time: 519 us -> 508 us (0.979)
  local copies, waits for them, and re-layouts: 6.44 us -> 0.01 us
  matrix products: 10.5 us -> 5.24 us
    dot_general x2 -> x1, matrix products: 10.5 us -> 5.24 us  [dot32(): lax.dot_general(left, right, (dims, ((), ())), preferred_element_type=F32)]
where the time goes in v6:
time: 508 us; the launch traced here: 507 us
  Pallas kernels  501 us (99%)
  matrix products  5.24 us (1%)
    pallas_call x5, Pallas kernels, call(): pl.pallas_call(kernel, out_shape=tuple((shape for shape, _ in outputs.val...  498 us

profile of v6, /device:TPU:1, one launch (start us, length us, event | category | flops | bytes accessed | tf_op | source)
XLA Modules:
  0.0 507.0 jit_solution(2083432161390635813)
XLA Ops:
  0.6 184.2 %block_forward.2 = (f32[128,3328]{1,0:T(8,128)}, f32[128,3328]{1,0:T(8,128)}, f32[128,3328]{1,0:T(8,128)}, f32[128,3072]{1,0:T(8,128)}, f32[128,128]{1,0:T(8,128...) custom-call(s32[1,2]{1,0:T(1,128)} %refs_0_.7, ...), custom_call_target="tpu_custom_call" | custom-call | tf_op jit(solution)/shard_map/block_forward/pallas_call | solution.py:153
  184.8 52.3 %block_forward.3 = (f32[128,3328]{1,0:T(8,128)}, f32[128,3328]{1,0:T(8,128)}, f32[128,3328]{1,0:T(8,128)}, f32[128,3072]{1,0:T(8,128)}, f32[128,128]{1,0:T(8,128...) custom-call(s32[1,2]{1,0:T(1,128)} %refs_0_.7, ...), custom_call_target="tpu_custom_call" | custom-call | tf_op jit(solution)/shard_map/block_forward/pallas_call | solution.py:153
  237.2 76.8 %block_backward.2 = (bf16[128,1536]{1,0:T(8,128)(2,1)}, f32[8,3328]{1,0:T(8,128)}, f32[8,1536]{1,0:T(8,128)}, f32[8,128]{1,0:T(8,128)}, bf16[1536,1536]{1,0:T(8,...) custom-call(s32[1,2]{1,0:T(1,128)} %refs_0_.7, ...), custom_call_target="tpu_custom_call" | custom-call | tf_op jit(solution)/shard_map/block_backward/pallas_call | solution.py:153
  314.0 0.0 copy-start
  314.0 115.1 %block_backward.3 = (bf16[128,1536]{1,0:T(8,128)(2,1)}, f32[8,3328]{1,0:T(8,128)}, f32[8,1536]{1,0:T(8,128)}, f32[8,128]{1,0:T(8,128)}, bf16[1536,1536]{1,0:T(8,...) custom-call(s32[1,2]{1,0:T(1,128)} %refs_0_.7, ...), custom_call_target="tpu_custom_call" | custom-call | tf_op jit(solution)/shard_map/block_backward/pallas_call | solution.py:153
  429.1 0.0 copy-done
  429.1 5.2 %bitcast_convert_fusion = bf16[1536,1792]{1,0:T(8,128)(2,1)} fusion(bf16[2,128,1536]{2,1,0:T(8,128)(2,1)S(1)} %copy-done, bf16[2,128,1792]{2,1,0:T(8,128)(2,1)} %get-tuple-element.133), kind=kOutput, calls=%fused_computation | convolution fusion | flops 1412038656 | bytes 7208960 | tf_op jit(solution)/shard_map/dot_general | solution.py:41
  434.4 69.3 %reduce_grads.1 = (bf16[2,128,1536]{2,1,0:T(8,128)(2,1)}, bf16[2,128,1536]{2,1,0:T(8,128)(2,1)}, f32[24,3072]{1,0:T(8,128)}, f32[24,256]{1,0:T(8,128)}, f32[24,4...) custom-call(bf16[4,4,96,1792]{3,2,1,0:T(8,128)(2,1)} %bitcast.38, ...), custom_call_target="tpu_custom_call" | custom-call | tf_op jit(solution)/shard_map/reduce_grads/pallas_call | solution.py:153
  503.7 3.2 deliver.1
Async XLA Ops:
  314.0 115.1 %copy-start = (bf16[2,128,1536]{2,1,0:T(8,128)(2,1)S(1)}, bf16[2,128,1536]{2,1,0:T(8,128)(2,1)}, u32[]{:S(2)}) copy-start(bf16[2,128,1536]{2,1,0:T(8,128)(2,1)} %get-tuple-element.92) | copy-start | bytes 2359300

commit v7 on v6

--- a/solution.py
+++ b/solution.py
@@ -749,6 +749,8 @@
     early_tiles = 1 if rider else HALF // 256
     lax.fori_loop(0, early_tiles, project_side, 0)
     r.move("pre")
+    if not rider:
+        r.move("side")
     pairs = [net.go(r.hidden, r.both_hidden.at[section], sibling())]
     owns = [fetch(r.hidden, r.both_hidden.at[section], r.load.at[3])]
     step = r.side[:, :128].astype(BF16).astype(F32) + heads[ROW_BIAS : ROW_BIAS + 1]
@@ -803,9 +805,9 @@
 
     lax.fori_loop(0, 8, states, 0)
     r.move("act", "dact")
-    lax.fori_loop(early_tiles, HALF // 256, project_side, 0)
-    r.move("side")
     if rider:
+        lax.fori_loop(early_tiles, HALF // 256, project_side, 0)
+        r.move("side")
         ga.relay(0)
     if rider:
         ga.relay(1)

time: 508 us -> 507 us (level)
  no operation moved by 1% of the time
where the time goes in v7:
time: 507 us
  Pallas kernels  501 us (99%)
  matrix products  5.24 us (1%)
    pallas_call x5, Pallas kernels, call(): pl.pallas_call(kernel, out_shape=tuple((shape for shape, _ in outputs.val...  497 us

profile of v7, /device:TPU:1, one launch (start us, length us, event | category | flops | bytes accessed | tf_op | source)
XLA Modules:
  0.0 506.7 jit_solution(7971670549894175686)
XLA Ops:
  0.6 184.2 %block_forward.2 = (f32[128,3328]{1,0:T(8,128)}, f32[128,3328]{1,0:T(8,128)}, f32[128,3328]{1,0:T(8,128)}, f32[128,3072]{1,0:T(8,128)}, f32[128,128]{1,0:T(8,128...) custom-call(s32[1,2]{1,0:T(1,128)} %refs_0_.7, ...), custom_call_target="tpu_custom_call" | custom-call | tf_op jit(solution)/shard_map/block_forward/pallas_call | solution.py:153
  184.8 52.3 %block_forward.3 = (f32[128,3328]{1,0:T(8,128)}, f32[128,3328]{1,0:T(8,128)}, f32[128,3328]{1,0:T(8,128)}, f32[128,3072]{1,0:T(8,128)}, f32[128,128]{1,0:T(8,128...) custom-call(s32[1,2]{1,0:T(1,128)} %refs_0_.7, ...), custom_call_target="tpu_custom_call" | custom-call | tf_op jit(solution)/shard_map/block_forward/pallas_call | solution.py:153
  237.2 76.9 %block_backward.2 = (bf16[128,1536]{1,0:T(8,128)(2,1)}, f32[8,3328]{1,0:T(8,128)}, f32[8,1536]{1,0:T(8,128)}, f32[8,128]{1,0:T(8,128)}, bf16[1536,1536]{1,0:T(8,...) custom-call(s32[1,2]{1,0:T(1,128)} %refs_0_.7, ...), custom_call_target="tpu_custom_call" | custom-call | tf_op jit(solution)/shard_map/block_backward/pallas_call | solution.py:153
  314.0 0.0 copy-start
  314.0 115.5 %block_backward.3 = (bf16[128,1536]{1,0:T(8,128)(2,1)}, f32[8,3328]{1,0:T(8,128)}, f32[8,1536]{1,0:T(8,128)}, f32[8,128]{1,0:T(8,128)}, bf16[1536,1536]{1,0:T(8,...) custom-call(s32[1,2]{1,0:T(1,128)} %refs_0_.7, ...), custom_call_target="tpu_custom_call" | custom-call | tf_op jit(solution)/shard_map/block_backward/pallas_call | solution.py:153
  429.6 0.0 copy-done
  429.6 5.2 %bitcast_convert_fusion = bf16[1536,1792]{1,0:T(8,128)(2,1)} fusion(bf16[2,128,1536]{2,1,0:T(8,128)(2,1)S(1)} %copy-done, bf16[2,128,1792]{2,1,0:T(8,128)(2,1)} %get-tuple-element.133), kind=kOutput, calls=%fused_computation | convolution fusion | flops 1412038656 | bytes 7208960 | tf_op jit(solution)/shard_map/dot_general | solution.py:41
  434.8 68.5 %reduce_grads.1 = (bf16[2,128,1536]{2,1,0:T(8,128)(2,1)}, bf16[2,128,1536]{2,1,0:T(8,128)(2,1)}, f32[24,3072]{1,0:T(8,128)}, f32[24,256]{1,0:T(8,128)}, f32[24,4...) custom-call(bf16[4,4,96,1792]{3,2,1,0:T(8,128)(2,1)} %bitcast.38, ...), custom_call_target="tpu_custom_call" | custom-call | tf_op jit(solution)/shard_map/reduce_grads/pallas_call | solution.py:153
  503.4 3.2 deliver.1
Async XLA Ops:
  314.0 115.6 %copy-start = (bf16[2,128,1536]{2,1,0:T(8,128)(2,1)S(1)}, bf16[2,128,1536]{2,1,0:T(8,128)(2,1)}, u32[]{:S(2)}) copy-start(bf16[2,128,1536]{2,1,0:T(8,128)(2,1)} %get-tuple-element.92) | copy-start | bytes 2359300
